TPU v7x, 32 devices: a whole 2x2x4 slice. The times are simulated.
32 devices in a mesh: fsdp: 8 (over y, x, core), rep: 4 (over z).
Axes of the slice: x: 2, y: 2, z: 4, core: 2. Of those that a mesh axis runs over, the one named last changes fastest.
Arguments:
- tokens: bfloat16 [16384, 768], P(('fsdp', 'rep')), may hold values from -6 to 6
- cotangent: bfloat16 [16384, 768], P(('fsdp', 'rep')), may hold values from -6 to 6
- segment_ids: int32 [64, 256], P(('fsdp', 'rep')), may hold values from 0 to 2, never falling along the last dimension, each value on 1 to 128 neighbouring positions
- block_slot_index: int32 [108], replicated, may hold values from 0 to 111, as said below
- weights: float32 [112, 256, 256], P('fsdp')
- first_moment: float32 [112, 256, 256], P('fsdp')
- second_moment: float32 [112, 256, 256], P('fsdp'), as said below
- left_basis: float32 [112, 256, 256], P('fsdp'), as said below
- right_basis: float32 [112, 256, 256], P('fsdp'), as said below
- norm_gains: float32 [2, 768], replicated, may hold values from 0.25 to 1.75
- gain_first: float32 [2, 768], replicated, may hold values from -768 to 768
- gain_second: float32 [2, 768], replicated, may hold values from 8192 to 131072
Outputs:
- block_out: bfloat16 [16384, 768], P(('fsdp', 'rep'))
- token_grad: bfloat16 [16384, 768], P(('fsdp', 'rep'))
- weight_gradients: float32 [112, 256, 256], P('fsdp')
- first_new: float32 [112, 256, 256], P('fsdp')
- second_new: float32 [112, 256, 256], P('fsdp')
- weights_new: float32 [112, 256, 256], P('fsdp')
- weights_low: bfloat16 [112, 256, 256], P('fsdp')
- gain_first_new: float32 [2, 768], replicated
- gain_second_new: float32 [2, 768], replicated
- gains_new: float32 [2, 768], replicated
Inputs may be any that keep to these rules, and one draw needn't show every extreme that they name: `block_slot_index`: distinct slot numbers. Slot s lies on fsdp device s // 14; slots that no block names are empty. `left_basis`: every 256 x 256 block is orthogonal. `right_basis`: every 256 x 256 block is orthogonal. `second_moment`: Positive.
All inputs are finite; a program needn't handle non-finite values.
Results may differ from a plain program's by a relative error of at most 0.015.
Values may be sent and summed in bfloat16 or wider, within the bound.
No kernel may reach another device: no remote copies, remote signals or barrier semaphores. Data moves between devices by JAX's collectives and lax.ppermute only.
A program may use at most 384 MiB of HBM per device.

v0:
```python
import jax
import jax.numpy as jnp
from jax import lax
from jax.sharding import PartitionSpec as P

D = 768
HEADS = 12
HEAD_DIM = 64
FF = 2048
BLOCK_ORDER = 256
STEP = 10


NORM_EPS = 1e-05
ROPE_BASE = 10000.0
BETA_ONE = 0.5
BETA_TWO = 0.5
ADAM_EPS = 1e-08
RATE = 0.03
GAIN_RATE = 0.4
DECAY = 0.01
MASKED = -1e30


def matrix_shapes():
    return [(D, D), (D, D), (D, D), (D, D), (D, FF), (D, FF), (FF, D)]


def to_matrices(blocks):
    result = []
    offset = 0
    for height, breadth in matrix_shapes():
        grid_rows = height // BLOCK_ORDER
        grid_cols = breadth // BLOCK_ORDER
        block_count = grid_rows * grid_cols
        block_grid = blocks[offset : offset + block_count].reshape(
            grid_rows, grid_cols, BLOCK_ORDER, BLOCK_ORDER
        )
        result.append(block_grid.transpose(0, 2, 1, 3).reshape(height, breadth))
        offset = offset + block_count
    return result


def split_into_blocks(matrices):
    pieces = []
    for matrix in matrices:
        height, breadth = matrix.shape
        grid_rows = height // BLOCK_ORDER
        grid_cols = breadth // BLOCK_ORDER
        pieces.append(
            matrix.reshape(grid_rows, BLOCK_ORDER, grid_cols, BLOCK_ORDER)
            .transpose(0, 2, 1, 3)
            .reshape(grid_rows * grid_cols, BLOCK_ORDER, BLOCK_ORDER)
        )
    return jnp.concatenate(pieces, axis=0)


def positions_of(segments):
    places = jnp.arange(segments.shape[0], dtype=jnp.int32)
    starts = jnp.concatenate([jnp.ones((1,), jnp.bool_), segments[1:] != segments[:-1]])
    first_place = lax.cummax(jnp.where(starts, places, 0), axis=0)
    return places - first_place


def rope_tables(positions):
    half_dim = HEAD_DIM // 2
    frequency = ROPE_BASE ** (-2.0 * jnp.arange(half_dim, dtype=jnp.float32) / HEAD_DIM)
    angles = positions.astype(jnp.float32)[:, None] * frequency[None, :]
    return (jnp.cos(angles)[:, None, :], jnp.sin(angles)[:, None, :])


def rotate(values, cosine, sine_table):
    half_dim = HEAD_DIM // 2
    lower_half = values[..., :half_dim]
    upper_half = values[..., half_dim:]
    return jnp.concatenate(
        [
            lower_half * cosine - upper_half * sine_table,
            upper_half * cosine + lower_half * sine_table,
        ],
        axis=-1,
    )


def split_heads(matrix):
    return matrix.reshape(matrix.shape[0], HEADS, HEAD_DIM)


def dot_low(operand_a, operand_b):
    return jnp.dot(operand_a, operand_b, preferred_element_type=jnp.float32)


def dot_rows(operand_a, operand_b):
    return lax.dot_general(
        operand_a, operand_b, (((0,), (0,)), ((), ())), preferred_element_type=jnp.float32
    )


def dot_back(operand_a, operand_b):
    return lax.dot_general(
        operand_a, operand_b, (((1,), (1,)), ((), ())), preferred_element_type=jnp.float32
    )


def norm_forward(hidden, gain):
    inv_rms = lax.rsqrt(jnp.mean(hidden * hidden, axis=-1, keepdims=True) + NORM_EPS)
    return (hidden * inv_rms * gain, inv_rms)


def norm_backward(hidden, inv_rms, gain, grad_out):
    scaled = grad_out * gain
    grad_in = inv_rms * scaled - hidden * inv_rms**3 * jnp.mean(
        hidden * scaled, axis=-1, keepdims=True
    )
    gain_term = jnp.sum(grad_out * hidden * inv_rms, axis=0)
    return (grad_in, gain_term)


def visible_mask(segments):
    places = jnp.arange(segments.shape[0], dtype=jnp.int32)
    return (segments[:, None] == segments[None, :]) & (places[None, :] <= places[:, None])


def attention_forward(queries, key_heads, values, segments):
    visible = visible_mask(segments)
    scores = jnp.einsum(
        "qhd,khd->hqk", queries, key_heads, preferred_element_type=jnp.float32
    ) * HEAD_DIM ** (-0.5)
    scores = jnp.where(visible[None], scores, MASKED)
    row_max = jnp.max(scores, axis=-1, keepdims=True)
    exp_scores = jnp.exp(scores - row_max)
    row_sum = jnp.sum(exp_scores, axis=-1, keepdims=True)
    probabilities = (exp_scores / row_sum).astype(jnp.bfloat16)
    outputs = jnp.einsum("hqk,khd->qhd", probabilities, values, preferred_element_type=jnp.float32)
    totals = row_max + jnp.log(row_sum)
    return (outputs, totals)


def attention_backward(queries, key_heads, values, segments, totals, grad_mixed):
    scale_factor = HEAD_DIM ** (-0.5)
    visible = visible_mask(segments)
    scores = (
        jnp.einsum("qhd,khd->hqk", queries, key_heads, preferred_element_type=jnp.float32)
        * scale_factor
    )
    probabilities = jnp.where(visible[None], jnp.exp(scores - totals), 0.0)
    grad_values = jnp.einsum(
        "hqk,qhd->khd",
        probabilities.astype(jnp.bfloat16),
        grad_mixed,
        preferred_element_type=jnp.float32,
    )
    grad_probs = jnp.einsum("qhd,khd->hqk", grad_mixed, values, preferred_element_type=jnp.float32)
    grad_scores = probabilities * (
        grad_probs - jnp.sum(probabilities * grad_probs, axis=-1, keepdims=True)
    )
    grad_low = grad_scores.astype(jnp.bfloat16)
    grad_queries = (
        jnp.einsum("hqk,khd->qhd", grad_low, key_heads, preferred_element_type=jnp.float32)
        * scale_factor
    )
    grad_keys = (
        jnp.einsum("hqk,qhd->khd", grad_low, queries, preferred_element_type=jnp.float32)
        * scale_factor
    )
    return (grad_queries, grad_keys, grad_values)


def micro_forward(token_rows, segments, matrices, norm_gains):
    w_query, w_key, w_value, w_out, w_gate, w_up, w_down = matrices
    seq_len = token_rows.shape[0]
    cosine, sine_table = rope_tables(positions_of(segments))
    queries = rotate(split_heads(dot_low(token_rows, w_query)), cosine, sine_table).astype(
        jnp.bfloat16
    )
    key_heads = rotate(split_heads(dot_low(token_rows, w_key)), cosine, sine_table).astype(
        jnp.bfloat16
    )
    values = split_heads(dot_low(token_rows, w_value)).astype(jnp.bfloat16)
    mixed_heads, totals = attention_forward(queries, key_heads, values, segments)
    attended = mixed_heads.reshape(seq_len, D).astype(jnp.bfloat16)
    hidden_one = token_rows.astype(jnp.float32) + dot_low(attended, w_out)
    normed_one, inv_one = norm_forward(hidden_one, norm_gains[0])
    normed_low = normed_one.astype(jnp.bfloat16)
    gate_proj = dot_low(normed_low, w_gate)
    up_proj = dot_low(normed_low, w_up)
    activation = (jax.nn.silu(gate_proj) * up_proj).astype(jnp.bfloat16)
    hidden_two = normed_one + dot_low(activation, w_down)
    block_out, inv_two = norm_forward(hidden_two, norm_gains[1])
    kept_values = (
        cosine,
        sine_table,
        queries,
        key_heads,
        values,
        totals,
        attended,
        hidden_one,
        inv_one,
        normed_low,
        gate_proj,
        up_proj,
        activation,
        hidden_two,
        inv_two,
    )
    return (block_out.astype(jnp.bfloat16), kept_values)


def micro_backward(kept_values, token_rows, segments, grad_output, matrices, norm_gains):
    w_query, w_key, w_value, w_out, w_gate, w_up, w_down = matrices
    (
        cosine,
        sine_table,
        queries,
        key_heads,
        values,
        totals,
        attended,
        hidden_one,
        inv_one,
        normed_low,
        gate_proj,
        up_proj,
        activation,
        hidden_two,
        inv_two,
    ) = kept_values
    seq_len = token_rows.shape[0]
    grad_hidden_two, gain_two = norm_backward(
        hidden_two, inv_two, norm_gains[1], grad_output.astype(jnp.float32)
    )
    grad_ffn = grad_hidden_two.astype(jnp.bfloat16)
    grad_w_down = dot_rows(activation, grad_ffn)
    grad_act = dot_back(grad_ffn, w_down)
    sigmoid_gate = jax.nn.sigmoid(gate_proj)
    grad_gate = (
        grad_act * up_proj * sigmoid_gate * (1.0 + gate_proj * (1.0 - sigmoid_gate))
    ).astype(jnp.bfloat16)
    grad_up = (grad_act * gate_proj * sigmoid_gate).astype(jnp.bfloat16)
    grad_w_gate = dot_rows(normed_low, grad_gate)
    grad_w_up = dot_rows(normed_low, grad_up)
    grad_normed = grad_hidden_two + dot_back(grad_gate, w_gate) + dot_back(grad_up, w_up)
    grad_hidden_one, gain_one = norm_backward(hidden_one, inv_one, norm_gains[0], grad_normed)
    grad_branch = grad_hidden_one.astype(jnp.bfloat16)
    grad_w_out = dot_rows(attended, grad_branch)
    grad_attended = dot_back(grad_branch, w_out).astype(jnp.bfloat16)
    grad_query, grad_keys, grad_values = attention_backward(
        queries, key_heads, values, segments, totals, split_heads(grad_attended)
    )
    grad_query_raw = (
        rotate(grad_query, cosine, -sine_table).reshape(seq_len, D).astype(jnp.bfloat16)
    )
    grad_key_raw = rotate(grad_keys, cosine, -sine_table).reshape(seq_len, D).astype(jnp.bfloat16)
    grad_value_raw = grad_values.reshape(seq_len, D).astype(jnp.bfloat16)
    grad_w_query = dot_rows(token_rows, grad_query_raw)
    grad_w_key = dot_rows(token_rows, grad_key_raw)
    grad_w_value = dot_rows(token_rows, grad_value_raw)
    grad_tokens = (
        grad_hidden_one
        + dot_back(grad_query_raw, w_query)
        + dot_back(grad_key_raw, w_key)
        + dot_back(grad_value_raw, w_value)
    )
    matrix_gradients = [
        grad_w_query,
        grad_w_key,
        grad_w_value,
        grad_w_out,
        grad_w_gate,
        grad_w_up,
        grad_w_down,
    ]
    return (grad_tokens.astype(jnp.bfloat16), matrix_gradients, jnp.stack([gain_one, gain_two]))


def adam_blocks(grads, weights, first_moment, second_moment, left_basis, right_basis):
    highest = lax.Precision.HIGHEST
    turned = jnp.einsum("sij,sik->sjk", left_basis, grads, precision=highest)
    turned = jnp.einsum("sjk,skl->sjl", turned, right_basis, precision=highest)
    first_new = BETA_ONE * first_moment + (1.0 - BETA_ONE) * turned
    second_new = BETA_TWO * second_moment + (1.0 - BETA_TWO) * turned * turned
    step_ratio = (
        first_new
        / (1.0 - BETA_ONE**STEP)
        / (jnp.sqrt(second_new / (1.0 - BETA_TWO**STEP)) + ADAM_EPS)
    )
    rotated_back = jnp.einsum("sij,sjk->sik", left_basis, step_ratio, precision=highest)
    rotated_back = jnp.einsum("sik,slk->sil", rotated_back, right_basis, precision=highest)
    weights_new = weights - RATE * (rotated_back + DECAY * weights)
    return (first_new, second_new, weights_new)


def adam_plain(grads, values, first_moment, second_moment):
    first_new = BETA_ONE * first_moment + (1.0 - BETA_ONE) * grads
    second_new = BETA_TWO * second_moment + (1.0 - BETA_TWO) * grads * grads
    step_ratio = (
        first_new
        / (1.0 - BETA_ONE**STEP)
        / (jnp.sqrt(second_new / (1.0 - BETA_TWO**STEP)) + ADAM_EPS)
    )
    return (first_new, second_new, values - GAIN_RATE * step_ratio)


def shards(
    tokens,
    cotangent,
    segment_ids,
    block_slot_index,
    weights,
    first_moment,
    second_moment,
    left_basis,
    right_basis,
    norm_gains,
    gain_first,
    gain_second,
):
    micro_count = segment_ids.shape[0]
    seq_len = segment_ids.shape[1]
    slot_total = weights.shape[0] * lax.axis_size("fsdp")
    owned_low = weights.astype(jnp.bfloat16)

    def gathered_matrices():
        every_slot = lax.all_gather(owned_low, "fsdp", axis=0, tiled=True)
        return to_matrices(every_slot[block_slot_index])

    outputs = []
    token_grads = []
    matrix_sums = None
    owner_sums = None
    gain_total = jnp.zeros((2, D), jnp.float32)
    for micro_step in range(micro_count):
        token_rows = tokens[micro_step * seq_len : (micro_step + 1) * seq_len]
        grad_rows = cotangent[micro_step * seq_len : (micro_step + 1) * seq_len]
        segments = segment_ids[micro_step]
        forward_mats = gathered_matrices()
        block_out, kept_values = micro_forward(token_rows, segments, forward_mats, norm_gains)
        backward_mats = gathered_matrices()
        grad_tokens, matrix_gradients, gain_grad = micro_backward(
            kept_values, token_rows, segments, grad_rows, backward_mats, norm_gains
        )
        outputs.append(block_out)
        token_grads.append(grad_tokens)
        gain_total = gain_total + gain_grad
        matrix_sums = (
            matrix_gradients
            if matrix_sums is None
            else [summed + fresh for summed, fresh in zip(matrix_sums, matrix_gradients)]
        )
    slotted = (
        jnp.zeros((slot_total, BLOCK_ORDER, BLOCK_ORDER), jnp.float32)
        .at[block_slot_index]
        .set(split_into_blocks(matrix_sums))
    )
    owner_sums = lax.psum_scatter(slotted, "fsdp", scatter_dimension=0, tiled=True)
    owner_grads = lax.psum(owner_sums.astype(jnp.bfloat16), "rep").astype(jnp.float32)
    gain_grads = lax.psum(gain_total, ("fsdp", "rep"))
    first_new, second_new, weights_new = adam_blocks(
        owner_grads, weights, first_moment, second_moment, left_basis, right_basis
    )
    gain_first_new, gain_second_new, gains_new = adam_plain(
        gain_grads, norm_gains, gain_first, gain_second
    )
    return (
        jnp.concatenate(outputs, axis=0),
        jnp.concatenate(token_grads, axis=0),
        owner_grads,
        first_new,
        second_new,
        weights_new,
        weights_new.astype(jnp.bfloat16),
        gain_first_new,
        gain_second_new,
        gains_new,
    )


def solution(mesh):
    return jax.shard_map(
        shards,
        mesh=mesh,
        in_specs=(
            P(("fsdp", "rep"), None),
            P(("fsdp", "rep"), None),
            P(("fsdp", "rep"), None),
            P(),
            P("fsdp", None, None),
            P("fsdp", None, None),
            P("fsdp", None, None),
            P("fsdp", None, None),
            P("fsdp", None, None),
            P(),
            P(),
            P(),
        ),
        out_specs=(
            P(("fsdp", "rep"), None),
            P(("fsdp", "rep"), None),
            P("fsdp", None, None),
            P("fsdp", None, None),
            P("fsdp", None, None),
            P("fsdp", None, None),
            P("fsdp", None, None),
            P(),
            P(),
            P(),
        ),
        check_vma=False,
    )
```

profile of v0, /device:TPU:0, one launch (start us, length us, event | category | flops | bytes accessed | tf_op | source)
XLA Modules:
  0.0 706.1 jit_solution(8923951169642514280)
XLA Ops:
  7.3 3.5 convert_element_type.229
  14.1 80.5 %all-gather.2.cloned.1.call-done = bf16[112,256,256]{2,1,0:T(8,128)(2,1)} async-done(((bf16[14,256,256]{2,1,0:T(8,128)(2,1)}), bf16[112,256,256]{2,1,0:T(8,128)(2,1)}) %all-gather.2.cloned.1.call-update) | async-done | bytes 14680080 | tf_op jit(solution)/shard_map/all_gather | solution.py:325
  94.6 12.8 %gather_fusion = bf16[108,256,256]{2,1,0:T(8,128)(2,1)} fusion(bf16[112,256,256]{2,1,0:T(8,128)(2,1)} %all-gather.2.cloned.1.call-done, s32[1024]{0:T(1024)S(1)} %pad_clamp_fusion), kind=kCustom, calls=%fused_computation | custom fusion | bytes 28311984 | tf_op jit(solution)/shard_map/gather | solution.py:326
  107.4 3.9 fusion.121
  111.2 5.9 fusion.120
  129.3 5.0 copy.104
  134.3 3.1 copy.147
  160.9 2.1 fusion.50
  165.9 2.1 multiply_convert_fusion.4
  178.9 3.6 fusion.36
  189.3 2.6 fusion.33
  197.1 3.8 fusion.67
  200.9 3.8 fusion.127
  204.6 3.7 fusion.126
  208.8 2.7 reshape.632
  211.5 3.8 copy.120
  216.4 2.0 copy.118
  218.3 4.5 reshape.630
  222.9 3.8 copy.119
  230.6 2.0 copy.116
  232.5 4.5 reshape.628
  237.1 3.7 copy.117
  242.5 2.0 copy.114
  244.4 3.1 reshape.626
  250.0 6.6 convolution_add_fusion
  256.6 6.7 copy.123
  263.2 8.4 %copy.150 = f32[96,8,8,256]{3,2,1,0:T(8,128)} copy(f32[96,8,8,256]{3,1,2,0:T(8,128)} %bitcast.242) | data formatting | bytes 12582912
  271.6 7.0 copy.124
  278.6 3.8 convolution_add_fusion.1
  282.4 3.0 copy.149
  285.9 2.0 copy.122
  289.7 3.0 copy.148
  293.2 2.4 copy.121
  303.9 3.5 constant_dynamic-update-slice_fusion.2
  307.4 3.3 constant_dynamic-update-slice_fusion.1
  310.7 3.3 constant_dynamic-update-slice_fusion
  313.9 13.4 %broadcast_in_dim.43 = f32[112,256,256]{2,1,0:T(8,128)} broadcast(f32[]{:T(128)} %constant.57.clone.1), dimensions={} | broadcast | bytes 29360132 | tf_op jit(solution)/shard_map/broadcast_in_dim | solution.py:352
  327.3 51.8 %scatter_fusion = f32[112,256,256]{2,1,0:T(8,128)} fusion(f32[112,256,256]{2,1,0:T(8,128)} %broadcast_in_dim.43, s32[108]{0:T(128)S(1)} %copy-done.132, f32[108,256,256]{2,1,0:T(8,128)} %constant_dynamic-update-slice_fusion), kind=kCustom, calls=%fused_computation.1 | custom fusion | bytes 84935088 | tf_op jit(solution)/shard_map/scatter | solution.py:354
  379.1 29.6 %copy.125 = f32[112,256,256]{1,2,0:T(8,128)} copy(f32[112,256,256]{2,1,0:T(8,128)} %scatter_fusion) | data formatting | bytes 58720256 | tf_op jit(solution)/shard_map/scatter | solution.py:354
  409.5 39.6 %psum.15 = f32[2,768]{1,0:T(2,128)S(1)} all-reduce(f32[2,768]{1,0:T(2,128)S(1)} %maximum_add_fusion), channel_id=1, replica_groups=mesh['fsdp'=8,'rep'=4] {'fsdp','rep'}, use_global_device_ids=true, to_apply=%region_25.26 | all-reduce | flops 1536 | bytes 12288 | tf_op jit(solution)/shard_map/psum | solution.py:358
  451.5 136.2 %reduce-scatter.2.cloned.1.call-done = f32[14,256,256]{1,2,0:T(8,128)} async-done(((f32[112,256,256]{1,2,0:T(8,128)}), f32[14,256,256]{1,2,0:T(8,128)}) %reduce-scatter.2.cloned.1.call-update) | async-done | bytes 3670032 | tf_op jit(solution)/shard_map/reduce_scatter | solution.py:356
  587.7 3.5 convert_element_type.285
  597.0 72.1 %all-reduce.2.cloned.1.call-done = bf16[14,256,256]{1,2,0:T(8,128)(2,1)} async-done(((bf16[14,256,256]{1,2,0:T(8,128)(2,1)}), bf16[14,256,256]{1,2,0:T(8,128)(2,1)}) %all-reduce.2.cloned.1.call-update) | async-done | bytes 1835024 | tf_op jit(solution)/shard_map/psum | solution.py:357
  669.1 5.9 fusion.128
  675.0 7.4 %fusion = (f32[14,256,256]{2,1,0:T(8,128)S(1)}, f32[14,256,256]{2,1,0:T(8,128)S(1)}) fusion(f32[14,256,256]{2,1,0:T(8,128)S(1)} %copy-done.31, f32[14,256,256]{2,1,0:T(8,128)} %param.17, f32[14,256,256]{1,2,0:T(8,128)S(1)} %fusion.128, f32[14,256,256]{2,1,0:T(8,128)S(1)} %copy-done.10), kind=kOutput, calls=%fused_computation.9 | convolution fusion | flops 2824077312 | bytes 22020096 | tf_op jit(solution)/shard_map/sjk,skl->sjl/dot_general | solution.py:280
  684.3 6.5 fusion.1
  690.8 5.6 fusion.123
  696.4 2.9 copy.129
  (403 shorter events, 94.5 us)
Async XLA Ops:
  7.2 3.6 copy-start.112
  7.2 4.9 copy-start.133
  7.2 4.9 copy-start.110
  7.2 87.4 %all-gather.2.cloned.1.call-start = ((), (), s32[]{:S(2)}) async-start(), calls=%async_computation.1 | async-start | bytes 16515072 | tf_op jit(solution)/shard_map/all_gather | solution.py:325
  10.8 577.0 %reduce-scatter.2.cloned.1.call-start = ((), (), s32[]{:S(2)}) async-start(), calls=%async_computation.2 | async-start | bytes 33030144 | tf_op jit(solution)/shard_map/reduce_scatter | solution.py:356
  13.0 138.9 %copy-start.66 = (pred[256,256]{0,1:T(8,128)(4,1)}, pred[256,256]{0,1:T(8,128)(4,1)S(1)}, u32[]{:S(2)}) copy-start(pred[256,256]{0,1:T(8,128)(4,1)S(1)} %fusion.55) | copy-start | bytes 196612
  13.1 133.5 %copy-start.64 = (pred[256,256]{0,1:T(8,128)(4,1)}, pred[256,256]{0,1:T(8,128)(4,1)S(1)}, u32[]{:S(2)}) copy-start(pred[256,256]{0,1:T(8,128)(4,1)S(1)} %fusion.56) | copy-start | bytes 196612
  14.1 130.6 %copy-start.102 = (f32[256,32]{0,1:T(8,128)}, f32[256,32]{0,1:T(8,128)S(1)}, u32[]{:S(2)}) copy-start(f32[256,32]{0,1:T(8,128)S(1)} %get-tuple-element.96) | copy-start | bytes 98308
  14.1 134.3 %copy-start.100 = (f32[256,32]{0,1:T(8,128)}, f32[256,32]{0,1:T(8,128)S(1)}, u32[]{:S(2)}) copy-start(f32[256,32]{0,1:T(8,128)S(1)} %get-tuple-element.109) | copy-start | bytes 98308
  158.2 6.5 copy-start.39
  158.2 6.5 copy-start.117
  158.2 6.5 copy-start.123
  159.4 3.6 copy-start.54
  160.7 7.4 %copy-start.52 = (f32[256,768]{1,0:T(8,128)}, f32[256,768]{1,0:T(8,128)S(1)}, u32[]{:S(2)}) copy-start(f32[256,768]{1,0:T(8,128)S(1)} %get-tuple-element.122) | copy-start | bytes 2359300
  160.7 7.4 %copy-start.119 = (f32[256]{0:T(256)}, f32[256]{0:T(256)S(1)}, u32[]{:S(2)}) copy-start(f32[256]{0:T(256)S(1)} %get-tuple-element.103) | copy-start | bytes 3076
  160.7 7.4 %copy-start.127 = (f32[256]{0:T(256)}, f32[256]{0:T(256)S(1)}, u32[]{:S(2)}) copy-start(f32[256]{0:T(256)S(1)} %get-tuple-element.102) | copy-start | bytes 3076
  163.0 5.1 copy-start.129
  164.6 4.6 copy-start.74
  178.9 3.6 copy-start.97
  178.9 3.6 copy-start.104
  197.1 3.8 copy-start.29
  200.9 3.8 copy-start.71
  204.6 3.7 copy-start.15
  204.6 3.7 copy-start.21
  204.6 3.7 copy-start.99
  211.5 3.8 copy-start.8
  211.5 3.8 copy-start.60
  211.5 4.3 copy-start.62
  222.8 3.8 copy-start.48
  222.9 3.8 copy-start.49
  222.9 3.8 copy-start.103
  222.9 3.8 copy-start.106
  271.6 7.0 copy-start.26
  271.6 7.0 copy-start.75
  303.9 6.8 slice-start.2
  313.9 13.4 %copy-start.132 = (s32[108]{0:T(128)S(1)}, s32[108]{0:T(128)}, u32[]{:S(2)}) copy-start(s32[108]{0:T(128)} %copy-done.131) | copy-start | bytes 1300
  408.7 40.4 %copy-start.56 = (bf16[256,768]{1,0:T(8,128)(2,1)S(1)}, bf16[256,768]{1,0:T(8,128)(2,1)}, u32[]{:S(2)}) copy-start(bf16[256,768]{1,0:T(8,128)(2,1)} %get-tuple-element.76) | copy-start | bytes 1179652
  408.7 40.4 %copy-start.57 = (bf16[256,768]{1,0:T(8,128)(2,1)S(1)}, bf16[256,768]{1,0:T(8,128)(2,1)}, u32[]{:S(2)}) copy-start(bf16[256,768]{1,0:T(8,128)(2,1)} %get-tuple-element.77) | copy-start | bytes 1179652
  408.7 41.3 %copy-start.3 = (bf16[96,8,3,256]{3,1,2,0:T(8,128)(2,1)S(1)}, bf16[96,8,3,256]{3,1,2,0:T(8,128)(2,1)}, u32[]{:S(2)}) copy-start(bf16[96,8,3,256]{3,1,2,0:T(8,128)(2,1)} %copy-done.2) | copy-start | bytes 3538948
  408.8 41.3 %copy-start.16 = (f32[256,768]{1,0:T(8,128)S(1)}, f32[256,768]{1,0:T(8,128)}, u32[]{:S(2)}) copy-start(f32[256,768]{1,0:T(8,128)} %copy-done.14) | copy-start | bytes 2359300
  408.8 260.3 %all-reduce.2.cloned.1.call-start = ((), (), s32[]{:S(2)}) async-start(), calls=%async_computation.3 | async-start | bytes 3670016 | tf_op jit(solution)/shard_map/psum | solution.py:357
  451.5 139.7 %copy-start.1 = (bf16[96,8,3,256]{3,1,2,0:T(8,128)(2,1)S(1)}, bf16[96,8,3,256]{3,1,2,0:T(8,128)(2,1)}, u32[]{:S(2)}) copy-start(bf16[96,8,3,256]{3,1,2,0:T(8,128)(2,1)} %copy-done) | copy-start | bytes 3538948
  669.1 5.9 copy-start.10
  669.1 6.0 copy-start.31
  675.0 9.2 %copy-start.30 = (f32[14,256,256]{2,1,0:T(8,128)S(1)}, f32[14,256,256]{2,1,0:T(8,128)}, u32[]{:S(2)}) copy-start(f32[14,256,256]{2,1,0:T(8,128)} %param.19) | copy-start | bytes 11010052
  682.4 8.4 %copy-start.32 = (f32[14,256,256]{2,1,0:T(8,128)}, f32[14,256,256]{2,1,0:T(8,128)S(1)}, u32[]{:S(2)}) copy-start(f32[14,256,256]{2,1,0:T(8,128)S(1)} %get-tuple-element.58) | copy-start | bytes 11010052
  684.3 6.5 copy-start.9
  690.8 5.6 copy-start.24
  (93 other events, 179.4 us)
Sparse Core Ops, SparseCore 0:
  10.9 83.6 all-gather.1
  408.9 178.7 reduce-scatter.1
  591.3 77.6 all-reduce.1
where the time goes:
time: 716 us; the launch traced here: 706 us
  waiting for transfers between devices  289 us (40%)
  local copies, waits for them, and re-layouts  238 us (33%)
  matrix products  104 us (15%)
  blocking collectives  39.6 us (6%)
  other arithmetic  20.1 us (3%)
  between operations  15.8 us (2%)
    reduce_scatter x1, waiting for transfers between devices, shards(): lax.psum_scatter(slotted, 'fsdp', scatter_dimension=0, tiled=True)  136 us
    scatter x2, local copies, waits for them, and re-layouts, shards(): slotted = jnp.zeros((slot_total, BLOCK_ORDER, BLOCK_ORDER), jnp.float32)....  81.4 us
    all_gather x1, waiting for transfers between devices, gathered_matrices(): every_slot = lax.all_gather(owned_low, 'fsdp', axis=0, tiled=True)  80.5 us
    psum x1, waiting for transfers between devices, shards(): lax.psum(owner_sums.astype(jnp.bfloat16), 'rep').astype(jnp.float32)  72.1 us
    unnamed x293, local copies, waits for them, and re-layouts  47 us
    psum x1, blocking collectives, shards(): gain_grads = lax.psum(gain_total, ('fsdp', 'rep'))  39.6 us
    dot_general x14, matrix products, dot_rows(): lax.dot_general(operand_a, operand_b, (((0,), (0,)), ((), ())), preferred...  27.8 us
    transpose x9, local copies, waits for them, and re-layouts, split_into_blocks(): pieces.append(matrix.reshape(grid_rows, BLOCK_ORDER, grid_cols, BLOCK_ORD...  25.4 us
  transfers between devices with their start and end apart: 3, of which 3 were waited for; matrix products, arithmetic and copies ran while one was open for 2% of the time, Pallas kernels for 0%

commit v1 on v0

v1 whole, which is shorter than its diff:
```python
import functools

import jax
import jax.numpy as jnp
import numpy as np
from jax import lax
from jax.experimental import pallas as pl
from jax.experimental.pallas import tpu as pltpu
from jax.sharding import PartitionSpec as P

D = 768
HEADS = 12
HEAD_DIM = 64
FF = 2048
BLOCK_ORDER = 256
STEP = 10


NORM_EPS = 1e-05
ROPE_BASE = 10000.0
BETA_ONE = 0.5
BETA_TWO = 0.5
ADAM_EPS = 1e-08
RATE = 0.03
GAIN_RATE = 0.4
DECAY = 0.01
MASKED = -1e30

B = BLOCK_ORDER
BF16 = jnp.bfloat16
F32 = jnp.float32
MIB = 1024 * 1024

LEFT_X, LEFT_A, LEFT_Y, LEFT_ACT = 0, D // B, 2 * D // B, 3 * D // B
LEFT_ROWS = 3 * D + FF
RIGHT_Q, RIGHT_K, RIGHT_V, RIGHT_O = 0, D, 2 * D, 3 * D
RIGHT_G, RIGHT_U, RIGHT_D = 4 * D, 4 * D + FF, 4 * D + 2 * FF
RIGHT_COLS = 5 * D + 2 * FF


def matrix_table():
    return [
        (D // B, D // B, LEFT_X, RIGHT_Q // B),
        (D // B, D // B, LEFT_X, RIGHT_K // B),
        (D // B, D // B, LEFT_X, RIGHT_V // B),
        (D // B, D // B, LEFT_A, RIGHT_O // B),
        (D // B, FF // B, LEFT_Y, RIGHT_G // B),
        (D // B, FF // B, LEFT_Y, RIGHT_U // B),
        (FF // B, D // B, LEFT_ACT, RIGHT_D // B),
    ]


def factor_tables():
    lefts, rights = [], []
    for grid_rows, grid_cols, left, right in matrix_table():
        for i in range(grid_rows):
            for j in range(grid_cols):
                lefts.append(left + i)
                rights.append(right + j)
    return np.array(lefts, np.int32), np.array(rights, np.int32)


def positions_of(segments):
    places = jnp.arange(segments.shape[-1], dtype=jnp.int32)[None, :]
    starts = jnp.concatenate(
        [jnp.ones((segments.shape[0], 1), jnp.bool_), segments[:, 1:] != segments[:, :-1]], axis=1
    )
    first_place = lax.cummax(jnp.where(starts, places, 0), axis=1)
    return places - first_place


def dot_nn(a, b):
    return jnp.dot(a, b, preferred_element_type=F32)


def dot_nt(a, b):
    return lax.dot_general(a, b, (((1,), (1,)), ((), ())), preferred_element_type=F32)


def half_swap(values, low_half):
    return jnp.where(low_half, pltpu.roll(values, 96, 1), pltpu.roll(values, 32, 1))


def layer_kernel(
    micro,
    slots,
    piece_slots,
    index_ref,
    left_ref,
    right_ref,
    x_ref,
    dy_ref,
    bias_ref,
    cos_ref,
    sin_ref,
    cos_t_ref,
    sin_t_ref,
    gains_ref,
    *rest,
):
    pieces = rest[: len(piece_slots)]
    out_ref, token_grad_ref, gain_ref, grads_ref = rest[len(piece_slots) : len(piece_slots) + 4]
    (
        w_qkv,
        w_o,
        w_gu,
        w_d,
        lefts,
        rights,
        q_scr,
        k_scr,
        v_scr,
        p_scr,
        a_scr,
        act_scr,
        cg_scr,
        cu_scr,
        y1_scr,
        y1_low_scr,
        h1_scr,
        dh2_scr,
        r1_scr,
        ring,
        w_sems,
        ring_sems,
    ) = rest[len(piece_slots) + 4 :]
    seq = bias_ref.shape[1]
    tokens = micro * seq

    def fetch(block, target, row, col, sem):
        slot = index_ref[block]
        first = 0
        for piece, count in zip(pieces, piece_slots):

            @pl.when((slot >= first) & (slot < first + count))
            def _(piece=piece, first=first):
                pltpu.make_async_copy(
                    piece.at[slot - first],
                    target.at[
                        pl.ds(pl.multiple_of(row * B, B), B), pl.ds(pl.multiple_of(col * B, B), B)
                    ],
                    sem,
                ).start()

            first += count

    def fetch_matrix(first_block, grid_rows, grid_cols, target, col_offset, sem):
        def one(t, carry):
            i = t // grid_cols
            j = t - i * grid_cols
            fetch(first_block + t, target, i, j + col_offset, sem)
            return carry

        lax.fori_loop(0, grid_rows * grid_cols, one, 0)

    nd, nf = D // B, FF // B
    for m in range(3):
        fetch_matrix(m * nd * nd, nd, nd, w_qkv, m * nd, w_sems.at[0])
    fetch_matrix(3 * nd * nd, nd, nd, w_o, 0, w_sems.at[1])
    for m in range(2):
        fetch_matrix(4 * nd * nd + m * nd * nf, nd, nf, w_gu, m * nf, w_sems.at[2])
    fetch_matrix(4 * nd * nd + 2 * nd * nf, nf, nd, w_d, 0, w_sems.at[3])

    def wait_for(target, sem):
        pltpu.make_async_copy(target, target, sem).wait()

    lefts[0:D, :] = x_ref[...].T
    lane = lax.broadcasted_iota(jnp.int32, (1, 128), 1)
    low_half = lax.rem(lane, HEAD_DIM) < HEAD_DIM // 2
    head_lanes = [lane < HEAD_DIM, lane >= HEAD_DIM]

    def of_head(values, h):
        return jnp.where(head_lanes[h], values, jnp.zeros_like(values))

    wait_for(w_qkv, w_sems.at[0])

    def attend(jb, carry):
        def columns(offset):
            return pl.ds(pl.multiple_of(offset + jb * B, B), B)

        x = x_ref[...]
        q_raw = dot_nn(x, w_qkv[:, columns(0)])
        k_raw = dot_nn(x, w_qkv[:, columns(D)])
        v_raw = dot_nn(x, w_qkv[:, columns(2 * D)])
        cosine = cos_ref[...]
        sine = sin_ref[...]
        for sub in range(2):
            part = slice(sub * 128, sub * 128 + 128)
            slab = pl.ds(pl.multiple_of(jb * B + sub * 128, 128), 128)
            q = q_raw[:, part]
            k = k_raw[:, part]
            q = ((q * cosine + half_swap(q, low_half) * sine) * HEAD_DIM**-0.5).astype(BF16)
            k = (k * cosine + half_swap(k, low_half) * sine).astype(BF16)
            v = v_raw[:, part].astype(BF16)
            q_scr[:, slab] = q
            k_scr[:, slab] = k
            v_scr[:, slab] = v
            for r in range(micro):
                rows = slice(r * seq, (r + 1) * seq)
                v_t = v[rows].T
                outs = []
                for h in range(2):
                    scores = dot_nt(k[rows], of_head(q[rows], h)) + bias_ref[r]
                    top = jnp.max(scores, axis=0, keepdims=True)
                    exps = jnp.exp(scores - top)
                    total = jnp.sum(exps, axis=0, keepdims=True)
                    probs = (exps * (1.0 / total)).astype(BF16)
                    p_scr[(jb * 2 + sub) * 2 * micro + 2 * r + h] = probs
                    outs.append(dot_nn(v_t[h * HEAD_DIM : (h + 1) * HEAD_DIM], probs))
                a_t = jnp.concatenate(outs, axis=0).astype(BF16)
                lefts[pl.ds(pl.multiple_of(D + jb * B + sub * 128, 128), 128), rows] = a_t
                a_scr[rows, slab] = a_t.T
        return carry

    lax.fori_loop(0, nd, attend, 0)

    wait_for(w_o, w_sems.at[1])
    for r in range(micro):
        rows = slice(r * seq, (r + 1) * seq)
        h1 = x_ref[rows, :].astype(F32) + dot_nn(a_scr[rows, :], w_o[...])
        r1 = lax.rsqrt(jnp.mean(h1 * h1, axis=-1, keepdims=True) + NORM_EPS)
        y1 = h1 * r1 * gains_ref[0:1, :]
        y1_low = y1.astype(BF16)
        h1_scr[rows, :] = h1
        r1_scr[rows, :] = r1
        y1_scr[rows, :] = y1
        y1_low_scr[rows, :] = y1_low
        lefts[2 * D : 3 * D, rows] = y1_low.T

    wait_for(w_gu, w_sems.at[2])

    def feed(j, carry):
        y1_low = y1_low_scr[...]
        cols = pl.ds(pl.multiple_of(j * B, B), B)
        gate = dot_nn(y1_low, w_gu[:, cols])
        up = dot_nn(y1_low, w_gu[:, pl.ds(pl.multiple_of(FF + j * B, B), B)])
        sig = 1.0 / (1.0 + jnp.exp(-gate))
        silu = gate * sig
        act = (silu * up).astype(BF16)
        act_scr[:, cols] = act
        cu_scr[:, cols] = silu.astype(BF16)
        cg_scr[:, cols] = (up * sig * (1.0 + gate * (1.0 - sig))).astype(BF16)
        lefts[pl.ds(pl.multiple_of(3 * D + j * B, B), B), :] = act.T
        return carry

    lax.fori_loop(0, nf, feed, 0)

    wait_for(w_d, w_sems.at[3])
    gain_two = jnp.zeros((1, D), F32)
    for r in range(micro):
        rows = slice(r * seq, (r + 1) * seq)
        h2 = y1_scr[rows, :] + dot_nn(act_scr[rows, :], w_d[...])
        r2 = lax.rsqrt(jnp.mean(h2 * h2, axis=-1, keepdims=True) + NORM_EPS)
        scaled = h2 * r2
        gain = gains_ref[1:2, :]
        out_ref[rows, :] = (scaled * gain).astype(BF16)
        dy = dy_ref[rows, :].astype(F32)
        gain_two += jnp.sum(dy * scaled, axis=0, keepdims=True)
        dyg = dy * gain
        dh2 = r2 * (dyg - scaled * jnp.mean(scaled * dyg, axis=-1, keepdims=True))
        dh2_scr[rows, :] = dh2
        rights[rows, RIGHT_D:] = dh2.astype(BF16)
    gain_ref[1:2, :] = gain_two

    def feed_back(j, carry):
        cols = pl.ds(pl.multiple_of(j * B, B), B)
        dact = dot_nt(rights[:, RIGHT_D:], w_d[cols, :])
        rights[:, pl.ds(pl.multiple_of(RIGHT_G + j * B, B), B)] = (
            dact * cg_scr[:, cols].astype(F32)
        ).astype(BF16)
        rights[:, pl.ds(pl.multiple_of(RIGHT_U + j * B, B), B)] = (
            dact * cu_scr[:, cols].astype(F32)
        ).astype(BF16)
        return carry

    lax.fori_loop(0, nf, feed_back, 0)

    def feed_in(j, carry):
        cols = pl.ds(pl.multiple_of(j * B, B), B)
        dh2_scr[:, cols] += dot_nt(rights[:, RIGHT_G:RIGHT_D], w_gu[cols, :])
        return carry

    lax.fori_loop(0, nd, feed_in, 0)

    gain_one = jnp.zeros((1, D), F32)
    for r in range(micro):
        rows = slice(r * seq, (r + 1) * seq)
        dy1 = dh2_scr[rows, :]
        r1 = r1_scr[rows, :]
        scaled = h1_scr[rows, :] * r1
        gain_one += jnp.sum(dy1 * scaled, axis=0, keepdims=True)
        dyg = dy1 * gains_ref[0:1, :]
        dh1 = r1 * (dyg - scaled * jnp.mean(scaled * dyg, axis=-1, keepdims=True))
        h1_scr[rows, :] = dh1
        do = dh1.astype(BF16)
        rights[rows, RIGHT_O : RIGHT_O + D] = do
        a_scr[rows, :] = dot_nt(do, w_o[...]).astype(BF16)
    gain_ref[0:1, :] = gain_one

    def attend_back(jb, carry):
        for sub in range(2):
            slab = pl.ds(pl.multiple_of(jb * B + sub * 128, 128), 128)
            for r in range(micro):
                rows = slice(r * seq, (r + 1) * seq)
                q = q_scr[rows, slab]
                k = k_scr[rows, slab]
                v = v_scr[rows, slab]
                da = a_scr[rows, slab]
                k_t = k.T
                dv = jnp.zeros((seq, 128), F32)
                dk = jnp.zeros((seq, 128), F32)
                dq_t = []
                for h in range(2):
                    probs = p_scr[(jb * 2 + sub) * 2 * micro + 2 * r + h]
                    da_h = of_head(da, h)
                    probs_wide = probs.astype(F32)
                    dprobs = dot_nt(v, da_h)
                    weighted = probs_wide * dprobs
                    row_sum = jnp.sum(weighted, axis=0, keepdims=True)
                    ds = (weighted - probs_wide * row_sum).astype(BF16)
                    dv += dot_nn(probs, da_h)
                    dk += dot_nn(ds, of_head(q, h))
                    dq_h = dot_nn(k_t[h * HEAD_DIM : (h + 1) * HEAD_DIM], ds) * HEAD_DIM**-0.5
                    low, high = dq_h[: HEAD_DIM // 2], dq_h[HEAD_DIM // 2 :]
                    cosine = cos_t_ref[:, rows]
                    sine = sin_t_ref[:, rows]
                    dq_t.append(low * cosine + high * sine)
                    dq_t.append(high * cosine - low * sine)
                dq = jnp.concatenate(dq_t, axis=0).astype(BF16).T
                dk = dk * cos_ref[rows, :] - half_swap(dk, low_half) * sin_ref[rows, :]
                rights[rows, slab] = dq
                rights[rows, pl.ds(pl.multiple_of(RIGHT_K + jb * B + sub * 128, 128), 128)] = (
                    dk.astype(BF16)
                )
                rights[rows, pl.ds(pl.multiple_of(RIGHT_V + jb * B + sub * 128, 128), 128)] = (
                    dv.astype(BF16)
                )
        return carry

    lax.fori_loop(0, nd, attend_back, 0)

    def token_back(j, carry):
        cols = pl.ds(pl.multiple_of(j * B, B), B)
        token_grad_ref[:, cols] = (
            h1_scr[:, cols] + dot_nt(rights[:, : 3 * D], w_qkv[cols, :])
        ).astype(BF16)
        return carry

    lax.fori_loop(0, nd, token_back, 0)

    group = ring.shape[1]
    groups = slots // group

    def ring_copy(g, half):
        return pltpu.make_async_copy(
            ring.at[half], grads_ref.at[pl.ds(g * group, group)], ring_sems.at[half]
        )

    def weigh(g, carry):
        half = lax.rem(g, 2)

        @pl.when(g >= 2)
        def _():
            ring_copy(g - 2, half).wait()

        for n in range(group):
            slot = g * group + n
            left = jnp.maximum(left_ref[slot], 0)
            grad = dot_nn(
                lefts[pl.ds(pl.multiple_of(left * B, B), B), :],
                rights[:, pl.ds(pl.multiple_of(right_ref[slot] * B, B), B)],
            )
            keep = jnp.where(left_ref[slot] >= 0, 1.0, 0.0)
            ring[half, n] = (grad * keep).astype(BF16)
        ring_copy(g, half).start()
        return carry

    lax.fori_loop(0, groups, weigh, 0)
    for g in range(max(0, groups - 2), groups):
        ring_copy(g, g % 2).wait()


def run_layer(tokens, cotangent, segment_ids, block_slot_index, norm_gains, pieces, slots):
    micro, seq = segment_ids.shape
    count = micro * seq
    half_dim = HEAD_DIM // 2
    frequency = ROPE_BASE ** (-2.0 * jnp.arange(half_dim, dtype=F32) / HEAD_DIM)
    angles = positions_of(segment_ids).reshape(count).astype(F32)[:, None] * frequency[None, :]
    cosine, sine = jnp.cos(angles), jnp.sin(angles)
    cos_wide = jnp.tile(cosine, (1, 4))
    sin_wide = jnp.concatenate([-sine, sine, -sine, sine], axis=1)
    places = jnp.arange(seq, dtype=jnp.int32)
    visible = (segment_ids[:, :, None] == segment_ids[:, None, :]) & (
        places[:, None] <= places[None, :]
    )
    bias = jnp.where(visible, 0.0, MASKED).astype(F32)
    left_table, right_table = factor_tables()
    slot_left = jnp.full((slots,), -1, jnp.int32).at[block_slot_index].set(left_table)
    slot_right = jnp.zeros((slots,), jnp.int32).at[block_slot_index].set(right_table)
    group = 4
    assert slots % group == 0

    vmem = pl.BlockSpec(memory_space=pltpu.VMEM)
    smem = pl.BlockSpec(memory_space=pltpu.SMEM)
    hbm = pl.BlockSpec(memory_space=pl.ANY)
    return pl.pallas_call(
        functools.partial(layer_kernel, micro, slots, [p.shape[0] for p in pieces]),
        out_shape=(
            jax.ShapeDtypeStruct((count, D), BF16),
            jax.ShapeDtypeStruct((count, D), BF16),
            jax.ShapeDtypeStruct((2, D), F32),
            jax.ShapeDtypeStruct((slots, B, B), BF16),
        ),
        in_specs=[smem] * 3 + [vmem] * 8 + [hbm] * len(pieces),
        out_specs=(vmem, vmem, vmem, hbm),
        scratch_shapes=[
            pltpu.VMEM((D, 3 * D), BF16),
            pltpu.VMEM((D, D), BF16),
            pltpu.VMEM((D, 2 * FF), BF16),
            pltpu.VMEM((FF, D), BF16),
            pltpu.VMEM((LEFT_ROWS, count), BF16),
            pltpu.VMEM((count, RIGHT_COLS), BF16),
            pltpu.VMEM((count, D), BF16),
            pltpu.VMEM((count, D), BF16),
            pltpu.VMEM((count, D), BF16),
            pltpu.VMEM((HEADS * micro, seq, seq), BF16),
            pltpu.VMEM((count, D), BF16),
            pltpu.VMEM((count, FF), BF16),
            pltpu.VMEM((count, FF), BF16),
            pltpu.VMEM((count, FF), BF16),
            pltpu.VMEM((count, D), F32),
            pltpu.VMEM((count, D), BF16),
            pltpu.VMEM((count, D), F32),
            pltpu.VMEM((count, D), F32),
            pltpu.VMEM((count, 1), F32),
            pltpu.VMEM((2, group, B, B), BF16),
            pltpu.SemaphoreType.DMA((4,)),
            pltpu.SemaphoreType.DMA((2,)),
        ],
        compiler_params=pltpu.CompilerParams(vmem_limit_bytes=60 * MIB),
        cost_estimate=pl.CostEstimate(
            flops=23_000_000_000, bytes_accessed=32_000_000, transcendentals=3_000_000
        ),
        name="layer",
    )(
        block_slot_index,
        slot_left,
        slot_right,
        tokens,
        cotangent,
        bias,
        cos_wide,
        sin_wide,
        cosine.T,
        sine.T,
        norm_gains,
        *pieces,
    )


def split_two(values):
    high = values.astype(BF16)
    return high, (values - high.astype(F32)).astype(BF16)


def dot_split(dot, a, b):
    a_high, a_low = a
    b_high, b_low = b
    total = dot(a_high, b_high)
    if b_low is not None:
        total = total + dot(a_high, b_low)
    if a_low is not None:
        total = total + dot(a_low, b_high)
    return total


def adam_kernel(
    grad_ref, weight_ref, first_ref, second_ref, left_ref, right_ref,
    grad_out, first_out, second_out, weight_out, low_out,
):
    for n in range(grad_ref.shape[0]):
        grad = grad_ref[n]
        left = left_ref[n]
        left_pair = split_two(left)
        left_t_pair = tuple(part.T for part in left_pair)
        right_pair = split_two(right_ref[n])
        grad_out[n] = grad.astype(F32)
        turned = dot_split(dot_nn, (grad, None), right_pair)
        turned = dot_split(dot_nn, left_t_pair, split_two(turned))
        first_new = BETA_ONE * first_ref[n] + (1.0 - BETA_ONE) * turned
        second_new = BETA_TWO * second_ref[n] + (1.0 - BETA_TWO) * turned * turned
        first_out[n] = first_new
        second_out[n] = second_new
        ratio = (
            first_new
            / (1.0 - BETA_ONE**STEP)
            / (jnp.sqrt(second_new / (1.0 - BETA_TWO**STEP)) + ADAM_EPS)
        )
        back = dot_split(dot_nn, left_pair, split_two(ratio))
        back = dot_split(dot_nt, split_two(back), right_pair)
        weight = weight_ref[n]
        weight_new = weight - RATE * (back + DECAY * weight)
        weight_out[n] = weight_new
        low_out[n] = weight_new.astype(BF16)


def adam_blocks(grads, weights, first_moment, second_moment, left_basis, right_basis):
    own = weights.shape[0]
    step = 2 if own % 2 == 0 else 1
    spec = pl.BlockSpec((step, B, B), lambda s: (s, 0, 0))
    wide = jax.ShapeDtypeStruct(weights.shape, F32)
    return pl.pallas_call(
        adam_kernel,
        grid=(own // step,),
        out_shape=(wide, wide, wide, wide, jax.ShapeDtypeStruct(weights.shape, BF16)),
        in_specs=[spec] * 6,
        out_specs=(spec,) * 5,
        compiler_params=pltpu.CompilerParams(vmem_limit_bytes=32 * MIB),
        cost_estimate=pl.CostEstimate(
            flops=own * 12 * 2 * B**3, bytes_accessed=own * B * B * 40, transcendentals=own * B * B
        ),
        name="adam",
    )(grads, weights, first_moment, second_moment, left_basis, right_basis)


def adam_plain(grads, values, first_moment, second_moment):
    first_new = BETA_ONE * first_moment + (1.0 - BETA_ONE) * grads
    second_new = BETA_TWO * second_moment + (1.0 - BETA_TWO) * grads * grads
    step_ratio = (
        first_new
        / (1.0 - BETA_ONE**STEP)
        / (jnp.sqrt(second_new / (1.0 - BETA_TWO**STEP)) + ADAM_EPS)
    )
    return (first_new, second_new, values - GAIN_RATE * step_ratio)


def sum_everywhere(values, axis):
    size = lax.axis_size(axis)
    if size & (size - 1):
        return lax.psum(values, axis)
    reach = 1
    while reach < size:
        values = values + lax.ppermute(values, axis, [(i, i ^ reach) for i in range(size)])
        reach *= 2
    return values


def shards(
    tokens,
    cotangent,
    segment_ids,
    block_slot_index,
    weights,
    first_moment,
    second_moment,
    left_basis,
    right_basis,
    norm_gains,
    gain_first,
    gain_second,
):
    slots = weights.shape[0] * lax.axis_size("fsdp")
    owned_low = weights.astype(BF16)
    pieces = [lax.all_gather(owned_low, "fsdp", axis=0, tiled=True)]
    block_out, token_grad, gain_grad, slot_grads = run_layer(
        tokens, cotangent, segment_ids, block_slot_index, norm_gains, pieces, slots
    )
    gain_grads = sum_everywhere(sum_everywhere(gain_grad, "fsdp"), "rep")
    owner_sums = lax.psum_scatter(slot_grads, "fsdp", scatter_dimension=0, tiled=True)
    owner_grads = lax.psum(owner_sums, "rep")
    grads_wide, first_new, second_new, weights_new, weights_low = adam_blocks(
        owner_grads, weights, first_moment, second_moment, left_basis, right_basis
    )
    gain_first_new, gain_second_new, gains_new = adam_plain(
        gain_grads, norm_gains, gain_first, gain_second
    )
    return (
        block_out,
        token_grad,
        grads_wide,
        first_new,
        second_new,
        weights_new,
        weights_low,
        gain_first_new,
        gain_second_new,
        gains_new,
    )


def solution(mesh):
    return jax.shard_map(
        shards,
        mesh=mesh,
        in_specs=(
            P(("fsdp", "rep"), None),
            P(("fsdp", "rep"), None),
            P(("fsdp", "rep"), None),
            P(),
            P("fsdp", None, None),
            P("fsdp", None, None),
            P("fsdp", None, None),
            P("fsdp", None, None),
            P("fsdp", None, None),
            P(),
            P(),
            P(),
        ),
        out_specs=(
            P(("fsdp", "rep"), None),
            P(("fsdp", "rep"), None),
            P("fsdp", None, None),
            P("fsdp", None, None),
            P("fsdp", None, None),
            P("fsdp", None, None),
            P("fsdp", None, None),
            P(),
            P(),
            P(),
        ),
        check_vma=False,
    )
```

time: 716 us -> 376 us (0.53); the launches traced: 706 us -> 375 us
  local copies, waits for them, and re-layouts: 238 us -> 16 us
  matrix products: 104 us -> 0 us
  Pallas kernels: 0 us -> 78.5 us
  blocking collectives: 39.6 us -> 0 us
  waiting for transfers between devices: 289 us -> 251 us
  other arithmetic: 20.1 us -> 9.07 us
    dot_general x58 -> x0, matrix products: 104 us -> none  [the longest x14 27.8 us: dot_rows(): lax.dot_general(operand_a, operand_b, (((0,), (0,)), ((), ())), preferred...]
    pallas_call x0 -> x2, Pallas kernels: none -> 78.5 us  [the longest x1 61.8 us: run_layer(): pl.pallas_call(functools.partial(layer_kernel, micro, slots, [p.shape[0]...]
    scatter x2, local copies, waits for them, and re-layouts: 81.4 us -> 3.07 us  [the longest x1 1.53 us: run_layer(): jnp.full((slots,), -1, jnp.int32).at[block_slot_index].set(left_table)]
    psum x1 -> x0, blocking collectives: 39.6 us -> none  [shards(): gain_grads = lax.psum(gain_total, ('fsdp', 'rep'))]
    unnamed x293 -> x26, local copies, waits for them, and re-layouts: 47 us -> 11.7 us
    reduce_scatter x1, waiting for transfers between devices: 136 us -> 104 us  [shards(): lax.psum_scatter(slot_grads, 'fsdp', scatter_dimension=0, tiled=True)]
    reshape x11 -> x1, local copies, waits for them, and re-layouts: 27.5 us -> 0.02 us  [the longest x4 14.9 us: split_into_blocks(): matrix.reshape(grid_rows, BLOCK_ORDER, grid_cols, BLOCK_ORDER)]
    transpose x9 -> x0, local copies, waits for them, and re-layouts: 25.4 us -> none  [split_into_blocks(): pieces.append(matrix.reshape(grid_rows, BLOCK_ORDER, grid_cols, BLOCK_ORD...]
  transfers between devices with their start and end apart: 3 -> 8, of which waited for: 3 -> 8; matrix products, arithmetic and copies ran while one was open for 2% -> 3% of each run, Pallas kernels for 0% -> 0%
where the time goes in v1:
time: 376 us; the launch traced here: 375 us
  waiting for transfers between devices  251 us (67%)
  Pallas kernels  78.5 us (21%)
  local copies, waits for them, and re-layouts  16 us (4%)
  between operations  13.9 us (4%)
  other arithmetic  9.07 us (2%)
  starting transfers between devices  6.67 us (2%)
    reduce_scatter x1, waiting for transfers between devices, shards(): lax.psum_scatter(slot_grads, 'fsdp', scatter_dimension=0, tiled=True)  104 us
    all_gather x1, waiting for transfers between devices, shards(): pieces = [lax.all_gather(owned_low, 'fsdp', axis=0, tiled=True)]  74.5 us
    psum x1, waiting for transfers between devices, shards(): owner_grads = lax.psum(owner_sums, 'rep')  62.6 us
    pallas_call x1, Pallas kernels, run_layer(): pl.pallas_call(functools.partial(layer_kernel, micro, slots, [p.shape[0]...  61.8 us
    pallas_call x1, Pallas kernels, adam_blocks(): pl.pallas_call(adam_kernel, grid=(own // step,), out_shape=(wide, wide, w...  16.7 us
    unnamed x26, local copies, waits for them, and re-layouts  11.7 us
    ppermute x5, waiting for transfers between devices, sum_everywhere(): lax.ppermute(values, axis, [(i, i ^ reach) for i in range(size)])  10.4 us
  transfers between devices with their start and end apart: 8, of which 8 were waited for; matrix products, arithmetic and copies ran while one was open for 3% of the time, Pallas kernels for 0%

profile of v1, /device:TPU:0, one launch (start us, length us, event | category | flops | bytes accessed | tf_op | source)
XLA Modules:
  0.0 375.4 jit_solution(1485617398410185183)
XLA Ops:
  7.2 0.0 copy-start.11
  7.2 0.0 all-gather.2.cloned.1.call-start
  7.2 3.5 convert_element_type.11
  10.7 0.0 all-gather.2.cloned.1.call-update
  10.7 0.0 reduce-scatter.2.cloned.1.call-start
  10.8 0.1 slice_compare_fusion
  10.9 0.1 pad_select_fusion
  11.0 0.6 reduce-window.6
  11.6 0.2 slice_reduce_fusion
  11.8 0.2 reduce-window.9
  12.0 0.1 broadcast_maximum_fusion
  12.1 1.0 fusion
  13.1 0.1 copy.29
  13.2 0.8 copy.30.cos_ref
  14.1 1.5 scatter_custom_fusion.left_ref
  15.6 1.5 scatter_custom_fusion.1.right_ref
  17.2 1.0 pad_maximum_fusion.sin_ref
  18.2 1.0 multiply_sine_fusion.1
  19.1 1.0 and_select_fusion.bias_ref
  20.1 74.5 %all-gather.2.cloned.1.call-done.rest_0_ = bf16[112,256,256]{2,1,0:T(8,128)(2,1)} async-done(((bf16[14,256,256]{2,1,0:T(8,128)(2,1)}), bf16[112,256,256]{2,1,0:T(8,128)(2,1)}) %all-gather.2.cloned.1.call-update) | async-done | bytes 14680080 | tf_op jit(solution)/shard_map/all_gather | solution.py:564
  94.6 61.8 %layer.1 = (bf16[512,768]{1,0:T(8,128)(2,1)}, bf16[512,768]{1,0:T(8,128)(2,1)}, f32[2,768]{1,0:T(2,128)}, bf16[112,256,256]{2,1,0:T(8,128)(2,1)}) custom-call(s32[108]{0:T(128)} %index_ref.1, s32[112]{0:T(128)} %scatter_custom_fusion.left_ref, s32[112]{0:T(128)} %scatter_custom_fusion.1.right_ref, bf16[512,768]{1,0:T(8,128)(2,1)} %x_ref.1, ...), custom_call_target="tpu_custom_call" | custom-call | flops 23000000512 | bytes 32000000 | tf_op jit(solution)/shard_map/layer/pallas_call | solution.py:406
  156.4 0.0 copy-start.10
  156.4 0.0 copy-start.7
  156.4 0.0 copy-start.8
  156.5 0.0 copy-start.9
  156.5 0.0 reduce-scatter.2.cloned.1.call-update
  156.5 0.0 all-reduce.3.cloned.1.call-start
  156.5 103.7 %reduce-scatter.2.cloned.1.call-done = bf16[14,256,256]{2,1,0:T(8,128)(2,1)} async-done(((bf16[112,256,256]{2,1,0:T(8,128)(2,1)}), bf16[14,256,256]{2,1,0:T(8,128)(2,1)}) %reduce-scatter.2.cloned.1.call-update) | async-done | bytes 1835024 | tf_op jit(solution)/shard_map/reduce_scatter | solution.py:569
  260.2 0.0 all-reduce.3.cloned.1.call-update
  260.2 0.1 collective-permute-start
  260.3 1.2 collective-permute-done
  261.5 1.3 collective-permute-start.1
  262.8 2.3 collective-permute-done.1
  265.1 1.3 collective-permute-start.2
  266.4 2.4 collective-permute-done.2
  268.7 1.5 collective-permute-start.3
  270.2 2.2 collective-permute-done.3
  272.5 2.4 collective-permute-start.4
  274.9 2.3 collective-permute-done.4
  277.2 0.6 multiply_subtract_fusion
  277.9 62.6 %all-reduce.3.cloned.1.call-done.grad_ref = bf16[14,256,256]{2,1,0:T(8,128)(2,1)} async-done(((bf16[14,256,256]{2,1,0:T(8,128)(2,1)}), bf16[14,256,256]{2,1,0:T(8,128)(2,1)}) %all-reduce.3.cloned.1.call-update) | async-done | bytes 1835024 | tf_op jit(solution)/shard_map/psum | solution.py:570
  340.5 2.0 copy-done
  342.5 2.0 copy-done.1
  344.6 2.0 copy-done.2
  346.6 2.0 copy-done.3
  348.6 2.0 copy-done.4
  350.7 1.5 copy-done.5
  352.2 16.7 %adam.1 = (f32[14,256,256]{2,1,0:T(8,128)}, f32[14,256,256]{2,1,0:T(8,128)}, f32[14,256,256]{2,1,0:T(8,128)}, f32[14,256,256]{2,1,0:T(8,128)}, bf16[14,256,256]{2,1,0:T(8,128)(2,1)}) custom-call(bf16[14,256,256]{2,1,0:T(8,128)(2,1)S(1)} %copy-done.5, f32[14,256,256]{2,1,0:T(8,128)S(1)} %copy-done, f32[14,256,256]{2,1,0:T(8,128)S(1)} %copy-done.1, ...), custom_call_target="tpu_custom_call" | custom-call | flops 5637144576 | bytes 36700160 | tf_op jit(solution)/shard_map/adam/pallas_call | solution.py:512
  (25 shorter events, 0.1 us)
Async XLA Ops:
  7.2 3.6 copy-start.6
  7.2 6.9 %copy-start.11 = (s32[108]{0:T(128)S(1)}, s32[108]{0:T(128)}, u32[]{:S(2)}) copy-start(s32[108]{0:T(128)} %index_ref.1) | copy-start | bytes 1300
  7.2 87.4 %all-gather.2.cloned.1.call-start = ((), (), s32[]{:S(2)}) async-start(), calls=%async_computation.1 | async-start | bytes 16515072 | tf_op jit(solution)/shard_map/all_gather | solution.py:564
  10.7 249.5 %reduce-scatter.2.cloned.1.call-start = ((), (), s32[]{:S(2)}) async-start(), calls=%async_computation.2 | async-start | bytes 16515072 | tf_op jit(solution)/shard_map/reduce_scatter | solution.py:569
  156.4 103.8 %copy-start.10 = (f32[2,768]{1,0:T(2,128)S(1)}, f32[2,768]{1,0:T(2,128)}, u32[]{:S(2)}) copy-start(f32[2,768]{1,0:T(2,128)} %get-tuple-element.27) | copy-start | bytes 18436
  156.4 120.8 %copy-start.7 = (f32[2,768]{1,0:T(2,128)S(1)}, f32[2,768]{1,0:T(2,128)}, u32[]{:S(2)}) copy-start(f32[2,768]{1,0:T(2,128)} %gains_ref.1) | copy-start | bytes 18436
  156.4 120.8 %copy-start.8 = (f32[2,768]{1,0:T(2,128)S(1)}, f32[2,768]{1,0:T(2,128)}, u32[]{:S(2)}) copy-start(f32[2,768]{1,0:T(2,128)} %param.25) | copy-start | bytes 18436
  156.5 120.8 %copy-start.9 = (f32[2,768]{1,0:T(2,128)S(1)}, f32[2,768]{1,0:T(2,128)}, u32[]{:S(2)}) copy-start(f32[2,768]{1,0:T(2,128)} %param.24) | copy-start | bytes 18436
  156.5 184.0 %all-reduce.3.cloned.1.call-start = ((), (), s32[]{:S(2)}) async-start(), calls=%async_computation.3 | async-start | bytes 3670016 | tf_op jit(solution)/shard_map/psum | solution.py:570
  260.2 1.2 collective-permute-start
  261.5 3.6 collective-permute-start.1
  265.1 3.6 collective-permute-start.2
  268.7 3.7 collective-permute-start.3
  272.5 4.7 %collective-permute-start.4 = (f32[2,768]{1,0:T(2,128)S(1)}, f32[2,768]{1,0:T(2,128)S(1)}, u32[]{:S(2)}, u32[]{:S(2)}) collective-permute-start(f32[2,768]{1,0:T(2,128)S(1)} %add.39), channel_id=1, source_target_pairs={{0,2},{1,3},{2,0},{3,1},{4,6},{5,7},{6,4},{7,5},{8,10},{9,11},{10,... | collective-permute-start | bytes 18440 | tf_op jit(solution)/shard_map/ppermute | solution.py:543
  340.5 2.0 copy-start
  342.5 2.0 copy-start.1
  344.6 2.0 copy-start.2
  346.6 2.0 copy-start.3
  348.6 2.0 copy-start.4
  350.7 1.5 copy-start.5
Sparse Core Ops, SparseCore 0:
  10.9 83.6 all-gather.1
  156.6 103.5 reduce-scatter.1
  262.6 77.8 all-reduce.2

commit v2 on v1

--- a/solution.py
+++ b/solution.py
@@ -83,9 +83,11 @@
 
 def layer_kernel(
     micro,
-    slots,
     piece_slots,
+    grad_slots,
     index_ref,
+    piece_first_ref,
+    grad_first_ref,
     left_ref,
     right_ref,
     x_ref,
@@ -99,7 +101,9 @@
     *rest,
 ):
     pieces = rest[: len(piece_slots)]
-    out_ref, token_grad_ref, gain_ref, grads_ref = rest[len(piece_slots) : len(piece_slots) + 4]
+    rest = rest[len(piece_slots) :]
+    out_ref, token_grad_ref, gain_ref = rest[:3]
+    grad_refs = rest[3 : 3 + len(grad_slots)]
     (
         w_qkv,
         w_o,
@@ -123,26 +127,23 @@
         ring,
         w_sems,
         ring_sems,
-    ) = rest[len(piece_slots) + 4 :]
+    ) = rest[3 + len(grad_slots) :]
     seq = bias_ref.shape[1]
-    tokens = micro * seq
 
     def fetch(block, target, row, col, sem):
         slot = index_ref[block]
-        first = 0
-        for piece, count in zip(pieces, piece_slots):
-
-            @pl.when((slot >= first) & (slot < first + count))
-            def _(piece=piece, first=first):
+        for number, (piece, count) in enumerate(zip(pieces, piece_slots)):
+            place = slot - piece_first_ref[number]
+
+            @pl.when((place >= 0) & (place < count))
+            def _(piece=piece, place=place):
                 pltpu.make_async_copy(
-                    piece.at[slot - first],
+                    piece.at[place],
                     target.at[
                         pl.ds(pl.multiple_of(row * B, B), B), pl.ds(pl.multiple_of(col * B, B), B)
                     ],
                     sem,
                 ).start()
-
-            first += count
 
     def fetch_matrix(first_block, grid_rows, grid_cols, target, col_offset, sem):
         def one(t, carry):
@@ -349,38 +350,52 @@
     lax.fori_loop(0, nd, token_back, 0)
 
     group = ring.shape[1]
-    groups = slots // group
-
-    def ring_copy(g, half):
-        return pltpu.make_async_copy(
-            ring.at[half], grads_ref.at[pl.ds(g * group, group)], ring_sems.at[half]
-        )
+    steps = [count // group for count in grad_slots]
+    total = sum(steps)
+
+    def ring_copy(target, half):
+        return pltpu.make_async_copy(ring.at[half], target, ring_sems.at[half])
 
     def weigh(g, carry):
         half = lax.rem(g, 2)
 
         @pl.when(g >= 2)
         def _():
-            ring_copy(g - 2, half).wait()
-
+            ring_copy(ring.at[half], half).wait()
+
+        first = jnp.int32(0)
+        start = 0
+        for number, count in enumerate(steps):
+            inside = (g >= start) & (g < start + count)
+            first = jnp.where(inside, grad_first_ref[number] + (g - start) * group, first)
+            start += count
         for n in range(group):
-            slot = g * group + n
-            left = jnp.maximum(left_ref[slot], 0)
+            left = left_ref[first + n]
             grad = dot_nn(
-                lefts[pl.ds(pl.multiple_of(left * B, B), B), :],
-                rights[:, pl.ds(pl.multiple_of(right_ref[slot] * B, B), B)],
+                lefts[pl.ds(pl.multiple_of(jnp.maximum(left, 0) * B, B), B), :],
+                rights[:, pl.ds(pl.multiple_of(right_ref[first + n] * B, B), B)],
             )
-            keep = jnp.where(left_ref[slot] >= 0, 1.0, 0.0)
+            keep = jnp.where(left >= 0, 1.0, 0.0)
             ring[half, n] = (grad * keep).astype(BF16)
-        ring_copy(g, half).start()
+        start = 0
+        for target, count in zip(grad_refs, steps):
+
+            @pl.when((g >= start) & (g < start + count))
+            def _(target=target, start=start):
+                ring_copy(target.at[pl.ds((g - start) * group, group)], half).start()
+
+            start += count
         return carry
 
-    lax.fori_loop(0, groups, weigh, 0)
-    for g in range(max(0, groups - 2), groups):
-        ring_copy(g, g % 2).wait()
-
-
-def run_layer(tokens, cotangent, segment_ids, block_slot_index, norm_gains, pieces, slots):
+    lax.fori_loop(0, total, weigh, 0)
+    for g in range(max(0, total - 2), total):
+        ring_copy(ring.at[g % 2], g % 2).wait()
+
+
+def run_layer(
+    tokens, cotangent, segment_ids, block_slot_index, norm_gains, pieces, piece_firsts,
+    grad_slots, grad_firsts, slots,
+):
     micro, seq = segment_ids.shape
     count = micro * seq
     half_dim = HEAD_DIM // 2
@@ -397,22 +412,21 @@
     left_table, right_table = factor_tables()
     slot_left = jnp.full((slots,), -1, jnp.int32).at[block_slot_index].set(left_table)
     slot_right = jnp.zeros((slots,), jnp.int32).at[block_slot_index].set(right_table)
-    group = 4
-    assert slots % group == 0
+    group = next(g for g in (7, 4, 2, 1) if all(count % g == 0 for count in grad_slots))
 
     vmem = pl.BlockSpec(memory_space=pltpu.VMEM)
     smem = pl.BlockSpec(memory_space=pltpu.SMEM)
     hbm = pl.BlockSpec(memory_space=pl.ANY)
     return pl.pallas_call(
-        functools.partial(layer_kernel, micro, slots, [p.shape[0] for p in pieces]),
+        functools.partial(layer_kernel, micro, [p.shape[0] for p in pieces], grad_slots),
         out_shape=(
             jax.ShapeDtypeStruct((count, D), BF16),
             jax.ShapeDtypeStruct((count, D), BF16),
             jax.ShapeDtypeStruct((2, D), F32),
-            jax.ShapeDtypeStruct((slots, B, B), BF16),
+            *(jax.ShapeDtypeStruct((n, B, B), BF16) for n in grad_slots),
         ),
-        in_specs=[smem] * 3 + [vmem] * 8 + [hbm] * len(pieces),
-        out_specs=(vmem, vmem, vmem, hbm),
+        in_specs=[smem] * 5 + [vmem] * 8 + [hbm] * len(pieces),
+        out_specs=(vmem,) * 3 + (hbm,) * len(grad_slots),
         scratch_shapes=[
             pltpu.VMEM((D, 3 * D), BF16),
             pltpu.VMEM((D, D), BF16),
@@ -444,6 +458,8 @@
         name="layer",
     )(
         block_slot_index,
+        jnp.stack(piece_firsts).astype(jnp.int32),
+        jnp.stack(grad_firsts).astype(jnp.int32),
         slot_left,
         slot_right,
         tokens,
@@ -475,9 +491,9 @@
 
 
 def adam_kernel(
-    grad_ref, weight_ref, first_ref, second_ref, left_ref, right_ref,
-    grad_out, first_out, second_out, weight_out, low_out,
+    grad_ref, weight_ref, first_ref, second_ref, left_ref, right_ref, *rest
 ):
+    grad_out, first_out, second_out, weight_out, low_out = rest[-5:]
     for n in range(grad_ref.shape[0]):
         grad = grad_ref[n]
         left = left_ref[n]
@@ -504,23 +520,29 @@
         low_out[n] = weight_new.astype(BF16)
 
 
-def adam_blocks(grads, weights, first_moment, second_moment, left_basis, right_basis):
-    own = weights.shape[0]
-    step = 2 if own % 2 == 0 else 1
-    spec = pl.BlockSpec((step, B, B), lambda s: (s, 0, 0))
-    wide = jax.ShapeDtypeStruct(weights.shape, F32)
+def adam_blocks(grads, start, state, done):
+    own = state[0].shape[0]
+    count = grads.shape[0]
+    step = next(n for n in (2, 1) if count % n == 0 and start % n == 0)
+    local = pl.BlockSpec((step, B, B), lambda s: (s, 0, 0))
+    offset = pl.BlockSpec((step, B, B), lambda s: (s + start // step, 0, 0))
+    hbm = pl.BlockSpec(memory_space=pl.ANY)
+    wide = jax.ShapeDtypeStruct((own, B, B), F32)
     return pl.pallas_call(
         adam_kernel,
-        grid=(own // step,),
-        out_shape=(wide, wide, wide, wide, jax.ShapeDtypeStruct(weights.shape, BF16)),
-        in_specs=[spec] * 6,
-        out_specs=(spec,) * 5,
+        grid=(count // step,),
+        out_shape=(wide, wide, wide, wide, jax.ShapeDtypeStruct((own, B, B), BF16)),
+        in_specs=[local] + [offset] * 5 + [hbm] * len(done),
+        out_specs=(offset,) * 5,
+        input_output_aliases={6 + n: n for n in range(len(done))},
         compiler_params=pltpu.CompilerParams(vmem_limit_bytes=32 * MIB),
         cost_estimate=pl.CostEstimate(
-            flops=own * 12 * 2 * B**3, bytes_accessed=own * B * B * 40, transcendentals=own * B * B
+            flops=count * 12 * 2 * B**3,
+            bytes_accessed=count * B * B * 40,
+            transcendentals=count * B * B,
         ),
         name="adam",
-    )(grads, weights, first_moment, second_moment, left_basis, right_basis)
+    )(grads, *state, *done)
 
 
 def adam_plain(grads, values, first_moment, second_moment):
@@ -543,6 +565,56 @@
         values = values + lax.ppermute(values, axis, [(i, i ^ reach) for i in range(size)])
         reach *= 2
     return values
+
+
+def add_low(*terms):
+    return sum(term.astype(F32) for term in terms).astype(BF16)
+
+
+CORE, ACROSS, ALONG = 1, 2, 4
+DIAGONAL = ACROSS | ALONG
+
+
+def exchange(values, bit):
+    return lax.ppermute(values, "fsdp", [(i, i ^ bit) for i in range(lax.axis_size("fsdp"))])
+
+
+def gather_pieces(owned, me):
+    own = owned.shape[0]
+    half = own // 2
+    first_half, second_half = owned[:half], owned[half:]
+    pieces, firsts = [owned], [me * own]
+
+    def keep(piece, relation, start):
+        pieces.append(piece)
+        firsts.append((me ^ relation) * own + start)
+
+    def keep_both(piece, relation, start):
+        keep(piece, relation, start)
+        keep(exchange(piece, CORE), relation | CORE, start)
+
+    keep(exchange(owned, CORE), CORE, 0)
+    along_first = exchange(first_half, ALONG)
+    across_second = exchange(second_half, ACROSS)
+    along_second = exchange(second_half, ALONG)
+    across_first = exchange(first_half, ACROSS)
+    keep_both(along_first, ALONG, 0)
+    keep_both(across_second, ACROSS, half)
+    keep_both(along_second, ALONG, half)
+    keep_both(across_first, ACROSS, 0)
+    keep_both(exchange(along_first, ACROSS), DIAGONAL, 0)
+    keep_both(exchange(across_second, ALONG), DIAGONAL, half)
+    return pieces, firsts
+
+
+def sum_along_line(values):
+    inner = lax.ppermute(values, "rep", [(0, 1), (3, 2)])
+    halfway = add_low(values, inner)
+    other = lax.ppermute(halfway, "rep", [(1, 2), (2, 1)])
+    total = add_low(halfway, other)
+    back = lax.ppermute(total, "rep", [(1, 0), (2, 3)])
+    place = lax.axis_index("rep")
+    return jnp.where((place == 1) | (place == 2), total, back)
 
 
 def shards(
@@ -559,18 +631,63 @@
     gain_first,
     gain_second,
 ):
-    slots = weights.shape[0] * lax.axis_size("fsdp")
+    owners = lax.axis_size("fsdp")
+    own = weights.shape[0]
+    slots = own * owners
+    me = lax.axis_index("fsdp")
+    state = (weights, first_moment, second_moment, left_basis, right_basis)
     owned_low = weights.astype(BF16)
-    pieces = [lax.all_gather(owned_low, "fsdp", axis=0, tiled=True)]
-    block_out, token_grad, gain_grad, slot_grads = run_layer(
-        tokens, cotangent, segment_ids, block_slot_index, norm_gains, pieces, slots
+    small = owners == 8 and lax.axis_size("rep") == 4 and own % 2 == 0
+
+    if small:
+        pieces, piece_firsts = gather_pieces(owned_low, me)
+        relations = [DIAGONAL | CORE, DIAGONAL, ACROSS | CORE, ALONG | CORE, ACROSS, ALONG, CORE, 0]
+        grad_slots = [own] * owners
+        grad_firsts = [(me ^ relation) * own for relation in relations]
+    else:
+        pieces = [lax.all_gather(owned_low, "fsdp", axis=0, tiled=True)]
+        piece_firsts = [jnp.int32(0)]
+        grad_slots = [slots]
+        grad_firsts = [jnp.int32(0)]
+    block_out, token_grad, gain_grad, *grads = run_layer(
+        tokens, cotangent, segment_ids, block_slot_index, norm_gains, pieces, piece_firsts,
+        grad_slots, grad_firsts, slots,
     )
+    done = ()
+    if small:
+        by_relation = dict(zip(relations, grads))
+        arrived = {
+            relation: exchange(by_relation[relation | CORE], CORE)
+            for relation in (DIAGONAL, ACROSS, ALONG, 0)
+        }
+
+        def chip_sum(relation, start, count):
+            part = slice(start, start + count)
+            return add_low(by_relation[relation][part], arrived[relation][part])
+
+        start = 0
+        while start < own:
+            half = min(2, (own - start) // 2)
+            a, b = (start, half), (start + half, half)
+            diagonal_a = exchange(chip_sum(DIAGONAL, *a), ACROSS)
+            diagonal_b = exchange(chip_sum(DIAGONAL, *b), ALONG)
+            across_a = exchange(chip_sum(ACROSS, *a), ACROSS)
+            along_b = exchange(chip_sum(ALONG, *b), ALONG)
+            across_b = exchange(add_low(chip_sum(ACROSS, *b), diagonal_b), ACROSS)
+            along_a = exchange(add_low(chip_sum(ALONG, *a), diagonal_a), ALONG)
+            total = jnp.concatenate(
+                [
+                    add_low(chip_sum(0, *a), across_a, along_a),
+                    add_low(chip_sum(0, *b), across_b, along_b),
+                ]
+            )
+            done = adam_blocks(sum_along_line(total), start, state, done)
+            start += 2 * half
+    else:
+        owner_sums = lax.psum_scatter(grads[0], "fsdp", scatter_dimension=0, tiled=True)
+        done = adam_blocks(lax.psum(owner_sums, "rep"), 0, state, done)
+    grads_wide, first_new, second_new, weights_new, weights_low = done
     gain_grads = sum_everywhere(sum_everywhere(gain_grad, "fsdp"), "rep")
-    owner_sums = lax.psum_scatter(slot_grads, "fsdp", scatter_dimension=0, tiled=True)
-    owner_grads = lax.psum(owner_sums, "rep")
-    grads_wide, first_new, second_new, weights_new, weights_low = adam_blocks(
-        owner_grads, weights, first_moment, second_moment, left_basis, right_basis
-    )
     gain_first_new, gain_second_new, gains_new = adam_plain(
         gain_grads, norm_gains, gain_first, gain_second
     )

time: 376 us -> 310 us (0.82)
  waiting for transfers between devices: 251 us -> 126 us
  starting transfers between devices: 6.67 us -> 69.4 us
  between operations: 13.9 us -> 1.22 us
  other arithmetic: 9.07 us -> 20.9 us
  local copies, waits for them, and re-layouts: 16 us -> 10.4 us
    ppermute x0 -> x53, waiting for transfers between devices: none -> 111 us  [the longest x41 79.5 us: exchange(): lax.ppermute(values, 'fsdp', [(i, i ^ bit) for i in range(lax.axis_size('...]
    reduce_scatter x1 -> x0, waiting for transfers between devices: 104 us -> none  [shards(): lax.psum_scatter(slot_grads, 'fsdp', scatter_dimension=0, tiled=True)]
    all_gather x1 -> x0, waiting for transfers between devices: 74.5 us -> none  [shards(): pieces = [lax.all_gather(owned_low, 'fsdp', axis=0, tiled=True)]]
    ppermute x0 -> x53, starting transfers between devices: none -> 64.1 us  [the longest x41 40.2 us: exchange(): lax.ppermute(values, 'fsdp', [(i, i ^ bit) for i in range(lax.axis_size('...]
    psum x1 -> x0, waiting for transfers between devices: 62.6 us -> none  [shards(): owner_grads = lax.psum(owner_sums, 'rep')]
    convert_element_type x0 -> x17, other arithmetic: none -> 12 us  [add_low(): return sum((term.astype(F32) for term in terms)).astype(BF16)]
    unnamed x26 -> x42, local copies, waits for them, and re-layouts: 11.7 us -> 2.24 us
    ppermute x5, waiting for transfers between devices: 10.4 us -> 14.9 us  [sum_everywhere(): lax.ppermute(values, axis, [(i, i ^ reach) for i in range(size)])]
  transfers between devices with their start and end apart: 8 -> 58, of which waited for: 8 -> 23; matrix products, arithmetic and copies ran while one was open for 3% -> 9% of each run, Pallas kernels for 0% -> 4%
where the time goes in v2:
time: 310 us; the launch traced here: 308 us
  waiting for transfers between devices  126 us (41%)
  Pallas kernels  80.2 us (26%)
  starting transfers between devices  69.4 us (22%)
  other arithmetic  20.9 us (7%)
  local copies, waits for them, and re-layouts  10.4 us (3%)
    ppermute x41, waiting for transfers between devices, exchange(): lax.ppermute(values, 'fsdp', [(i, i ^ bit) for i in range(lax.axis_size('...  79.5 us
    pallas_call x1, Pallas kernels, run_layer(): pl.pallas_call(functools.partial(layer_kernel, micro, [p.shape[0] for p i...  60.6 us
    ppermute x41, starting transfers between devices, exchange(): lax.ppermute(values, 'fsdp', [(i, i ^ bit) for i in range(lax.axis_size('...  40.2 us
    ppermute x4, waiting for transfers between devices, sum_along_line(): back = lax.ppermute(total, 'rep', [(1, 0), (2, 3)])  21.6 us
    pallas_call x4, Pallas kernels, adam_blocks(): pl.pallas_call(adam_kernel, grid=(count // step,), out_shape=(wide, wide,...  19.6 us
    ppermute x4, starting transfers between devices, sum_along_line(): inner = lax.ppermute(values, 'rep', [(0, 1), (3, 2)])  15 us
    ppermute x5, waiting for transfers between devices, sum_everywhere(): lax.ppermute(values, axis, [(i, i ^ reach) for i in range(size)])  14.9 us
    convert_element_type x17, other arithmetic, add_low(): return sum((term.astype(F32) for term in terms)).astype(BF16)  12 us
  transfers between devices with their start and end apart: 58, of which 23 were waited for; matrix products, arithmetic and copies ran while one was open for 9% of the time, Pallas kernels for 4%

profile of v2, /device:TPU:0, one launch (start us, length us, event | category | flops | bytes accessed | tf_op | source)
XLA Modules:
  0.0 307.9 jit_solution(8924561799953091760)
XLA Ops:
  0.6 2.2 convert_element_type.539.rest_0_
  4.5 2.9 collective-permute-start.1
  7.4 1.5 collective-permute-start.3
  9.6 19.0 %collective-permute-done.1.rest_2_ = bf16[7,256,256]{2,1,0:T(8,128)(2,1)} collective-permute-done((bf16[7,256,256]{2,1,0:T(8,128)(2,1)S(1)}, bf16[7,256,256]{2,1,0:T(8,128)(2,1)}, u32[]{:S(2)}, u32[]{:S(2)}) %collective-permute-start.1) | collective-permute-done | bytes 917536 | tf_op jit(solution)/shard_map/ppermute | solution.py:579
  28.6 2.3 collective-permute-done.3.rest_4_
  32.4 15.3 %collective-permute-done.5.rest_6_ = bf16[7,256,256]{2,1,0:T(8,128)(2,1)} collective-permute-done((bf16[7,256,256]{2,1,0:T(8,128)(2,1)}, bf16[7,256,256]{2,1,0:T(8,128)(2,1)}, u32[]{:S(2)}, u32[]{:S(2)}) %collective-permute-start.5) | collective-permute-done | bytes 917536 | tf_op jit(solution)/shard_map/ppermute | solution.py:579
  47.8 1.7 collective-permute-start.11
  54.7 14.5 %collective-permute-done.9.rest_10_ = bf16[7,256,256]{2,1,0:T(8,128)(2,1)} collective-permute-done((bf16[7,256,256]{2,1,0:T(8,128)(2,1)}, bf16[7,256,256]{2,1,0:T(8,128)(2,1)}, u32[]{:S(2)}, u32[]{:S(2)}) %collective-permute-start.9) | collective-permute-done | bytes 917536 | tf_op jit(solution)/shard_map/ppermute | solution.py:579
  70.0 1.6 scatter_custom_fusion.left_ref
  71.5 1.6 scatter_custom_fusion.1.right_ref
  78.9 60.6 %layer.1 = (bf16[512,768]{1,0:T(8,128)(2,1)}, bf16[512,768]{1,0:T(8,128)(2,1)}, f32[2,768]{1,0:T(2,128)}, bf16[14,256,256]{2,1,0:T(8,128)(2,1)}, bf16[14,256,256...) custom-call(s32[108]{0:T(128)} %index_ref.1, ...), custom_call_target="tpu_custom_call" | custom-call | flops 23000000512 | bytes 32000000 | tf_op jit(solution)/shard_map/layer/pallas_call | solution.py:420
  141.1 10.5 %collective-permute-done.53 = f32[2,768]{1,0:T(2,128)S(1)} collective-permute-done((f32[2,768]{1,0:T(2,128)}, f32[2,768]{1,0:T(2,128)S(1)}, u32[]{:S(2)}, u32[]{:S(2)}) %collective-permute-start.53) | collective-permute-done | bytes 6176 | tf_op jit(solution)/shard_map/ppermute | solution.py:565
  153.7 2.2 collective-permute-done.54
  157.4 2.2 collective-permute-done.55
  162.1 1.5 collective-permute-start.20
  163.6 1.8 add_convert_fusion.14
  168.2 1.6 collective-permute-start.56
  170.6 4.2 %collective-permute-done.45 = bf16[2,256,256]{2,1,0:T(8,128)(2,1)S(1)} collective-permute-done((bf16[2,256,256]{2,1,0:T(8,128)(2,1)S(1)}, bf16[2,256,256]{2,1,0:T(8,128)(2,1)S(1)}, u32[]{:S(2)}, u32[]{:S(2)}) %collective-permute-start.45) | collective-permute-done | bytes 262176 | tf_op jit(solution)/shard_map/ppermute | solution.py:579
  175.5 4.2 %collective-permute-done.36 = bf16[2,256,256]{2,1,0:T(8,128)(2,1)S(1)} collective-permute-done((bf16[2,256,256]{2,1,0:T(8,128)(2,1)S(1)}, bf16[2,256,256]{2,1,0:T(8,128)(2,1)S(1)}, u32[]{:S(2)}, u32[]{:S(2)}) %collective-permute-start.36) | collective-permute-done | bytes 262176 | tf_op jit(solution)/shard_map/ppermute | solution.py:579
  186.0 2.9 collective-permute-done.38
  190.1 3.9 %collective-permute-done.29 = bf16[2,256,256]{2,1,0:T(8,128)(2,1)S(1)} collective-permute-done((bf16[2,256,256]{2,1,0:T(8,128)(2,1)S(1)}, bf16[2,256,256]{2,1,0:T(8,128)(2,1)S(1)}, u32[]{:S(2)}, u32[]{:S(2)}) %collective-permute-start.29) | collective-permute-done | bytes 262176 | tf_op jit(solution)/shard_map/ppermute | solution.py:579
  194.0 1.7 collective-permute-start.46
  200.4 1.5 collective-permute-start.21
  201.9 5.6 %collective-permute-done.22 = bf16[1,256,256]{2,1,0:T(8,128)(2,1)} collective-permute-done((bf16[1,256,256]{2,1,0:T(8,128)(2,1)S(1)}, bf16[1,256,256]{2,1,0:T(8,128)(2,1)}, u32[]{:S(2)}, u32[]{:S(2)}) %collective-permute-start.22) | collective-permute-done | bytes 131104 | tf_op jit(solution)/shard_map/ppermute | solution.py:579
  207.5 2.5 collective-permute-start.48
  212.1 2.0 collective-permute-start.35
  215.5 2.0 collective-permute-done.48
  217.5 3.6 %collective-permute-start.23 = (bf16[2,256,256]{2,1,0:T(8,128)(2,1)S(1)}, bf16[2,256,256]{2,1,0:T(8,128)(2,1)S(1)}, u32[]{:S(2)}, u32[]{:S(2)}) collective-permute-start(bf16[2,256,256]{2,1,0:T(8,128)(2,1)S(1)} %pad_maximum_fusion.4), channel_id=1, source_target_pairs={{0,1},{3,2},{4,5},{7,6},{8,9},{11,10},{12,13},{15,14},{16,17},{19,... | collective-permute-start | bytes 786440 | tf_op jit(solution)/shard_map/ppermute | solution.py:611
  223.1 2.0 collective-permute-start.26
  226.2 2.5 collective-permute-done.35
  228.7 2.0 collective-permute-start.30
  230.7 1.7 add_convert_fusion.12
  232.5 3.6 %collective-permute-start.50 = (bf16[4,256,256]{2,1,0:T(8,128)(2,1)S(1)}, bf16[4,256,256]{2,1,0:T(8,128)(2,1)S(1)}, u32[]{:S(2)}, u32[]{:S(2)}) collective-permute-start(bf16[4,256,256]{2,1,0:T(8,128)(2,1)S(1)} %pad_maximum_fusion.2), channel_id=1, source_target_pairs={{0,1},{3,2},{4,5},{7,6},{8,9},{11,10},{12,13},{15,14},{16,17},{19,... | collective-permute-start | bytes 1572872 | tf_op jit(solution)/shard_map/ppermute | solution.py:611
  237.5 6.2 %collective-permute-start.41 = (bf16[4,256,256]{2,1,0:T(8,128)(2,1)S(1)}, bf16[4,256,256]{2,1,0:T(8,128)(2,1)S(1)}, u32[]{:S(2)}, u32[]{:S(2)}) collective-permute-start(bf16[4,256,256]{2,1,0:T(8,128)(2,1)S(1)} %pad_maximum_fusion.1), channel_id=1, source_target_pairs={{0,1},{3,2},{4,5},{7,6},{8,9},{11,10},{12,13},{15,14},{16,17},{19,... | collective-permute-start | bytes 1572872 | tf_op jit(solution)/shard_map/ppermute | solution.py:611
  245.1 1.7 collective-permute-start.32
  246.8 1.7 collective-permute-done.50
  249.3 4.8 %collective-permute-done.41 = bf16[4,256,256]{2,1,0:T(8,128)(2,1)S(1)} collective-permute-done((bf16[4,256,256]{2,1,0:T(8,128)(2,1)S(1)}, bf16[4,256,256]{2,1,0:T(8,128)(2,1)S(1)}, u32[]{:S(2)}, u32[]{:S(2)}) %collective-permute-start.41) | collective-permute-done | bytes 524320 | tf_op jit(solution)/shard_map/ppermute | solution.py:611
  255.1 1.6 collective-permute-start.25
  256.7 3.1 collective-permute-done.32
  260.9 1.6 collective-permute-start.52
  264.6 4.5 %collective-permute-done.25 = bf16[2,256,256]{2,1,0:T(8,128)(2,1)S(1)} collective-permute-done((bf16[2,256,256]{2,1,0:T(8,128)(2,1)S(1)}, bf16[2,256,256]{2,1,0:T(8,128)(2,1)S(1)}, u32[]{:S(2)}, u32[]{:S(2)}) %collective-permute-start.25) | collective-permute-done | bytes 262176 | tf_op jit(solution)/shard_map/ppermute | solution.py:615
  269.4 1.6 collective-permute-start.34
  270.9 10.7 %collective-permute-done.52 = bf16[4,256,256]{2,1,0:T(8,128)(2,1)S(1)} collective-permute-done((bf16[4,256,256]{2,1,0:T(8,128)(2,1)S(1)}, bf16[4,256,256]{2,1,0:T(8,128)(2,1)S(1)}, u32[]{:S(2)}, u32[]{:S(2)}) %collective-permute-start.52) | collective-permute-done | bytes 524320 | tf_op jit(solution)/shard_map/ppermute | solution.py:615
  281.6 6.4 %collective-permute-done.43 = bf16[4,256,256]{2,1,0:T(8,128)(2,1)S(1)} collective-permute-done((bf16[4,256,256]{2,1,0:T(8,128)(2,1)S(1)}, bf16[4,256,256]{2,1,0:T(8,128)(2,1)S(1)}, u32[]{:S(2)}, u32[]{:S(2)}) %collective-permute-start.43) | collective-permute-done | bytes 524320 | tf_op jit(solution)/shard_map/ppermute | solution.py:615
  288.2 5.7 %adam.4 = (f32[14,256,256]{2,1,0:T(8,128)}, f32[14,256,256]{2,1,0:T(8,128)}, f32[14,256,256]{2,1,0:T(8,128)}, f32[14,256,256]{2,1,0:T(8,128)}, bf16[14,256,256]{2,1,0:T(8,128)(2,1)}) custom-call(bf16[4,256,256]{2,1,0:T(8,128)(2,1)S(1)} %get-tuple-element.114.grad_ref, f32[14,256,256]{2,1,0:T(8,128)S(1)} %copy-done, f32[14,256,256]{2,1,0:T(8,128)S(1)} %copy-done.1, ...), custom_call_target="tpu_custom_call" | custom-call | flops 1610612736 | bytes 10485760 | tf_op jit(solution)/shard_map/adam/pallas_call | solution.py:531
  293.9 5.4 %adam.5 = (f32[14,256,256]{2,1,0:T(8,128)}, f32[14,256,256]{2,1,0:T(8,128)}, f32[14,256,256]{2,1,0:T(8,128)}, f32[14,256,256]{2,1,0:T(8,128)}, bf16[14,256,256]{2,1,0:T(8,128)(2,1)}) custom-call(bf16[4,256,256]{2,1,0:T(8,128)(2,1)S(1)} %get-tuple-element.115.grad_ref, ...), custom_call_target="tpu_custom_call", output_to_operand_aliasing={{0}: (6, {}), {1}: (7, {}), {2}: (8, {}), {3}: (9, {}), {4}... | custom-call | flops 1610612736 | bytes 10485760 | tf_op jit(solution)/shard_map/adam/pallas_call | solution.py:531
  299.3 5.4 %adam.6 = (f32[14,256,256]{2,1,0:T(8,128)}, f32[14,256,256]{2,1,0:T(8,128)}, f32[14,256,256]{2,1,0:T(8,128)}, f32[14,256,256]{2,1,0:T(8,128)}, bf16[14,256,256]{2,1,0:T(8,128)(2,1)}) custom-call(bf16[4,256,256]{2,1,0:T(8,128)(2,1)S(1)} %broadcast_select_fusion.2.grad_ref, ...), custom_call_target="tpu_custom_call", output_to_operand_aliasing={{0}: (6, {}), {1}: (7, {}), {2}: (8, {}), {3}: (9, {}), {4}... | custom-call | flops 1610612736 | bytes 10485760 | tf_op jit(solution)/shard_map/adam/pallas_call | solution.py:531
  304.8 3.1 %adam.7 = (f32[14,256,256]{2,1,0:T(8,128)}, f32[14,256,256]{2,1,0:T(8,128)}, f32[14,256,256]{2,1,0:T(8,128)}, f32[14,256,256]{2,1,0:T(8,128)}, bf16[14,256,256]{2,1,0:T(8,128)(2,1)}) custom-call(bf16[2,256,256]{2,1,0:T(8,128)(2,1)S(1)} %broadcast_select_fusion.3.grad_ref, ...), custom_call_target="tpu_custom_call", output_to_operand_aliasing={{0}: (6, {}), {1}: (7, {}), {2}: (8, {}), {3}: (9, {}), {4}... | custom-call | flops 805306368 | bytes 5242880 | tf_op jit(solution)/shard_map/adam/pallas_call | solution.py:531
  (168 shorter events, 54.1 us)
Async XLA Ops:
  2.9 51.2 %collective-permute-start = (bf16[14,256,256]{2,1,0:T(8,128)(2,1)S(1)}, bf16[14,256,256]{2,1,0:T(8,128)(2,1)}, u32[]{:S(2)}, u32[]{:S(2)}) collective-permute-start(bf16[14,256,256]{2,1,0:T(8,128)(2,1)S(1)} %convert_element_type.539.rest_0_), channel_id=1, source_target_pairs={{0,4},{4,0},{8,12},{12,8},{16,20},{20,16},{24,28},{28,24},{1,5},{5... | collective-permute-start | bytes 5505032 | tf_op jit(solution)/shard_map/ppermute | solution.py:579
  4.5 24.2 %collective-permute-start.1 = (bf16[7,256,256]{2,1,0:T(8,128)(2,1)S(1)}, bf16[7,256,256]{2,1,0:T(8,128)(2,1)}, u32[]{:S(2)}, u32[]{:S(2)}) collective-permute-start(bf16[7,256,256]{2,1,0:T(8,128)(2,1)S(1)} %get-tuple-element.108), channel_id=1, source_target_pairs={{0,16},{4,20},{8,24},{12,28},{16,0},{20,4},{24,8},{28,12},{1,17},{... | collective-permute-start | bytes 2752520 | tf_op jit(solution)/shard_map/ppermute | solution.py:579
  7.4 23.6 %collective-permute-start.3 = (bf16[7,256,256]{2,1,0:T(8,128)(2,1)}, bf16[7,256,256]{2,1,0:T(8,128)(2,1)}, u32[]{:S(2)}, u32[]{:S(2)}) collective-permute-start(bf16[7,256,256]{2,1,0:T(8,128)(2,1)} %get-tuple-element.107), channel_id=1, source_target_pairs={{0,8},{4,12},{8,0},{12,4},{16,24},{20,28},{24,16},{28,20},{1,9},{5... | collective-permute-start | bytes 2752520 | tf_op jit(solution)/shard_map/ppermute | solution.py:579
  8.9 38.9 %collective-permute-start.5 = (bf16[7,256,256]{2,1,0:T(8,128)(2,1)}, bf16[7,256,256]{2,1,0:T(8,128)(2,1)}, u32[]{:S(2)}, u32[]{:S(2)}) collective-permute-start(bf16[7,256,256]{2,1,0:T(8,128)(2,1)} %get-tuple-element.107), channel_id=1, source_target_pairs={{0,16},{4,20},{8,24},{12,28},{16,0},{20,4},{24,8},{28,12},{1,17},{... | collective-permute-start | bytes 2752520 | tf_op jit(solution)/shard_map/ppermute | solution.py:579
  9.4 44.7 %collective-permute-start.7 = (bf16[7,256,256]{2,1,0:T(8,128)(2,1)S(1)}, bf16[7,256,256]{2,1,0:T(8,128)(2,1)}, u32[]{:S(2)}, u32[]{:S(2)}) collective-permute-start(bf16[7,256,256]{2,1,0:T(8,128)(2,1)S(1)} %get-tuple-element.108), channel_id=1, source_target_pairs={{0,8},{4,12},{8,0},{12,4},{16,24},{20,28},{24,16},{28,20},{1,9},{5... | collective-permute-start | bytes 2752520 | tf_op jit(solution)/shard_map/ppermute | solution.py:579
  28.6 25.9 %collective-permute-start.2 = (bf16[7,256,256]{2,1,0:T(8,128)(2,1)}, bf16[7,256,256]{2,1,0:T(8,128)(2,1)}, u32[]{:S(2)}, u32[]{:S(2)}) collective-permute-start(bf16[7,256,256]{2,1,0:T(8,128)(2,1)} %collective-permute-done.1.rest_2_), channel_id=1, source_target_pairs={{0,4},{4,0},{8,12},{12,8},{16,20},{20,16},{24,28},{28,24},{1,5},{5... | collective-permute-start | bytes 2752520 | tf_op jit(solution)/shard_map/ppermute | solution.py:579
  30.9 38.2 %collective-permute-start.9 = (bf16[7,256,256]{2,1,0:T(8,128)(2,1)}, bf16[7,256,256]{2,1,0:T(8,128)(2,1)}, u32[]{:S(2)}, u32[]{:S(2)}) collective-permute-start(bf16[7,256,256]{2,1,0:T(8,128)(2,1)} %collective-permute-done.1.rest_2_), channel_id=1, source_target_pairs={{0,8},{4,12},{8,0},{12,4},{16,24},{20,28},{24,16},{28,20},{1,9},{5... | collective-permute-start | bytes 2752520 | tf_op jit(solution)/shard_map/ppermute | solution.py:579
  47.8 22.2 %collective-permute-start.11 = (bf16[7,256,256]{2,1,0:T(8,128)(2,1)}, bf16[7,256,256]{2,1,0:T(8,128)(2,1)}, u32[]{:S(2)}, u32[]{:S(2)}) collective-permute-start(bf16[7,256,256]{2,1,0:T(8,128)(2,1)} %collective-permute-done.3.rest_4_), channel_id=1, source_target_pairs={{0,16},{4,20},{8,24},{12,28},{16,0},{20,4},{24,8},{28,12},{1,17},{... | collective-permute-start | bytes 2752520 | tf_op jit(solution)/shard_map/ppermute | solution.py:579
  54.1 23.3 %collective-permute-start.4 = (bf16[7,256,256]{2,1,0:T(8,128)(2,1)}, bf16[7,256,256]{2,1,0:T(8,128)(2,1)S(1)}, u32[]{:S(2)}, u32[]{:S(2)}) collective-permute-start(bf16[7,256,256]{2,1,0:T(8,128)(2,1)} %collective-permute-done.3.rest_4_), channel_id=1, source_target_pairs={{0,4},{4,0},{8,12},{12,8},{16,20},{20,16},{24,28},{28,24},{1,5},{5... | collective-permute-start | bytes 2752520 | tf_op jit(solution)/shard_map/ppermute | solution.py:579
  54.1 23.3 %collective-permute-start.6 = (bf16[7,256,256]{2,1,0:T(8,128)(2,1)}, bf16[7,256,256]{2,1,0:T(8,128)(2,1)S(1)}, u32[]{:S(2)}, u32[]{:S(2)}) collective-permute-start(bf16[7,256,256]{2,1,0:T(8,128)(2,1)} %collective-permute-done.5.rest_6_), channel_id=1, source_target_pairs={{0,4},{4,0},{8,12},{12,8},{16,20},{20,16},{24,28},{28,24},{1,5},{5... | collective-permute-start | bytes 2752520 | tf_op jit(solution)/shard_map/ppermute | solution.py:579
  54.6 22.8 %collective-permute-start.8 = (bf16[7,256,256]{2,1,0:T(8,128)(2,1)}, bf16[7,256,256]{2,1,0:T(8,128)(2,1)S(1)}, u32[]{:S(2)}, u32[]{:S(2)}) collective-permute-start(bf16[7,256,256]{2,1,0:T(8,128)(2,1)} %collective-permute-done.7.rest_8_), channel_id=1, source_target_pairs={{0,4},{4,0},{8,12},{12,8},{16,20},{20,16},{24,28},{28,24},{1,5},{5... | collective-permute-start | bytes 2752520 | tf_op jit(solution)/shard_map/ppermute | solution.py:579
  139.5 20.1 %collective-permute-start.17 = (bf16[14,256,256]{2,1,0:T(8,128)(2,1)}, bf16[14,256,256]{2,1,0:T(8,128)(2,1)S(1)}, u32[]{:S(2)}, u32[]{:S(2)}) collective-permute-start(bf16[14,256,256]{2,1,0:T(8,128)(2,1)} %get-tuple-element.50), channel_id=1, source_target_pairs={{0,4},{4,0},{8,12},{12,8},{16,20},{20,16},{24,28},{28,24},{1,5},{5... | collective-permute-start | bytes 5505032 | tf_op jit(solution)/shard_map/ppermute | solution.py:579
  140.1 25.4 %collective-permute-start.16 = (bf16[14,256,256]{2,1,0:T(8,128)(2,1)}, bf16[14,256,256]{2,1,0:T(8,128)(2,1)S(1)}, u32[]{:S(2)}, u32[]{:S(2)}) collective-permute-start(bf16[14,256,256]{2,1,0:T(8,128)(2,1)} %get-tuple-element.48), channel_id=1, source_target_pairs={{0,4},{4,0},{8,12},{12,8},{16,20},{20,16},{24,28},{28,24},{1,5},{5... | collective-permute-start | bytes 5505032 | tf_op jit(solution)/shard_map/ppermute | solution.py:579
  140.2 25.9 %collective-permute-start.14 = (bf16[14,256,256]{2,1,0:T(8,128)(2,1)}, bf16[14,256,256]{2,1,0:T(8,128)(2,1)S(1)}, u32[]{:S(2)}, u32[]{:S(2)}) collective-permute-start(bf16[14,256,256]{2,1,0:T(8,128)(2,1)} %get-tuple-element.46), channel_id=1, source_target_pairs={{0,4},{4,0},{8,12},{12,8},{16,20},{20,16},{24,28},{28,24},{1,5},{5... | collective-permute-start | bytes 5505032 | tf_op jit(solution)/shard_map/ppermute | solution.py:579
  140.6 57.0 %collective-permute-start.13 = (bf16[14,256,256]{2,1,0:T(8,128)(2,1)}, bf16[14,256,256]{2,1,0:T(8,128)(2,1)}, u32[]{:S(2)}, u32[]{:S(2)}) collective-permute-start(bf16[14,256,256]{2,1,0:T(8,128)(2,1)} %get-tuple-element.44), channel_id=1, source_target_pairs={{0,4},{4,0},{8,12},{12,8},{16,20},{20,16},{24,28},{28,24},{1,5},{5... | collective-permute-start | bytes 5505032 | tf_op jit(solution)/shard_map/ppermute | solution.py:579
  140.7 10.9 %collective-permute-start.53 = (f32[2,768]{1,0:T(2,128)}, f32[2,768]{1,0:T(2,128)S(1)}, u32[]{:S(2)}, u32[]{:S(2)}) collective-permute-start(f32[2,768]{1,0:T(2,128)} %get-tuple-element.71), channel_id=1, source_target_pairs={{0,4},{4,0},{8,12},{12,8},{16,20},{20,16},{24,28},{28,24},{1,5},{5... | collective-permute-start | bytes 18440 | tf_op jit(solution)/shard_map/ppermute | solution.py:565
  165.5 9.3 %collective-permute-start.45 = (bf16[2,256,256]{2,1,0:T(8,128)(2,1)S(1)}, bf16[2,256,256]{2,1,0:T(8,128)(2,1)S(1)}, u32[]{:S(2)}, u32[]{:S(2)}) collective-permute-start(bf16[2,256,256]{2,1,0:T(8,128)(2,1)S(1)} %get-tuple-element.91), channel_id=1, source_target_pairs={{0,8},{4,12},{8,0},{12,4},{16,24},{20,28},{24,16},{28,20},{1,9},{5... | collective-permute-start | bytes 786440 | tf_op jit(solution)/shard_map/ppermute | solution.py:579
  166.1 13.6 %collective-permute-start.36 = (bf16[2,256,256]{2,1,0:T(8,128)(2,1)S(1)}, bf16[2,256,256]{2,1,0:T(8,128)(2,1)S(1)}, u32[]{:S(2)}, u32[]{:S(2)}) collective-permute-start(bf16[2,256,256]{2,1,0:T(8,128)(2,1)S(1)} %get-tuple-element.94), channel_id=1, source_target_pairs={{0,8},{4,12},{8,0},{12,4},{16,24},{20,28},{24,16},{28,20},{1,9},{5... | collective-permute-start | bytes 786440 | tf_op jit(solution)/shard_map/ppermute | solution.py:579
  167.6 14.9 %collective-permute-start.27 = (bf16[2,256,256]{2,1,0:T(8,128)(2,1)S(1)}, bf16[2,256,256]{2,1,0:T(8,128)(2,1)S(1)}, u32[]{:S(2)}, u32[]{:S(2)}) collective-permute-start(bf16[2,256,256]{2,1,0:T(8,128)(2,1)S(1)} %get-tuple-element.96), channel_id=1, source_target_pairs={{0,8},{4,12},{8,0},{12,4},{16,24},{20,28},{24,16},{28,20},{1,9},{5... | collective-permute-start | bytes 786440 | tf_op jit(solution)/shard_map/ppermute | solution.py:579
  168.2 28.9 %collective-permute-start.56 = (f32[2,768]{1,0:T(2,128)S(1)}, f32[2,768]{1,0:T(2,128)S(1)}, u32[]{:S(2)}, u32[]{:S(2)}) collective-permute-start(f32[2,768]{1,0:T(2,128)S(1)} %add.314), channel_id=1, source_target_pairs={{0,1},{1,0},{2,3},{3,2},{4,5},{5,4},{6,7},{7,6},{8,9},{9,8},{10,11... | collective-permute-start | bytes 18440 | tf_op jit(solution)/shard_map/ppermute | solution.py:565
  174.8 10.6 %collective-permute-start.47 = (bf16[2,256,256]{2,1,0:T(8,128)(2,1)S(1)}, bf16[2,256,256]{2,1,0:T(8,128)(2,1)S(1)}, u32[]{:S(2)}, u32[]{:S(2)}) collective-permute-start(bf16[2,256,256]{2,1,0:T(8,128)(2,1)S(1)} %get-tuple-element.92), channel_id=1, source_target_pairs={{0,16},{4,20},{8,24},{12,28},{16,0},{20,4},{24,8},{28,12},{1,17},{... | collective-permute-start | bytes 786440 | tf_op jit(solution)/shard_map/ppermute | solution.py:579
  182.5 11.5 %collective-permute-start.29 = (bf16[2,256,256]{2,1,0:T(8,128)(2,1)S(1)}, bf16[2,256,256]{2,1,0:T(8,128)(2,1)S(1)}, u32[]{:S(2)}, u32[]{:S(2)}) collective-permute-start(bf16[2,256,256]{2,1,0:T(8,128)(2,1)S(1)} %get-tuple-element.95), channel_id=1, source_target_pairs={{0,16},{4,20},{8,24},{12,28},{16,0},{20,4},{24,8},{28,12},{1,17},{... | collective-permute-start | bytes 786440 | tf_op jit(solution)/shard_map/ppermute | solution.py:579
  185.4 13.2 %collective-permute-start.19 = (bf16[1,256,256]{2,1,0:T(8,128)(2,1)S(1)}, bf16[1,256,256]{2,1,0:T(8,128)(2,1)S(1)}, u32[]{:S(2)}, u32[]{:S(2)}) collective-permute-start(bf16[1,256,256]{2,1,0:T(8,128)(2,1)S(1)} %get-tuple-element.103), channel_id=1, source_target_pairs={{0,16},{4,20},{8,24},{12,28},{16,0},{20,4},{24,8},{28,12},{1,17},{... | collective-permute-start | bytes 393224 | tf_op jit(solution)/shard_map/ppermute | solution.py:579
  188.9 10.8 %collective-permute-start.15 = (bf16[1,256,256]{2,1,0:T(8,128)(2,1)S(1)}, bf16[1,256,256]{2,1,0:T(8,128)(2,1)S(1)}, u32[]{:S(2)}, u32[]{:S(2)}) collective-permute-start(bf16[1,256,256]{2,1,0:T(8,128)(2,1)S(1)} %get-tuple-element.101), channel_id=1, source_target_pairs={{0,8},{4,12},{8,0},{12,4},{16,24},{20,28},{24,16},{28,20},{1,9},{5... | collective-permute-start | bytes 393224 | tf_op jit(solution)/shard_map/ppermute | solution.py:579
  194.0 17.1 %collective-permute-start.46 = (bf16[2,256,256]{2,1,0:T(8,128)(2,1)}, bf16[2,256,256]{2,1,0:T(8,128)(2,1)S(1)}, u32[]{:S(2)}, u32[]{:S(2)}) collective-permute-start(bf16[2,256,256]{2,1,0:T(8,128)(2,1)} %get-tuple-element.85), channel_id=1, source_target_pairs={{0,16},{4,20},{8,24},{12,28},{16,0},{20,4},{24,8},{28,12},{1,17},{... | collective-permute-start | bytes 786440 | tf_op jit(solution)/shard_map/ppermute | solution.py:579
  197.2 14.1 %collective-permute-start.44 = (bf16[2,256,256]{2,1,0:T(8,128)(2,1)}, bf16[2,256,256]{2,1,0:T(8,128)(2,1)S(1)}, u32[]{:S(2)}, u32[]{:S(2)}) collective-permute-start(bf16[2,256,256]{2,1,0:T(8,128)(2,1)} %get-tuple-element.79), channel_id=1, source_target_pairs={{0,8},{4,12},{8,0},{12,4},{16,24},{20,28},{24,16},{28,20},{1,9},{5... | collective-permute-start | bytes 786440 | tf_op jit(solution)/shard_map/ppermute | solution.py:579
  197.7 14.5 %collective-permute-start.49 = (bf16[2,256,256]{2,1,0:T(8,128)(2,1)}, bf16[2,256,256]{2,1,0:T(8,128)(2,1)S(1)}, u32[]{:S(2)}, u32[]{:S(2)}) collective-permute-start(bf16[2,256,256]{2,1,0:T(8,128)(2,1)} %get-tuple-element.86), channel_id=1, source_target_pairs={{0,16},{4,20},{8,24},{12,28},{16,0},{20,4},{24,8},{28,12},{1,17},{... | collective-permute-start | bytes 786440 | tf_op jit(solution)/shard_map/ppermute | solution.py:579
  200.4 9.7 %collective-permute-start.21 = (bf16[1,256,256]{2,1,0:T(8,128)(2,1)}, bf16[1,256,256]{2,1,0:T(8,128)(2,1)}, u32[]{:S(2)}, u32[]{:S(2)}) collective-permute-start(bf16[1,256,256]{2,1,0:T(8,128)(2,1)} %get-tuple-element.102), channel_id=1, source_target_pairs={{0,8},{4,12},{8,0},{12,4},{16,24},{20,28},{24,16},{28,20},{1,9},{5... | collective-permute-start | bytes 393224 | tf_op jit(solution)/shard_map/ppermute | solution.py:579
  207.5 10.0 %collective-permute-start.48 = (bf16[2,256,256]{2,1,0:T(8,128)(2,1)}, bf16[2,256,256]{2,1,0:T(8,128)(2,1)S(1)}, u32[]{:S(2)}, u32[]{:S(2)}) collective-permute-start(bf16[2,256,256]{2,1,0:T(8,128)(2,1)} %get-tuple-element.80), channel_id=1, source_target_pairs={{0,8},{4,12},{8,0},{12,4},{16,24},{20,28},{24,16},{28,20},{1,9},{5... | collective-permute-start | bytes 786440 | tf_op jit(solution)/shard_map/ppermute | solution.py:579
  210.0 11.0 %collective-permute-start.40 = (bf16[2,256,256]{2,1,0:T(8,128)(2,1)}, bf16[2,256,256]{2,1,0:T(8,128)(2,1)S(1)}, u32[]{:S(2)}, u32[]{:S(2)}) collective-permute-start(bf16[2,256,256]{2,1,0:T(8,128)(2,1)} %get-tuple-element.87), channel_id=1, source_target_pairs={{0,16},{4,20},{8,24},{12,28},{16,0},{20,4},{24,8},{28,12},{1,17},{... | collective-permute-start | bytes 786440 | tf_op jit(solution)/shard_map/ppermute | solution.py:579
  211.1 11.9 %collective-permute-start.39 = (bf16[2,256,256]{2,1,0:T(8,128)(2,1)}, bf16[2,256,256]{2,1,0:T(8,128)(2,1)S(1)}, u32[]{:S(2)}, u32[]{:S(2)}) collective-permute-start(bf16[2,256,256]{2,1,0:T(8,128)(2,1)} %get-tuple-element.81), channel_id=1, source_target_pairs={{0,8},{4,12},{8,0},{12,4},{16,24},{20,28},{24,16},{28,20},{1,9},{5... | collective-permute-start | bytes 786440 | tf_op jit(solution)/shard_map/ppermute | solution.py:579
  211.3 13.8 %collective-permute-start.37 = (bf16[2,256,256]{2,1,0:T(8,128)(2,1)}, bf16[2,256,256]{2,1,0:T(8,128)(2,1)S(1)}, u32[]{:S(2)}, u32[]{:S(2)}) collective-permute-start(bf16[2,256,256]{2,1,0:T(8,128)(2,1)} %get-tuple-element.88), channel_id=1, source_target_pairs={{0,16},{4,20},{8,24},{12,28},{16,0},{20,4},{24,8},{28,12},{1,17},{... | collective-permute-start | bytes 786440 | tf_op jit(solution)/shard_map/ppermute | solution.py:579
  212.1 16.6 %collective-permute-start.35 = (bf16[2,256,256]{2,1,0:T(8,128)(2,1)}, bf16[2,256,256]{2,1,0:T(8,128)(2,1)S(1)}, u32[]{:S(2)}, u32[]{:S(2)}) collective-permute-start(bf16[2,256,256]{2,1,0:T(8,128)(2,1)} %get-tuple-element.82), channel_id=1, source_target_pairs={{0,8},{4,12},{8,0},{12,4},{16,24},{20,28},{24,16},{28,20},{1,9},{5... | collective-permute-start | bytes 786440 | tf_op jit(solution)/shard_map/ppermute | solution.py:579
  217.5 15.1 %collective-permute-start.23 = (bf16[2,256,256]{2,1,0:T(8,128)(2,1)S(1)}, bf16[2,256,256]{2,1,0:T(8,128)(2,1)S(1)}, u32[]{:S(2)}, u32[]{:S(2)}) collective-permute-start(bf16[2,256,256]{2,1,0:T(8,128)(2,1)S(1)} %pad_maximum_fusion.4), channel_id=1, source_target_pairs={{0,1},{3,2},{4,5},{7,6},{8,9},{11,10},{12,13},{15,14},{16,17},{19,... | collective-permute-start | bytes 786440 | tf_op jit(solution)/shard_map/ppermute | solution.py:611
  221.0 15.2 %collective-permute-start.28 = (bf16[2,256,256]{2,1,0:T(8,128)(2,1)S(1)}, bf16[2,256,256]{2,1,0:T(8,128)(2,1)S(1)}, u32[]{:S(2)}, u32[]{:S(2)}) collective-permute-start(bf16[2,256,256]{2,1,0:T(8,128)(2,1)S(1)} %get-tuple-element.90), channel_id=1, source_target_pairs={{0,16},{4,20},{8,24},{12,28},{16,0},{20,4},{24,8},{28,12},{1,17},{... | collective-permute-start | bytes 786440 | tf_op jit(solution)/shard_map/ppermute | solution.py:579
  223.1 13.6 %collective-permute-start.26 = (bf16[2,256,256]{2,1,0:T(8,128)(2,1)S(1)}, bf16[2,256,256]{2,1,0:T(8,128)(2,1)S(1)}, u32[]{:S(2)}, u32[]{:S(2)}) collective-permute-start(bf16[2,256,256]{2,1,0:T(8,128)(2,1)S(1)} %copy-done.9), channel_id=1, source_target_pairs={{0,8},{4,12},{8,0},{12,4},{16,24},{20,28},{24,16},{28,20},{1,9},{5... | collective-permute-start | bytes 786440 | tf_op jit(solution)/shard_map/ppermute | solution.py:579
  225.1 12.4 %collective-permute-start.31 = (bf16[2,256,256]{2,1,0:T(8,128)(2,1)S(1)}, bf16[2,256,256]{2,1,0:T(8,128)(2,1)S(1)}, u32[]{:S(2)}, u32[]{:S(2)}) collective-permute-start(bf16[2,256,256]{2,1,0:T(8,128)(2,1)S(1)} %get-tuple-element.89), channel_id=1, source_target_pairs={{0,16},{4,20},{8,24},{12,28},{16,0},{20,4},{24,8},{28,12},{1,17},{... | collective-permute-start | bytes 786440 | tf_op jit(solution)/shard_map/ppermute | solution.py:579
  228.7 15.0 %collective-permute-start.30 = (bf16[2,256,256]{2,1,0:T(8,128)(2,1)S(1)}, bf16[2,256,256]{2,1,0:T(8,128)(2,1)S(1)}, u32[]{:S(2)}, u32[]{:S(2)}) collective-permute-start(bf16[2,256,256]{2,1,0:T(8,128)(2,1)S(1)} %get-tuple-element.83), channel_id=1, source_target_pairs={{0,8},{4,12},{8,0},{12,4},{16,24},{20,28},{24,16},{28,20},{1,9},{5... | collective-permute-start | bytes 786440 | tf_op jit(solution)/shard_map/ppermute | solution.py:579
  232.5 15.9 %collective-permute-start.50 = (bf16[4,256,256]{2,1,0:T(8,128)(2,1)S(1)}, bf16[4,256,256]{2,1,0:T(8,128)(2,1)S(1)}, u32[]{:S(2)}, u32[]{:S(2)}) collective-permute-start(bf16[4,256,256]{2,1,0:T(8,128)(2,1)S(1)} %pad_maximum_fusion.2), channel_id=1, source_target_pairs={{0,1},{3,2},{4,5},{7,6},{8,9},{11,10},{12,13},{15,14},{16,17},{19,... | collective-permute-start | bytes 1572872 | tf_op jit(solution)/shard_map/ppermute | solution.py:611
  236.3 27.7 %collective-permute-start.57 = (f32[2,768]{1,0:T(2,128)S(1)}, f32[2,768]{1,0:T(2,128)S(1)}, u32[]{:S(2)}, u32[]{:S(2)}) collective-permute-start(f32[2,768]{1,0:T(2,128)S(1)} %add.315), channel_id=1, source_target_pairs={{0,2},{1,3},{2,0},{3,1},{4,6},{5,7},{6,4},{7,5},{8,10},{9,11},{10,... | collective-permute-start | bytes 18440 | tf_op jit(solution)/shard_map/ppermute | solution.py:565
  236.7 18.3 %collective-permute-start.24 = (bf16[2,256,256]{2,1,0:T(8,128)(2,1)S(1)}, bf16[2,256,256]{2,1,0:T(8,128)(2,1)S(1)}, u32[]{:S(2)}, u32[]{:S(2)}) collective-permute-start(bf16[2,256,256]{2,1,0:T(8,128)(2,1)S(1)} %add_convert_fusion.43), channel_id=1, source_target_pairs={{1,2},{2,1},{5,6},{6,5},{9,10},{10,9},{13,14},{14,13},{17,18},{18,... | collective-permute-start | bytes 786440 | tf_op jit(solution)/shard_map/ppermute | solution.py:613
  237.5 16.6 %collective-permute-start.41 = (bf16[4,256,256]{2,1,0:T(8,128)(2,1)S(1)}, bf16[4,256,256]{2,1,0:T(8,128)(2,1)S(1)}, u32[]{:S(2)}, u32[]{:S(2)}) collective-permute-start(bf16[4,256,256]{2,1,0:T(8,128)(2,1)S(1)} %pad_maximum_fusion.1), channel_id=1, source_target_pairs={{0,1},{3,2},{4,5},{7,6},{8,9},{11,10},{12,13},{15,14},{16,17},{19,... | collective-permute-start | bytes 1572872 | tf_op jit(solution)/shard_map/ppermute | solution.py:611
  245.1 14.7 %collective-permute-start.32 = (bf16[4,256,256]{2,1,0:T(8,128)(2,1)S(1)}, bf16[4,256,256]{2,1,0:T(8,128)(2,1)S(1)}, u32[]{:S(2)}, u32[]{:S(2)}) collective-permute-start(bf16[4,256,256]{2,1,0:T(8,128)(2,1)S(1)} %pad_maximum_fusion), channel_id=1, source_target_pairs={{0,1},{3,2},{4,5},{7,6},{8,9},{11,10},{12,13},{15,14},{16,17},{19,... | collective-permute-start | bytes 1572872 | tf_op jit(solution)/shard_map/ppermute | solution.py:611
  248.6 12.2 %collective-permute-start.51 = (bf16[4,256,256]{2,1,0:T(8,128)(2,1)S(1)}, bf16[4,256,256]{2,1,0:T(8,128)(2,1)S(1)}, u32[]{:S(2)}, u32[]{:S(2)}) collective-permute-start(bf16[4,256,256]{2,1,0:T(8,128)(2,1)S(1)} %add_convert_fusion.1), channel_id=1, source_target_pairs={{1,2},{2,1},{5,6},{6,5},{9,10},{10,9},{13,14},{14,13},{17,18},{18,... | collective-permute-start | bytes 1572872 | tf_op jit(solution)/shard_map/ppermute | solution.py:613
  255.1 14.0 %collective-permute-start.25 = (bf16[2,256,256]{2,1,0:T(8,128)(2,1)S(1)}, bf16[2,256,256]{2,1,0:T(8,128)(2,1)S(1)}, u32[]{:S(2)}, u32[]{:S(2)}) collective-permute-start(bf16[2,256,256]{2,1,0:T(8,128)(2,1)S(1)} %add_convert_fusion.42), channel_id=1, source_target_pairs={{1,0},{2,3},{5,4},{6,7},{9,8},{10,11},{13,12},{14,15},{17,16},{18,... | collective-permute-start | bytes 786440 | tf_op jit(solution)/shard_map/ppermute | solution.py:615
  260.9 20.7 %collective-permute-start.52 = (bf16[4,256,256]{2,1,0:T(8,128)(2,1)S(1)}, bf16[4,256,256]{2,1,0:T(8,128)(2,1)S(1)}, u32[]{:S(2)}, u32[]{:S(2)}) collective-permute-start(bf16[4,256,256]{2,1,0:T(8,128)(2,1)S(1)} %add_convert_fusion), channel_id=1, source_target_pairs={{1,0},{2,3},{5,4},{6,7},{9,8},{10,11},{13,12},{14,15},{17,16},{18,... | collective-permute-start | bytes 1572872 | tf_op jit(solution)/shard_map/ppermute | solution.py:615
  262.7 25.4 %collective-permute-start.43 = (bf16[4,256,256]{2,1,0:T(8,128)(2,1)S(1)}, bf16[4,256,256]{2,1,0:T(8,128)(2,1)S(1)}, u32[]{:S(2)}, u32[]{:S(2)}) collective-permute-start(bf16[4,256,256]{2,1,0:T(8,128)(2,1)S(1)} %add_convert_fusion.2), channel_id=1, source_target_pairs={{1,0},{2,3},{5,4},{6,7},{9,8},{10,11},{13,12},{14,15},{17,16},{18,... | collective-permute-start | bytes 1572872 | tf_op jit(solution)/shard_map/ppermute | solution.py:615
  269.4 29.9 %collective-permute-start.34 = (bf16[4,256,256]{2,1,0:T(8,128)(2,1)S(1)}, bf16[4,256,256]{2,1,0:T(8,128)(2,1)S(1)}, u32[]{:S(2)}, u32[]{:S(2)}) collective-permute-start(bf16[4,256,256]{2,1,0:T(8,128)(2,1)S(1)} %add_convert_fusion.4), channel_id=1, source_target_pairs={{1,0},{2,3},{5,4},{6,7},{9,8},{10,11},{13,12},{14,15},{17,16},{18,... | collective-permute-start | bytes 1572872 | tf_op jit(solution)/shard_map/ppermute | solution.py:615
  (30 other events, 392.7 us)

commit v3 on v2

--- a/solution.py
+++ b/solution.py
@@ -81,13 +81,49 @@
     return jnp.where(low_half, pltpu.roll(values, 96, 1), pltpu.roll(values, 32, 1))
 
 
+def weigh_slots(count, first_ref, at, left_ref, right_ref, lefts, rights, outs, ring, sems):
+    per_out = outs[0].shape[0] // count
+    total = per_out * len(outs)
+
+    def put(target, half):
+        return pltpu.make_async_copy(ring.at[half, pl.ds(0, count)], target, sems.at[half])
+
+    def run(g, carry):
+        half = lax.rem(g, 2)
+
+        @pl.when(g >= 2)
+        def _():
+            put(ring.at[half, pl.ds(0, count)], half).wait()
+
+        first = first_ref[at + g]
+        for n in range(count):
+            left = left_ref[first + n]
+            grad = dot_nn(
+                lefts[pl.ds(pl.multiple_of(jnp.maximum(left, 0) * B, B), B), :],
+                rights[:, pl.ds(pl.multiple_of(right_ref[first + n] * B, B), B)],
+            )
+            keep = jnp.where(left >= 0, 1.0, 0.0)
+            ring[half, n] = (grad * keep).astype(BF16)
+        for number, out in enumerate(outs):
+
+            @pl.when((g >= number * per_out) & (g < (number + 1) * per_out))
+            def _(number=number, out=out):
+                put(out.at[pl.ds((g - number * per_out) * count, count)], half).start()
+
+        return carry
+
+    lax.fori_loop(0, total, run, 0)
+    for g in range(max(0, total - 2), total):
+        put(ring.at[g % 2, pl.ds(0, count)], g % 2).wait()
+
+
 def layer_kernel(
     micro,
     piece_slots,
-    grad_slots,
+    counts,
     index_ref,
     piece_first_ref,
-    grad_first_ref,
+    slot_first_ref,
     left_ref,
     right_ref,
     x_ref,
@@ -103,7 +139,7 @@
     pieces = rest[: len(piece_slots)]
     rest = rest[len(piece_slots) :]
     out_ref, token_grad_ref, gain_ref = rest[:3]
-    grad_refs = rest[3 : 3 + len(grad_slots)]
+    grad_refs, rest = rest[3 : 3 + 2 * len(counts)], rest[3 + 2 * len(counts) :]
     (
         w_qkv,
         w_o,
@@ -124,10 +160,10 @@
         h1_scr,
         dh2_scr,
         r1_scr,
+        w_sems,
         ring,
-        w_sems,
         ring_sems,
-    ) = rest[3 + len(grad_slots) :]
+    ) = rest
     seq = bias_ref.shape[1]
 
     def fetch(block, target, row, col, sem):
@@ -349,84 +385,39 @@
 
     lax.fori_loop(0, nd, token_back, 0)
 
-    group = ring.shape[1]
-    steps = [count // group for count in grad_slots]
-    total = sum(steps)
-
-    def ring_copy(target, half):
-        return pltpu.make_async_copy(ring.at[half], target, ring_sems.at[half])
-
-    def weigh(g, carry):
-        half = lax.rem(g, 2)
-
-        @pl.when(g >= 2)
-        def _():
-            ring_copy(ring.at[half], half).wait()
-
-        first = jnp.int32(0)
-        start = 0
-        for number, count in enumerate(steps):
-            inside = (g >= start) & (g < start + count)
-            first = jnp.where(inside, grad_first_ref[number] + (g - start) * group, first)
-            start += count
-        for n in range(group):
-            left = left_ref[first + n]
-            grad = dot_nn(
-                lefts[pl.ds(pl.multiple_of(jnp.maximum(left, 0) * B, B), B), :],
-                rights[:, pl.ds(pl.multiple_of(right_ref[first + n] * B, B), B)],
-            )
-            keep = jnp.where(left >= 0, 1.0, 0.0)
-            ring[half, n] = (grad * keep).astype(BF16)
-        start = 0
-        for target, count in zip(grad_refs, steps):
-
-            @pl.when((g >= start) & (g < start + count))
-            def _(target=target, start=start):
-                ring_copy(target.at[pl.ds((g - start) * group, group)], half).start()
-
-            start += count
-        return carry
-
-    lax.fori_loop(0, total, weigh, 0)
-    for g in range(max(0, total - 2), total):
-        ring_copy(ring.at[g % 2], g % 2).wait()
+    at = 0
+    for group, count in enumerate(counts):
+        outs = grad_refs[2 * group : 2 * group + 2]
+        weigh_slots(
+            count, slot_first_ref, at, left_ref, right_ref, lefts, rights, outs, ring, ring_sems
+        )
+        at += 2 * outs[0].shape[0] // count
 
 
 def run_layer(
-    tokens, cotangent, segment_ids, block_slot_index, norm_gains, pieces, piece_firsts,
-    grad_slots, grad_firsts, slots,
+    tokens, cotangent, segment_ids, block_slot_index, norm_gains, tables, pieces, piece_firsts,
+    slot_tables, slot_firsts, counts,
 ):
     micro, seq = segment_ids.shape
     count = micro * seq
-    half_dim = HEAD_DIM // 2
-    frequency = ROPE_BASE ** (-2.0 * jnp.arange(half_dim, dtype=F32) / HEAD_DIM)
-    angles = positions_of(segment_ids).reshape(count).astype(F32)[:, None] * frequency[None, :]
-    cosine, sine = jnp.cos(angles), jnp.sin(angles)
-    cos_wide = jnp.tile(cosine, (1, 4))
-    sin_wide = jnp.concatenate([-sine, sine, -sine, sine], axis=1)
-    places = jnp.arange(seq, dtype=jnp.int32)
-    visible = (segment_ids[:, :, None] == segment_ids[:, None, :]) & (
-        places[:, None] <= places[None, :]
-    )
-    bias = jnp.where(visible, 0.0, MASKED).astype(F32)
-    left_table, right_table = factor_tables()
-    slot_left = jnp.full((slots,), -1, jnp.int32).at[block_slot_index].set(left_table)
-    slot_right = jnp.zeros((slots,), jnp.int32).at[block_slot_index].set(right_table)
-    group = next(g for g in (7, 4, 2, 1) if all(count % g == 0 for count in grad_slots))
-
+    grads = [
+        jax.ShapeDtypeStruct((slots * len(firsts) // 2, B, B), BF16)
+        for slots, firsts in zip(counts, slot_firsts)
+        for _ in range(2)
+    ]
     vmem = pl.BlockSpec(memory_space=pltpu.VMEM)
     smem = pl.BlockSpec(memory_space=pltpu.SMEM)
     hbm = pl.BlockSpec(memory_space=pl.ANY)
     return pl.pallas_call(
-        functools.partial(layer_kernel, micro, [p.shape[0] for p in pieces], grad_slots),
+        functools.partial(layer_kernel, micro, [p.shape[0] for p in pieces], counts),
         out_shape=(
             jax.ShapeDtypeStruct((count, D), BF16),
             jax.ShapeDtypeStruct((count, D), BF16),
             jax.ShapeDtypeStruct((2, D), F32),
-            *(jax.ShapeDtypeStruct((n, B, B), BF16) for n in grad_slots),
+            *grads,
         ),
         in_specs=[smem] * 5 + [vmem] * 8 + [hbm] * len(pieces),
-        out_specs=(vmem,) * 3 + (hbm,) * len(grad_slots),
+        out_specs=(vmem,) * 3 + (hbm,) * len(grads),
         scratch_shapes=[
             pltpu.VMEM((D, 3 * D), BF16),
             pltpu.VMEM((D, D), BF16),
@@ -447,11 +438,11 @@
             pltpu.VMEM((count, D), F32),
             pltpu.VMEM((count, D), F32),
             pltpu.VMEM((count, 1), F32),
-            pltpu.VMEM((2, group, B, B), BF16),
             pltpu.SemaphoreType.DMA((4,)),
+            pltpu.VMEM((2, max(counts), B, B), BF16),
             pltpu.SemaphoreType.DMA((2,)),
         ],
-        compiler_params=pltpu.CompilerParams(vmem_limit_bytes=60 * MIB),
+        compiler_params=pltpu.CompilerParams(vmem_limit_bytes=56 * MIB),
         cost_estimate=pl.CostEstimate(
             flops=23_000_000_000, bytes_accessed=32_000_000, transcendentals=3_000_000
         ),
@@ -459,50 +450,58 @@
     )(
         block_slot_index,
         jnp.stack(piece_firsts).astype(jnp.int32),
-        jnp.stack(grad_firsts).astype(jnp.int32),
-        slot_left,
-        slot_right,
+        jnp.stack([first for firsts in slot_firsts for first in firsts]).astype(jnp.int32),
+        *slot_tables,
         tokens,
         cotangent,
-        bias,
-        cos_wide,
-        sin_wide,
-        cosine.T,
-        sine.T,
+        *tables,
         norm_gains,
         *pieces,
     )
 
 
+def layer_tables(segment_ids):
+    micro, seq = segment_ids.shape
+    count = micro * seq
+    half_dim = HEAD_DIM // 2
+    frequency = ROPE_BASE ** (-2.0 * jnp.arange(half_dim, dtype=F32) / HEAD_DIM)
+    angles = positions_of(segment_ids).reshape(count).astype(F32)[:, None] * frequency[None, :]
+    cosine, sine = jnp.cos(angles), jnp.sin(angles)
+    cos_wide = jnp.tile(cosine, (1, 4))
+    sin_wide = jnp.concatenate([-sine, sine, -sine, sine], axis=1)
+    places = jnp.arange(seq, dtype=jnp.int32)
+    visible = (segment_ids[:, :, None] == segment_ids[:, None, :]) & (
+        places[:, None] <= places[None, :]
+    )
+    bias = jnp.where(visible, 0.0, MASKED).astype(F32)
+    return bias, cos_wide, sin_wide, cosine.T, sine.T
+
+
+def slot_tables(block_slot_index, slots):
+    left_table, right_table = factor_tables()
+    slot_left = jnp.full((slots,), -1, jnp.int32).at[block_slot_index].set(left_table)
+    slot_right = jnp.zeros((slots,), jnp.int32).at[block_slot_index].set(right_table)
+    return slot_left, slot_right
+
+
 def split_two(values):
     high = values.astype(BF16)
     return high, (values - high.astype(F32)).astype(BF16)
 
 
-def dot_split(dot, a, b):
-    a_high, a_low = a
-    b_high, b_low = b
-    total = dot(a_high, b_high)
-    if b_low is not None:
-        total = total + dot(a_high, b_low)
-    if a_low is not None:
-        total = total + dot(a_low, b_high)
-    return total
-
-
 def adam_kernel(
-    grad_ref, weight_ref, first_ref, second_ref, left_ref, right_ref, *rest
+    inner_ref, whole_ref, outward_ref, weight_ref, first_ref, second_ref, left_ref, right_ref, *rest
 ):
     grad_out, first_out, second_out, weight_out, low_out = rest[-5:]
-    for n in range(grad_ref.shape[0]):
-        grad = grad_ref[n]
-        left = left_ref[n]
-        left_pair = split_two(left)
-        left_t_pair = tuple(part.T for part in left_pair)
-        right_pair = split_two(right_ref[n])
+    inner = inner_ref[0] != 0
+    for n in range(weight_ref.shape[0]):
+        block = pl.ds(n * B, B)
+        grad = jnp.where(inner, whole_ref[block, :], outward_ref[block, :])
+        left, left_rest = split_two(left_ref[n])
+        right, right_rest = split_two(right_ref[n])
         grad_out[n] = grad.astype(F32)
-        turned = dot_split(dot_nn, (grad, None), right_pair)
-        turned = dot_split(dot_nn, left_t_pair, split_two(turned))
+        turned = (dot_nn(grad, right) + dot_nn(grad, right_rest)).astype(BF16)
+        turned = dot_nn(left.T, turned) + dot_nn(left_rest.T, turned)
         first_new = BETA_ONE * first_ref[n] + (1.0 - BETA_ONE) * turned
         second_new = BETA_TWO * second_ref[n] + (1.0 - BETA_TWO) * turned * turned
         first_out[n] = first_new
@@ -512,37 +511,36 @@
             / (1.0 - BETA_ONE**STEP)
             / (jnp.sqrt(second_new / (1.0 - BETA_TWO**STEP)) + ADAM_EPS)
         )
-        back = dot_split(dot_nn, left_pair, split_two(ratio))
-        back = dot_split(dot_nt, split_two(back), right_pair)
+        back = dot_nt(dot_nn(left, ratio.astype(BF16)).astype(BF16), right)
         weight = weight_ref[n]
         weight_new = weight - RATE * (back + DECAY * weight)
         weight_out[n] = weight_new
         low_out[n] = weight_new.astype(BF16)
 
 
-def adam_blocks(grads, start, state, done):
+def adam_blocks(whole, outward, inner, start, count, state, done):
     own = state[0].shape[0]
-    count = grads.shape[0]
     step = next(n for n in (2, 1) if count % n == 0 and start % n == 0)
-    local = pl.BlockSpec((step, B, B), lambda s: (s, 0, 0))
+    local = pl.BlockSpec((step * B, B), lambda s: (s, 0))
     offset = pl.BlockSpec((step, B, B), lambda s: (s + start // step, 0, 0))
     hbm = pl.BlockSpec(memory_space=pl.ANY)
+    smem = pl.BlockSpec(memory_space=pltpu.SMEM)
     wide = jax.ShapeDtypeStruct((own, B, B), F32)
     return pl.pallas_call(
         adam_kernel,
         grid=(count // step,),
         out_shape=(wide, wide, wide, wide, jax.ShapeDtypeStruct((own, B, B), BF16)),
-        in_specs=[local] + [offset] * 5 + [hbm] * len(done),
+        in_specs=[smem] + [local] * 2 + [offset] * 5 + [hbm] * len(done),
         out_specs=(offset,) * 5,
-        input_output_aliases={6 + n: n for n in range(len(done))},
-        compiler_params=pltpu.CompilerParams(vmem_limit_bytes=32 * MIB),
+        input_output_aliases={8 + n: n for n in range(len(done))},
+        compiler_params=pltpu.CompilerParams(vmem_limit_bytes=60 * MIB),
         cost_estimate=pl.CostEstimate(
-            flops=count * 12 * 2 * B**3,
-            bytes_accessed=count * B * B * 40,
+            flops=count * 6 * 2 * B**3,
+            bytes_accessed=count * B * B * 42,
             transcendentals=count * B * B,
         ),
         name="adam",
-    )(grads, *state, *done)
+    )(inner.reshape(1), whole, outward, *state, *done)
 
 
 def adam_plain(grads, values, first_moment, second_moment):
@@ -579,11 +577,16 @@
     return lax.ppermute(values, "fsdp", [(i, i ^ bit) for i in range(lax.axis_size("fsdp"))])
 
 
-def gather_pieces(owned, me):
-    own = owned.shape[0]
+def after(values, *others):
+    return lax.optimization_barrier((values, *others))[0]
+
+
+def gather_pieces(weights, me, make_tables):
+    own = weights.shape[0]
     half = own // 2
-    first_half, second_half = owned[:half], owned[half:]
-    pieces, firsts = [owned], [me * own]
+    first_half = weights[:half].astype(BF16)
+    second_half = weights[half:].astype(BF16)
+    pieces, firsts = [], []
 
     def keep(piece, relation, start):
         pieces.append(piece)
@@ -593,28 +596,202 @@
         keep(piece, relation, start)
         keep(exchange(piece, CORE), relation | CORE, start)
 
-    keep(exchange(owned, CORE), CORE, 0)
     along_first = exchange(first_half, ALONG)
     across_second = exchange(second_half, ACROSS)
     along_second = exchange(second_half, ALONG)
     across_first = exchange(first_half, ACROSS)
+    tables = make_tables(along_first, across_second)
+    (along_first, across_second), tables = lax.optimization_barrier(
+        ((along_first, across_second), tables)
+    )
+    keep_both(first_half, 0, 0)
+    keep_both(second_half, 0, half)
     keep_both(along_first, ALONG, 0)
     keep_both(across_second, ACROSS, half)
+    diagonal_first = exchange(along_first, ACROSS)
+    diagonal_second = exchange(across_second, ALONG)
     keep_both(along_second, ALONG, half)
     keep_both(across_first, ACROSS, 0)
-    keep_both(exchange(along_first, ACROSS), DIAGONAL, 0)
-    keep_both(exchange(across_second, ALONG), DIAGONAL, half)
-    return pieces, firsts
-
-
-def sum_along_line(values):
-    inner = lax.ppermute(values, "rep", [(0, 1), (3, 2)])
-    halfway = add_low(values, inner)
-    other = lax.ppermute(halfway, "rep", [(1, 2), (2, 1)])
-    total = add_low(halfway, other)
-    back = lax.ppermute(total, "rep", [(1, 0), (2, 3)])
+    keep_both(diagonal_first, DIAGONAL, 0)
+    keep_both(diagonal_second, DIAGONAL, half)
+    return pieces, firsts, tables
+
+
+class Plan:
+    def __init__(self):
+        self.tasks = {}
+
+    def core(self, name, needs, run):
+        self.tasks[name] = (True, needs, run)
+
+    def send(self, name, needs, run):
+        self.tasks[name] = (False, needs, run)
+
+    def run(self, order):
+        assert sorted(order) == sorted(self.tasks)
+        values, last = {}, None
+        for name in order:
+            on_core, needs, run = self.tasks[name]
+            inputs = [values[n] for n in needs]
+            if last is not None:
+                *inputs, _ = lax.optimization_barrier((*inputs, last))
+            values[name] = run(*inputs)
+            if on_core:
+                last = jax.tree.leaves(values[name])[0]
+        return values
+
+
+GROUPS = (((4, 1),), ((6, 2), (4, 2)))
+ORDER = (
+    "grads0 grads1 core0 gain_far near_sum0 near0 core1 near_sum1 near1 gain1 "
+    "far_sum0_0 far0_0 plane_sum0_0 inward0_0a halfway0_0a middle0_0a far_sum1_0 far1_0 far_sum1_1 far1_1 gain_near "
+    "whole0_0a outward0_0a plane_sum1_0 inward1_0a inward1_0b plane_sum1_1 inward1_1a inward1_1b gain2 gain_core "
+    "halfway1_0a middle1_0a halfway1_0b middle1_0b gain3 gain_pair whole1_0a outward1_0a halfway1_1a middle1_1a "
+    "whole1_0b outward1_0b halfway1_1b middle1_1b adam0_0a whole1_1a outward1_1a whole1_1b outward1_1b gain4 gain_line "
+    "adam1_0a adam1_0b gain5 adam1_1a adam1_1b"
+).split()
+
+
+def group_sizes():
+    return [sum(size for size, _ in sets) for sets in GROUPS]
+
+
+def core_neighbours(me):
+    near = jnp.where((me & CORE) == 0, ACROSS, ALONG)
+    return near, DIAGONAL ^ near
+
+
+def group_firsts(me, own):
+    near, far = core_neighbours(me)
+    relations = [DIAGONAL | CORE, far | CORE, near | CORE, CORE, DIAGONAL, near, far, 0]
+    firsts, start = [], 0
+    for size in group_sizes():
+        firsts.append([(me ^ relation) * own + start for relation in relations])
+        start += size
+    return firsts
+
+
+def flat(blocks):
+    return blocks.reshape(-1, B)
+
+
+def reduce_and_step(me, own, grads, state, gain_grad):
+    plan = Plan()
+    owners = lax.axis_size("fsdp")
+    near_pairs = [(i, i ^ (ALONG if i & CORE else ACROSS)) for i in range(owners)]
+    far_pairs = [(i, i ^ (ACROSS if i & CORE else ALONG)) for i in range(owners)]
     place = lax.axis_index("rep")
-    return jnp.where((place == 1) | (place == 2), total, back)
+    inner = ((place == 1) | (place == 2)).astype(jnp.int32)
+    done = ()
+
+    start = 0
+    for number, sets in enumerate(GROUPS):
+        total = sum(size for size, _ in sets)
+
+        def name(text, number=number):
+            return text + str(number)
+
+        both = [name("grads"), name("core")]
+
+        def chip(pair, arrived, first, last):
+            return flat(pair[1][first:last]), flat(arrived[first:last])
+
+        plan.core(
+            name("grads"), [],
+            lambda pair=grads[2 * number : 2 * number + 2]: pair,
+        )
+        plan.send(name("core"), [name("grads")], lambda pair: exchange(pair[0], CORE))
+        plan.core(
+            name("near_sum"), both,
+            lambda pair, arrived, total=total: add_low(*chip(pair, arrived, 0, 2 * total)),
+        )
+        plan.send(
+            name("near"), [name("near_sum")], lambda t: lax.ppermute(t, "fsdp", near_pairs)
+        )
+        inside = 0
+        for member, (size, parts) in enumerate(sets):
+
+            def at(text, number=number, member=member):
+                return "%s%d_%d" % (text, number, member)
+
+            def far_sum(pair, arrived, r, inside=inside, size=size, total=total):
+                first = 2 * total + inside
+                return add_low(
+                    *chip(pair, arrived, first, first + size), r[inside * B : (inside + size) * B]
+                )
+
+            plan.core(at("far_sum"), both + [name("near")], far_sum)
+            plan.send(
+                at("far"), [at("far_sum")], lambda t: lax.ppermute(t, "fsdp", far_pairs)
+            )
+            firsts = [size * p // parts for p in range(parts + 1)]
+
+            def plane_sum(pair, arrived, r, q, inside=inside, total=total, firsts=firsts):
+                sums = []
+                for a, b in zip(firsts[:-1], firsts[1:]):
+                    first, last = inside + a, inside + b
+                    sums.append(
+                        add_low(
+                            *chip(pair, arrived, 3 * total + first, 3 * total + last),
+                            r[(total + first) * B : (total + last) * B],
+                            q[a * B : b * B],
+                        )
+                    )
+                return sums
+
+            plan.core(at("plane_sum"), both + [name("near"), at("far")], plane_sum)
+            for part in range(parts):
+
+                def of(text, part=part, at=at):
+                    return at(text) + "abcd"[part]
+
+                plan.send(
+                    of("inward"), [at("plane_sum")],
+                    lambda t, part=part: lax.ppermute(t[part], "rep", [(0, 1), (3, 2)]),
+                )
+                plan.core(
+                    of("halfway"), [at("plane_sum"), of("inward")],
+                    lambda t, r, part=part: add_low(t[part], r),
+                )
+                plan.send(
+                    of("middle"), [of("halfway")],
+                    lambda t: lax.ppermute(t, "rep", [(1, 2), (2, 1)]),
+                )
+                plan.core(of("whole"), [of("halfway"), of("middle")], add_low)
+                plan.send(
+                    of("outward"), [of("whole")],
+                    lambda t: lax.ppermute(t, "rep", [(1, 0), (2, 3)]),
+                )
+                first, last = firsts[part : part + 2]
+
+                def adam(whole, outward, first=start + inside + first, count=last - first):
+                    nonlocal done
+                    done = adam_blocks(whole, outward, inner, first, count, state, done)
+                    return done
+
+                plan.core(of("adam"), [of("whole"), of("outward")], adam)
+            inside += size
+        start += total
+
+    old = None
+    line = [[(i, i ^ bit) for i in range(4)] for bit in (1, 2)]
+    for n, (text, axis, pairs) in enumerate(
+        (("far", "fsdp", far_pairs), ("near", "fsdp", near_pairs),
+         ("core", "fsdp", [(i, i ^ CORE) for i in range(owners)]),
+         ("pair", "rep", line[0]), ("line", "rep", line[1]))
+    ):
+        plan.send(
+            "gain_" + text, [old] if old else [],
+            lambda gain=gain_grad, axis=axis, pairs=pairs: lax.ppermute(gain, axis, pairs),
+        )
+        new = "gain" + str(n + 1)
+        if old:
+            plan.core(new, [old, "gain_" + text], lambda a, b: a + b)
+        else:
+            plan.core(new, ["gain_" + text], lambda b: gain_grad + b)
+        old = new
+    values = plan.run(ORDER)
+    return done, values[old]
 
 
 def shards(
@@ -636,58 +813,40 @@
     slots = own * owners
     me = lax.axis_index("fsdp")
     state = (weights, first_moment, second_moment, left_basis, right_basis)
-    owned_low = weights.astype(BF16)
-    small = owners == 8 and lax.axis_size("rep") == 4 and own % 2 == 0
+    small = owners == 8 and lax.axis_size("rep") == 4 and own == sum(group_sizes())
+
+    def make_tables(*others):
+        segments, index = segment_ids, block_slot_index
+        if others:
+            segments, index, *_ = lax.optimization_barrier((segments, index, *others))
+        return layer_tables(segments), slot_tables(index, slots)
 
     if small:
-        pieces, piece_firsts = gather_pieces(owned_low, me)
-        relations = [DIAGONAL | CORE, DIAGONAL, ACROSS | CORE, ALONG | CORE, ACROSS, ALONG, CORE, 0]
-        grad_slots = [own] * owners
-        grad_firsts = [(me ^ relation) * own for relation in relations]
+        pieces, piece_firsts, (tables, slot_factors) = gather_pieces(weights, me, make_tables)
     else:
-        pieces = [lax.all_gather(owned_low, "fsdp", axis=0, tiled=True)]
+        pieces = [lax.all_gather(weights.astype(BF16), "fsdp", axis=0, tiled=True)]
         piece_firsts = [jnp.int32(0)]
-        grad_slots = [slots]
-        grad_firsts = [jnp.int32(0)]
+        tables, slot_factors = make_tables()
+    if small:
+        counts = group_sizes()
+        slot_firsts = group_firsts(me, own)
+    else:
+        counts = [next(n for n in (8, 4, 2) if slots % (2 * n) == 0)]
+        slot_firsts = [[jnp.int32(first) for first in range(0, slots, counts[0])]]
     block_out, token_grad, gain_grad, *grads = run_layer(
-        tokens, cotangent, segment_ids, block_slot_index, norm_gains, pieces, piece_firsts,
-        grad_slots, grad_firsts, slots,
+        tokens, cotangent, segment_ids, block_slot_index, norm_gains, tables, pieces, piece_firsts,
+        slot_factors, slot_firsts, counts,
     )
-    done = ()
     if small:
-        by_relation = dict(zip(relations, grads))
-        arrived = {
-            relation: exchange(by_relation[relation | CORE], CORE)
-            for relation in (DIAGONAL, ACROSS, ALONG, 0)
-        }
-
-        def chip_sum(relation, start, count):
-            part = slice(start, start + count)
-            return add_low(by_relation[relation][part], arrived[relation][part])
-
-        start = 0
-        while start < own:
-            half = min(2, (own - start) // 2)
-            a, b = (start, half), (start + half, half)
-            diagonal_a = exchange(chip_sum(DIAGONAL, *a), ACROSS)
-            diagonal_b = exchange(chip_sum(DIAGONAL, *b), ALONG)
-            across_a = exchange(chip_sum(ACROSS, *a), ACROSS)
-            along_b = exchange(chip_sum(ALONG, *b), ALONG)
-            across_b = exchange(add_low(chip_sum(ACROSS, *b), diagonal_b), ACROSS)
-            along_a = exchange(add_low(chip_sum(ALONG, *a), diagonal_a), ALONG)
-            total = jnp.concatenate(
-                [
-                    add_low(chip_sum(0, *a), across_a, along_a),
-                    add_low(chip_sum(0, *b), across_b, along_b),
-                ]
-            )
-            done = adam_blocks(sum_along_line(total), start, state, done)
-            start += 2 * half
+        done, gain_grads = reduce_and_step(me, own, grads, state, gain_grad)
     else:
-        owner_sums = lax.psum_scatter(grads[0], "fsdp", scatter_dimension=0, tiled=True)
-        done = adam_blocks(lax.psum(owner_sums, "rep"), 0, state, done)
+        owner_sums = lax.psum_scatter(
+            jnp.concatenate(grads), "fsdp", scatter_dimension=0, tiled=True
+        )
+        owner_grads = flat(lax.psum(owner_sums, "rep"))
+        done = adam_blocks(owner_grads, owner_grads, jnp.int32(1), 0, own, state, ())
+        gain_grads = sum_everywhere(sum_everywhere(gain_grad, "fsdp"), "rep")
     grads_wide, first_new, second_new, weights_new, weights_low = done
-    gain_grads = sum_everywhere(sum_everywhere(gain_grad, "fsdp"), "rep")
     gain_first_new, gain_second_new, gains_new = adam_plain(
         gain_grads, norm_gains, gain_first, gain_second
     )

time: 310 us -> 288 us (0.929)
  starting transfers between devices: 69.4 us -> 54.7 us
  Pallas kernels: 80.2 us -> 88.5 us
  waiting for transfers between devices: 126 us -> 118 us
  other arithmetic: 20.9 us -> 15.1 us
    ppermute x41 -> x16, starting transfers between devices: 40.2 us -> 9.92 us  [exchange(): lax.ppermute(values, 'fsdp', [(i, i ^ bit) for i in range(lax.axis_size('...]
    ppermute x41 -> x16, waiting for transfers between devices: 79.5 us -> 59 us  [exchange(): lax.ppermute(values, 'fsdp', [(i, i ^ bit) for i in range(lax.axis_size('...]
    ppermute x17 -> x25, starting transfers between devices: 29.3 us -> 44.7 us  [the longest x5 16.9 us: reduce_and_step(): lax.ppermute(t[part], 'rep', [(0, 1), (3, 2)])]
    ppermute x17 -> x25, waiting for transfers between devices: 46.2 us -> 58.5 us  [the longest x3 27 us: reduce_and_step(): lax.ppermute(t, 'fsdp', far_pairs)]
    pallas_call x4 -> x5, Pallas kernels: 19.6 us -> 26.5 us  [adam_blocks(): pl.pallas_call(adam_kernel, grid=(count // step,), out_shape=(wide, wide,...]
    convert_element_type x17 -> x18, other arithmetic: 12 us -> 6.38 us  [add_low(): return sum((term.astype(F32) for term in terms)).astype(BF16)]
  transfers between devices with their start and end apart: 58 -> 41, of which waited for: 23 -> 20; matrix products, arithmetic and copies ran while one was open for 9% -> 6% of each run, Pallas kernels for 4% -> 8%
where the time goes in v3:
time: 288 us
  waiting for transfers between devices  118 us (41%)
  Pallas kernels  88.5 us (31%)
  starting transfers between devices  54.7 us (19%)
  other arithmetic  15.1 us (5%)
  local copies, waits for them, and re-layouts  10.7 us (4%)
    pallas_call x1, Pallas kernels, run_layer(): pl.pallas_call(functools.partial(layer_kernel, micro, [p.shape[0] for p i...  62 us
    ppermute x16, waiting for transfers between devices, exchange(): lax.ppermute(values, 'fsdp', [(i, i ^ bit) for i in range(lax.axis_size('...  59 us
    ppermute x3, waiting for transfers between devices, reduce_and_step(): lax.ppermute(t, 'fsdp', far_pairs)  27 us
    pallas_call x5, Pallas kernels, adam_blocks(): pl.pallas_call(adam_kernel, grid=(count // step,), out_shape=(wide, wide,...  26.5 us
    ppermute x5, waiting for transfers between devices, reduce_and_step(): lax.ppermute(t[part], 'rep', [(0, 1), (3, 2)])  24 us
    ppermute x5, starting transfers between devices, reduce_and_step(): lax.ppermute(t[part], 'rep', [(0, 1), (3, 2)])  16.9 us
    ppermute x5, starting transfers between devices, reduce_and_step(): lax.ppermute(gain, axis, pairs)  11.8 us
    ppermute x16, starting transfers between devices, exchange(): lax.ppermute(values, 'fsdp', [(i, i ^ bit) for i in range(lax.axis_size('...  9.92 us
  transfers between devices with their start and end apart: 41, of which 20 were waited for; matrix products, arithmetic and copies ran while one was open for 6% of the time, Pallas kernels for 8%

profile of v3, /device:TPU:0, one launch (start us, length us, event | category | flops | bytes accessed | tf_op | source)
XLA Modules:
  0.0 287.7 jit_solution(16224725798759361173)
XLA Ops:
  0.7 2.2 convert.5
  3.1 3.0 %collective-permute-start = (bf16[7,256,256]{2,1,0:T(8,128)(2,1)S(1)}, bf16[7,256,256]{2,1,0:T(8,128)(2,1)S(1)}, u32[]{:S(2)}, u32[]{:S(2)}) collective-permute-start(bf16[7,256,256]{2,1,0:T(8,128)(2,1)S(1)} %get-tuple-element.289.rest_0_), channel_id=1, source_target_pairs={{0,16},{4,20},{8,24},{12,28},{16,0},{20,4},{24,8},{28,12},{1,17},{... | collective-permute-start | bytes 2752520 | tf_op jit(solution)/shard_map/ppermute | solution.py:577
  6.1 1.5 collective-permute-start.1
  8.3 19.0 %collective-permute-done.rest_4_ = bf16[7,256,256]{2,1,0:T(8,128)(2,1)S(1)} collective-permute-done((bf16[7,256,256]{2,1,0:T(8,128)(2,1)S(1)}, bf16[7,256,256]{2,1,0:T(8,128)(2,1)S(1)}, u32[]{:S(2)}, u32[]{:S(2)}) %collective-permute-start) | collective-permute-done | bytes 917536 | tf_op jit(solution)/shard_map/ppermute | solution.py:577
  28.2 1.2 collective-permute-done.1.rest_6_
  32.6 1.6 scatter_custom_fusion.left_ref
  34.2 1.6 scatter_custom_fusion.1.right_ref
  38.8 1.6 collective-permute-start.10
  40.3 5.9 %collective-permute-done.6.rest_8_ = bf16[7,256,256]{2,1,0:T(8,128)(2,1)} collective-permute-done((bf16[7,256,256]{2,1,0:T(8,128)(2,1)S(1)}, bf16[7,256,256]{2,1,0:T(8,128)(2,1)}, u32[]{:S(2)}, u32[]{:S(2)}) %collective-permute-start.6) | collective-permute-done | bytes 917536 | tf_op jit(solution)/shard_map/ppermute | solution.py:577
  46.2 1.7 collective-permute-start.12
  48.0 1.2 collective-permute-done.8.rest_10_
  49.7 17.5 %collective-permute-done.10.rest_12_ = bf16[7,256,256]{2,1,0:T(8,128)(2,1)S(1)} collective-permute-done((bf16[7,256,256]{2,1,0:T(8,128)(2,1)}, bf16[7,256,256]{2,1,0:T(8,128)(2,1)S(1)}, u32[]{:S(2)}, u32[]{:S(2)}) %collective-permute-start.10) | collective-permute-done | bytes 917536 | tf_op jit(solution)/shard_map/ppermute | solution.py:577
  70.8 1.7 collective-permute-done.11.rest_13_
  72.7 62.0 %layer.1 = (bf16[512,768]{1,0:T(8,128)(2,1)}, bf16[512,768]{1,0:T(8,128)(2,1)}, f32[2,768]{1,0:T(2,128)}, bf16[16,256,256]{2,1,0:T(8,128)(2,1)}, bf16[16,256,256...) custom-call(s32[108]{0:T(128)} %index_ref.1, s32[16]{0:T(128)} %stack.110.piece_first_ref, ...), custom_call_target="tpu_custom_call" | custom-call | flops 23000000512 | bytes 32000000 | tf_op jit(solution)/shard_map/layer/pallas_call | solution.py:411
  134.9 4.2 %collective-permute-done.14 = bf16[16,256,256]{2,1,0:T(8,128)(2,1)S(1)} collective-permute-done((bf16[16,256,256]{2,1,0:T(8,128)(2,1)}, bf16[16,256,256]{2,1,0:T(8,128)(2,1)S(1)}, u32[]{:S(2)}, u32[]{:S(2)}) %collective-permute-start.14) | collective-permute-done | bytes 2097184 | tf_op jit(solution)/shard_map/ppermute | solution.py:577
  139.1 1.5 add_convert_fusion.1
  140.9 1.5 collective-permute-start.17
  142.4 7.2 %collective-permute-done.15 = bf16[40,256,256]{2,1,0:T(8,128)(2,1)S(1)} collective-permute-done((bf16[40,256,256]{2,1,0:T(8,128)(2,1)}, bf16[40,256,256]{2,1,0:T(8,128)(2,1)S(1)}, u32[]{:S(2)}, u32[]{:S(2)}) %collective-permute-start.15) | collective-permute-done | bytes 5242912 | tf_op jit(solution)/shard_map/ppermute | solution.py:577
  149.6 2.7 add_convert_fusion
  152.3 1.6 collective-permute-start.16
  154.9 2.8 collective-permute-done.18
  159.0 13.9 %collective-permute-done.19 = bf16[1024,256]{1,0:T(8,128)(2,1)S(1)} collective-permute-done((bf16[1024,256]{1,0:T(8,128)(2,1)S(1)}, bf16[1024,256]{1,0:T(8,128)(2,1)S(1)}, u32[]{:S(2)}, u32[]{:S(2)}) %collective-permute-start.19) | collective-permute-done | bytes 524320 | tf_op jit(solution)/shard_map/ppermute | solution.py:725
  173.2 3.5 %collective-permute-start.20 = (bf16[1024,256]{1,0:T(8,128)(2,1)S(1)}, bf16[1024,256]{1,0:T(8,128)(2,1)S(1)}, u32[]{:S(2)}, u32[]{:S(2)}) collective-permute-start(bf16[1024,256]{1,0:T(8,128)(2,1)S(1)} %fusion.3), channel_id=1, source_target_pairs={{0,1},{3,2},{4,5},{7,6},{8,9},{11,10},{12,13},{15,14},{16,17},{19,... | collective-permute-start | bytes 1572872 | tf_op jit(solution)/shard_map/ppermute | solution.py:750
  176.7 8.6 %collective-permute-done.20 = bf16[1024,256]{1,0:T(8,128)(2,1)S(1)} collective-permute-done((bf16[1024,256]{1,0:T(8,128)(2,1)S(1)}, bf16[1024,256]{1,0:T(8,128)(2,1)S(1)}, u32[]{:S(2)}, u32[]{:S(2)}) %collective-permute-start.20) | collective-permute-done | bytes 524320 | tf_op jit(solution)/shard_map/ppermute | solution.py:750
  186.2 3.5 %collective-permute-done.16 = bf16[5120,256]{1,0:T(8,128)(2,1)S(1)} collective-permute-done((bf16[5120,256]{1,0:T(8,128)(2,1)S(1)}, bf16[5120,256]{1,0:T(8,128)(2,1)S(1)}, u32[]{:S(2)}, u32[]{:S(2)}) %collective-permute-start.16) | collective-permute-done | bytes 2621472 | tf_op jit(solution)/shard_map/ppermute | solution.py:709
  191.4 1.6 collective-permute-start.27
  194.2 8.0 %collective-permute-done.22 = bf16[1536,256]{1,0:T(8,128)(2,1)S(1)} collective-permute-done((bf16[1536,256]{1,0:T(8,128)(2,1)S(1)}, bf16[1536,256]{1,0:T(8,128)(2,1)S(1)}, u32[]{:S(2)}, u32[]{:S(2)}) %collective-permute-start.22) | collective-permute-done | bytes 786464 | tf_op jit(solution)/shard_map/ppermute | solution.py:725
  202.6 5.1 %collective-permute-done.21 = bf16[1024,256]{1,0:T(8,128)(2,1)S(1)} collective-permute-done((bf16[1024,256]{1,0:T(8,128)(2,1)S(1)}, bf16[1024,256]{1,0:T(8,128)(2,1)S(1)}, u32[]{:S(2)}, u32[]{:S(2)}) %collective-permute-start.21) | collective-permute-done | bytes 524320 | tf_op jit(solution)/shard_map/ppermute | solution.py:725
  207.8 3.7 %collective-permute-start.26 = (bf16[768,256]{1,0:T(8,128)(2,1)S(1)}, bf16[768,256]{1,0:T(8,128)(2,1)S(1)}, u32[]{:S(2)}, u32[]{:S(2)}) collective-permute-start(bf16[768,256]{1,0:T(8,128)(2,1)S(1)} %get-tuple-element.206), channel_id=1, source_target_pairs={{0,1},{3,2},{4,5},{7,6},{8,9},{11,10},{12,13},{15,14},{16,17},{19,... | collective-permute-start | bytes 1179656 | tf_op jit(solution)/shard_map/ppermute | solution.py:750
  211.5 1.3 collective-permute-start.25
  213.2 7.8 %collective-permute-done.26 = bf16[768,256]{1,0:T(8,128)(2,1)S(1)} collective-permute-done((bf16[768,256]{1,0:T(8,128)(2,1)S(1)}, bf16[768,256]{1,0:T(8,128)(2,1)S(1)}, u32[]{:S(2)}, u32[]{:S(2)}) %collective-permute-start.26) | collective-permute-done | bytes 393248 | tf_op jit(solution)/shard_map/ppermute | solution.py:750
  221.9 1.3 collective-permute-start.34
  223.2 7.0 %collective-permute-start.29 = (bf16[512,256]{1,0:T(8,128)(2,1)S(1)}, bf16[512,256]{1,0:T(8,128)(2,1)S(1)}, u32[]{:S(2)}, u32[]{:S(2)}) collective-permute-start(bf16[512,256]{1,0:T(8,128)(2,1)S(1)} %get-tuple-element.218), channel_id=1, source_target_pairs={{0,1},{3,2},{4,5},{7,6},{8,9},{11,10},{12,13},{15,14},{16,17},{19,... | collective-permute-start | bytes 786440 | tf_op jit(solution)/shard_map/ppermute | solution.py:750
  230.3 1.3 collective-permute-start.24
  232.4 1.8 collective-permute-start.37
  234.3 2.5 collective-permute-done.29
  237.0 5.1 %collective-permute-done.24 = bf16[512,256]{1,0:T(8,128)(2,1)S(1)} collective-permute-done((bf16[512,256]{1,0:T(8,128)(2,1)S(1)}, bf16[512,256]{1,0:T(8,128)(2,1)S(1)}, u32[]{:S(2)}, u32[]{:S(2)}) %collective-permute-start.24) | collective-permute-done | bytes 262176 | tf_op jit(solution)/shard_map/ppermute | solution.py:750
  243.6 1.3 collective-permute-start.40
  244.9 1.3 collective-permute-start.39
  246.2 6.4 %adam.5 = (f32[14,256,256]{2,1,0:T(8,128)}, f32[14,256,256]{2,1,0:T(8,128)}, f32[14,256,256]{2,1,0:T(8,128)}, f32[14,256,256]{2,1,0:T(8,128)}, bf16[14,256,256]{2,1,0:T(8,128)(2,1)}) custom-call(s32[1]{0:T(128)} %bitcast.30.inner_ref, bf16[1024,256]{1,0:T(8,128)(2,1)} %copy-done, bf16[1024,256]{1,0:T(8,128)(2,1)} %copy-done.8, f32[14,256,256]{2,1,0:T(8,128)} %weight_ref.9, ...), custom_call_target="tpu_custom_call" | custom-call | flops 805306368 | bytes 11010048 | tf_op jit(solution)/shard_map/adam/pallas_call | solution.py:529
  252.8 7.4 %collective-permute-start.38 = (f32[2,768]{1,0:T(2,128)S(1)}, f32[2,768]{1,0:T(2,128)S(1)}, u32[]{:S(2)}, u32[]{:S(2)}) collective-permute-start(f32[2,768]{1,0:T(2,128)S(1)} %add.265), channel_id=1, source_target_pairs={{0,2},{1,3},{2,0},{3,1},{4,6},{5,7},{6,4},{7,5},{8,10},{9,11},{10,... | collective-permute-start | bytes 18440 | tf_op jit(solution)/shard_map/ppermute | solution.py:785
  260.2 1.3 collective-permute-start.36
  261.5 1.3 collective-permute-start.35
  263.6 5.7 %adam.6 = (f32[14,256,256]{2,1,0:T(8,128)}, f32[14,256,256]{2,1,0:T(8,128)}, f32[14,256,256]{2,1,0:T(8,128)}, f32[14,256,256]{2,1,0:T(8,128)}, bf16[14,256,256]{2,1,0:T(8,128)(2,1)}) custom-call(s32[1]{0:T(128)} %bitcast.30.inner_ref, bf16[768,256]{1,0:T(8,128)(2,1)} %copy-done.3, ...), custom_call_target="tpu_custom_call", output_to_operand_aliasing={{0}: (8, {}), {1}: (9, {}), {2}: (10, {}), {3}: (11, {}), {... | custom-call | flops 603979776 | bytes 8257536 | tf_op jit(solution)/shard_map/adam/pallas_call | solution.py:529
  269.3 1.1 collective-permute-done.39.outward_ref
  271.2 5.7 %adam.7 = (f32[14,256,256]{2,1,0:T(8,128)}, f32[14,256,256]{2,1,0:T(8,128)}, f32[14,256,256]{2,1,0:T(8,128)}, f32[14,256,256]{2,1,0:T(8,128)}, bf16[14,256,256]{2,1,0:T(8,128)(2,1)}) custom-call(s32[1]{0:T(128)} %bitcast.30.inner_ref, bf16[768,256]{1,0:T(8,128)(2,1)} %copy-done.2, ...), custom_call_target="tpu_custom_call", output_to_operand_aliasing={{0}: (8, {}), {1}: (9, {}), {2}: (10, {}), {3}: (11, {}), {... | custom-call | flops 603979776 | bytes 8257536 | tf_op jit(solution)/shard_map/adam/pallas_call | solution.py:529
  278.2 4.4 %adam.8 = (f32[14,256,256]{2,1,0:T(8,128)}, f32[14,256,256]{2,1,0:T(8,128)}, f32[14,256,256]{2,1,0:T(8,128)}, f32[14,256,256]{2,1,0:T(8,128)}, bf16[14,256,256]{2,1,0:T(8,128)(2,1)}) custom-call(s32[1]{0:T(128)} %bitcast.30.inner_ref, bf16[512,256]{1,0:T(8,128)(2,1)} %copy-done.5, ...), custom_call_target="tpu_custom_call", output_to_operand_aliasing={{0}: (8, {}), {1}: (9, {}), {2}: (10, {}), {3}: (11, {}), {... | custom-call | flops 402653184 | bytes 5505024 | tf_op jit(solution)/shard_map/adam/pallas_call | solution.py:529
  283.3 4.4 %adam.9 = (f32[14,256,256]{2,1,0:T(8,128)}, f32[14,256,256]{2,1,0:T(8,128)}, f32[14,256,256]{2,1,0:T(8,128)}, f32[14,256,256]{2,1,0:T(8,128)}, bf16[14,256,256]{2,1,0:T(8,128)(2,1)}) custom-call(s32[1]{0:T(128)} %bitcast.30.inner_ref, bf16[512,256]{1,0:T(8,128)(2,1)} %copy-done.4, ...), custom_call_target="tpu_custom_call", output_to_operand_aliasing={{0}: (8, {}), {1}: (9, {}), {2}: (10, {}), {3}: (11, {}), {... | custom-call | flops 402653184 | bytes 5505024 | tf_op jit(solution)/shard_map/adam/pallas_call | solution.py:529
  (144 shorter events, 26.8 us)
Async XLA Ops:
  0.6 28.7 %copy-start.13 = (s32[2,256]{1,0:T(2,128)S(1)}, s32[2,256]{1,0:T(2,128)}, u32[]{:S(2)}) copy-start(s32[2,256]{1,0:T(2,128)} %param.16) | copy-start | bytes 6148
  2.9 29.7 %copy-start.21 = (s32[108]{0:T(128)S(1)}, s32[108]{0:T(128)}, u32[]{:S(2)}) copy-start(s32[108]{0:T(128)} %index_ref.1) | copy-start | bytes 1300
  3.0 69.6 %copy-start.6 = (bf16[7,256,256]{2,1,0:T(8,128)(2,1)}, bf16[7,256,256]{2,1,0:T(8,128)(2,1)S(1)}, u32[]{:S(2)}) copy-start(bf16[7,256,256]{2,1,0:T(8,128)(2,1)S(1)} %get-tuple-element.288.rest_2_) | copy-start | bytes 2752516
  3.1 69.6 %copy-start.7 = (bf16[7,256,256]{2,1,0:T(8,128)(2,1)}, bf16[7,256,256]{2,1,0:T(8,128)(2,1)S(1)}, u32[]{:S(2)}) copy-start(bf16[7,256,256]{2,1,0:T(8,128)(2,1)S(1)} %get-tuple-element.289.rest_0_) | copy-start | bytes 2752516
  3.1 24.2 %collective-permute-start = (bf16[7,256,256]{2,1,0:T(8,128)(2,1)S(1)}, bf16[7,256,256]{2,1,0:T(8,128)(2,1)S(1)}, u32[]{:S(2)}, u32[]{:S(2)}) collective-permute-start(bf16[7,256,256]{2,1,0:T(8,128)(2,1)S(1)} %get-tuple-element.289.rest_0_), channel_id=1, source_target_pairs={{0,16},{4,20},{8,24},{12,28},{16,0},{20,4},{24,8},{28,12},{1,17},{... | collective-permute-start | bytes 2752520 | tf_op jit(solution)/shard_map/ppermute | solution.py:577
  6.1 23.3 %collective-permute-start.1 = (bf16[7,256,256]{2,1,0:T(8,128)(2,1)S(1)}, bf16[7,256,256]{2,1,0:T(8,128)(2,1)S(1)}, u32[]{:S(2)}, u32[]{:S(2)}) collective-permute-start(bf16[7,256,256]{2,1,0:T(8,128)(2,1)S(1)} %get-tuple-element.288.rest_2_), channel_id=1, source_target_pairs={{0,8},{4,12},{8,0},{12,4},{16,24},{20,28},{24,16},{28,20},{1,9},{5... | collective-permute-start | bytes 2752520 | tf_op jit(solution)/shard_map/ppermute | solution.py:577
  7.6 38.6 %collective-permute-start.6 = (bf16[7,256,256]{2,1,0:T(8,128)(2,1)S(1)}, bf16[7,256,256]{2,1,0:T(8,128)(2,1)}, u32[]{:S(2)}, u32[]{:S(2)}) collective-permute-start(bf16[7,256,256]{2,1,0:T(8,128)(2,1)S(1)} %get-tuple-element.288.rest_2_), channel_id=1, source_target_pairs={{0,16},{4,20},{8,24},{12,28},{16,0},{20,4},{24,8},{28,12},{1,17},{... | collective-permute-start | bytes 2752520 | tf_op jit(solution)/shard_map/ppermute | solution.py:577
  8.1 41.0 %collective-permute-start.8 = (bf16[7,256,256]{2,1,0:T(8,128)(2,1)S(1)}, bf16[7,256,256]{2,1,0:T(8,128)(2,1)}, u32[]{:S(2)}, u32[]{:S(2)}) collective-permute-start(bf16[7,256,256]{2,1,0:T(8,128)(2,1)S(1)} %get-tuple-element.289.rest_0_), channel_id=1, source_target_pairs={{0,8},{4,12},{8,0},{12,4},{16,24},{20,28},{24,16},{28,20},{1,9},{5... | collective-permute-start | bytes 2752520 | tf_op jit(solution)/shard_map/ppermute | solution.py:577
  8.2 40.9 %collective-permute-start.2 = (bf16[7,256,256]{2,1,0:T(8,128)(2,1)S(1)}, bf16[7,256,256]{2,1,0:T(8,128)(2,1)}, u32[]{:S(2)}, u32[]{:S(2)}) collective-permute-start(bf16[7,256,256]{2,1,0:T(8,128)(2,1)S(1)} %get-tuple-element.289.rest_0_), channel_id=1, source_target_pairs={{0,4},{4,0},{8,12},{12,8},{16,20},{20,16},{24,28},{28,24},{1,5},{5... | collective-permute-start | bytes 2752520 | tf_op jit(solution)/shard_map/ppermute | solution.py:577
  27.3 22.4 %collective-permute-start.3 = (bf16[7,256,256]{2,1,0:T(8,128)(2,1)S(1)}, bf16[7,256,256]{2,1,0:T(8,128)(2,1)}, u32[]{:S(2)}, u32[]{:S(2)}) collective-permute-start(bf16[7,256,256]{2,1,0:T(8,128)(2,1)S(1)} %get-tuple-element.288.rest_2_), channel_id=1, source_target_pairs={{0,4},{4,0},{8,12},{12,8},{16,20},{20,16},{24,28},{28,24},{1,5},{5... | collective-permute-start | bytes 2752520 | tf_op jit(solution)/shard_map/ppermute | solution.py:577
  38.8 28.5 %collective-permute-start.10 = (bf16[7,256,256]{2,1,0:T(8,128)(2,1)}, bf16[7,256,256]{2,1,0:T(8,128)(2,1)S(1)}, u32[]{:S(2)}, u32[]{:S(2)}) collective-permute-start(bf16[7,256,256]{2,1,0:T(8,128)(2,1)} %copy-done.18), channel_id=1, source_target_pairs={{0,8},{4,12},{8,0},{12,4},{16,24},{20,28},{24,16},{28,20},{1,9},{5... | collective-permute-start | bytes 2752520 | tf_op jit(solution)/shard_map/ppermute | solution.py:577
  46.2 21.9 %collective-permute-start.12 = (bf16[7,256,256]{2,1,0:T(8,128)(2,1)}, bf16[7,256,256]{2,1,0:T(8,128)(2,1)}, u32[]{:S(2)}, u32[]{:S(2)}) collective-permute-start(bf16[7,256,256]{2,1,0:T(8,128)(2,1)} %copy-done.19), channel_id=1, source_target_pairs={{0,16},{4,20},{8,24},{12,28},{16,0},{20,4},{24,8},{28,12},{1,17},{... | collective-permute-start | bytes 2752520 | tf_op jit(solution)/shard_map/ppermute | solution.py:577
  49.1 18.9 %collective-permute-start.4 = (bf16[7,256,256]{2,1,0:T(8,128)(2,1)}, bf16[7,256,256]{2,1,0:T(8,128)(2,1)}, u32[]{:S(2)}, u32[]{:S(2)}) collective-permute-start(bf16[7,256,256]{2,1,0:T(8,128)(2,1)} %copy-done.18), channel_id=1, source_target_pairs={{0,4},{4,0},{8,12},{12,8},{16,20},{20,16},{24,28},{28,24},{1,5},{5... | collective-permute-start | bytes 2752520 | tf_op jit(solution)/shard_map/ppermute | solution.py:577
  49.2 21.6 %collective-permute-start.5 = (bf16[7,256,256]{2,1,0:T(8,128)(2,1)}, bf16[7,256,256]{2,1,0:T(8,128)(2,1)}, u32[]{:S(2)}, u32[]{:S(2)}) collective-permute-start(bf16[7,256,256]{2,1,0:T(8,128)(2,1)} %copy-done.19), channel_id=1, source_target_pairs={{0,4},{4,0},{8,12},{12,8},{16,20},{20,16},{24,28},{28,24},{1,5},{5... | collective-permute-start | bytes 2752520 | tf_op jit(solution)/shard_map/ppermute | solution.py:577
  49.7 21.1 %collective-permute-start.7 = (bf16[7,256,256]{2,1,0:T(8,128)(2,1)}, bf16[7,256,256]{2,1,0:T(8,128)(2,1)}, u32[]{:S(2)}, u32[]{:S(2)}) collective-permute-start(bf16[7,256,256]{2,1,0:T(8,128)(2,1)} %collective-permute-done.6.rest_8_), channel_id=1, source_target_pairs={{0,4},{4,0},{8,12},{12,8},{16,20},{20,16},{24,28},{28,24},{1,5},{5... | collective-permute-start | bytes 2752520 | tf_op jit(solution)/shard_map/ppermute | solution.py:577
  67.2 3.5 %collective-permute-start.9 = (bf16[7,256,256]{2,1,0:T(8,128)(2,1)}, bf16[7,256,256]{2,1,0:T(8,128)(2,1)}, u32[]{:S(2)}, u32[]{:S(2)}) collective-permute-start(bf16[7,256,256]{2,1,0:T(8,128)(2,1)} %collective-permute-done.8.rest_10_), channel_id=1, source_target_pairs={{0,4},{4,0},{8,12},{12,8},{16,20},{20,16},{24,28},{28,24},{1,5},{5... | collective-permute-start | bytes 2752520 | tf_op jit(solution)/shard_map/ppermute | solution.py:577
  68.1 4.4 %collective-permute-start.11 = (bf16[7,256,256]{2,1,0:T(8,128)(2,1)S(1)}, bf16[7,256,256]{2,1,0:T(8,128)(2,1)}, u32[]{:S(2)}, u32[]{:S(2)}) collective-permute-start(bf16[7,256,256]{2,1,0:T(8,128)(2,1)S(1)} %collective-permute-done.10.rest_12_), channel_id=1, source_target_pairs={{0,4},{4,0},{8,12},{12,8},{16,20},{20,16},{24,28},{28,24},{1,5},{5... | collective-permute-start | bytes 2752520 | tf_op jit(solution)/shard_map/ppermute | solution.py:577
  68.1 4.6 %collective-permute-start.13 = (bf16[7,256,256]{2,1,0:T(8,128)(2,1)}, bf16[7,256,256]{2,1,0:T(8,128)(2,1)}, u32[]{:S(2)}, u32[]{:S(2)}) collective-permute-start(bf16[7,256,256]{2,1,0:T(8,128)(2,1)} %collective-permute-done.12.rest_14_), channel_id=1, source_target_pairs={{0,4},{4,0},{8,12},{12,8},{16,20},{20,16},{24,28},{28,24},{1,5},{5... | collective-permute-start | bytes 2752520 | tf_op jit(solution)/shard_map/ppermute | solution.py:577
  134.7 4.4 %collective-permute-start.14 = (bf16[16,256,256]{2,1,0:T(8,128)(2,1)}, bf16[16,256,256]{2,1,0:T(8,128)(2,1)S(1)}, u32[]{:S(2)}, u32[]{:S(2)}) collective-permute-start(bf16[16,256,256]{2,1,0:T(8,128)(2,1)} %get-tuple-element.160), channel_id=1, source_target_pairs={{0,4},{4,0},{8,12},{12,8},{16,20},{20,16},{24,28},{28,24},{1,5},{5... | collective-permute-start | bytes 6291464 | tf_op jit(solution)/shard_map/ppermute | solution.py:577
  140.7 8.9 %collective-permute-start.15 = (bf16[40,256,256]{2,1,0:T(8,128)(2,1)}, bf16[40,256,256]{2,1,0:T(8,128)(2,1)S(1)}, u32[]{:S(2)}, u32[]{:S(2)}) collective-permute-start(bf16[40,256,256]{2,1,0:T(8,128)(2,1)} %get-tuple-element.163), channel_id=1, source_target_pairs={{0,4},{4,0},{8,12},{12,8},{16,20},{20,16},{24,28},{28,24},{1,5},{5... | collective-permute-start | bytes 15728648 | tf_op jit(solution)/shard_map/ppermute | solution.py:577
  140.9 16.8 %collective-permute-start.17 = (bf16[2048,256]{1,0:T(8,128)(2,1)S(1)}, bf16[2048,256]{1,0:T(8,128)(2,1)S(1)}, u32[]{:S(2)}, u32[]{:S(2)}) collective-permute-start(bf16[2048,256]{1,0:T(8,128)(2,1)S(1)} %bitcast.82), channel_id=1, source_target_pairs={{0,8},{4,20},{8,0},{12,28},{16,24},{20,4},{24,16},{28,12},{1,9},{5... | collective-permute-start | bytes 3145736 | tf_op jit(solution)/shard_map/ppermute | solution.py:709
  149.6 40.0 %slice-start = ((s8[5242880]{0:T(1024)(128)(4,1)}), s8[1048576]{0:T(1024)(128)(4,1)S(1)}, s32[]{:S(2)}) async-start(s8[5242880]{0:T(1024)(128)(4,1)} %bitcast.79), calls=%async_computation | async-start | bytes 2097152
  152.3 37.3 %collective-permute-start.16 = (bf16[5120,256]{1,0:T(8,128)(2,1)S(1)}, bf16[5120,256]{1,0:T(8,128)(2,1)S(1)}, u32[]{:S(2)}, u32[]{:S(2)}) collective-permute-start(bf16[5120,256]{1,0:T(8,128)(2,1)S(1)} %bitcast.81), channel_id=1, source_target_pairs={{0,8},{4,20},{8,0},{12,28},{16,24},{20,4},{24,16},{28,12},{1,9},{5... | collective-permute-start | bytes 7864328 | tf_op jit(solution)/shard_map/ppermute | solution.py:709
  153.9 3.8 %collective-permute-start.18 = (f32[2,768]{1,0:T(2,128)S(1)}, f32[2,768]{1,0:T(2,128)S(1)}, u32[]{:S(2)}, u32[]{:S(2)}) collective-permute-start(f32[2,768]{1,0:T(2,128)S(1)} %copy-done.17), channel_id=1, source_target_pairs={{0,16},{4,12},{8,24},{12,4},{16,0},{20,28},{24,8},{28,20},{1,17},{... | collective-permute-start | bytes 18440 | tf_op jit(solution)/shard_map/ppermute | solution.py:785
  157.7 32.0 %slice-start.1 = ((s8[5242880]{0:T(1024)(128)(4,1)}), s8[4194304]{0:T(1024)(128)(4,1)S(1)}, s32[]{:S(2)}) async-start(s8[5242880]{0:T(1024)(128)(4,1)} %bitcast.79), calls=%async_computation.1 | async-start | bytes 8388608
  157.9 14.9 %collective-permute-start.19 = (bf16[1024,256]{1,0:T(8,128)(2,1)S(1)}, bf16[1024,256]{1,0:T(8,128)(2,1)S(1)}, u32[]{:S(2)}, u32[]{:S(2)}) collective-permute-start(bf16[1024,256]{1,0:T(8,128)(2,1)S(1)} %fusion.4), channel_id=1, source_target_pairs={{0,16},{4,12},{8,24},{12,4},{16,0},{20,28},{24,8},{28,20},{1,17},{... | collective-permute-start | bytes 1572872 | tf_op jit(solution)/shard_map/ppermute | solution.py:725
  173.2 12.1 %collective-permute-start.20 = (bf16[1024,256]{1,0:T(8,128)(2,1)S(1)}, bf16[1024,256]{1,0:T(8,128)(2,1)S(1)}, u32[]{:S(2)}, u32[]{:S(2)}) collective-permute-start(bf16[1024,256]{1,0:T(8,128)(2,1)S(1)} %fusion.3), channel_id=1, source_target_pairs={{0,1},{3,2},{4,5},{7,6},{8,9},{11,10},{12,13},{15,14},{16,17},{19,... | collective-permute-start | bytes 1572872 | tf_op jit(solution)/shard_map/ppermute | solution.py:750
  185.5 7.5 %collective-permute-start.23 = (bf16[1024,256]{1,0:T(8,128)(2,1)S(1)}, bf16[1024,256]{1,0:T(8,128)(2,1)S(1)}, u32[]{:S(2)}, u32[]{:S(2)}) collective-permute-start(bf16[1024,256]{1,0:T(8,128)(2,1)S(1)} %add_convert_fusion.3), channel_id=1, source_target_pairs={{1,2},{2,1},{5,6},{6,5},{9,10},{10,9},{13,14},{14,13},{17,18},{18,... | collective-permute-start | bytes 1572872 | tf_op jit(solution)/shard_map/ppermute | solution.py:758
  190.1 12.1 %collective-permute-start.22 = (bf16[1536,256]{1,0:T(8,128)(2,1)S(1)}, bf16[1536,256]{1,0:T(8,128)(2,1)S(1)}, u32[]{:S(2)}, u32[]{:S(2)}) collective-permute-start(bf16[1536,256]{1,0:T(8,128)(2,1)S(1)} %fusion), channel_id=1, source_target_pairs={{0,16},{4,12},{8,24},{12,4},{16,0},{20,28},{24,8},{28,20},{1,17},{... | collective-permute-start | bytes 2359304 | tf_op jit(solution)/shard_map/ppermute | solution.py:725
  191.4 21.8 %collective-permute-start.27 = (f32[2,768]{1,0:T(2,128)S(1)}, f32[2,768]{1,0:T(2,128)S(1)}, u32[]{:S(2)}, u32[]{:S(2)}) collective-permute-start(f32[2,768]{1,0:T(2,128)S(1)} %add.223), channel_id=1, source_target_pairs={{0,8},{4,20},{8,0},{12,28},{16,24},{20,4},{24,16},{28,12},{1,9},{5... | collective-permute-start | bytes 18440 | tf_op jit(solution)/shard_map/ppermute | solution.py:785
  193.0 14.8 %collective-permute-start.21 = (bf16[1024,256]{1,0:T(8,128)(2,1)S(1)}, bf16[1024,256]{1,0:T(8,128)(2,1)S(1)}, u32[]{:S(2)}, u32[]{:S(2)}) collective-permute-start(bf16[1024,256]{1,0:T(8,128)(2,1)S(1)} %fusion.1), channel_id=1, source_target_pairs={{0,16},{4,12},{8,24},{12,4},{16,0},{20,28},{24,8},{28,20},{1,17},{... | collective-permute-start | bytes 1572872 | tf_op jit(solution)/shard_map/ppermute | solution.py:725
  194.2 27.7 %copy-start = (bf16[1024,256]{1,0:T(8,128)(2,1)}, bf16[1024,256]{1,0:T(8,128)(2,1)S(1)}, u32[]{:S(2)}) copy-start(bf16[1024,256]{1,0:T(8,128)(2,1)S(1)} %add_convert_fusion.2.whole_ref) | copy-start | bytes 1572868
  207.8 13.2 %collective-permute-start.26 = (bf16[768,256]{1,0:T(8,128)(2,1)S(1)}, bf16[768,256]{1,0:T(8,128)(2,1)S(1)}, u32[]{:S(2)}, u32[]{:S(2)}) collective-permute-start(bf16[768,256]{1,0:T(8,128)(2,1)S(1)} %get-tuple-element.206), channel_id=1, source_target_pairs={{0,1},{3,2},{4,5},{7,6},{8,9},{11,10},{12,13},{15,14},{16,17},{19,... | collective-permute-start | bytes 1179656 | tf_op jit(solution)/shard_map/ppermute | solution.py:750
  211.5 18.8 %collective-permute-start.25 = (bf16[768,256]{1,0:T(8,128)(2,1)S(1)}, bf16[768,256]{1,0:T(8,128)(2,1)S(1)}, u32[]{:S(2)}, u32[]{:S(2)}) collective-permute-start(bf16[768,256]{1,0:T(8,128)(2,1)S(1)} %get-tuple-element.208), channel_id=1, source_target_pairs={{0,1},{3,2},{4,5},{7,6},{8,9},{11,10},{12,13},{15,14},{16,17},{19,... | collective-permute-start | bytes 1179656 | tf_op jit(solution)/shard_map/ppermute | solution.py:750
  221.1 11.3 %collective-permute-start.30 = (bf16[768,256]{1,0:T(8,128)(2,1)S(1)}, bf16[768,256]{1,0:T(8,128)(2,1)S(1)}, u32[]{:S(2)}, u32[]{:S(2)}) collective-permute-start(bf16[768,256]{1,0:T(8,128)(2,1)S(1)} %add_convert_fusion.7), channel_id=1, source_target_pairs={{1,2},{2,1},{5,6},{6,5},{9,10},{10,9},{13,14},{14,13},{17,18},{18,... | collective-permute-start | bytes 1179656 | tf_op jit(solution)/shard_map/ppermute | solution.py:758
  221.9 21.0 %collective-permute-start.34 = (bf16[1024,256]{1,0:T(8,128)(2,1)S(1)}, bf16[1024,256]{1,0:T(8,128)(2,1)S(1)}, u32[]{:S(2)}, u32[]{:S(2)}) collective-permute-start(bf16[1024,256]{1,0:T(8,128)(2,1)S(1)} %add_convert_fusion.2.whole_ref), channel_id=1, source_target_pairs={{1,0},{2,3},{5,4},{6,7},{9,8},{10,11},{13,12},{14,15},{17,16},{18,... | collective-permute-start | bytes 1572872 | tf_op jit(solution)/shard_map/ppermute | solution.py:763
  223.2 8.5 %collective-permute-start.31 = (f32[2,768]{1,0:T(2,128)S(1)}, f32[2,768]{1,0:T(2,128)S(1)}, u32[]{:S(2)}, u32[]{:S(2)}) collective-permute-start(f32[2,768]{1,0:T(2,128)S(1)} %add.255), channel_id=1, source_target_pairs={{0,4},{4,0},{8,12},{12,8},{16,20},{20,16},{24,28},{28,24},{1,5},{5... | collective-permute-start | bytes 18440 | tf_op jit(solution)/shard_map/ppermute | solution.py:785
  223.2 13.6 %collective-permute-start.29 = (bf16[512,256]{1,0:T(8,128)(2,1)S(1)}, bf16[512,256]{1,0:T(8,128)(2,1)S(1)}, u32[]{:S(2)}, u32[]{:S(2)}) collective-permute-start(bf16[512,256]{1,0:T(8,128)(2,1)S(1)} %get-tuple-element.218), channel_id=1, source_target_pairs={{0,1},{3,2},{4,5},{7,6},{8,9},{11,10},{12,13},{15,14},{16,17},{19,... | collective-permute-start | bytes 786440 | tf_op jit(solution)/shard_map/ppermute | solution.py:750
  230.3 11.9 %collective-permute-start.24 = (bf16[512,256]{1,0:T(8,128)(2,1)S(1)}, bf16[512,256]{1,0:T(8,128)(2,1)S(1)}, u32[]{:S(2)}, u32[]{:S(2)}) collective-permute-start(bf16[512,256]{1,0:T(8,128)(2,1)S(1)} %get-tuple-element.222), channel_id=1, source_target_pairs={{0,1},{3,2},{4,5},{7,6},{8,9},{11,10},{12,13},{15,14},{16,17},{19,... | collective-permute-start | bytes 786440 | tf_op jit(solution)/shard_map/ppermute | solution.py:750
  231.7 5.2 %collective-permute-start.28 = (bf16[768,256]{1,0:T(8,128)(2,1)S(1)}, bf16[768,256]{1,0:T(8,128)(2,1)S(1)}, u32[]{:S(2)}, u32[]{:S(2)}) collective-permute-start(bf16[768,256]{1,0:T(8,128)(2,1)S(1)} %add_convert_fusion.6), channel_id=1, source_target_pairs={{1,2},{2,1},{5,6},{6,5},{9,10},{10,9},{13,14},{14,13},{17,18},{18,... | collective-permute-start | bytes 1179656 | tf_op jit(solution)/shard_map/ppermute | solution.py:758
  232.4 20.4 %collective-permute-start.37 = (f32[2,768]{1,0:T(2,128)S(1)}, f32[2,768]{1,0:T(2,128)S(1)}, u32[]{:S(2)}, u32[]{:S(2)}) collective-permute-start(f32[2,768]{1,0:T(2,128)S(1)} %add.258), channel_id=1, source_target_pairs={{0,1},{1,0},{2,3},{3,2},{4,5},{5,4},{6,7},{7,6},{8,9},{9,8},{10,11... | collective-permute-start | bytes 18440 | tf_op jit(solution)/shard_map/ppermute | solution.py:785
  242.1 10.5 %collective-permute-start.33 = (bf16[512,256]{1,0:T(8,128)(2,1)S(1)}, bf16[512,256]{1,0:T(8,128)(2,1)S(1)}, u32[]{:S(2)}, u32[]{:S(2)}) collective-permute-start(bf16[512,256]{1,0:T(8,128)(2,1)S(1)} %add_convert_fusion.11), channel_id=1, source_target_pairs={{1,2},{2,1},{5,6},{6,5},{9,10},{10,9},{13,14},{14,13},{17,18},{18,... | collective-permute-start | bytes 786440 | tf_op jit(solution)/shard_map/ppermute | solution.py:758
  242.9 9.8 %collective-permute-start.32 = (bf16[512,256]{1,0:T(8,128)(2,1)S(1)}, bf16[512,256]{1,0:T(8,128)(2,1)S(1)}, u32[]{:S(2)}, u32[]{:S(2)}) collective-permute-start(bf16[512,256]{1,0:T(8,128)(2,1)S(1)} %add_convert_fusion.10), channel_id=1, source_target_pairs={{1,2},{2,1},{5,6},{6,5},{9,10},{10,9},{13,14},{14,13},{17,18},{18,... | collective-permute-start | bytes 786440 | tf_op jit(solution)/shard_map/ppermute | solution.py:758
  243.6 19.2 %collective-permute-start.40 = (bf16[768,256]{1,0:T(8,128)(2,1)S(1)}, bf16[768,256]{1,0:T(8,128)(2,1)S(1)}, u32[]{:S(2)}, u32[]{:S(2)}) collective-permute-start(bf16[768,256]{1,0:T(8,128)(2,1)S(1)} %add_convert_fusion.5.whole_ref), channel_id=1, source_target_pairs={{1,0},{2,3},{5,4},{6,7},{9,8},{10,11},{13,12},{14,15},{17,16},{18,... | collective-permute-start | bytes 1179656 | tf_op jit(solution)/shard_map/ppermute | solution.py:763
  244.9 25.5 %collective-permute-start.39 = (bf16[768,256]{1,0:T(8,128)(2,1)S(1)}, bf16[768,256]{1,0:T(8,128)(2,1)S(1)}, u32[]{:S(2)}, u32[]{:S(2)}) collective-permute-start(bf16[768,256]{1,0:T(8,128)(2,1)S(1)} %add_convert_fusion.4.whole_ref), channel_id=1, source_target_pairs={{1,0},{2,3},{5,4},{6,7},{9,8},{10,11},{13,12},{14,15},{17,16},{18,... | collective-permute-start | bytes 1179656 | tf_op jit(solution)/shard_map/ppermute | solution.py:763
  252.8 24.1 %collective-permute-start.38 = (f32[2,768]{1,0:T(2,128)S(1)}, f32[2,768]{1,0:T(2,128)S(1)}, u32[]{:S(2)}, u32[]{:S(2)}) collective-permute-start(f32[2,768]{1,0:T(2,128)S(1)} %add.265), channel_id=1, source_target_pairs={{0,2},{1,3},{2,0},{3,1},{4,6},{5,7},{6,4},{7,5},{8,10},{9,11},{10,... | collective-permute-start | bytes 18440 | tf_op jit(solution)/shard_map/ppermute | solution.py:785
  260.2 17.3 %collective-permute-start.36 = (bf16[512,256]{1,0:T(8,128)(2,1)S(1)}, bf16[512,256]{1,0:T(8,128)(2,1)S(1)}, u32[]{:S(2)}, u32[]{:S(2)}) collective-permute-start(bf16[512,256]{1,0:T(8,128)(2,1)S(1)} %add_convert_fusion.9.whole_ref), channel_id=1, source_target_pairs={{1,0},{2,3},{5,4},{6,7},{9,8},{10,11},{13,12},{14,15},{17,16},{18,... | collective-permute-start | bytes 786440 | tf_op jit(solution)/shard_map/ppermute | solution.py:763
  261.5 21.1 %collective-permute-start.35 = (bf16[512,256]{1,0:T(8,128)(2,1)S(1)}, bf16[512,256]{1,0:T(8,128)(2,1)S(1)}, u32[]{:S(2)}, u32[]{:S(2)}) collective-permute-start(bf16[512,256]{1,0:T(8,128)(2,1)S(1)} %add_convert_fusion.8.whole_ref), channel_id=1, source_target_pairs={{1,0},{2,3},{5,4},{6,7},{9,8},{10,11},{13,12},{14,15},{17,16},{18,... | collective-permute-start | bytes 786440 | tf_op jit(solution)/shard_map/ppermute | solution.py:763
  (17 other events, 127.7 us)

commit v4 on v3

--- a/solution.py
+++ b/solution.py
@@ -1,4 +1,5 @@
 import functools
+import math
 
 import jax
 import jax.numpy as jnp
@@ -60,15 +61,6 @@
     return np.array(lefts, np.int32), np.array(rights, np.int32)
 
 
-def positions_of(segments):
-    places = jnp.arange(segments.shape[-1], dtype=jnp.int32)[None, :]
-    starts = jnp.concatenate(
-        [jnp.ones((segments.shape[0], 1), jnp.bool_), segments[:, 1:] != segments[:, :-1]], axis=1
-    )
-    first_place = lax.cummax(jnp.where(starts, places, 0), axis=1)
-    return places - first_place
-
-
 def dot_nn(a, b):
     return jnp.dot(a, b, preferred_element_type=F32)
 
@@ -81,65 +73,93 @@
     return jnp.where(low_half, pltpu.roll(values, 96, 1), pltpu.roll(values, 32, 1))
 
 
-def weigh_slots(count, first_ref, at, left_ref, right_ref, lefts, rights, outs, ring, sems):
-    per_out = outs[0].shape[0] // count
-    total = per_out * len(outs)
-
-    def put(target, half):
-        return pltpu.make_async_copy(ring.at[half, pl.ds(0, count)], target, sems.at[half])
+def list_factors(index_ref, block_left_ref, block_right_ref, left_ref, right_ref):
+    def clear(g, carry):
+        for n in range(4):
+            left_ref[4 * g + n] = -1
+            right_ref[4 * g + n] = 0
+        return carry
+
+    lax.fori_loop(0, left_ref.shape[0] // 4, clear, 0)
+
+    def enter(g, carry):
+        for n in range(4):
+            slot = index_ref[4 * g + n]
+            left_ref[slot] = block_left_ref[4 * g + n]
+            right_ref[slot] = block_right_ref[4 * g + n]
+        return carry
+
+    lax.fori_loop(0, index_ref.shape[0] // 4, enter, 0)
+
+
+WEIGH_COPY = 4
+
+
+def weigh_slots(slot_ref, left_ref, right_ref, lefts, rights, outs, ring, sems):
+    copies = [out.shape[0] // WEIGH_COPY for out in outs]
+    total = sum(copies)
+    assert total % 2 == 0
+
+    def put(target, place):
+        return pltpu.make_async_copy(ring.at[place], target, sems.at[place])
 
     def run(g, carry):
-        half = lax.rem(g, 2)
-
-        @pl.when(g >= 2)
-        def _():
-            put(ring.at[half, pl.ds(0, count)], half).wait()
-
-        first = first_ref[at + g]
-        for n in range(count):
-            left = left_ref[first + n]
+        first_place = 2 * lax.rem(g, 2)
+        for half in range(2):
+
+            @pl.when(g >= 2)
+            def _(half=half):
+                put(ring.at[first_place + half], first_place + half).wait()
+
+        for n in range(2 * WEIGH_COPY):
+            slot = slot_ref[2 * g * WEIGH_COPY + n]
+            left = left_ref[slot]
             grad = dot_nn(
                 lefts[pl.ds(pl.multiple_of(jnp.maximum(left, 0) * B, B), B), :],
-                rights[:, pl.ds(pl.multiple_of(right_ref[first + n] * B, B), B)],
+                rights[:, pl.ds(pl.multiple_of(right_ref[slot] * B, B), B)],
             )
             keep = jnp.where(left >= 0, 1.0, 0.0)
-            ring[half, n] = (grad * keep).astype(BF16)
-        for number, out in enumerate(outs):
-
-            @pl.when((g >= number * per_out) & (g < (number + 1) * per_out))
-            def _(number=number, out=out):
-                put(out.at[pl.ds((g - number * per_out) * count, count)], half).start()
-
+            ring[first_place + n // WEIGH_COPY, n % WEIGH_COPY] = (grad * keep).astype(BF16)
+        for half in range(2):
+            copy = 2 * g + half
+            first = 0
+            for out, count in zip(outs, copies):
+
+                @pl.when((copy >= first) & (copy < first + count))
+                def _(out=out, first=first, half=half, copy=copy):
+                    at = pl.ds((copy - first) * WEIGH_COPY, WEIGH_COPY)
+                    put(out.at[at], first_place + half).start()
+
+                first += count
         return carry
 
-    lax.fori_loop(0, total, run, 0)
-    for g in range(max(0, total - 2), total):
-        put(ring.at[g % 2, pl.ds(0, count)], g % 2).wait()
+    assert total >= 4
+    lax.fori_loop(0, total // 2, run, 0)
+    for place in range(4):
+        put(ring.at[place], place).wait()
 
 
 def layer_kernel(
     micro,
+    own,
     piece_slots,
-    counts,
+    out_count,
     index_ref,
-    piece_first_ref,
-    slot_first_ref,
-    left_ref,
-    right_ref,
+    base_ref,
+    slot_ref,
+    block_left_ref,
+    block_right_ref,
+    segments_ref,
+    segments_t_ref,
     x_ref,
     dy_ref,
-    bias_ref,
-    cos_ref,
-    sin_ref,
-    cos_t_ref,
-    sin_t_ref,
     gains_ref,
     *rest,
 ):
     pieces = rest[: len(piece_slots)]
     rest = rest[len(piece_slots) :]
     out_ref, token_grad_ref, gain_ref = rest[:3]
-    grad_refs, rest = rest[3 : 3 + 2 * len(counts)], rest[3 + 2 * len(counts) :]
+    grad_refs, rest = rest[3 : 3 + out_count], rest[3 + out_count :]
     (
         w_qkv,
         w_o,
@@ -163,23 +183,43 @@
         w_sems,
         ring,
         ring_sems,
+        left_ref,
+        right_ref,
+        bias_ref,
+        cos_ref,
+        sin_ref,
+        cos_t_ref,
+        sin_t_ref,
     ) = rest
-    seq = bias_ref.shape[1]
+    seq = segments_ref.shape[1]
+
+    starts = [sum(piece_slots[:n]) for n in range(len(piece_slots) + 1)]
+    reciprocal = (1 << 16) // own + 1
+    assert all(slot * reciprocal >> 16 == slot // own for slot in range(starts[-1]))
 
     def fetch(block, target, row, col, sem):
         slot = index_ref[block]
-        for number, (piece, count) in enumerate(zip(pieces, piece_slots)):
-            place = slot - piece_first_ref[number]
-
-            @pl.when((place >= 0) & (place < count))
-            def _(piece=piece, place=place):
+        owner = lax.shift_right_logical(slot * reciprocal, 16)
+        place = base_ref[owner] + slot - owner * own
+
+        def among(low, high):
+            if high - low > 1:
+                middle = (low + high) // 2
+                lax.cond(
+                    place < starts[middle],
+                    lambda: among(low, middle),
+                    lambda: among(middle, high),
+                )
+            else:
                 pltpu.make_async_copy(
-                    piece.at[place],
+                    pieces[low].at[place - starts[low]],
                     target.at[
                         pl.ds(pl.multiple_of(row * B, B), B), pl.ds(pl.multiple_of(col * B, B), B)
                     ],
                     sem,
                 ).start()
+
+        among(0, len(pieces))
 
     def fetch_matrix(first_block, grid_rows, grid_cols, target, col_offset, sem):
         def one(t, carry):
@@ -193,6 +233,26 @@
     nd, nf = D // B, FF // B
     for m in range(3):
         fetch_matrix(m * nd * nd, nd, nd, w_qkv, m * nd, w_sems.at[0])
+
+    list_factors(index_ref, block_left_ref, block_right_ref, left_ref, right_ref)
+    half_dim = HEAD_DIM // 2
+    step = lax.broadcasted_iota(jnp.int32, (half_dim, 1), 0).astype(F32)
+    frequency = jnp.exp(step * (-2.0 / HEAD_DIM * math.log(ROPE_BASE)))
+    keys = lax.broadcasted_iota(jnp.int32, (seq, seq), 0)
+    queries = lax.broadcasted_iota(jnp.int32, (seq, seq), 1)
+    for r in range(micro):
+        rows = slice(r * seq, (r + 1) * seq)
+        same = segments_t_ref[:, r : r + 1] == segments_ref[r : r + 1, :]
+        bias_ref[r] = jnp.where(same & (keys <= queries), 0.0, MASKED)
+        first = jnp.min(jnp.where(same, keys, seq), axis=0, keepdims=True)
+        angles = frequency * (queries[0:1, :] - first).astype(F32)
+        cosine_t, sine_t = jnp.cos(angles), jnp.sin(angles)
+        cos_t_ref[:, rows] = cosine_t
+        sin_t_ref[:, rows] = sine_t
+        cosine, sine = cosine_t.T, sine_t.T
+        cos_ref[rows, :] = jnp.concatenate([cosine] * 4, axis=1)
+        sin_ref[rows, :] = jnp.concatenate([-sine, sine, -sine, sine], axis=1)
+
     fetch_matrix(3 * nd * nd, nd, nd, w_o, 0, w_sems.at[1])
     for m in range(2):
         fetch_matrix(4 * nd * nd + m * nd * nf, nd, nf, w_gu, m * nf, w_sems.at[2])
@@ -385,38 +445,29 @@
 
     lax.fori_loop(0, nd, token_back, 0)
 
-    at = 0
-    for group, count in enumerate(counts):
-        outs = grad_refs[2 * group : 2 * group + 2]
-        weigh_slots(
-            count, slot_first_ref, at, left_ref, right_ref, lefts, rights, outs, ring, ring_sems
-        )
-        at += 2 * outs[0].shape[0] // count
+    weigh_slots(slot_ref, left_ref, right_ref, lefts, rights, grad_refs, ring, ring_sems)
 
 
 def run_layer(
-    tokens, cotangent, segment_ids, block_slot_index, norm_gains, tables, pieces, piece_firsts,
-    slot_tables, slot_firsts, counts,
+    tokens, cotangent, segment_ids, block_slot_index, norm_gains, pieces, own, bases, slot_order,
+    out_sizes,
 ):
     micro, seq = segment_ids.shape
     count = micro * seq
-    grads = [
-        jax.ShapeDtypeStruct((slots * len(firsts) // 2, B, B), BF16)
-        for slots, firsts in zip(counts, slot_firsts)
-        for _ in range(2)
-    ]
+    slots = own * bases.shape[0]
+    grads = [jax.ShapeDtypeStruct((size, B, B), BF16) for size in out_sizes]
     vmem = pl.BlockSpec(memory_space=pltpu.VMEM)
     smem = pl.BlockSpec(memory_space=pltpu.SMEM)
     hbm = pl.BlockSpec(memory_space=pl.ANY)
     return pl.pallas_call(
-        functools.partial(layer_kernel, micro, [p.shape[0] for p in pieces], counts),
+        functools.partial(layer_kernel, micro, own, [p.shape[0] for p in pieces], len(grads)),
         out_shape=(
             jax.ShapeDtypeStruct((count, D), BF16),
             jax.ShapeDtypeStruct((count, D), BF16),
             jax.ShapeDtypeStruct((2, D), F32),
             *grads,
         ),
-        in_specs=[smem] * 5 + [vmem] * 8 + [hbm] * len(pieces),
+        in_specs=[smem] * 5 + [vmem] * 5 + [hbm] * len(pieces),
         out_specs=(vmem,) * 3 + (hbm,) * len(grads),
         scratch_shapes=[
             pltpu.VMEM((D, 3 * D), BF16),
@@ -439,8 +490,15 @@
             pltpu.VMEM((count, D), F32),
             pltpu.VMEM((count, 1), F32),
             pltpu.SemaphoreType.DMA((4,)),
-            pltpu.VMEM((2, max(counts), B, B), BF16),
-            pltpu.SemaphoreType.DMA((2,)),
+            pltpu.VMEM((4, WEIGH_COPY, B, B), BF16),
+            pltpu.SemaphoreType.DMA((4,)),
+            pltpu.SMEM((slots,), jnp.int32),
+            pltpu.SMEM((slots,), jnp.int32),
+            pltpu.VMEM((micro, seq, seq), F32),
+            pltpu.VMEM((count, 128), F32),
+            pltpu.VMEM((count, 128), F32),
+            pltpu.VMEM((HEAD_DIM // 2, count), F32),
+            pltpu.VMEM((HEAD_DIM // 2, count), F32),
         ],
         compiler_params=pltpu.CompilerParams(vmem_limit_bytes=56 * MIB),
         cost_estimate=pl.CostEstimate(
@@ -449,54 +507,36 @@
         name="layer",
     )(
         block_slot_index,
-        jnp.stack(piece_firsts).astype(jnp.int32),
-        jnp.stack([first for firsts in slot_firsts for first in firsts]).astype(jnp.int32),
-        *slot_tables,
+        bases,
+        slot_order,
+        *(jnp.asarray(table) for table in factor_tables()),
+        segment_ids,
+        segment_ids.T,
         tokens,
         cotangent,
-        *tables,
         norm_gains,
         *pieces,
     )
 
 
-def layer_tables(segment_ids):
-    micro, seq = segment_ids.shape
-    count = micro * seq
-    half_dim = HEAD_DIM // 2
-    frequency = ROPE_BASE ** (-2.0 * jnp.arange(half_dim, dtype=F32) / HEAD_DIM)
-    angles = positions_of(segment_ids).reshape(count).astype(F32)[:, None] * frequency[None, :]
-    cosine, sine = jnp.cos(angles), jnp.sin(angles)
-    cos_wide = jnp.tile(cosine, (1, 4))
-    sin_wide = jnp.concatenate([-sine, sine, -sine, sine], axis=1)
-    places = jnp.arange(seq, dtype=jnp.int32)
-    visible = (segment_ids[:, :, None] == segment_ids[:, None, :]) & (
-        places[:, None] <= places[None, :]
-    )
-    bias = jnp.where(visible, 0.0, MASKED).astype(F32)
-    return bias, cos_wide, sin_wide, cosine.T, sine.T
-
-
-def slot_tables(block_slot_index, slots):
-    left_table, right_table = factor_tables()
-    slot_left = jnp.full((slots,), -1, jnp.int32).at[block_slot_index].set(left_table)
-    slot_right = jnp.zeros((slots,), jnp.int32).at[block_slot_index].set(right_table)
-    return slot_left, slot_right
-
-
 def split_two(values):
     high = values.astype(BF16)
     return high, (values - high.astype(F32)).astype(BF16)
 
 
-def adam_kernel(
-    inner_ref, whole_ref, outward_ref, weight_ref, first_ref, second_ref, left_ref, right_ref, *rest
-):
-    grad_out, first_out, second_out, weight_out, low_out = rest[-5:]
-    inner = inner_ref[0] != 0
+def adam_kernel(steps, weight_ref, first_ref, second_ref, left_ref, right_ref, *rest):
+    grad_refs = rest[: len(steps)]
+    grad_out, first_out, second_out, weight_out, low_out, grads = rest[-6:]
+    now, start = pl.program_id(0), 0
+    for count, grad_ref in zip(steps, grad_refs):
+
+        @pl.when((now >= start) & (now < start + count))
+        def _(grad_ref=grad_ref):
+            grads[...] = grad_ref[...]
+
+        start += count
     for n in range(weight_ref.shape[0]):
-        block = pl.ds(n * B, B)
-        grad = jnp.where(inner, whole_ref[block, :], outward_ref[block, :])
+        grad = grads[n * B : (n + 1) * B, :]
         left, left_rest = split_two(left_ref[n])
         right, right_rest = split_two(right_ref[n])
         grad_out[n] = grad.astype(F32)
@@ -518,29 +558,40 @@
         low_out[n] = weight_new.astype(BF16)
 
 
-def adam_blocks(whole, outward, inner, start, count, state, done):
+def adam_blocks(grads, start, state, done):
     own = state[0].shape[0]
-    step = next(n for n in (2, 1) if count % n == 0 and start % n == 0)
-    local = pl.BlockSpec((step * B, B), lambda s: (s, 0))
-    offset = pl.BlockSpec((step, B, B), lambda s: (s + start // step, 0, 0))
+    step = math.gcd(2, start, *(part.shape[0] // B for part in grads))
+    steps = [part.shape[0] // B // step for part in grads]
+    local = []
+    for number, count in enumerate(steps):
+        local.append(
+            pl.BlockSpec(
+                (step * B, B),
+                lambda s, first=sum(steps[:number]), count=count: (
+                    jnp.clip(s - first, 0, count - 1),
+                    0,
+                ),
+            )
+        )
+    spec = pl.BlockSpec((step, B, B), lambda s: (s + start // step, 0, 0))
     hbm = pl.BlockSpec(memory_space=pl.ANY)
-    smem = pl.BlockSpec(memory_space=pltpu.SMEM)
     wide = jax.ShapeDtypeStruct((own, B, B), F32)
     return pl.pallas_call(
-        adam_kernel,
-        grid=(count // step,),
+        functools.partial(adam_kernel, steps),
+        grid=(sum(steps),),
         out_shape=(wide, wide, wide, wide, jax.ShapeDtypeStruct((own, B, B), BF16)),
-        in_specs=[smem] + [local] * 2 + [offset] * 5 + [hbm] * len(done),
-        out_specs=(offset,) * 5,
-        input_output_aliases={8 + n: n for n in range(len(done))},
+        in_specs=[spec] * 5 + local + [hbm] * len(done),
+        out_specs=(spec,) * 5,
+        input_output_aliases={5 + len(local) + n: n for n in range(len(done))},
+        scratch_shapes=[pltpu.VMEM((step * B, B), BF16)],
         compiler_params=pltpu.CompilerParams(vmem_limit_bytes=60 * MIB),
         cost_estimate=pl.CostEstimate(
-            flops=count * 6 * 2 * B**3,
-            bytes_accessed=count * B * B * 42,
-            transcendentals=count * B * B,
+            flops=sum(steps) * step * 12 * B**3,
+            bytes_accessed=sum(steps) * step * B * B * 42,
+            transcendentals=sum(steps) * step * B * B,
         ),
         name="adam",
-    )(inner.reshape(1), whole, outward, *state, *done)
+    )(*state, *grads, *done)
 
 
 def adam_plain(grads, values, first_moment, second_moment):
@@ -577,44 +628,51 @@
     return lax.ppermute(values, "fsdp", [(i, i ^ bit) for i in range(lax.axis_size("fsdp"))])
 
 
+def core_neighbours(me):
+    near = jnp.where((me & CORE) == 0, ACROSS, ALONG)
+    return near, DIAGONAL ^ near
+
+
+def plane_pairs(owners):
+    near = [(i, i ^ (ALONG if i & CORE else ACROSS)) for i in range(owners)]
+    far = [(i, i ^ (ACROSS if i & CORE else ALONG)) for i in range(owners)]
+    return near, far
+
+
 def after(values, *others):
     return lax.optimization_barrier((values, *others))[0]
 
 
-def gather_pieces(weights, me, make_tables):
+def gather_pieces(weights, me):
     own = weights.shape[0]
     half = own // 2
-    first_half = weights[:half].astype(BF16)
-    second_half = weights[half:].astype(BF16)
-    pieces, firsts = [], []
-
-    def keep(piece, relation, start):
-        pieces.append(piece)
-        firsts.append((me ^ relation) * own + start)
-
-    def keep_both(piece, relation, start):
-        keep(piece, relation, start)
-        keep(exchange(piece, CORE), relation | CORE, start)
-
-    along_first = exchange(first_half, ALONG)
-    across_second = exchange(second_half, ACROSS)
-    along_second = exchange(second_half, ALONG)
-    across_first = exchange(first_half, ACROSS)
-    tables = make_tables(along_first, across_second)
-    (along_first, across_second), tables = lax.optimization_barrier(
-        ((along_first, across_second), tables)
+    near, far = core_neighbours(me)
+    near_pairs, far_pairs = plane_pairs(lax.axis_size("fsdp"))
+    mine = weights.astype(BF16)
+    first_near = lax.ppermute(weights[:half].astype(BF16), "fsdp", near_pairs)
+    last_near = lax.ppermute(weights[half:].astype(BF16), "fsdp", near_pairs)
+    all_far = lax.ppermute(mine, "fsdp", far_pairs)
+    first_diagonal = lax.ppermute(first_near, "fsdp", far_pairs)
+    last_diagonal = lax.ppermute(last_near, "fsdp", far_pairs)
+    pieces, relations = [], []
+    for parts, relation, others in (
+        ((mine,), 0, 0),
+        ((first_near, last_near), near, far),
+        ((all_far,), far, near),
+        ((first_diagonal, last_diagonal), DIAGONAL, DIAGONAL),
+    ):
+        pieces += [*parts, *(exchange(part, CORE) for part in parts)]
+        relations += [relation, others | CORE]
+    owners = me ^ jnp.stack(relations).astype(jnp.int32)
+    bases = jnp.sum(
+        jnp.where(
+            jnp.arange(len(relations), dtype=jnp.int32)[:, None] == owners[None, :],
+            jnp.arange(len(relations), dtype=jnp.int32)[None, :] * own,
+            0,
+        ),
+        axis=1,
     )
-    keep_both(first_half, 0, 0)
-    keep_both(second_half, 0, half)
-    keep_both(along_first, ALONG, 0)
-    keep_both(across_second, ACROSS, half)
-    diagonal_first = exchange(along_first, ACROSS)
-    diagonal_second = exchange(across_second, ALONG)
-    keep_both(along_second, ALONG, half)
-    keep_both(across_first, ACROSS, 0)
-    keep_both(diagonal_first, DIAGONAL, 0)
-    keep_both(diagonal_second, DIAGONAL, half)
-    return pieces, firsts, tables
+    return pieces, bases
 
 
 class Plan:
@@ -641,34 +699,29 @@
         return values
 
 
-GROUPS = (((4, 1),), ((6, 2), (4, 2)))
+GROUPS = (((4,),), ((6,), (2, 2)))
 ORDER = (
-    "grads0 grads1 core0 gain_far near_sum0 near0 core1 near_sum1 near1 gain1 "
-    "far_sum0_0 far0_0 plane_sum0_0 inward0_0a halfway0_0a middle0_0a far_sum1_0 far1_0 far_sum1_1 far1_1 gain_near "
-    "whole0_0a outward0_0a plane_sum1_0 inward1_0a inward1_0b plane_sum1_1 inward1_1a inward1_1b gain2 gain_core "
-    "halfway1_0a middle1_0a halfway1_0b middle1_0b gain3 gain_pair whole1_0a outward1_0a halfway1_1a middle1_1a "
-    "whole1_0b outward1_0b halfway1_1b middle1_1b adam0_0a whole1_1a outward1_1a whole1_1b outward1_1b gain4 gain_line "
-    "adam1_0a adam1_0b gain5 adam1_1a adam1_1b"
+    "grads0 grads1 core0 gain_far near_sum0 near0 core1 near_sum1 near1 gain1 far_sum0_0 far0_0 plane_sum0_0 "
+    "inward0_0a halfway0_0a middle0_0a far_sum1_0 far1_0 far_sum1_1 far1_1 gain_near whole0_0a outward0_0a "
+    "plane_sum1_0 inward1_0a plane_sum1_1 inward1_1a inward1_1b gain2 gain_core halfway1_0a middle1_0a "
+    "final0_0a gain3 gain_pair halfway1_1a middle1_1a whole1_0a outward1_0a halfway1_1b middle1_1b step0 "
+    "whole1_1a outward1_1a final1_0a whole1_1b outward1_1b gain4 gain_line final1_1a gain5 final1_1b step1"
 ).split()
 
 
 def group_sizes():
-    return [sum(size for size, _ in sets) for sets in GROUPS]
-
-
-def core_neighbours(me):
-    near = jnp.where((me & CORE) == 0, ACROSS, ALONG)
-    return near, DIAGONAL ^ near
-
-
-def group_firsts(me, own):
+    return [sum(sum(parts) for parts in sets) for sets in GROUPS]
+
+
+def slot_order_of(me, own):
     near, far = core_neighbours(me)
     relations = [DIAGONAL | CORE, far | CORE, near | CORE, CORE, DIAGONAL, near, far, 0]
-    firsts, start = [], 0
+    slots, start = [], 0
     for size in group_sizes():
-        firsts.append([(me ^ relation) * own + start for relation in relations])
+        for relation in relations:
+            slots.append((me ^ relation) * own + start + jnp.arange(size, dtype=jnp.int32))
         start += size
-    return firsts
+    return jnp.concatenate(slots).astype(jnp.int32)
 
 
 def flat(blocks):
@@ -678,20 +731,20 @@
 def reduce_and_step(me, own, grads, state, gain_grad):
     plan = Plan()
     owners = lax.axis_size("fsdp")
-    near_pairs = [(i, i ^ (ALONG if i & CORE else ACROSS)) for i in range(owners)]
-    far_pairs = [(i, i ^ (ACROSS if i & CORE else ALONG)) for i in range(owners)]
+    near_pairs, far_pairs = plane_pairs(owners)
     place = lax.axis_index("rep")
-    inner = ((place == 1) | (place == 2)).astype(jnp.int32)
+    inner = (place == 1) | (place == 2)
     done = ()
-
     start = 0
+
     for number, sets in enumerate(GROUPS):
-        total = sum(size for size, _ in sets)
+        total = group_sizes()[number]
 
         def name(text, number=number):
             return text + str(number)
 
         both = [name("grads"), name("core")]
+        finals = []
 
         def chip(pair, arrived, first, last):
             return flat(pair[1][first:last]), flat(arrived[first:last])
@@ -709,7 +762,8 @@
             name("near"), [name("near_sum")], lambda t: lax.ppermute(t, "fsdp", near_pairs)
         )
         inside = 0
-        for member, (size, parts) in enumerate(sets):
+        for member, parts in enumerate(sets):
+            size = sum(parts)
 
             def at(text, number=number, member=member):
                 return "%s%d_%d" % (text, number, member)
@@ -724,7 +778,7 @@
             plan.send(
                 at("far"), [at("far_sum")], lambda t: lax.ppermute(t, "fsdp", far_pairs)
             )
-            firsts = [size * p // parts for p in range(parts + 1)]
+            firsts = [sum(parts[:p]) for p in range(len(parts) + 1)]
 
             def plane_sum(pair, arrived, r, q, inside=inside, total=total, firsts=firsts):
                 sums = []
@@ -740,7 +794,7 @@
                 return sums
 
             plan.core(at("plane_sum"), both + [name("near"), at("far")], plane_sum)
-            for part in range(parts):
+            for part in range(len(parts)):
 
                 def of(text, part=part, at=at):
                     return at(text) + "abcd"[part]
@@ -762,15 +816,19 @@
                     of("outward"), [of("whole")],
                     lambda t: lax.ppermute(t, "rep", [(1, 0), (2, 3)]),
                 )
-                first, last = firsts[part : part + 2]
-
-                def adam(whole, outward, first=start + inside + first, count=last - first):
-                    nonlocal done
-                    done = adam_blocks(whole, outward, inner, first, count, state, done)
-                    return done
-
-                plan.core(of("adam"), [of("whole"), of("outward")], adam)
+                plan.core(
+                    of("final"), [of("whole"), of("outward")],
+                    lambda whole, outward: jnp.where(inner, whole, outward),
+                )
+                finals.append(of("final"))
             inside += size
+
+        def step(*grads, start=start):
+            nonlocal done
+            done = adam_blocks(grads, start, state, done)
+            return done
+
+        plan.core(name("step"), finals, step)
         start += total
 
     old = None
@@ -815,36 +873,27 @@
     state = (weights, first_moment, second_moment, left_basis, right_basis)
     small = owners == 8 and lax.axis_size("rep") == 4 and own == sum(group_sizes())
 
-    def make_tables(*others):
-        segments, index = segment_ids, block_slot_index
-        if others:
-            segments, index, *_ = lax.optimization_barrier((segments, index, *others))
-        return layer_tables(segments), slot_tables(index, slots)
-
     if small:
-        pieces, piece_firsts, (tables, slot_factors) = gather_pieces(weights, me, make_tables)
+        pieces, bases = gather_pieces(weights, me)
+        slot_order = slot_order_of(me, own)
+        out_sizes = [4 * size for size in group_sizes() for _ in range(2)]
     else:
         pieces = [lax.all_gather(weights.astype(BF16), "fsdp", axis=0, tiled=True)]
-        piece_firsts = [jnp.int32(0)]
-        tables, slot_factors = make_tables()
-    if small:
-        counts = group_sizes()
-        slot_firsts = group_firsts(me, own)
-    else:
-        counts = [next(n for n in (8, 4, 2) if slots % (2 * n) == 0)]
-        slot_firsts = [[jnp.int32(first) for first in range(0, slots, counts[0])]]
+        bases = jnp.arange(owners, dtype=jnp.int32) * own
+        slot_order = jnp.arange(slots, dtype=jnp.int32)
+        out_sizes = [slots]
     block_out, token_grad, gain_grad, *grads = run_layer(
-        tokens, cotangent, segment_ids, block_slot_index, norm_gains, tables, pieces, piece_firsts,
-        slot_factors, slot_firsts, counts,
+        tokens, cotangent, segment_ids, block_slot_index, norm_gains, pieces, own, bases,
+        slot_order, out_sizes,
     )
     if small:
         done, gain_grads = reduce_and_step(me, own, grads, state, gain_grad)
     else:
         owner_sums = lax.psum_scatter(
-            jnp.concatenate(grads), "fsdp", scatter_dimension=0, tiled=True
+            grads[0], "fsdp", scatter_dimension=0, tiled=True
         )
         owner_grads = flat(lax.psum(owner_sums, "rep"))
-        done = adam_blocks(owner_grads, owner_grads, jnp.int32(1), 0, own, state, ())
+        done = adam_blocks([owner_grads], 0, state, ())
         gain_grads = sum_everywhere(sum_everywhere(gain_grad, "fsdp"), "rep")
     grads_wide, first_new, second_new, weights_new, weights_low = done
     gain_first_new, gain_second_new, gains_new = adam_plain(

time: 288 us -> 283 us (0.983)
  waiting for transfers between devices: 118 us -> 137 us
  local copies, waits for them, and re-layouts: 10.7 us -> 1.67 us
  Pallas kernels: 88.5 us -> 80.1 us
  starting transfers between devices: 54.7 us -> 48.2 us
    ppermute x0 -> x5, waiting for transfers between devices: none -> 57.4 us  [the longest x1 21.3 us: gather_pieces(): last_near = lax.ppermute(weights[half:].astype(BF16), 'fsdp', near_pairs)]
    ppermute x16 -> x8, waiting for transfers between devices: 59 us -> 12.5 us  [exchange(): lax.ppermute(values, 'fsdp', [(i, i ^ bit) for i in range(lax.axis_size('...]
    ppermute x5 -> x4, waiting for transfers between devices: 1.15 us -> 13.8 us  [reduce_and_step(): lax.ppermute(t, 'rep', [(1, 0), (2, 3)])]
    ppermute x16 -> x8, starting transfers between devices: 9.92 us -> 1.4 us  [exchange(): lax.ppermute(values, 'fsdp', [(i, i ^ bit) for i in range(lax.axis_size('...]
    pallas_call x6 -> x3, Pallas kernels: 88.5 us -> 80.1 us  [the longest x1 61.2 us: run_layer(): pl.pallas_call(functools.partial(layer_kernel, micro, own, [p.shape[0] fo...]
    ppermute x0 -> x5, starting transfers between devices: none -> 5.13 us  [the longest x1 3.03 us: gather_pieces(): all_far = lax.ppermute(mine, 'fsdp', far_pairs)]
    ppermute x3, waiting for transfers between devices: 27 us -> 22.6 us  [reduce_and_step(): lax.ppermute(t, 'fsdp', far_pairs)]
    unnamed x50 -> x21, local copies, waits for them, and re-layouts: 4.79 us -> 0.86 us
  transfers between devices with their start and end apart: 41 -> 35, of which waited for: 20 -> 18; matrix products, arithmetic and copies ran while one was open for 6% -> 4% of each run, Pallas kernels for 8% -> 2%
where the time goes in v4:
time: 283 us; the launch traced here: 282 us
  waiting for transfers between devices  137 us (48%)
  Pallas kernels  80.1 us (28%)
  starting transfers between devices  48.2 us (17%)
  other arithmetic  14 us (5%)
    pallas_call x1, Pallas kernels, run_layer(): pl.pallas_call(functools.partial(layer_kernel, micro, own, [p.shape[0] fo...  61.2 us
    ppermute x4, waiting for transfers between devices, reduce_and_step(): lax.ppermute(t[part], 'rep', [(0, 1), (3, 2)])  25.1 us
    ppermute x3, waiting for transfers between devices, reduce_and_step(): lax.ppermute(t, 'fsdp', far_pairs)  22.6 us
    ppermute x1, waiting for transfers between devices, gather_pieces(): last_near = lax.ppermute(weights[half:].astype(BF16), 'fsdp', near_pairs)  21.3 us
    ppermute x1, waiting for transfers between devices, gather_pieces(): first_near = lax.ppermute(weights[:half].astype(BF16), 'fsdp', near_pairs)  19.8 us
    pallas_call x2, Pallas kernels, adam_blocks(): pl.pallas_call(functools.partial(adam_kernel, steps), grid=(sum(steps),),...  18.9 us
    ppermute x4, starting transfers between devices, reduce_and_step(): lax.ppermute(t[part], 'rep', [(0, 1), (3, 2)])  17.2 us
    ppermute x4, waiting for transfers between devices, reduce_and_step(): lax.ppermute(t, 'rep', [(1, 0), (2, 3)])  13.8 us
  transfers between devices with their start and end apart: 35, of which 18 were waited for; matrix products, arithmetic and copies ran while one was open for 4% of the time, Pallas kernels for 2%

profile of v4, /device:TPU:0, one launch (start us, length us, event | category | flops | bytes accessed | tf_op | source)
XLA Modules:
  0.0 282.3 jit_solution(16076121619069445269)
XLA Ops:
  0.6 2.2 convert_element_type.215.rest_0_
  2.9 3.0 %collective-permute-start.5 = (bf16[14,256,256]{2,1,0:T(8,128)(2,1)S(1)}, bf16[14,256,256]{2,1,0:T(8,128)(2,1)}, u32[]{:S(2)}, u32[]{:S(2)}) collective-permute-start(bf16[14,256,256]{2,1,0:T(8,128)(2,1)S(1)} %convert_element_type.215.rest_0_), channel_id=1, source_target_pairs={{0,16},{4,12},{8,24},{12,4},{16,0},{20,28},{24,8},{28,20},{1,17},{... | collective-permute-start | bytes 5505032 | tf_op jit(solution)/shard_map/ppermute | solution.py:654
  6.1 1.6 collective-permute-start.2
  8.2 21.3 %collective-permute-done.2.rest_3_ = bf16[7,256,256]{2,1,0:T(8,128)(2,1)S(1)} collective-permute-done((bf16[7,256,256]{2,1,0:T(8,128)(2,1)S(1)}, bf16[7,256,256]{2,1,0:T(8,128)(2,1)S(1)}, u32[]{:S(2)}, u32[]{:S(2)}) %collective-permute-start.2) | collective-permute-done | bytes 917536 | tf_op jit(solution)/shard_map/ppermute | solution.py:653
  29.4 19.8 %collective-permute-done.1.rest_2_ = bf16[7,256,256]{2,1,0:T(8,128)(2,1)} collective-permute-done((bf16[7,256,256]{2,1,0:T(8,128)(2,1)S(1)}, bf16[7,256,256]{2,1,0:T(8,128)(2,1)}, u32[]{:S(2)}, u32[]{:S(2)}) %collective-permute-start.1) | collective-permute-done | bytes 917536 | tf_op jit(solution)/shard_map/ppermute | solution.py:652
  49.7 7.0 %collective-permute-done.8.rest_9_ = bf16[7,256,256]{2,1,0:T(8,128)(2,1)} collective-permute-done((bf16[7,256,256]{2,1,0:T(8,128)(2,1)S(1)}, bf16[7,256,256]{2,1,0:T(8,128)(2,1)}, u32[]{:S(2)}, u32[]{:S(2)}) %collective-permute-start.8) | collective-permute-done | bytes 917536 | tf_op jit(solution)/shard_map/ppermute | solution.py:656
  57.3 9.3 %collective-permute-done.7.rest_8_ = bf16[7,256,256]{2,1,0:T(8,128)(2,1)} collective-permute-done((bf16[7,256,256]{2,1,0:T(8,128)(2,1)}, bf16[7,256,256]{2,1,0:T(8,128)(2,1)}, u32[]{:S(2)}, u32[]{:S(2)}) %collective-permute-start.7) | collective-permute-done | bytes 917536 | tf_op jit(solution)/shard_map/ppermute | solution.py:655
  66.6 0.8 copy.30
  69.4 61.2 %layer.1 = (bf16[512,768]{1,0:T(8,128)(2,1)}, bf16[512,768]{1,0:T(8,128)(2,1)}, f32[2,768]{1,0:T(2,128)}, bf16[16,256,256]{2,1,0:T(8,128)(2,1)}, bf16[16,256,256...) custom-call(s32[108]{0:T(128)} %index_ref.1, s32[8]{0:T(128)} %select_reduce_fusion.base_ref, ...), custom_call_target="tpu_custom_call" | custom-call | flops 23000000512 | bytes 32000000 | tf_op jit(solution)/shard_map/layer/pallas_call | solution.py:462
  130.8 4.3 %collective-permute-done.11 = bf16[16,256,256]{2,1,0:T(8,128)(2,1)S(1)} collective-permute-done((bf16[16,256,256]{2,1,0:T(8,128)(2,1)}, bf16[16,256,256]{2,1,0:T(8,128)(2,1)S(1)}, u32[]{:S(2)}, u32[]{:S(2)}) %collective-permute-start.11) | collective-permute-done | bytes 2097184 | tf_op jit(solution)/shard_map/ppermute | solution.py:628
  135.1 1.5 add_convert_fusion.1
  136.8 1.1 collective-permute-start.14
  137.9 7.6 %collective-permute-done.12 = bf16[40,256,256]{2,1,0:T(8,128)(2,1)S(1)} collective-permute-done((bf16[40,256,256]{2,1,0:T(8,128)(2,1)}, bf16[40,256,256]{2,1,0:T(8,128)(2,1)S(1)}, u32[]{:S(2)}, u32[]{:S(2)}) %collective-permute-start.12) | collective-permute-done | bytes 5242912 | tf_op jit(solution)/shard_map/ppermute | solution.py:628
  145.6 2.7 add_convert_fusion
  148.3 1.2 collective-permute-start.13
  149.4 1.7 collective-permute-start.15
  151.1 2.1 collective-permute-done.15
  153.5 1.8 collective-permute-start.16
  155.2 13.2 %collective-permute-done.16 = bf16[1024,256]{1,0:T(8,128)(2,1)S(1)} collective-permute-done((bf16[1024,256]{1,0:T(8,128)(2,1)S(1)}, bf16[1024,256]{1,0:T(8,128)(2,1)S(1)}, u32[]{:S(2)}, u32[]{:S(2)}) %collective-permute-start.16) | collective-permute-done | bytes 524320 | tf_op jit(solution)/shard_map/ppermute | solution.py:779
  168.7 3.7 %collective-permute-start.17 = (bf16[1024,256]{1,0:T(8,128)(2,1)S(1)}, bf16[1024,256]{1,0:T(8,128)(2,1)S(1)}, u32[]{:S(2)}, u32[]{:S(2)}) collective-permute-start(bf16[1024,256]{1,0:T(8,128)(2,1)S(1)} %fusion.5), channel_id=1, source_target_pairs={{0,1},{3,2},{4,5},{7,6},{8,9},{11,10},{12,13},{15,14},{16,17},{19,... | collective-permute-start | bytes 1572872 | tf_op jit(solution)/shard_map/ppermute | solution.py:804
  172.5 10.2 %collective-permute-done.17 = bf16[1024,256]{1,0:T(8,128)(2,1)S(1)} collective-permute-done((bf16[1024,256]{1,0:T(8,128)(2,1)S(1)}, bf16[1024,256]{1,0:T(8,128)(2,1)S(1)}, u32[]{:S(2)}, u32[]{:S(2)}) %collective-permute-start.17) | collective-permute-done | bytes 524320 | tf_op jit(solution)/shard_map/ppermute | solution.py:804
  182.8 0.7 collective-permute-start.19
  183.5 2.2 collective-permute-done.13
  186.1 2.2 collective-permute-start.18
  188.7 9.5 %collective-permute-done.18 = bf16[1536,256]{1,0:T(8,128)(2,1)S(1)} collective-permute-done((bf16[1536,256]{1,0:T(8,128)(2,1)S(1)}, bf16[1536,256]{1,0:T(8,128)(2,1)S(1)}, u32[]{:S(2)}, u32[]{:S(2)}) %collective-permute-start.18) | collective-permute-done | bytes 786464 | tf_op jit(solution)/shard_map/ppermute | solution.py:779
  198.7 5.0 %collective-permute-start.20 = (bf16[1536,256]{1,0:T(8,128)(2,1)S(1)}, bf16[1536,256]{1,0:T(8,128)(2,1)S(1)}, u32[]{:S(2)}, u32[]{:S(2)}) collective-permute-start(bf16[1536,256]{1,0:T(8,128)(2,1)S(1)} %fusion.1), channel_id=1, source_target_pairs={{0,1},{3,2},{4,5},{7,6},{8,9},{11,10},{12,13},{15,14},{16,17},{19,... | collective-permute-start | bytes 2359304 | tf_op jit(solution)/shard_map/ppermute | solution.py:804
  203.7 0.7 collective-permute-start.21
  204.4 1.3 collective-permute-start.26
  206.0 1.4 collective-permute-done.21
  207.4 10.6 %collective-permute-done.20 = bf16[1536,256]{1,0:T(8,128)(2,1)S(1)} collective-permute-done((bf16[1536,256]{1,0:T(8,128)(2,1)S(1)}, bf16[1536,256]{1,0:T(8,128)(2,1)S(1)}, u32[]{:S(2)}, u32[]{:S(2)}) %collective-permute-start.20) | collective-permute-done | bytes 786464 | tf_op jit(solution)/shard_map/ppermute | solution.py:804
  218.2 0.7 collective-permute-start.23
  219.0 7.2 %collective-permute-start.24 = (bf16[512,256]{1,0:T(8,128)(2,1)S(1)}, bf16[512,256]{1,0:T(8,128)(2,1)S(1)}, u32[]{:S(2)}, u32[]{:S(2)}) collective-permute-start(bf16[512,256]{1,0:T(8,128)(2,1)S(1)} %get-tuple-element.172), channel_id=1, source_target_pairs={{0,1},{3,2},{4,5},{7,6},{8,9},{11,10},{12,13},{15,14},{16,17},{19,... | collective-permute-start | bytes 786440 | tf_op jit(solution)/shard_map/ppermute | solution.py:804
  226.2 1.3 collective-permute-start.29
  227.5 0.9 broadcast_select_fusion.1.rest_0_
  228.4 4.4 %collective-permute-done.24 = bf16[512,256]{1,0:T(8,128)(2,1)S(1)} collective-permute-done((bf16[512,256]{1,0:T(8,128)(2,1)S(1)}, bf16[512,256]{1,0:T(8,128)(2,1)S(1)}, u32[]{:S(2)}, u32[]{:S(2)}) %collective-permute-start.24) | collective-permute-done | bytes 262176 | tf_op jit(solution)/shard_map/ppermute | solution.py:804
  233.0 1.3 collective-permute-start.27
  234.3 6.6 %collective-permute-start.31 = (f32[2,768]{1,0:T(2,128)S(1)}, f32[2,768]{1,0:T(2,128)S(1)}, u32[]{:S(2)}, u32[]{:S(2)}) collective-permute-start(f32[2,768]{1,0:T(2,128)S(1)} %add.326), channel_id=1, source_target_pairs={{0,1},{1,0},{2,3},{3,2},{4,5},{5,4},{6,7},{7,6},{8,9},{9,8},{10,11... | collective-permute-start | bytes 18440 | tf_op jit(solution)/shard_map/ppermute | solution.py:843
  242.4 6.3 %adam.2 = (f32[14,256,256]{2,1,0:T(8,128)}, f32[14,256,256]{2,1,0:T(8,128)}, f32[14,256,256]{2,1,0:T(8,128)}, f32[14,256,256]{2,1,0:T(8,128)}, bf16[14,256,256]{2,1,0:T(8,128)(2,1)}) custom-call(f32[14,256,256]{2,1,0:T(8,128)} %weight_ref.3, f32[14,256,256]{2,1,0:T(8,128)} %first_ref.3, f32[14,256,256]{2,1,0:T(8,128)} %second_ref.3, ...), custom_call_target="tpu_custom_call" | custom-call | flops 805306368 | bytes 11010048 | tf_op jit(solution)/shard_map/adam/pallas_call | solution.py:579
  248.8 1.4 collective-permute-start.30
  250.3 8.2 %collective-permute-done.27 = bf16[1536,256]{1,0:T(8,128)(2,1)S(1)} collective-permute-done((bf16[1536,256]{1,0:T(8,128)(2,1)S(1)}, bf16[1536,256]{1,0:T(8,128)(2,1)S(1)}, u32[]{:S(2)}, u32[]{:S(2)}) %collective-permute-start.27) | collective-permute-done | bytes 786464 | tf_op jit(solution)/shard_map/ppermute | solution.py:817
  258.4 1.0 broadcast_select_fusion.rest_0_
  259.5 1.1 collective-permute-start.34
  260.6 1.3 collective-permute-start.33
  261.9 1.7 collective-permute-done.30
  263.6 0.7 broadcast_select_fusion.3.rest_1_
  265.0 3.9 %collective-permute-done.33 = bf16[512,256]{1,0:T(8,128)(2,1)S(1)} collective-permute-done((bf16[512,256]{1,0:T(8,128)(2,1)S(1)}, bf16[512,256]{1,0:T(8,128)(2,1)S(1)}, u32[]{:S(2)}, u32[]{:S(2)}) %collective-permute-start.33) | collective-permute-done | bytes 262176 | tf_op jit(solution)/shard_map/ppermute | solution.py:817
  268.9 0.8 broadcast_select_fusion.2.rest_2_
  269.6 12.6 %adam.3 = (f32[14,256,256]{2,1,0:T(8,128)}, f32[14,256,256]{2,1,0:T(8,128)}, f32[14,256,256]{2,1,0:T(8,128)}, f32[14,256,256]{2,1,0:T(8,128)}, bf16[14,256,256]{2,1,0:T(8,128)(2,1)}) custom-call(f32[14,256,256]{2,1,0:T(8,128)} %weight_ref.3, ...), custom_call_target="tpu_custom_call", output_to_operand_aliasing={{0}: (8, {}), {1}: (9, {}), {2}: (10, {}), {3}: (11, {}), {... | custom-call | flops 2013265920 | bytes 27525120 | tf_op jit(solution)/shard_map/adam/pallas_call | solution.py:579
  (92 shorter events, 9.1 us)
Async XLA Ops:
  2.9 66.5 %copy-start = (bf16[14,256,256]{2,1,0:T(8,128)(2,1)}, bf16[14,256,256]{2,1,0:T(8,128)(2,1)S(1)}, u32[]{:S(2)}) copy-start(bf16[14,256,256]{2,1,0:T(8,128)(2,1)S(1)} %convert_element_type.215.rest_0_) | copy-start | bytes 5505028
  2.9 63.7 %copy-start.6 = (s32[2,256]{1,0:T(2,128)S(1)}, s32[2,256]{1,0:T(2,128)}, u32[]{:S(2)}) copy-start(s32[2,256]{1,0:T(2,128)} %segments_ref.1) | copy-start | bytes 6148
  2.9 46.3 %collective-permute-start.5 = (bf16[14,256,256]{2,1,0:T(8,128)(2,1)S(1)}, bf16[14,256,256]{2,1,0:T(8,128)(2,1)}, u32[]{:S(2)}, u32[]{:S(2)}) collective-permute-start(bf16[14,256,256]{2,1,0:T(8,128)(2,1)S(1)} %convert_element_type.215.rest_0_), channel_id=1, source_target_pairs={{0,16},{4,12},{8,24},{12,4},{16,0},{20,28},{24,8},{28,20},{1,17},{... | collective-permute-start | bytes 5505032 | tf_op jit(solution)/shard_map/ppermute | solution.py:654
  6.1 23.4 %collective-permute-start.2 = (bf16[7,256,256]{2,1,0:T(8,128)(2,1)S(1)}, bf16[7,256,256]{2,1,0:T(8,128)(2,1)S(1)}, u32[]{:S(2)}, u32[]{:S(2)}) collective-permute-start(bf16[7,256,256]{2,1,0:T(8,128)(2,1)S(1)} %get-tuple-element.222), channel_id=1, source_target_pairs={{0,8},{4,20},{8,0},{12,28},{16,24},{20,4},{24,16},{28,12},{1,9},{5... | collective-permute-start | bytes 2752520 | tf_op jit(solution)/shard_map/ppermute | solution.py:653
  7.6 41.5 %collective-permute-start.1 = (bf16[7,256,256]{2,1,0:T(8,128)(2,1)S(1)}, bf16[7,256,256]{2,1,0:T(8,128)(2,1)}, u32[]{:S(2)}, u32[]{:S(2)}) collective-permute-start(bf16[7,256,256]{2,1,0:T(8,128)(2,1)S(1)} %get-tuple-element.223), channel_id=1, source_target_pairs={{0,8},{4,20},{8,0},{12,28},{16,24},{20,4},{24,16},{28,12},{1,9},{5... | collective-permute-start | bytes 2752520 | tf_op jit(solution)/shard_map/ppermute | solution.py:652
  29.4 40.0 %copy-start.7 = (bf16[7,256,256]{2,1,0:T(8,128)(2,1)}, bf16[7,256,256]{2,1,0:T(8,128)(2,1)S(1)}, u32[]{:S(2)}) copy-start(bf16[7,256,256]{2,1,0:T(8,128)(2,1)S(1)} %collective-permute-done.2.rest_3_) | copy-start | bytes 2752516
  29.4 27.3 %collective-permute-start.8 = (bf16[7,256,256]{2,1,0:T(8,128)(2,1)S(1)}, bf16[7,256,256]{2,1,0:T(8,128)(2,1)}, u32[]{:S(2)}, u32[]{:S(2)}) collective-permute-start(bf16[7,256,256]{2,1,0:T(8,128)(2,1)S(1)} %collective-permute-done.2.rest_3_), channel_id=1, source_target_pairs={{0,16},{4,12},{8,24},{12,4},{16,0},{20,28},{24,8},{28,20},{1,17},{... | collective-permute-start | bytes 2752520 | tf_op jit(solution)/shard_map/ppermute | solution.py:656
  29.4 27.3 %collective-permute-start.4 = (bf16[7,256,256]{2,1,0:T(8,128)(2,1)S(1)}, bf16[7,256,256]{2,1,0:T(8,128)(2,1)}, u32[]{:S(2)}, u32[]{:S(2)}) collective-permute-start(bf16[7,256,256]{2,1,0:T(8,128)(2,1)S(1)} %collective-permute-done.2.rest_3_), channel_id=1, source_target_pairs={{0,4},{4,0},{8,12},{12,8},{16,20},{20,16},{24,28},{28,24},{1,5},{5... | collective-permute-start | bytes 2752520 | tf_op jit(solution)/shard_map/ppermute | solution.py:628
  49.2 17.4 %collective-permute-start.7 = (bf16[7,256,256]{2,1,0:T(8,128)(2,1)}, bf16[7,256,256]{2,1,0:T(8,128)(2,1)}, u32[]{:S(2)}, u32[]{:S(2)}) collective-permute-start(bf16[7,256,256]{2,1,0:T(8,128)(2,1)} %collective-permute-done.1.rest_2_), channel_id=1, source_target_pairs={{0,16},{4,12},{8,24},{12,4},{16,0},{20,28},{24,8},{28,20},{1,17},{... | collective-permute-start | bytes 2752520 | tf_op jit(solution)/shard_map/ppermute | solution.py:655
  49.2 19.6 %collective-permute-start = (bf16[14,256,256]{2,1,0:T(8,128)(2,1)S(1)}, bf16[14,256,256]{2,1,0:T(8,128)(2,1)}, u32[]{:S(2)}, u32[]{:S(2)}) collective-permute-start(bf16[14,256,256]{2,1,0:T(8,128)(2,1)S(1)} %convert_element_type.215.rest_0_), channel_id=1, source_target_pairs={{0,4},{4,0},{8,12},{12,8},{16,20},{20,16},{24,28},{28,24},{1,5},{5... | collective-permute-start | bytes 5505032 | tf_op jit(solution)/shard_map/ppermute | solution.py:628
  49.2 20.2 %collective-permute-start.6 = (bf16[14,256,256]{2,1,0:T(8,128)(2,1)}, bf16[14,256,256]{2,1,0:T(8,128)(2,1)}, u32[]{:S(2)}, u32[]{:S(2)}) collective-permute-start(bf16[14,256,256]{2,1,0:T(8,128)(2,1)} %collective-permute-done.5.rest_6_), channel_id=1, source_target_pairs={{0,4},{4,0},{8,12},{12,8},{16,20},{20,16},{24,28},{28,24},{1,5},{5... | collective-permute-start | bytes 5505032 | tf_op jit(solution)/shard_map/ppermute | solution.py:628
  56.8 12.0 %collective-permute-start.3 = (bf16[7,256,256]{2,1,0:T(8,128)(2,1)}, bf16[7,256,256]{2,1,0:T(8,128)(2,1)}, u32[]{:S(2)}, u32[]{:S(2)}) collective-permute-start(bf16[7,256,256]{2,1,0:T(8,128)(2,1)} %collective-permute-done.1.rest_2_), channel_id=1, source_target_pairs={{0,4},{4,0},{8,12},{12,8},{16,20},{20,16},{24,28},{28,24},{1,5},{5... | collective-permute-start | bytes 2752520 | tf_op jit(solution)/shard_map/ppermute | solution.py:628
  56.8 12.0 %collective-permute-start.10 = (bf16[7,256,256]{2,1,0:T(8,128)(2,1)}, bf16[7,256,256]{2,1,0:T(8,128)(2,1)}, u32[]{:S(2)}, u32[]{:S(2)}) collective-permute-start(bf16[7,256,256]{2,1,0:T(8,128)(2,1)} %collective-permute-done.8.rest_9_), channel_id=1, source_target_pairs={{0,4},{4,0},{8,12},{12,8},{16,20},{20,16},{24,28},{28,24},{1,5},{5... | collective-permute-start | bytes 2752520 | tf_op jit(solution)/shard_map/ppermute | solution.py:628
  66.6 2.8 collective-permute-start.9
  130.6 4.4 %collective-permute-start.11 = (bf16[16,256,256]{2,1,0:T(8,128)(2,1)}, bf16[16,256,256]{2,1,0:T(8,128)(2,1)S(1)}, u32[]{:S(2)}, u32[]{:S(2)}) collective-permute-start(bf16[16,256,256]{2,1,0:T(8,128)(2,1)} %get-tuple-element.118), channel_id=1, source_target_pairs={{0,4},{4,0},{8,12},{12,8},{16,20},{20,16},{24,28},{28,24},{1,5},{5... | collective-permute-start | bytes 6291464 | tf_op jit(solution)/shard_map/ppermute | solution.py:628
  136.6 12.8 %copy-start.5 = (f32[2,768]{1,0:T(2,128)S(1)}, f32[2,768]{1,0:T(2,128)}, u32[]{:S(2)}) copy-start(f32[2,768]{1,0:T(2,128)} %get-tuple-element.126) | copy-start | bytes 18436
  136.6 16.6 %copy-start.1 = (bf16[16,256,256]{2,1,0:T(8,128)(2,1)S(1)}, bf16[16,256,256]{2,1,0:T(8,128)(2,1)}, u32[]{:S(2)}) copy-start(bf16[16,256,256]{2,1,0:T(8,128)(2,1)} %get-tuple-element.132) | copy-start | bytes 6291460
  136.6 8.9 %collective-permute-start.12 = (bf16[40,256,256]{2,1,0:T(8,128)(2,1)}, bf16[40,256,256]{2,1,0:T(8,128)(2,1)S(1)}, u32[]{:S(2)}, u32[]{:S(2)}) collective-permute-start(bf16[40,256,256]{2,1,0:T(8,128)(2,1)} %get-tuple-element.121), channel_id=1, source_target_pairs={{0,4},{4,0},{8,12},{12,8},{16,20},{20,16},{24,28},{28,24},{1,5},{5... | collective-permute-start | bytes 15728648 | tf_op jit(solution)/shard_map/ppermute | solution.py:628
  136.8 16.4 %collective-permute-start.14 = (bf16[2048,256]{1,0:T(8,128)(2,1)S(1)}, bf16[2048,256]{1,0:T(8,128)(2,1)S(1)}, u32[]{:S(2)}, u32[]{:S(2)}) collective-permute-start(bf16[2048,256]{1,0:T(8,128)(2,1)S(1)} %bitcast.46), channel_id=1, source_target_pairs={{0,8},{4,20},{8,0},{12,28},{16,24},{20,4},{24,16},{28,12},{1,9},{5... | collective-permute-start | bytes 3145736 | tf_op jit(solution)/shard_map/ppermute | solution.py:762
  145.6 40.1 %slice-start = ((s8[5242880]{0:T(1024)(128)(4,1)}), s8[1048576]{0:T(1024)(128)(4,1)S(1)}, s32[]{:S(2)}) async-start(s8[5242880]{0:T(1024)(128)(4,1)} %bitcast.43), calls=%async_computation | async-start | bytes 2097152
  148.3 37.4 %collective-permute-start.13 = (bf16[5120,256]{1,0:T(8,128)(2,1)S(1)}, bf16[5120,256]{1,0:T(8,128)(2,1)S(1)}, u32[]{:S(2)}, u32[]{:S(2)}) collective-permute-start(bf16[5120,256]{1,0:T(8,128)(2,1)S(1)} %bitcast.45), channel_id=1, source_target_pairs={{0,8},{4,20},{8,0},{12,28},{16,24},{20,4},{24,16},{28,12},{1,9},{5... | collective-permute-start | bytes 7864328 | tf_op jit(solution)/shard_map/ppermute | solution.py:762
  149.4 3.8 %collective-permute-start.15 = (f32[2,768]{1,0:T(2,128)S(1)}, f32[2,768]{1,0:T(2,128)S(1)}, u32[]{:S(2)}, u32[]{:S(2)}) collective-permute-start(f32[2,768]{1,0:T(2,128)S(1)} %copy-done.5), channel_id=1, source_target_pairs={{0,16},{4,12},{8,24},{12,4},{16,0},{20,28},{24,8},{28,20},{1,17},{... | collective-permute-start | bytes 18440 | tf_op jit(solution)/shard_map/ppermute | solution.py:843
  153.2 32.5 %slice-start.1 = ((s8[5242880]{0:T(1024)(128)(4,1)}), s8[4194304]{0:T(1024)(128)(4,1)S(1)}, s32[]{:S(2)}) async-start(s8[5242880]{0:T(1024)(128)(4,1)} %bitcast.43), calls=%async_computation.1 | async-start | bytes 8388608
  153.5 14.9 %collective-permute-start.16 = (bf16[1024,256]{1,0:T(8,128)(2,1)S(1)}, bf16[1024,256]{1,0:T(8,128)(2,1)S(1)}, u32[]{:S(2)}, u32[]{:S(2)}) collective-permute-start(bf16[1024,256]{1,0:T(8,128)(2,1)S(1)} %fusion.6), channel_id=1, source_target_pairs={{0,16},{4,12},{8,24},{12,4},{16,0},{20,28},{24,8},{28,20},{1,17},{... | collective-permute-start | bytes 1572872 | tf_op jit(solution)/shard_map/ppermute | solution.py:779
  168.7 13.9 %collective-permute-start.17 = (bf16[1024,256]{1,0:T(8,128)(2,1)S(1)}, bf16[1024,256]{1,0:T(8,128)(2,1)S(1)}, u32[]{:S(2)}, u32[]{:S(2)}) collective-permute-start(bf16[1024,256]{1,0:T(8,128)(2,1)S(1)} %fusion.5), channel_id=1, source_target_pairs={{0,1},{3,2},{4,5},{7,6},{8,9},{11,10},{12,13},{15,14},{16,17},{19,... | collective-permute-start | bytes 1572872 | tf_op jit(solution)/shard_map/ppermute | solution.py:804
  182.8 5.7 %collective-permute-start.19 = (bf16[1024,256]{1,0:T(8,128)(2,1)S(1)}, bf16[1024,256]{1,0:T(8,128)(2,1)S(1)}, u32[]{:S(2)}, u32[]{:S(2)}) collective-permute-start(bf16[1024,256]{1,0:T(8,128)(2,1)S(1)} %add_convert_fusion.5), channel_id=1, source_target_pairs={{1,2},{2,1},{5,6},{6,5},{9,10},{10,9},{13,14},{14,13},{17,18},{18,... | collective-permute-start | bytes 1572872 | tf_op jit(solution)/shard_map/ppermute | solution.py:812
  186.1 12.2 %collective-permute-start.18 = (bf16[1536,256]{1,0:T(8,128)(2,1)S(1)}, bf16[1536,256]{1,0:T(8,128)(2,1)S(1)}, u32[]{:S(2)}, u32[]{:S(2)}) collective-permute-start(bf16[1536,256]{1,0:T(8,128)(2,1)S(1)} %fusion.2), channel_id=1, source_target_pairs={{0,16},{4,12},{8,24},{12,4},{16,0},{20,28},{24,8},{28,20},{1,17},{... | collective-permute-start | bytes 2359304 | tf_op jit(solution)/shard_map/ppermute | solution.py:779
  188.5 17.2 %collective-permute-start.22 = (bf16[1024,256]{1,0:T(8,128)(2,1)S(1)}, bf16[1024,256]{1,0:T(8,128)(2,1)S(1)}, u32[]{:S(2)}, u32[]{:S(2)}) collective-permute-start(bf16[1024,256]{1,0:T(8,128)(2,1)S(1)} %fusion.3), channel_id=1, source_target_pairs={{0,16},{4,12},{8,24},{12,4},{16,0},{20,28},{24,8},{28,20},{1,17},{... | collective-permute-start | bytes 1572872 | tf_op jit(solution)/shard_map/ppermute | solution.py:779
  198.7 19.3 %collective-permute-start.20 = (bf16[1536,256]{1,0:T(8,128)(2,1)S(1)}, bf16[1536,256]{1,0:T(8,128)(2,1)S(1)}, u32[]{:S(2)}, u32[]{:S(2)}) collective-permute-start(bf16[1536,256]{1,0:T(8,128)(2,1)S(1)} %fusion.1), channel_id=1, source_target_pairs={{0,1},{3,2},{4,5},{7,6},{8,9},{11,10},{12,13},{15,14},{16,17},{19,... | collective-permute-start | bytes 2359304 | tf_op jit(solution)/shard_map/ppermute | solution.py:804
  203.7 3.7 %collective-permute-start.21 = (f32[2,768]{1,0:T(2,128)S(1)}, f32[2,768]{1,0:T(2,128)S(1)}, u32[]{:S(2)}, u32[]{:S(2)}) collective-permute-start(f32[2,768]{1,0:T(2,128)S(1)} %add.296), channel_id=1, source_target_pairs={{0,8},{4,20},{8,0},{12,28},{16,24},{20,4},{24,16},{28,12},{1,9},{5... | collective-permute-start | bytes 18440 | tf_op jit(solution)/shard_map/ppermute | solution.py:843
  204.4 23.1 %collective-permute-start.26 = (bf16[1024,256]{1,0:T(8,128)(2,1)S(1)}, bf16[1024,256]{1,0:T(8,128)(2,1)S(1)}, u32[]{:S(2)}, u32[]{:S(2)}) collective-permute-start(bf16[1024,256]{1,0:T(8,128)(2,1)S(1)} %add_convert_fusion.4), channel_id=1, source_target_pairs={{1,0},{2,3},{5,4},{6,7},{9,8},{10,11},{13,12},{14,15},{17,16},{18,... | collective-permute-start | bytes 1572872 | tf_op jit(solution)/shard_map/ppermute | solution.py:817
  218.2 14.7 %collective-permute-start.23 = (bf16[1536,256]{1,0:T(8,128)(2,1)S(1)}, bf16[1536,256]{1,0:T(8,128)(2,1)S(1)}, u32[]{:S(2)}, u32[]{:S(2)}) collective-permute-start(bf16[1536,256]{1,0:T(8,128)(2,1)S(1)} %add_convert_fusion.3), channel_id=1, source_target_pairs={{1,2},{2,1},{5,6},{6,5},{9,10},{10,9},{13,14},{14,13},{17,18},{18,... | collective-permute-start | bytes 2359304 | tf_op jit(solution)/shard_map/ppermute | solution.py:812
  218.9 9.5 %collective-permute-start.25 = (f32[2,768]{1,0:T(2,128)S(1)}, f32[2,768]{1,0:T(2,128)S(1)}, u32[]{:S(2)}, u32[]{:S(2)}) collective-permute-start(f32[2,768]{1,0:T(2,128)S(1)} %add.320), channel_id=1, source_target_pairs={{0,4},{4,0},{8,12},{12,8},{16,20},{20,16},{24,28},{28,24},{1,5},{5... | collective-permute-start | bytes 18440 | tf_op jit(solution)/shard_map/ppermute | solution.py:843
  219.0 13.8 %collective-permute-start.24 = (bf16[512,256]{1,0:T(8,128)(2,1)S(1)}, bf16[512,256]{1,0:T(8,128)(2,1)S(1)}, u32[]{:S(2)}, u32[]{:S(2)}) collective-permute-start(bf16[512,256]{1,0:T(8,128)(2,1)S(1)} %get-tuple-element.172), channel_id=1, source_target_pairs={{0,1},{3,2},{4,5},{7,6},{8,9},{11,10},{12,13},{15,14},{16,17},{19,... | collective-permute-start | bytes 786440 | tf_op jit(solution)/shard_map/ppermute | solution.py:804
  226.2 15.5 %collective-permute-start.29 = (bf16[512,256]{1,0:T(8,128)(2,1)S(1)}, bf16[512,256]{1,0:T(8,128)(2,1)S(1)}, u32[]{:S(2)}, u32[]{:S(2)}) collective-permute-start(bf16[512,256]{1,0:T(8,128)(2,1)S(1)} %get-tuple-element.179), channel_id=1, source_target_pairs={{0,1},{3,2},{4,5},{7,6},{8,9},{11,10},{12,13},{15,14},{16,17},{19,... | collective-permute-start | bytes 786440 | tf_op jit(solution)/shard_map/ppermute | solution.py:804
  233.0 25.4 %collective-permute-start.27 = (bf16[1536,256]{1,0:T(8,128)(2,1)S(1)}, bf16[1536,256]{1,0:T(8,128)(2,1)S(1)}, u32[]{:S(2)}, u32[]{:S(2)}) collective-permute-start(bf16[1536,256]{1,0:T(8,128)(2,1)S(1)} %add_convert_fusion.2), channel_id=1, source_target_pairs={{1,0},{2,3},{5,4},{6,7},{9,8},{10,11},{13,12},{14,15},{17,16},{18,... | collective-permute-start | bytes 2359304 | tf_op jit(solution)/shard_map/ppermute | solution.py:817
  234.3 25.2 %collective-permute-start.31 = (f32[2,768]{1,0:T(2,128)S(1)}, f32[2,768]{1,0:T(2,128)S(1)}, u32[]{:S(2)}, u32[]{:S(2)}) collective-permute-start(f32[2,768]{1,0:T(2,128)S(1)} %add.326), channel_id=1, source_target_pairs={{0,1},{1,0},{2,3},{3,2},{4,5},{5,4},{6,7},{7,6},{8,9},{9,8},{10,11... | collective-permute-start | bytes 18440 | tf_op jit(solution)/shard_map/ppermute | solution.py:843
  241.0 7.8 %collective-permute-start.28 = (bf16[512,256]{1,0:T(8,128)(2,1)S(1)}, bf16[512,256]{1,0:T(8,128)(2,1)S(1)}, u32[]{:S(2)}, u32[]{:S(2)}) collective-permute-start(bf16[512,256]{1,0:T(8,128)(2,1)S(1)} %add_convert_fusion.9), channel_id=1, source_target_pairs={{1,2},{2,1},{5,6},{6,5},{9,10},{10,9},{13,14},{14,13},{17,18},{18,... | collective-permute-start | bytes 786440 | tf_op jit(solution)/shard_map/ppermute | solution.py:812
  241.7 17.7 %collective-permute-start.32 = (bf16[512,256]{1,0:T(8,128)(2,1)S(1)}, bf16[512,256]{1,0:T(8,128)(2,1)S(1)}, u32[]{:S(2)}, u32[]{:S(2)}) collective-permute-start(bf16[512,256]{1,0:T(8,128)(2,1)S(1)} %add_convert_fusion.8), channel_id=1, source_target_pairs={{1,2},{2,1},{5,6},{6,5},{9,10},{10,9},{13,14},{14,13},{17,18},{18,... | collective-permute-start | bytes 786440 | tf_op jit(solution)/shard_map/ppermute | solution.py:812
  248.8 15.5 %copy-start.2 = (f32[2,768]{1,0:T(2,128)S(1)}, f32[2,768]{1,0:T(2,128)}, u32[]{:S(2)}) copy-start(f32[2,768]{1,0:T(2,128)} %gains_ref.1) | copy-start | bytes 18436
  248.8 15.5 %copy-start.3 = (f32[2,768]{1,0:T(2,128)S(1)}, f32[2,768]{1,0:T(2,128)}, u32[]{:S(2)}) copy-start(f32[2,768]{1,0:T(2,128)} %param.25) | copy-start | bytes 18436
  248.8 15.5 %copy-start.4 = (f32[2,768]{1,0:T(2,128)S(1)}, f32[2,768]{1,0:T(2,128)}, u32[]{:S(2)}) copy-start(f32[2,768]{1,0:T(2,128)} %param.24) | copy-start | bytes 18436
  248.8 14.8 %collective-permute-start.30 = (bf16[512,256]{1,0:T(8,128)(2,1)S(1)}, bf16[512,256]{1,0:T(8,128)(2,1)S(1)}, u32[]{:S(2)}, u32[]{:S(2)}) collective-permute-start(bf16[512,256]{1,0:T(8,128)(2,1)S(1)} %add_convert_fusion.7), channel_id=1, source_target_pairs={{1,0},{2,3},{5,4},{6,7},{9,8},{10,11},{13,12},{14,15},{17,16},{18,... | collective-permute-start | bytes 786440 | tf_op jit(solution)/shard_map/ppermute | solution.py:817
  259.5 4.8 %collective-permute-start.34 = (f32[2,768]{1,0:T(2,128)S(1)}, f32[2,768]{1,0:T(2,128)S(1)}, u32[]{:S(2)}, u32[]{:S(2)}) collective-permute-start(f32[2,768]{1,0:T(2,128)S(1)} %add.332), channel_id=1, source_target_pairs={{0,2},{1,3},{2,0},{3,1},{4,6},{5,7},{6,4},{7,5},{8,10},{9,11},{10,... | collective-permute-start | bytes 18440 | tf_op jit(solution)/shard_map/ppermute | solution.py:843
  260.6 8.3 %collective-permute-start.33 = (bf16[512,256]{1,0:T(8,128)(2,1)S(1)}, bf16[512,256]{1,0:T(8,128)(2,1)S(1)}, u32[]{:S(2)}, u32[]{:S(2)}) collective-permute-start(bf16[512,256]{1,0:T(8,128)(2,1)S(1)} %add_convert_fusion.6), channel_id=1, source_target_pairs={{1,0},{2,3},{5,4},{6,7},{9,8},{10,11},{13,12},{14,15},{17,16},{18,... | collective-permute-start | bytes 786440 | tf_op jit(solution)/shard_map/ppermute | solution.py:817

commit v5 on v4

--- a/solution.py
+++ b/solution.py
@@ -699,13 +699,13 @@
         return values
 
 
-GROUPS = (((4,),), ((6,), (2, 2)))
+GROUPS = (((4,),), ((6,), (4,)))
 ORDER = (
     "grads0 grads1 core0 gain_far near_sum0 near0 core1 near_sum1 near1 gain1 far_sum0_0 far0_0 plane_sum0_0 "
     "inward0_0a halfway0_0a middle0_0a far_sum1_0 far1_0 far_sum1_1 far1_1 gain_near whole0_0a outward0_0a "
-    "plane_sum1_0 inward1_0a plane_sum1_1 inward1_1a inward1_1b gain2 gain_core halfway1_0a middle1_0a "
-    "final0_0a gain3 gain_pair halfway1_1a middle1_1a whole1_0a outward1_0a halfway1_1b middle1_1b step0 "
-    "whole1_1a outward1_1a final1_0a whole1_1b outward1_1b gain4 gain_line final1_1a gain5 final1_1b step1"
+    "plane_sum1_0 inward1_0a plane_sum1_1 inward1_1a gain2 gain_core halfway1_0a middle1_0a final0_0a gain3 "
+    "gain_pair halfway1_1a middle1_1a whole1_0a outward1_0a step0_0 whole1_1a outward1_1a final1_0a gain4 "
+    "gain_line step1_0 gain5 final1_1a step1_1"
 ).split()
 
 
@@ -744,7 +744,6 @@
             return text + str(number)
 
         both = [name("grads"), name("core")]
-        finals = []
 
         def chip(pair, arrived, first, last):
             return flat(pair[1][first:last]), flat(arrived[first:last])
@@ -764,6 +763,7 @@
         inside = 0
         for member, parts in enumerate(sets):
             size = sum(parts)
+            finals = []
 
             def at(text, number=number, member=member):
                 return "%s%d_%d" % (text, number, member)
@@ -823,13 +823,13 @@
                 finals.append(of("final"))
             inside += size
 
-        def step(*grads, start=start):
-            nonlocal done
-            done = adam_blocks(grads, start, state, done)
-            return done
-
-        plan.core(name("step"), finals, step)
-        start += total
+            def step(*grads, start=start):
+                nonlocal done
+                done = adam_blocks(grads, start, state, done)
+                return done
+
+            plan.core(at("step"), finals, step)
+            start += size
 
     old = None
     line = [[(i, i ^ bit) for i in range(4)] for bit in (1, 2)]

time: 283 us -> 280 us (0.989)
  waiting for transfers between devices: 137 us -> 130 us
    ppermute x5, starting transfers between devices: 10.2 us -> 18.5 us  [reduce_and_step(): lax.ppermute(gain, axis, pairs)]
    ppermute x4 -> x3, waiting for transfers between devices: 13.8 us -> 7.15 us  [reduce_and_step(): lax.ppermute(t, 'rep', [(1, 0), (2, 3)])]
    ppermute x4 -> x3, starting transfers between devices: 17.2 us -> 12.9 us  [reduce_and_step(): lax.ppermute(t[part], 'rep', [(0, 1), (3, 2)])]
    pallas_call x2 -> x3, Pallas kernels: 18.9 us -> 21.1 us  [adam_blocks(): pl.pallas_call(functools.partial(adam_kernel, steps), grid=(sum(steps),),...]
    ppermute x4 -> x3, waiting for transfers between devices: 25.1 us -> 24.9 us  [reduce_and_step(): lax.ppermute(t[part], 'rep', [(0, 1), (3, 2)])]
    convert_element_type x16 -> x14, other arithmetic: 6.28 us -> 6.31 us  [add_low(): return sum((term.astype(F32) for term in terms)).astype(BF16)]
  transfers between devices with their start and end apart: 35 -> 32, of which waited for: 18 -> 16; matrix products, arithmetic and copies ran while one was open for 4% -> 4% of each run, Pallas kernels for 2% -> 5%
where the time goes in v5:
time: 280 us
  waiting for transfers between devices  130 us (46%)
  Pallas kernels  82.3 us (29%)
  starting transfers between devices  50.1 us (18%)
  other arithmetic  14.4 us (5%)
    pallas_call x1, Pallas kernels, run_layer(): pl.pallas_call(functools.partial(layer_kernel, micro, own, [p.shape[0] fo...  61.2 us
    ppermute x3, waiting for transfers between devices, reduce_and_step(): lax.ppermute(t[part], 'rep', [(0, 1), (3, 2)])  24.9 us
    ppermute x3, waiting for transfers between devices, reduce_and_step(): lax.ppermute(t, 'fsdp', far_pairs)  22.6 us
    ppermute x1, waiting for transfers between devices, gather_pieces(): last_near = lax.ppermute(weights[half:].astype(BF16), 'fsdp', near_pairs)  21.3 us
    pallas_call x3, Pallas kernels, adam_blocks(): pl.pallas_call(functools.partial(adam_kernel, steps), grid=(sum(steps),),...  21.1 us
    ppermute x1, waiting for transfers between devices, gather_pieces(): first_near = lax.ppermute(weights[:half].astype(BF16), 'fsdp', near_pairs)  19.8 us
    ppermute x5, starting transfers between devices, reduce_and_step(): lax.ppermute(gain, axis, pairs)  18.5 us
    ppermute x3, starting transfers between devices, reduce_and_step(): lax.ppermute(t[part], 'rep', [(0, 1), (3, 2)])  12.9 us
  transfers between devices with their start and end apart: 32, of which 16 were waited for; matrix products, arithmetic and copies ran while one was open for 4% of the time, Pallas kernels for 5%

profile of v5, /device:TPU:0, one launch (start us, length us, event | category | flops | bytes accessed | tf_op | source)
XLA Modules:
  0.0 279.6 jit_solution(15576279420462658665)
XLA Ops:
  0.6 2.2 convert_element_type.180.rest_0_
  2.9 3.0 %collective-permute-start.5 = (bf16[14,256,256]{2,1,0:T(8,128)(2,1)S(1)}, bf16[14,256,256]{2,1,0:T(8,128)(2,1)}, u32[]{:S(2)}, u32[]{:S(2)}) collective-permute-start(bf16[14,256,256]{2,1,0:T(8,128)(2,1)S(1)} %convert_element_type.180.rest_0_), channel_id=1, source_target_pairs={{0,16},{4,12},{8,24},{12,4},{16,0},{20,28},{24,8},{28,20},{1,17},{... | collective-permute-start | bytes 5505032 | tf_op jit(solution)/shard_map/ppermute | solution.py:654
  6.1 1.6 collective-permute-start.2
  8.2 21.3 %collective-permute-done.2.rest_3_ = bf16[7,256,256]{2,1,0:T(8,128)(2,1)S(1)} collective-permute-done((bf16[7,256,256]{2,1,0:T(8,128)(2,1)S(1)}, bf16[7,256,256]{2,1,0:T(8,128)(2,1)S(1)}, u32[]{:S(2)}, u32[]{:S(2)}) %collective-permute-start.2) | collective-permute-done | bytes 917536 | tf_op jit(solution)/shard_map/ppermute | solution.py:653
  29.4 19.8 %collective-permute-done.1.rest_2_ = bf16[7,256,256]{2,1,0:T(8,128)(2,1)} collective-permute-done((bf16[7,256,256]{2,1,0:T(8,128)(2,1)S(1)}, bf16[7,256,256]{2,1,0:T(8,128)(2,1)}, u32[]{:S(2)}, u32[]{:S(2)}) %collective-permute-start.1) | collective-permute-done | bytes 917536 | tf_op jit(solution)/shard_map/ppermute | solution.py:652
  49.7 7.0 %collective-permute-done.8.rest_9_ = bf16[7,256,256]{2,1,0:T(8,128)(2,1)} collective-permute-done((bf16[7,256,256]{2,1,0:T(8,128)(2,1)S(1)}, bf16[7,256,256]{2,1,0:T(8,128)(2,1)}, u32[]{:S(2)}, u32[]{:S(2)}) %collective-permute-start.8) | collective-permute-done | bytes 917536 | tf_op jit(solution)/shard_map/ppermute | solution.py:656
  57.3 9.3 %collective-permute-done.7.rest_8_ = bf16[7,256,256]{2,1,0:T(8,128)(2,1)} collective-permute-done((bf16[7,256,256]{2,1,0:T(8,128)(2,1)}, bf16[7,256,256]{2,1,0:T(8,128)(2,1)}, u32[]{:S(2)}, u32[]{:S(2)}) %collective-permute-start.7) | collective-permute-done | bytes 917536 | tf_op jit(solution)/shard_map/ppermute | solution.py:655
  66.6 0.8 copy.35
  67.5 0.6 concatenate.7.slot_ref
  68.2 0.6 select_reduce_fusion.base_ref
  69.4 61.2 %layer.1 = (bf16[512,768]{1,0:T(8,128)(2,1)}, bf16[512,768]{1,0:T(8,128)(2,1)}, f32[2,768]{1,0:T(2,128)}, bf16[16,256,256]{2,1,0:T(8,128)(2,1)}, bf16[16,256,256...) custom-call(s32[108]{0:T(128)} %index_ref.1, s32[8]{0:T(128)} %select_reduce_fusion.base_ref, ...), custom_call_target="tpu_custom_call" | custom-call | flops 23000000512 | bytes 32000000 | tf_op jit(solution)/shard_map/layer/pallas_call | solution.py:462
  130.8 4.2 %collective-permute-done.11 = bf16[16,256,256]{2,1,0:T(8,128)(2,1)S(1)} collective-permute-done((bf16[16,256,256]{2,1,0:T(8,128)(2,1)}, bf16[16,256,256]{2,1,0:T(8,128)(2,1)S(1)}, u32[]{:S(2)}, u32[]{:S(2)}) %collective-permute-start.11) | collective-permute-done | bytes 2097184 | tf_op jit(solution)/shard_map/ppermute | solution.py:628
  135.0 1.5 add_convert_fusion.1
  136.8 1.1 collective-permute-start.14
  137.9 7.6 %collective-permute-done.12 = bf16[40,256,256]{2,1,0:T(8,128)(2,1)S(1)} collective-permute-done((bf16[40,256,256]{2,1,0:T(8,128)(2,1)}, bf16[40,256,256]{2,1,0:T(8,128)(2,1)S(1)}, u32[]{:S(2)}, u32[]{:S(2)}) %collective-permute-start.12) | collective-permute-done | bytes 5242912 | tf_op jit(solution)/shard_map/ppermute | solution.py:628
  145.5 2.7 add_convert_fusion
  148.2 1.2 collective-permute-start.13
  149.4 1.7 collective-permute-start.15
  151.1 2.0 collective-permute-done.15
  153.4 1.8 collective-permute-start.16
  155.2 13.1 %collective-permute-done.16 = bf16[1024,256]{1,0:T(8,128)(2,1)S(1)} collective-permute-done((bf16[1024,256]{1,0:T(8,128)(2,1)S(1)}, bf16[1024,256]{1,0:T(8,128)(2,1)S(1)}, u32[]{:S(2)}, u32[]{:S(2)}) %collective-permute-start.16) | collective-permute-done | bytes 524320 | tf_op jit(solution)/shard_map/ppermute | solution.py:779
  168.7 3.7 %collective-permute-start.17 = (bf16[1024,256]{1,0:T(8,128)(2,1)S(1)}, bf16[1024,256]{1,0:T(8,128)(2,1)S(1)}, u32[]{:S(2)}, u32[]{:S(2)}) collective-permute-start(bf16[1024,256]{1,0:T(8,128)(2,1)S(1)} %fusion.7), channel_id=1, source_target_pairs={{0,1},{3,2},{4,5},{7,6},{8,9},{11,10},{12,13},{15,14},{16,17},{19,... | collective-permute-start | bytes 1572872 | tf_op jit(solution)/shard_map/ppermute | solution.py:804
  172.4 10.0 %collective-permute-done.17 = bf16[1024,256]{1,0:T(8,128)(2,1)S(1)} collective-permute-done((bf16[1024,256]{1,0:T(8,128)(2,1)S(1)}, bf16[1024,256]{1,0:T(8,128)(2,1)S(1)}, u32[]{:S(2)}, u32[]{:S(2)}) %collective-permute-start.17) | collective-permute-done | bytes 524320 | tf_op jit(solution)/shard_map/ppermute | solution.py:804
  182.6 0.7 collective-permute-start.20
  183.3 2.3 collective-permute-done.13
  186.0 2.0 collective-permute-start.19
  188.6 9.5 %collective-permute-done.19 = bf16[1536,256]{1,0:T(8,128)(2,1)S(1)} collective-permute-done((bf16[1536,256]{1,0:T(8,128)(2,1)S(1)}, bf16[1536,256]{1,0:T(8,128)(2,1)S(1)}, u32[]{:S(2)}, u32[]{:S(2)}) %collective-permute-start.19) | collective-permute-done | bytes 786464 | tf_op jit(solution)/shard_map/ppermute | solution.py:779
  198.6 5.0 %collective-permute-start.25 = (bf16[1536,256]{1,0:T(8,128)(2,1)S(1)}, bf16[1536,256]{1,0:T(8,128)(2,1)S(1)}, u32[]{:S(2)}, u32[]{:S(2)}) collective-permute-start(bf16[1536,256]{1,0:T(8,128)(2,1)S(1)} %fusion.1), channel_id=1, source_target_pairs={{0,1},{3,2},{4,5},{7,6},{8,9},{11,10},{12,13},{15,14},{16,17},{19,... | collective-permute-start | bytes 2359304 | tf_op jit(solution)/shard_map/ppermute | solution.py:804
  203.5 0.9 collective-permute-start.22
  204.4 1.3 collective-permute-start.24
  206.0 1.2 collective-permute-done.22
  207.2 4.2 %collective-permute-start.21 = (bf16[1024,256]{1,0:T(8,128)(2,1)S(1)}, bf16[1024,256]{1,0:T(8,128)(2,1)S(1)}, u32[]{:S(2)}, u32[]{:S(2)}) collective-permute-start(bf16[1024,256]{1,0:T(8,128)(2,1)S(1)} %fusion.4), channel_id=1, source_target_pairs={{0,1},{3,2},{4,5},{7,6},{8,9},{11,10},{12,13},{15,14},{16,17},{19,... | collective-permute-start | bytes 1572872 | tf_op jit(solution)/shard_map/ppermute | solution.py:804
  211.4 10.0 %collective-permute-done.25 = bf16[1536,256]{1,0:T(8,128)(2,1)S(1)} collective-permute-done((bf16[1536,256]{1,0:T(8,128)(2,1)S(1)}, bf16[1536,256]{1,0:T(8,128)(2,1)S(1)}, u32[]{:S(2)}, u32[]{:S(2)}) %collective-permute-start.25) | collective-permute-done | bytes 786464 | tf_op jit(solution)/shard_map/ppermute | solution.py:804
  221.7 0.7 collective-permute-start.27
  222.5 1.9 broadcast_select_fusion.2.rest_0_
  224.4 4.8 %collective-permute-done.21 = bf16[1024,256]{1,0:T(8,128)(2,1)S(1)} collective-permute-done((bf16[1024,256]{1,0:T(8,128)(2,1)S(1)}, bf16[1024,256]{1,0:T(8,128)(2,1)S(1)}, u32[]{:S(2)}, u32[]{:S(2)}) %collective-permute-start.21) | collective-permute-done | bytes 524320 | tf_op jit(solution)/shard_map/ppermute | solution.py:804
  229.3 0.7 collective-permute-start.26
  230.2 1.3 collective-permute-start.30
  231.5 15.0 %collective-permute-start.29 = (f32[2,768]{1,0:T(2,128)S(1)}, f32[2,768]{1,0:T(2,128)S(1)}, u32[]{:S(2)}, u32[]{:S(2)}) collective-permute-start(f32[2,768]{1,0:T(2,128)S(1)} %add.304), channel_id=1, source_target_pairs={{0,1},{1,0},{2,3},{3,2},{4,5},{5,4},{6,7},{7,6},{8,9},{9,8},{10,11... | collective-permute-start | bytes 18440 | tf_op jit(solution)/shard_map/ppermute | solution.py:843
  246.5 6.3 %adam.3 = (f32[14,256,256]{2,1,0:T(8,128)}, f32[14,256,256]{2,1,0:T(8,128)}, f32[14,256,256]{2,1,0:T(8,128)}, f32[14,256,256]{2,1,0:T(8,128)}, bf16[14,256,256]{2,1,0:T(8,128)(2,1)}) custom-call(f32[14,256,256]{2,1,0:T(8,128)} %weight_ref.5, f32[14,256,256]{2,1,0:T(8,128)} %first_ref.5, f32[14,256,256]{2,1,0:T(8,128)} %second_ref.5, ...), custom_call_target="tpu_custom_call" | custom-call | flops 805306368 | bytes 11010048 | tf_op jit(solution)/shard_map/adam/pallas_call | solution.py:579
  253.0 1.3 collective-permute-start.28
  254.3 7.1 %collective-permute-done.30 = bf16[1536,256]{1,0:T(8,128)(2,1)S(1)} collective-permute-done((bf16[1536,256]{1,0:T(8,128)(2,1)S(1)}, bf16[1536,256]{1,0:T(8,128)(2,1)S(1)}, u32[]{:S(2)}, u32[]{:S(2)}) %collective-permute-start.30) | collective-permute-done | bytes 786464 | tf_op jit(solution)/shard_map/ppermute | solution.py:817
  261.4 1.0 broadcast_select_fusion.rest_0_
  262.4 0.8 collective-permute-start.31
  263.2 8.5 %adam.4 = (f32[14,256,256]{2,1,0:T(8,128)}, f32[14,256,256]{2,1,0:T(8,128)}, f32[14,256,256]{2,1,0:T(8,128)}, f32[14,256,256]{2,1,0:T(8,128)}, bf16[14,256,256]{2,1,0:T(8,128)(2,1)}) custom-call(f32[14,256,256]{2,1,0:T(8,128)} %weight_ref.5, ...), custom_call_target="tpu_custom_call", output_to_operand_aliasing={{0}: (6, {}), {1}: (7, {}), {2}: (8, {}), {3}: (9, {}), {4}... | custom-call | flops 1207959552 | bytes 16515072 | tf_op jit(solution)/shard_map/adam/pallas_call | solution.py:579
  271.7 0.6 multiply_subtract_fusion
  272.4 0.9 broadcast_select_fusion.1.rest_0_
  273.2 6.3 %adam.5 = (f32[14,256,256]{2,1,0:T(8,128)}, f32[14,256,256]{2,1,0:T(8,128)}, f32[14,256,256]{2,1,0:T(8,128)}, f32[14,256,256]{2,1,0:T(8,128)}, bf16[14,256,256]{2,1,0:T(8,128)(2,1)}) custom-call(f32[14,256,256]{2,1,0:T(8,128)} %weight_ref.5, ...), custom_call_target="tpu_custom_call", output_to_operand_aliasing={{0}: (6, {}), {1}: (7, {}), {2}: (8, {}), {3}: (9, {}), {4}... | custom-call | flops 805306368 | bytes 11010048 | tf_op jit(solution)/shard_map/adam/pallas_call | solution.py:579
  (84 shorter events, 6.0 us)
Async XLA Ops:
  2.9 66.5 %copy-start = (bf16[14,256,256]{2,1,0:T(8,128)(2,1)}, bf16[14,256,256]{2,1,0:T(8,128)(2,1)S(1)}, u32[]{:S(2)}) copy-start(bf16[14,256,256]{2,1,0:T(8,128)(2,1)S(1)} %convert_element_type.180.rest_0_) | copy-start | bytes 5505028
  2.9 63.7 %copy-start.6 = (s32[2,256]{1,0:T(2,128)S(1)}, s32[2,256]{1,0:T(2,128)}, u32[]{:S(2)}) copy-start(s32[2,256]{1,0:T(2,128)} %segments_ref.1) | copy-start | bytes 6148
  2.9 46.3 %collective-permute-start.5 = (bf16[14,256,256]{2,1,0:T(8,128)(2,1)S(1)}, bf16[14,256,256]{2,1,0:T(8,128)(2,1)}, u32[]{:S(2)}, u32[]{:S(2)}) collective-permute-start(bf16[14,256,256]{2,1,0:T(8,128)(2,1)S(1)} %convert_element_type.180.rest_0_), channel_id=1, source_target_pairs={{0,16},{4,12},{8,24},{12,4},{16,0},{20,28},{24,8},{28,20},{1,17},{... | collective-permute-start | bytes 5505032 | tf_op jit(solution)/shard_map/ppermute | solution.py:654
  6.1 23.4 %collective-permute-start.2 = (bf16[7,256,256]{2,1,0:T(8,128)(2,1)S(1)}, bf16[7,256,256]{2,1,0:T(8,128)(2,1)S(1)}, u32[]{:S(2)}, u32[]{:S(2)}) collective-permute-start(bf16[7,256,256]{2,1,0:T(8,128)(2,1)S(1)} %get-tuple-element.206), channel_id=1, source_target_pairs={{0,8},{4,20},{8,0},{12,28},{16,24},{20,4},{24,16},{28,12},{1,9},{5... | collective-permute-start | bytes 2752520 | tf_op jit(solution)/shard_map/ppermute | solution.py:653
  7.6 41.5 %collective-permute-start.1 = (bf16[7,256,256]{2,1,0:T(8,128)(2,1)S(1)}, bf16[7,256,256]{2,1,0:T(8,128)(2,1)}, u32[]{:S(2)}, u32[]{:S(2)}) collective-permute-start(bf16[7,256,256]{2,1,0:T(8,128)(2,1)S(1)} %get-tuple-element.207), channel_id=1, source_target_pairs={{0,8},{4,20},{8,0},{12,28},{16,24},{20,4},{24,16},{28,12},{1,9},{5... | collective-permute-start | bytes 2752520 | tf_op jit(solution)/shard_map/ppermute | solution.py:652
  29.4 40.0 %copy-start.7 = (bf16[7,256,256]{2,1,0:T(8,128)(2,1)}, bf16[7,256,256]{2,1,0:T(8,128)(2,1)S(1)}, u32[]{:S(2)}) copy-start(bf16[7,256,256]{2,1,0:T(8,128)(2,1)S(1)} %collective-permute-done.2.rest_3_) | copy-start | bytes 2752516
  29.4 27.3 %collective-permute-start.8 = (bf16[7,256,256]{2,1,0:T(8,128)(2,1)S(1)}, bf16[7,256,256]{2,1,0:T(8,128)(2,1)}, u32[]{:S(2)}, u32[]{:S(2)}) collective-permute-start(bf16[7,256,256]{2,1,0:T(8,128)(2,1)S(1)} %collective-permute-done.2.rest_3_), channel_id=1, source_target_pairs={{0,16},{4,12},{8,24},{12,4},{16,0},{20,28},{24,8},{28,20},{1,17},{... | collective-permute-start | bytes 2752520 | tf_op jit(solution)/shard_map/ppermute | solution.py:656
  29.4 27.3 %collective-permute-start.4 = (bf16[7,256,256]{2,1,0:T(8,128)(2,1)S(1)}, bf16[7,256,256]{2,1,0:T(8,128)(2,1)}, u32[]{:S(2)}, u32[]{:S(2)}) collective-permute-start(bf16[7,256,256]{2,1,0:T(8,128)(2,1)S(1)} %collective-permute-done.2.rest_3_), channel_id=1, source_target_pairs={{0,4},{4,0},{8,12},{12,8},{16,20},{20,16},{24,28},{28,24},{1,5},{5... | collective-permute-start | bytes 2752520 | tf_op jit(solution)/shard_map/ppermute | solution.py:628
  49.2 17.4 %collective-permute-start.7 = (bf16[7,256,256]{2,1,0:T(8,128)(2,1)}, bf16[7,256,256]{2,1,0:T(8,128)(2,1)}, u32[]{:S(2)}, u32[]{:S(2)}) collective-permute-start(bf16[7,256,256]{2,1,0:T(8,128)(2,1)} %collective-permute-done.1.rest_2_), channel_id=1, source_target_pairs={{0,16},{4,12},{8,24},{12,4},{16,0},{20,28},{24,8},{28,20},{1,17},{... | collective-permute-start | bytes 2752520 | tf_op jit(solution)/shard_map/ppermute | solution.py:655
  49.2 19.6 %collective-permute-start = (bf16[14,256,256]{2,1,0:T(8,128)(2,1)S(1)}, bf16[14,256,256]{2,1,0:T(8,128)(2,1)}, u32[]{:S(2)}, u32[]{:S(2)}) collective-permute-start(bf16[14,256,256]{2,1,0:T(8,128)(2,1)S(1)} %convert_element_type.180.rest_0_), channel_id=1, source_target_pairs={{0,4},{4,0},{8,12},{12,8},{16,20},{20,16},{24,28},{28,24},{1,5},{5... | collective-permute-start | bytes 5505032 | tf_op jit(solution)/shard_map/ppermute | solution.py:628
  49.2 20.2 %collective-permute-start.6 = (bf16[14,256,256]{2,1,0:T(8,128)(2,1)}, bf16[14,256,256]{2,1,0:T(8,128)(2,1)}, u32[]{:S(2)}, u32[]{:S(2)}) collective-permute-start(bf16[14,256,256]{2,1,0:T(8,128)(2,1)} %collective-permute-done.5.rest_6_), channel_id=1, source_target_pairs={{0,4},{4,0},{8,12},{12,8},{16,20},{20,16},{24,28},{28,24},{1,5},{5... | collective-permute-start | bytes 5505032 | tf_op jit(solution)/shard_map/ppermute | solution.py:628
  56.8 12.0 %collective-permute-start.3 = (bf16[7,256,256]{2,1,0:T(8,128)(2,1)}, bf16[7,256,256]{2,1,0:T(8,128)(2,1)}, u32[]{:S(2)}, u32[]{:S(2)}) collective-permute-start(bf16[7,256,256]{2,1,0:T(8,128)(2,1)} %collective-permute-done.1.rest_2_), channel_id=1, source_target_pairs={{0,4},{4,0},{8,12},{12,8},{16,20},{20,16},{24,28},{28,24},{1,5},{5... | collective-permute-start | bytes 2752520 | tf_op jit(solution)/shard_map/ppermute | solution.py:628
  56.8 12.0 %collective-permute-start.10 = (bf16[7,256,256]{2,1,0:T(8,128)(2,1)}, bf16[7,256,256]{2,1,0:T(8,128)(2,1)}, u32[]{:S(2)}, u32[]{:S(2)}) collective-permute-start(bf16[7,256,256]{2,1,0:T(8,128)(2,1)} %collective-permute-done.8.rest_9_), channel_id=1, source_target_pairs={{0,4},{4,0},{8,12},{12,8},{16,20},{20,16},{24,28},{28,24},{1,5},{5... | collective-permute-start | bytes 2752520 | tf_op jit(solution)/shard_map/ppermute | solution.py:628
  66.6 2.8 %collective-permute-start.9 = (bf16[7,256,256]{2,1,0:T(8,128)(2,1)}, bf16[7,256,256]{2,1,0:T(8,128)(2,1)}, u32[]{:S(2)}, u32[]{:S(2)}) collective-permute-start(bf16[7,256,256]{2,1,0:T(8,128)(2,1)} %collective-permute-done.7.rest_8_), channel_id=1, source_target_pairs={{0,4},{4,0},{8,12},{12,8},{16,20},{20,16},{24,28},{28,24},{1,5},{5... | collective-permute-start | bytes 2752520 | tf_op jit(solution)/shard_map/ppermute | solution.py:628
  130.6 4.4 %collective-permute-start.11 = (bf16[16,256,256]{2,1,0:T(8,128)(2,1)}, bf16[16,256,256]{2,1,0:T(8,128)(2,1)S(1)}, u32[]{:S(2)}, u32[]{:S(2)}) collective-permute-start(bf16[16,256,256]{2,1,0:T(8,128)(2,1)} %get-tuple-element.112), channel_id=1, source_target_pairs={{0,4},{4,0},{8,12},{12,8},{16,20},{20,16},{24,28},{28,24},{1,5},{5... | collective-permute-start | bytes 6291464 | tf_op jit(solution)/shard_map/ppermute | solution.py:628
  136.6 12.8 %copy-start.5 = (f32[2,768]{1,0:T(2,128)S(1)}, f32[2,768]{1,0:T(2,128)}, u32[]{:S(2)}) copy-start(f32[2,768]{1,0:T(2,128)} %get-tuple-element.120) | copy-start | bytes 18436
  136.6 16.6 %copy-start.1 = (bf16[16,256,256]{2,1,0:T(8,128)(2,1)S(1)}, bf16[16,256,256]{2,1,0:T(8,128)(2,1)}, u32[]{:S(2)}) copy-start(bf16[16,256,256]{2,1,0:T(8,128)(2,1)} %get-tuple-element.126) | copy-start | bytes 6291460
  136.6 8.9 %collective-permute-start.12 = (bf16[40,256,256]{2,1,0:T(8,128)(2,1)}, bf16[40,256,256]{2,1,0:T(8,128)(2,1)S(1)}, u32[]{:S(2)}, u32[]{:S(2)}) collective-permute-start(bf16[40,256,256]{2,1,0:T(8,128)(2,1)} %get-tuple-element.115), channel_id=1, source_target_pairs={{0,4},{4,0},{8,12},{12,8},{16,20},{20,16},{24,28},{28,24},{1,5},{5... | collective-permute-start | bytes 15728648 | tf_op jit(solution)/shard_map/ppermute | solution.py:628
  136.8 16.4 %collective-permute-start.14 = (bf16[2048,256]{1,0:T(8,128)(2,1)S(1)}, bf16[2048,256]{1,0:T(8,128)(2,1)S(1)}, u32[]{:S(2)}, u32[]{:S(2)}) collective-permute-start(bf16[2048,256]{1,0:T(8,128)(2,1)S(1)} %bitcast.40), channel_id=1, source_target_pairs={{0,8},{4,20},{8,0},{12,28},{16,24},{20,4},{24,16},{28,12},{1,9},{5... | collective-permute-start | bytes 3145736 | tf_op jit(solution)/shard_map/ppermute | solution.py:761
  145.5 40.1 %slice-start = ((s8[5242880]{0:T(1024)(128)(4,1)}), s8[1048576]{0:T(1024)(128)(4,1)S(1)}, s32[]{:S(2)}) async-start(s8[5242880]{0:T(1024)(128)(4,1)} %bitcast.37), calls=%async_computation | async-start | bytes 2097152
  148.2 37.4 %collective-permute-start.13 = (bf16[5120,256]{1,0:T(8,128)(2,1)S(1)}, bf16[5120,256]{1,0:T(8,128)(2,1)S(1)}, u32[]{:S(2)}, u32[]{:S(2)}) collective-permute-start(bf16[5120,256]{1,0:T(8,128)(2,1)S(1)} %bitcast.39), channel_id=1, source_target_pairs={{0,8},{4,20},{8,0},{12,28},{16,24},{20,4},{24,16},{28,12},{1,9},{5... | collective-permute-start | bytes 7864328 | tf_op jit(solution)/shard_map/ppermute | solution.py:761
  149.4 3.8 %collective-permute-start.15 = (f32[2,768]{1,0:T(2,128)S(1)}, f32[2,768]{1,0:T(2,128)S(1)}, u32[]{:S(2)}, u32[]{:S(2)}) collective-permute-start(f32[2,768]{1,0:T(2,128)S(1)} %copy-done.5), channel_id=1, source_target_pairs={{0,16},{4,12},{8,24},{12,4},{16,0},{20,28},{24,8},{28,20},{1,17},{... | collective-permute-start | bytes 18440 | tf_op jit(solution)/shard_map/ppermute | solution.py:843
  153.2 32.5 %slice-start.1 = ((s8[5242880]{0:T(1024)(128)(4,1)}), s8[4194304]{0:T(1024)(128)(4,1)S(1)}, s32[]{:S(2)}) async-start(s8[5242880]{0:T(1024)(128)(4,1)} %bitcast.37), calls=%async_computation.1 | async-start | bytes 8388608
  153.4 14.9 %collective-permute-start.16 = (bf16[1024,256]{1,0:T(8,128)(2,1)S(1)}, bf16[1024,256]{1,0:T(8,128)(2,1)S(1)}, u32[]{:S(2)}, u32[]{:S(2)}) collective-permute-start(bf16[1024,256]{1,0:T(8,128)(2,1)S(1)} %fusion.8), channel_id=1, source_target_pairs={{0,16},{4,12},{8,24},{12,4},{16,0},{20,28},{24,8},{28,20},{1,17},{... | collective-permute-start | bytes 1572872 | tf_op jit(solution)/shard_map/ppermute | solution.py:779
  168.7 13.8 %collective-permute-start.17 = (bf16[1024,256]{1,0:T(8,128)(2,1)S(1)}, bf16[1024,256]{1,0:T(8,128)(2,1)S(1)}, u32[]{:S(2)}, u32[]{:S(2)}) collective-permute-start(bf16[1024,256]{1,0:T(8,128)(2,1)S(1)} %fusion.7), channel_id=1, source_target_pairs={{0,1},{3,2},{4,5},{7,6},{8,9},{11,10},{12,13},{15,14},{16,17},{19,... | collective-permute-start | bytes 1572872 | tf_op jit(solution)/shard_map/ppermute | solution.py:804
  182.6 5.7 %collective-permute-start.20 = (bf16[1024,256]{1,0:T(8,128)(2,1)S(1)}, bf16[1024,256]{1,0:T(8,128)(2,1)S(1)}, u32[]{:S(2)}, u32[]{:S(2)}) collective-permute-start(bf16[1024,256]{1,0:T(8,128)(2,1)S(1)} %add_convert_fusion.7), channel_id=1, source_target_pairs={{1,2},{2,1},{5,6},{6,5},{9,10},{10,9},{13,14},{14,13},{17,18},{18,... | collective-permute-start | bytes 1572872 | tf_op jit(solution)/shard_map/ppermute | solution.py:812
  186.0 12.1 %collective-permute-start.19 = (bf16[1536,256]{1,0:T(8,128)(2,1)S(1)}, bf16[1536,256]{1,0:T(8,128)(2,1)S(1)}, u32[]{:S(2)}, u32[]{:S(2)}) collective-permute-start(bf16[1536,256]{1,0:T(8,128)(2,1)S(1)} %fusion.2), channel_id=1, source_target_pairs={{0,16},{4,12},{8,24},{12,4},{16,0},{20,28},{24,8},{28,20},{1,17},{... | collective-permute-start | bytes 2359304 | tf_op jit(solution)/shard_map/ppermute | solution.py:779
  188.3 17.3 %collective-permute-start.18 = (bf16[1024,256]{1,0:T(8,128)(2,1)S(1)}, bf16[1024,256]{1,0:T(8,128)(2,1)S(1)}, u32[]{:S(2)}, u32[]{:S(2)}) collective-permute-start(bf16[1024,256]{1,0:T(8,128)(2,1)S(1)} %fusion.5), channel_id=1, source_target_pairs={{0,16},{4,12},{8,24},{12,4},{16,0},{20,28},{24,8},{28,20},{1,17},{... | collective-permute-start | bytes 1572872 | tf_op jit(solution)/shard_map/ppermute | solution.py:779
  198.6 22.9 %collective-permute-start.25 = (bf16[1536,256]{1,0:T(8,128)(2,1)S(1)}, bf16[1536,256]{1,0:T(8,128)(2,1)S(1)}, u32[]{:S(2)}, u32[]{:S(2)}) collective-permute-start(bf16[1536,256]{1,0:T(8,128)(2,1)S(1)} %fusion.1), channel_id=1, source_target_pairs={{0,1},{3,2},{4,5},{7,6},{8,9},{11,10},{12,13},{15,14},{16,17},{19,... | collective-permute-start | bytes 2359304 | tf_op jit(solution)/shard_map/ppermute | solution.py:804
  203.5 3.7 %collective-permute-start.22 = (f32[2,768]{1,0:T(2,128)S(1)}, f32[2,768]{1,0:T(2,128)S(1)}, u32[]{:S(2)}, u32[]{:S(2)}) collective-permute-start(f32[2,768]{1,0:T(2,128)S(1)} %add.278), channel_id=1, source_target_pairs={{0,8},{4,20},{8,0},{12,28},{16,24},{20,4},{24,16},{28,12},{1,9},{5... | collective-permute-start | bytes 18440 | tf_op jit(solution)/shard_map/ppermute | solution.py:843
  204.4 18.1 %collective-permute-start.24 = (bf16[1024,256]{1,0:T(8,128)(2,1)S(1)}, bf16[1024,256]{1,0:T(8,128)(2,1)}, u32[]{:S(2)}, u32[]{:S(2)}) collective-permute-start(bf16[1024,256]{1,0:T(8,128)(2,1)S(1)} %add_convert_fusion.6), channel_id=1, source_target_pairs={{1,0},{2,3},{5,4},{6,7},{9,8},{10,11},{13,12},{14,15},{17,16},{18,... | collective-permute-start | bytes 1572872 | tf_op jit(solution)/shard_map/ppermute | solution.py:817
  207.2 22.0 %collective-permute-start.21 = (bf16[1024,256]{1,0:T(8,128)(2,1)S(1)}, bf16[1024,256]{1,0:T(8,128)(2,1)S(1)}, u32[]{:S(2)}, u32[]{:S(2)}) collective-permute-start(bf16[1024,256]{1,0:T(8,128)(2,1)S(1)} %fusion.4), channel_id=1, source_target_pairs={{0,1},{3,2},{4,5},{7,6},{8,9},{11,10},{12,13},{15,14},{16,17},{19,... | collective-permute-start | bytes 1572872 | tf_op jit(solution)/shard_map/ppermute | solution.py:804
  221.7 8.4 %collective-permute-start.27 = (bf16[1536,256]{1,0:T(8,128)(2,1)S(1)}, bf16[1536,256]{1,0:T(8,128)(2,1)S(1)}, u32[]{:S(2)}, u32[]{:S(2)}) collective-permute-start(bf16[1536,256]{1,0:T(8,128)(2,1)S(1)} %add_convert_fusion.3), channel_id=1, source_target_pairs={{1,2},{2,1},{5,6},{6,5},{9,10},{10,9},{13,14},{14,13},{17,18},{18,... | collective-permute-start | bytes 2359304 | tf_op jit(solution)/shard_map/ppermute | solution.py:812
  222.4 2.0 collective-permute-start.23
  229.3 23.5 %collective-permute-start.26 = (bf16[1024,256]{1,0:T(8,128)(2,1)S(1)}, bf16[1024,256]{1,0:T(8,128)(2,1)S(1)}, u32[]{:S(2)}, u32[]{:S(2)}) collective-permute-start(bf16[1024,256]{1,0:T(8,128)(2,1)S(1)} %add_convert_fusion.5), channel_id=1, source_target_pairs={{1,2},{2,1},{5,6},{6,5},{9,10},{10,9},{13,14},{14,13},{17,18},{18,... | collective-permute-start | bytes 1572872 | tf_op jit(solution)/shard_map/ppermute | solution.py:812
  230.2 31.2 %collective-permute-start.30 = (bf16[1536,256]{1,0:T(8,128)(2,1)S(1)}, bf16[1536,256]{1,0:T(8,128)(2,1)S(1)}, u32[]{:S(2)}, u32[]{:S(2)}) collective-permute-start(bf16[1536,256]{1,0:T(8,128)(2,1)S(1)} %add_convert_fusion.2), channel_id=1, source_target_pairs={{1,0},{2,3},{5,4},{6,7},{9,8},{10,11},{13,12},{14,15},{17,16},{18,... | collective-permute-start | bytes 2359304 | tf_op jit(solution)/shard_map/ppermute | solution.py:817
  231.5 30.9 %collective-permute-start.29 = (f32[2,768]{1,0:T(2,128)S(1)}, f32[2,768]{1,0:T(2,128)S(1)}, u32[]{:S(2)}, u32[]{:S(2)}) collective-permute-start(f32[2,768]{1,0:T(2,128)S(1)} %add.304), channel_id=1, source_target_pairs={{0,1},{1,0},{2,3},{3,2},{4,5},{5,4},{6,7},{7,6},{8,9},{9,8},{10,11... | collective-permute-start | bytes 18440 | tf_op jit(solution)/shard_map/ppermute | solution.py:843
  253.0 19.4 %collective-permute-start.28 = (bf16[1024,256]{1,0:T(8,128)(2,1)S(1)}, bf16[1024,256]{1,0:T(8,128)(2,1)S(1)}, u32[]{:S(2)}, u32[]{:S(2)}) collective-permute-start(bf16[1024,256]{1,0:T(8,128)(2,1)S(1)} %add_convert_fusion.4), channel_id=1, source_target_pairs={{1,0},{2,3},{5,4},{6,7},{9,8},{10,11},{13,12},{14,15},{17,16},{18,... | collective-permute-start | bytes 1572872 | tf_op jit(solution)/shard_map/ppermute | solution.py:817
  262.4 9.3 %collective-permute-start.31 = (f32[2,768]{1,0:T(2,128)S(1)}, f32[2,768]{1,0:T(2,128)S(1)}, u32[]{:S(2)}, u32[]{:S(2)}) collective-permute-start(f32[2,768]{1,0:T(2,128)S(1)} %add.308), channel_id=1, source_target_pairs={{0,2},{1,3},{2,0},{3,1},{4,6},{5,7},{6,4},{7,5},{8,10},{9,11},{10,... | collective-permute-start | bytes 18440 | tf_op jit(solution)/shard_map/ppermute | solution.py:843
  263.2 8.5 %copy-start.2 = (f32[2,768]{1,0:T(2,128)S(1)}, f32[2,768]{1,0:T(2,128)}, u32[]{:S(2)}) copy-start(f32[2,768]{1,0:T(2,128)} %gains_ref.1) | copy-start | bytes 18436
  263.2 8.5 %copy-start.3 = (f32[2,768]{1,0:T(2,128)S(1)}, f32[2,768]{1,0:T(2,128)}, u32[]{:S(2)}) copy-start(f32[2,768]{1,0:T(2,128)} %param.25) | copy-start | bytes 18436
  263.2 8.5 %copy-start.4 = (f32[2,768]{1,0:T(2,128)S(1)}, f32[2,768]{1,0:T(2,128)}, u32[]{:S(2)}) copy-start(f32[2,768]{1,0:T(2,128)} %param.24) | copy-start | bytes 18436

commit v6 on v5

--- a/solution.py
+++ b/solution.py
@@ -151,14 +151,14 @@
     block_right_ref,
     segments_ref,
     segments_t_ref,
-    x_ref,
-    dy_ref,
+    x_hbm,
+    dy_hbm,
     gains_ref,
     *rest,
 ):
     pieces = rest[: len(piece_slots)]
     rest = rest[len(piece_slots) :]
-    out_ref, token_grad_ref, gain_ref = rest[:3]
+    out_hbm, token_grad_hbm, gain_ref = rest[:3]
     grad_refs, rest = rest[3 : 3 + out_count], rest[3 + out_count :]
     (
         w_qkv,
@@ -190,8 +190,19 @@
         sin_ref,
         cos_t_ref,
         sin_t_ref,
+        x_ref,
+        dy_ref,
+        out_ref,
+        token_grad_ref,
+        row_sems,
     ) = rest
     seq = segments_ref.shape[1]
+    bring_x = pltpu.make_async_copy(x_hbm, x_ref, row_sems.at[0])
+    bring_dy = pltpu.make_async_copy(dy_hbm, dy_ref, row_sems.at[1])
+    take_out = pltpu.make_async_copy(out_ref, out_hbm, row_sems.at[2])
+    take_token_grad = pltpu.make_async_copy(token_grad_ref, token_grad_hbm, row_sems.at[3])
+    bring_x.start()
+    bring_dy.start()
 
     starts = [sum(piece_slots[:n]) for n in range(len(piece_slots) + 1)]
     reciprocal = (1 << 16) // own + 1
@@ -261,6 +272,7 @@
     def wait_for(target, sem):
         pltpu.make_async_copy(target, target, sem).wait()
 
+    bring_x.wait()
     lefts[0:D, :] = x_ref[...].T
     lane = lax.broadcasted_iota(jnp.int32, (1, 128), 1)
     low_half = lax.rem(lane, HEAD_DIM) < HEAD_DIM // 2
@@ -340,9 +352,10 @@
         lefts[pl.ds(pl.multiple_of(3 * D + j * B, B), B), :] = act.T
         return carry
 
-    lax.fori_loop(0, nf, feed, 0)
+    lax.fori_loop(0, nf, feed, 0, unroll=2)
 
     wait_for(w_d, w_sems.at[3])
+    bring_dy.wait()
     gain_two = jnp.zeros((1, D), F32)
     for r in range(micro):
         rows = slice(r * seq, (r + 1) * seq)
@@ -358,6 +371,7 @@
         dh2_scr[rows, :] = dh2
         rights[rows, RIGHT_D:] = dh2.astype(BF16)
     gain_ref[1:2, :] = gain_two
+    take_out.start()
 
     def feed_back(j, carry):
         cols = pl.ds(pl.multiple_of(j * B, B), B)
@@ -444,8 +458,11 @@
         return carry
 
     lax.fori_loop(0, nd, token_back, 0)
+    take_token_grad.start()
 
     weigh_slots(slot_ref, left_ref, right_ref, lefts, rights, grad_refs, ring, ring_sems)
+    take_out.wait()
+    take_token_grad.wait()
 
 
 def run_layer(
@@ -467,8 +484,8 @@
             jax.ShapeDtypeStruct((2, D), F32),
             *grads,
         ),
-        in_specs=[smem] * 5 + [vmem] * 5 + [hbm] * len(pieces),
-        out_specs=(vmem,) * 3 + (hbm,) * len(grads),
+        in_specs=[smem] * 5 + [vmem] * 2 + [hbm] * 2 + [vmem] + [hbm] * len(pieces),
+        out_specs=(hbm, hbm, vmem) + (hbm,) * len(grads),
         scratch_shapes=[
             pltpu.VMEM((D, 3 * D), BF16),
             pltpu.VMEM((D, D), BF16),
@@ -499,6 +516,8 @@
             pltpu.VMEM((count, 128), F32),
             pltpu.VMEM((HEAD_DIM // 2, count), F32),
             pltpu.VMEM((HEAD_DIM // 2, count), F32),
+            *(pltpu.VMEM((count, D), BF16) for _ in range(4)),
+            pltpu.SemaphoreType.DMA((4,)),
         ],
         compiler_params=pltpu.CompilerParams(vmem_limit_bytes=56 * MIB),
         cost_estimate=pl.CostEstimate(

time: 280 us -> 278 us (level)
  no operation moved by 1% of the time
where the time goes in v6:
time: 278 us
  waiting for transfers between devices  130 us (47%)
  Pallas kernels  80.3 us (29%)
  starting transfers between devices  50 us (18%)
  other arithmetic  14.4 us (5%)
    pallas_call x1, Pallas kernels, run_layer(): pl.pallas_call(functools.partial(layer_kernel, micro, own, [p.shape[0] fo...  59 us
    ppermute x3, waiting for transfers between devices, reduce_and_step(): lax.ppermute(t[part], 'rep', [(0, 1), (3, 2)])  24.9 us
    ppermute x3, waiting for transfers between devices, reduce_and_step(): lax.ppermute(t, 'fsdp', far_pairs)  22.6 us
    pallas_call x3, Pallas kernels, adam_blocks(): pl.pallas_call(functools.partial(adam_kernel, steps), grid=(sum(steps),),...  21.3 us
    ppermute x1, waiting for transfers between devices, gather_pieces(): last_near = lax.ppermute(weights[half:].astype(BF16), 'fsdp', near_pairs)  21.3 us
    ppermute x1, waiting for transfers between devices, gather_pieces(): first_near = lax.ppermute(weights[:half].astype(BF16), 'fsdp', near_pairs)  19.8 us
    ppermute x5, starting transfers between devices, reduce_and_step(): lax.ppermute(gain, axis, pairs)  18.5 us
    ppermute x3, starting transfers between devices, reduce_and_step(): lax.ppermute(t[part], 'rep', [(0, 1), (3, 2)])  12.9 us
  transfers between devices with their start and end apart: 32, of which 16 were waited for; matrix products, arithmetic and copies ran while one was open for 4% of the time, Pallas kernels for 5%

profile of v6, /device:TPU:0, one launch (start us, length us, event | category | flops | bytes accessed | tf_op | source)
XLA Modules:
  0.0 277.6 jit_solution(4386431127757799687)
XLA Ops:
  0.6 2.2 convert_element_type.180.rest_0_
  2.9 3.0 %collective-permute-start.5 = (bf16[14,256,256]{2,1,0:T(8,128)(2,1)S(1)}, bf16[14,256,256]{2,1,0:T(8,128)(2,1)}, u32[]{:S(2)}, u32[]{:S(2)}) collective-permute-start(bf16[14,256,256]{2,1,0:T(8,128)(2,1)S(1)} %convert_element_type.180.rest_0_), channel_id=1, source_target_pairs={{0,16},{4,12},{8,24},{12,4},{16,0},{20,28},{24,8},{28,20},{1,17},{... | collective-permute-start | bytes 5505032 | tf_op jit(solution)/shard_map/ppermute | solution.py:673
  6.1 1.6 collective-permute-start.2
  8.2 21.3 %collective-permute-done.2.rest_3_ = bf16[7,256,256]{2,1,0:T(8,128)(2,1)S(1)} collective-permute-done((bf16[7,256,256]{2,1,0:T(8,128)(2,1)S(1)}, bf16[7,256,256]{2,1,0:T(8,128)(2,1)S(1)}, u32[]{:S(2)}, u32[]{:S(2)}) %collective-permute-start.2) | collective-permute-done | bytes 917536 | tf_op jit(solution)/shard_map/ppermute | solution.py:672
  29.4 19.8 %collective-permute-done.1.rest_2_ = bf16[7,256,256]{2,1,0:T(8,128)(2,1)} collective-permute-done((bf16[7,256,256]{2,1,0:T(8,128)(2,1)S(1)}, bf16[7,256,256]{2,1,0:T(8,128)(2,1)}, u32[]{:S(2)}, u32[]{:S(2)}) %collective-permute-start.1) | collective-permute-done | bytes 917536 | tf_op jit(solution)/shard_map/ppermute | solution.py:671
  49.7 7.0 %collective-permute-done.8.rest_9_ = bf16[7,256,256]{2,1,0:T(8,128)(2,1)} collective-permute-done((bf16[7,256,256]{2,1,0:T(8,128)(2,1)S(1)}, bf16[7,256,256]{2,1,0:T(8,128)(2,1)}, u32[]{:S(2)}, u32[]{:S(2)}) %collective-permute-start.8) | collective-permute-done | bytes 917536 | tf_op jit(solution)/shard_map/ppermute | solution.py:675
  57.3 9.3 %collective-permute-done.7.rest_8_ = bf16[7,256,256]{2,1,0:T(8,128)(2,1)} collective-permute-done((bf16[7,256,256]{2,1,0:T(8,128)(2,1)}, bf16[7,256,256]{2,1,0:T(8,128)(2,1)}, u32[]{:S(2)}, u32[]{:S(2)}) %collective-permute-start.7) | collective-permute-done | bytes 917536 | tf_op jit(solution)/shard_map/ppermute | solution.py:674
  66.6 0.8 copy.35
  67.5 0.6 concatenate.7.slot_ref
  68.2 0.6 select_reduce_fusion.base_ref
  69.4 59.0 %layer.1 = (bf16[512,768]{1,0:T(8,128)(2,1)}, bf16[512,768]{1,0:T(8,128)(2,1)}, f32[2,768]{1,0:T(2,128)}, bf16[16,256,256]{2,1,0:T(8,128)(2,1)}, bf16[16,256,256...) custom-call(s32[108]{0:T(128)} %index_ref.1, s32[8]{0:T(128)} %select_reduce_fusion.base_ref, ...), custom_call_target="tpu_custom_call" | custom-call | flops 23000000512 | bytes 32000000 | tf_op jit(solution)/shard_map/layer/pallas_call | solution.py:479
  128.6 4.2 %collective-permute-done.11 = bf16[16,256,256]{2,1,0:T(8,128)(2,1)S(1)} collective-permute-done((bf16[16,256,256]{2,1,0:T(8,128)(2,1)}, bf16[16,256,256]{2,1,0:T(8,128)(2,1)S(1)}, u32[]{:S(2)}, u32[]{:S(2)}) %collective-permute-start.11) | collective-permute-done | bytes 2097184 | tf_op jit(solution)/shard_map/ppermute | solution.py:647
  132.9 1.5 add_convert_fusion.1
  134.6 1.1 collective-permute-start.14
  135.7 7.6 %collective-permute-done.12 = bf16[40,256,256]{2,1,0:T(8,128)(2,1)S(1)} collective-permute-done((bf16[40,256,256]{2,1,0:T(8,128)(2,1)}, bf16[40,256,256]{2,1,0:T(8,128)(2,1)S(1)}, u32[]{:S(2)}, u32[]{:S(2)}) %collective-permute-start.12) | collective-permute-done | bytes 5242912 | tf_op jit(solution)/shard_map/ppermute | solution.py:647
  143.4 2.7 add_convert_fusion
  146.1 1.2 collective-permute-start.13
  147.2 1.7 collective-permute-start.15
  149.0 2.0 collective-permute-done.15
  151.3 1.8 collective-permute-start.16
  153.1 13.1 %collective-permute-done.16 = bf16[1024,256]{1,0:T(8,128)(2,1)S(1)} collective-permute-done((bf16[1024,256]{1,0:T(8,128)(2,1)S(1)}, bf16[1024,256]{1,0:T(8,128)(2,1)S(1)}, u32[]{:S(2)}, u32[]{:S(2)}) %collective-permute-start.16) | collective-permute-done | bytes 524320 | tf_op jit(solution)/shard_map/ppermute | solution.py:798
  166.5 3.7 %collective-permute-start.17 = (bf16[1024,256]{1,0:T(8,128)(2,1)S(1)}, bf16[1024,256]{1,0:T(8,128)(2,1)S(1)}, u32[]{:S(2)}, u32[]{:S(2)}) collective-permute-start(bf16[1024,256]{1,0:T(8,128)(2,1)S(1)} %fusion.7), channel_id=1, source_target_pairs={{0,1},{3,2},{4,5},{7,6},{8,9},{11,10},{12,13},{15,14},{16,17},{19,... | collective-permute-start | bytes 1572872 | tf_op jit(solution)/shard_map/ppermute | solution.py:823
  170.3 10.0 %collective-permute-done.17 = bf16[1024,256]{1,0:T(8,128)(2,1)S(1)} collective-permute-done((bf16[1024,256]{1,0:T(8,128)(2,1)S(1)}, bf16[1024,256]{1,0:T(8,128)(2,1)S(1)}, u32[]{:S(2)}, u32[]{:S(2)}) %collective-permute-start.17) | collective-permute-done | bytes 524320 | tf_op jit(solution)/shard_map/ppermute | solution.py:823
  180.4 0.7 collective-permute-start.20
  181.1 2.3 collective-permute-done.13
  183.9 2.0 collective-permute-start.19
  186.4 9.5 %collective-permute-done.19 = bf16[1536,256]{1,0:T(8,128)(2,1)S(1)} collective-permute-done((bf16[1536,256]{1,0:T(8,128)(2,1)S(1)}, bf16[1536,256]{1,0:T(8,128)(2,1)S(1)}, u32[]{:S(2)}, u32[]{:S(2)}) %collective-permute-start.19) | collective-permute-done | bytes 786464 | tf_op jit(solution)/shard_map/ppermute | solution.py:798
  196.4 4.9 %collective-permute-start.25 = (bf16[1536,256]{1,0:T(8,128)(2,1)S(1)}, bf16[1536,256]{1,0:T(8,128)(2,1)S(1)}, u32[]{:S(2)}, u32[]{:S(2)}) collective-permute-start(bf16[1536,256]{1,0:T(8,128)(2,1)S(1)} %fusion.1), channel_id=1, source_target_pairs={{0,1},{3,2},{4,5},{7,6},{8,9},{11,10},{12,13},{15,14},{16,17},{19,... | collective-permute-start | bytes 2359304 | tf_op jit(solution)/shard_map/ppermute | solution.py:823
  201.3 0.9 collective-permute-start.22
  202.2 1.3 collective-permute-start.24
  203.9 1.2 collective-permute-done.22
  205.0 4.2 %collective-permute-start.21 = (bf16[1024,256]{1,0:T(8,128)(2,1)S(1)}, bf16[1024,256]{1,0:T(8,128)(2,1)S(1)}, u32[]{:S(2)}, u32[]{:S(2)}) collective-permute-start(bf16[1024,256]{1,0:T(8,128)(2,1)S(1)} %fusion.4), channel_id=1, source_target_pairs={{0,1},{3,2},{4,5},{7,6},{8,9},{11,10},{12,13},{15,14},{16,17},{19,... | collective-permute-start | bytes 1572872 | tf_op jit(solution)/shard_map/ppermute | solution.py:823
  209.3 10.0 %collective-permute-done.25 = bf16[1536,256]{1,0:T(8,128)(2,1)S(1)} collective-permute-done((bf16[1536,256]{1,0:T(8,128)(2,1)S(1)}, bf16[1536,256]{1,0:T(8,128)(2,1)S(1)}, u32[]{:S(2)}, u32[]{:S(2)}) %collective-permute-start.25) | collective-permute-done | bytes 786464 | tf_op jit(solution)/shard_map/ppermute | solution.py:823
  219.5 0.7 collective-permute-start.27
  220.3 1.9 broadcast_select_fusion.2.rest_0_
  222.2 4.8 %collective-permute-done.21 = bf16[1024,256]{1,0:T(8,128)(2,1)S(1)} collective-permute-done((bf16[1024,256]{1,0:T(8,128)(2,1)S(1)}, bf16[1024,256]{1,0:T(8,128)(2,1)S(1)}, u32[]{:S(2)}, u32[]{:S(2)}) %collective-permute-start.21) | collective-permute-done | bytes 524320 | tf_op jit(solution)/shard_map/ppermute | solution.py:823
  227.2 0.7 collective-permute-start.26
  228.1 1.3 collective-permute-start.30
  229.4 15.0 %collective-permute-start.29 = (f32[2,768]{1,0:T(2,128)S(1)}, f32[2,768]{1,0:T(2,128)S(1)}, u32[]{:S(2)}, u32[]{:S(2)}) collective-permute-start(f32[2,768]{1,0:T(2,128)S(1)} %add.304), channel_id=1, source_target_pairs={{0,1},{1,0},{2,3},{3,2},{4,5},{5,4},{6,7},{7,6},{8,9},{9,8},{10,11... | collective-permute-start | bytes 18440 | tf_op jit(solution)/shard_map/ppermute | solution.py:862
  244.4 6.3 %adam.3 = (f32[14,256,256]{2,1,0:T(8,128)}, f32[14,256,256]{2,1,0:T(8,128)}, f32[14,256,256]{2,1,0:T(8,128)}, f32[14,256,256]{2,1,0:T(8,128)}, bf16[14,256,256]{2,1,0:T(8,128)(2,1)}) custom-call(f32[14,256,256]{2,1,0:T(8,128)} %weight_ref.5, f32[14,256,256]{2,1,0:T(8,128)} %first_ref.5, f32[14,256,256]{2,1,0:T(8,128)} %second_ref.5, ...), custom_call_target="tpu_custom_call" | custom-call | flops 805306368 | bytes 11010048 | tf_op jit(solution)/shard_map/adam/pallas_call | solution.py:598
  250.8 1.3 collective-permute-start.28
  252.1 7.1 %collective-permute-done.30 = bf16[1536,256]{1,0:T(8,128)(2,1)S(1)} collective-permute-done((bf16[1536,256]{1,0:T(8,128)(2,1)S(1)}, bf16[1536,256]{1,0:T(8,128)(2,1)S(1)}, u32[]{:S(2)}, u32[]{:S(2)}) %collective-permute-start.30) | collective-permute-done | bytes 786464 | tf_op jit(solution)/shard_map/ppermute | solution.py:836
  259.3 1.0 broadcast_select_fusion.rest_0_
  260.3 0.8 collective-permute-start.31
  261.0 8.7 %adam.4 = (f32[14,256,256]{2,1,0:T(8,128)}, f32[14,256,256]{2,1,0:T(8,128)}, f32[14,256,256]{2,1,0:T(8,128)}, f32[14,256,256]{2,1,0:T(8,128)}, bf16[14,256,256]{2,1,0:T(8,128)(2,1)}) custom-call(f32[14,256,256]{2,1,0:T(8,128)} %weight_ref.5, ...), custom_call_target="tpu_custom_call", output_to_operand_aliasing={{0}: (6, {}), {1}: (7, {}), {2}: (8, {}), {3}: (9, {}), {4}... | custom-call | flops 1207959552 | bytes 16515072 | tf_op jit(solution)/shard_map/adam/pallas_call | solution.py:598
  269.8 0.6 multiply_subtract_fusion
  270.4 0.9 broadcast_select_fusion.1.rest_0_
  271.3 6.3 %adam.5 = (f32[14,256,256]{2,1,0:T(8,128)}, f32[14,256,256]{2,1,0:T(8,128)}, f32[14,256,256]{2,1,0:T(8,128)}, f32[14,256,256]{2,1,0:T(8,128)}, bf16[14,256,256]{2,1,0:T(8,128)(2,1)}) custom-call(f32[14,256,256]{2,1,0:T(8,128)} %weight_ref.5, ...), custom_call_target="tpu_custom_call", output_to_operand_aliasing={{0}: (6, {}), {1}: (7, {}), {2}: (8, {}), {3}: (9, {}), {4}... | custom-call | flops 805306368 | bytes 11010048 | tf_op jit(solution)/shard_map/adam/pallas_call | solution.py:598
  (84 shorter events, 6.0 us)
Async XLA Ops:
  2.9 66.5 %copy-start = (bf16[14,256,256]{2,1,0:T(8,128)(2,1)}, bf16[14,256,256]{2,1,0:T(8,128)(2,1)S(1)}, u32[]{:S(2)}) copy-start(bf16[14,256,256]{2,1,0:T(8,128)(2,1)S(1)} %convert_element_type.180.rest_0_) | copy-start | bytes 5505028
  2.9 63.7 %copy-start.6 = (s32[2,256]{1,0:T(2,128)S(1)}, s32[2,256]{1,0:T(2,128)}, u32[]{:S(2)}) copy-start(s32[2,256]{1,0:T(2,128)} %segments_ref.1) | copy-start | bytes 6148
  2.9 46.3 %collective-permute-start.5 = (bf16[14,256,256]{2,1,0:T(8,128)(2,1)S(1)}, bf16[14,256,256]{2,1,0:T(8,128)(2,1)}, u32[]{:S(2)}, u32[]{:S(2)}) collective-permute-start(bf16[14,256,256]{2,1,0:T(8,128)(2,1)S(1)} %convert_element_type.180.rest_0_), channel_id=1, source_target_pairs={{0,16},{4,12},{8,24},{12,4},{16,0},{20,28},{24,8},{28,20},{1,17},{... | collective-permute-start | bytes 5505032 | tf_op jit(solution)/shard_map/ppermute | solution.py:673
  6.1 23.4 %collective-permute-start.2 = (bf16[7,256,256]{2,1,0:T(8,128)(2,1)S(1)}, bf16[7,256,256]{2,1,0:T(8,128)(2,1)S(1)}, u32[]{:S(2)}, u32[]{:S(2)}) collective-permute-start(bf16[7,256,256]{2,1,0:T(8,128)(2,1)S(1)} %get-tuple-element.206), channel_id=1, source_target_pairs={{0,8},{4,20},{8,0},{12,28},{16,24},{20,4},{24,16},{28,12},{1,9},{5... | collective-permute-start | bytes 2752520 | tf_op jit(solution)/shard_map/ppermute | solution.py:672
  7.6 41.5 %collective-permute-start.1 = (bf16[7,256,256]{2,1,0:T(8,128)(2,1)S(1)}, bf16[7,256,256]{2,1,0:T(8,128)(2,1)}, u32[]{:S(2)}, u32[]{:S(2)}) collective-permute-start(bf16[7,256,256]{2,1,0:T(8,128)(2,1)S(1)} %get-tuple-element.207), channel_id=1, source_target_pairs={{0,8},{4,20},{8,0},{12,28},{16,24},{20,4},{24,16},{28,12},{1,9},{5... | collective-permute-start | bytes 2752520 | tf_op jit(solution)/shard_map/ppermute | solution.py:671
  29.4 40.0 %copy-start.7 = (bf16[7,256,256]{2,1,0:T(8,128)(2,1)}, bf16[7,256,256]{2,1,0:T(8,128)(2,1)S(1)}, u32[]{:S(2)}) copy-start(bf16[7,256,256]{2,1,0:T(8,128)(2,1)S(1)} %collective-permute-done.2.rest_3_) | copy-start | bytes 2752516
  29.4 27.3 %collective-permute-start.8 = (bf16[7,256,256]{2,1,0:T(8,128)(2,1)S(1)}, bf16[7,256,256]{2,1,0:T(8,128)(2,1)}, u32[]{:S(2)}, u32[]{:S(2)}) collective-permute-start(bf16[7,256,256]{2,1,0:T(8,128)(2,1)S(1)} %collective-permute-done.2.rest_3_), channel_id=1, source_target_pairs={{0,16},{4,12},{8,24},{12,4},{16,0},{20,28},{24,8},{28,20},{1,17},{... | collective-permute-start | bytes 2752520 | tf_op jit(solution)/shard_map/ppermute | solution.py:675
  29.4 27.3 %collective-permute-start.4 = (bf16[7,256,256]{2,1,0:T(8,128)(2,1)S(1)}, bf16[7,256,256]{2,1,0:T(8,128)(2,1)}, u32[]{:S(2)}, u32[]{:S(2)}) collective-permute-start(bf16[7,256,256]{2,1,0:T(8,128)(2,1)S(1)} %collective-permute-done.2.rest_3_), channel_id=1, source_target_pairs={{0,4},{4,0},{8,12},{12,8},{16,20},{20,16},{24,28},{28,24},{1,5},{5... | collective-permute-start | bytes 2752520 | tf_op jit(solution)/shard_map/ppermute | solution.py:647
  49.2 17.4 %collective-permute-start.7 = (bf16[7,256,256]{2,1,0:T(8,128)(2,1)}, bf16[7,256,256]{2,1,0:T(8,128)(2,1)}, u32[]{:S(2)}, u32[]{:S(2)}) collective-permute-start(bf16[7,256,256]{2,1,0:T(8,128)(2,1)} %collective-permute-done.1.rest_2_), channel_id=1, source_target_pairs={{0,16},{4,12},{8,24},{12,4},{16,0},{20,28},{24,8},{28,20},{1,17},{... | collective-permute-start | bytes 2752520 | tf_op jit(solution)/shard_map/ppermute | solution.py:674
  49.2 19.6 %collective-permute-start = (bf16[14,256,256]{2,1,0:T(8,128)(2,1)S(1)}, bf16[14,256,256]{2,1,0:T(8,128)(2,1)}, u32[]{:S(2)}, u32[]{:S(2)}) collective-permute-start(bf16[14,256,256]{2,1,0:T(8,128)(2,1)S(1)} %convert_element_type.180.rest_0_), channel_id=1, source_target_pairs={{0,4},{4,0},{8,12},{12,8},{16,20},{20,16},{24,28},{28,24},{1,5},{5... | collective-permute-start | bytes 5505032 | tf_op jit(solution)/shard_map/ppermute | solution.py:647
  49.2 20.2 %collective-permute-start.6 = (bf16[14,256,256]{2,1,0:T(8,128)(2,1)}, bf16[14,256,256]{2,1,0:T(8,128)(2,1)}, u32[]{:S(2)}, u32[]{:S(2)}) collective-permute-start(bf16[14,256,256]{2,1,0:T(8,128)(2,1)} %collective-permute-done.5.rest_6_), channel_id=1, source_target_pairs={{0,4},{4,0},{8,12},{12,8},{16,20},{20,16},{24,28},{28,24},{1,5},{5... | collective-permute-start | bytes 5505032 | tf_op jit(solution)/shard_map/ppermute | solution.py:647
  56.8 12.0 %collective-permute-start.3 = (bf16[7,256,256]{2,1,0:T(8,128)(2,1)}, bf16[7,256,256]{2,1,0:T(8,128)(2,1)}, u32[]{:S(2)}, u32[]{:S(2)}) collective-permute-start(bf16[7,256,256]{2,1,0:T(8,128)(2,1)} %collective-permute-done.1.rest_2_), channel_id=1, source_target_pairs={{0,4},{4,0},{8,12},{12,8},{16,20},{20,16},{24,28},{28,24},{1,5},{5... | collective-permute-start | bytes 2752520 | tf_op jit(solution)/shard_map/ppermute | solution.py:647
  56.8 12.0 %collective-permute-start.10 = (bf16[7,256,256]{2,1,0:T(8,128)(2,1)}, bf16[7,256,256]{2,1,0:T(8,128)(2,1)}, u32[]{:S(2)}, u32[]{:S(2)}) collective-permute-start(bf16[7,256,256]{2,1,0:T(8,128)(2,1)} %collective-permute-done.8.rest_9_), channel_id=1, source_target_pairs={{0,4},{4,0},{8,12},{12,8},{16,20},{20,16},{24,28},{28,24},{1,5},{5... | collective-permute-start | bytes 2752520 | tf_op jit(solution)/shard_map/ppermute | solution.py:647
  66.6 2.8 %collective-permute-start.9 = (bf16[7,256,256]{2,1,0:T(8,128)(2,1)}, bf16[7,256,256]{2,1,0:T(8,128)(2,1)}, u32[]{:S(2)}, u32[]{:S(2)}) collective-permute-start(bf16[7,256,256]{2,1,0:T(8,128)(2,1)} %collective-permute-done.7.rest_8_), channel_id=1, source_target_pairs={{0,4},{4,0},{8,12},{12,8},{16,20},{20,16},{24,28},{28,24},{1,5},{5... | collective-permute-start | bytes 2752520 | tf_op jit(solution)/shard_map/ppermute | solution.py:647
  128.4 4.4 %collective-permute-start.11 = (bf16[16,256,256]{2,1,0:T(8,128)(2,1)}, bf16[16,256,256]{2,1,0:T(8,128)(2,1)S(1)}, u32[]{:S(2)}, u32[]{:S(2)}) collective-permute-start(bf16[16,256,256]{2,1,0:T(8,128)(2,1)} %get-tuple-element.112), channel_id=1, source_target_pairs={{0,4},{4,0},{8,12},{12,8},{16,20},{20,16},{24,28},{28,24},{1,5},{5... | collective-permute-start | bytes 6291464 | tf_op jit(solution)/shard_map/ppermute | solution.py:647
  134.4 12.8 %copy-start.5 = (f32[2,768]{1,0:T(2,128)S(1)}, f32[2,768]{1,0:T(2,128)}, u32[]{:S(2)}) copy-start(f32[2,768]{1,0:T(2,128)} %get-tuple-element.120) | copy-start | bytes 18436
  134.4 16.6 %copy-start.1 = (bf16[16,256,256]{2,1,0:T(8,128)(2,1)S(1)}, bf16[16,256,256]{2,1,0:T(8,128)(2,1)}, u32[]{:S(2)}) copy-start(bf16[16,256,256]{2,1,0:T(8,128)(2,1)} %get-tuple-element.126) | copy-start | bytes 6291460
  134.4 8.9 %collective-permute-start.12 = (bf16[40,256,256]{2,1,0:T(8,128)(2,1)}, bf16[40,256,256]{2,1,0:T(8,128)(2,1)S(1)}, u32[]{:S(2)}, u32[]{:S(2)}) collective-permute-start(bf16[40,256,256]{2,1,0:T(8,128)(2,1)} %get-tuple-element.115), channel_id=1, source_target_pairs={{0,4},{4,0},{8,12},{12,8},{16,20},{20,16},{24,28},{28,24},{1,5},{5... | collective-permute-start | bytes 15728648 | tf_op jit(solution)/shard_map/ppermute | solution.py:647
  134.6 16.4 %collective-permute-start.14 = (bf16[2048,256]{1,0:T(8,128)(2,1)S(1)}, bf16[2048,256]{1,0:T(8,128)(2,1)S(1)}, u32[]{:S(2)}, u32[]{:S(2)}) collective-permute-start(bf16[2048,256]{1,0:T(8,128)(2,1)S(1)} %bitcast.40), channel_id=1, source_target_pairs={{0,8},{4,20},{8,0},{12,28},{16,24},{20,4},{24,16},{28,12},{1,9},{5... | collective-permute-start | bytes 3145736 | tf_op jit(solution)/shard_map/ppermute | solution.py:780
  143.4 40.1 %slice-start = ((s8[5242880]{0:T(1024)(128)(4,1)}), s8[1048576]{0:T(1024)(128)(4,1)S(1)}, s32[]{:S(2)}) async-start(s8[5242880]{0:T(1024)(128)(4,1)} %bitcast.37), calls=%async_computation | async-start | bytes 2097152
  146.1 37.4 %collective-permute-start.13 = (bf16[5120,256]{1,0:T(8,128)(2,1)S(1)}, bf16[5120,256]{1,0:T(8,128)(2,1)S(1)}, u32[]{:S(2)}, u32[]{:S(2)}) collective-permute-start(bf16[5120,256]{1,0:T(8,128)(2,1)S(1)} %bitcast.39), channel_id=1, source_target_pairs={{0,8},{4,20},{8,0},{12,28},{16,24},{20,4},{24,16},{28,12},{1,9},{5... | collective-permute-start | bytes 7864328 | tf_op jit(solution)/shard_map/ppermute | solution.py:780
  147.2 3.8 %collective-permute-start.15 = (f32[2,768]{1,0:T(2,128)S(1)}, f32[2,768]{1,0:T(2,128)S(1)}, u32[]{:S(2)}, u32[]{:S(2)}) collective-permute-start(f32[2,768]{1,0:T(2,128)S(1)} %copy-done.5), channel_id=1, source_target_pairs={{0,16},{4,12},{8,24},{12,4},{16,0},{20,28},{24,8},{28,20},{1,17},{... | collective-permute-start | bytes 18440 | tf_op jit(solution)/shard_map/ppermute | solution.py:862
  151.0 32.5 %slice-start.1 = ((s8[5242880]{0:T(1024)(128)(4,1)}), s8[4194304]{0:T(1024)(128)(4,1)S(1)}, s32[]{:S(2)}) async-start(s8[5242880]{0:T(1024)(128)(4,1)} %bitcast.37), calls=%async_computation.1 | async-start | bytes 8388608
  151.3 14.9 %collective-permute-start.16 = (bf16[1024,256]{1,0:T(8,128)(2,1)S(1)}, bf16[1024,256]{1,0:T(8,128)(2,1)S(1)}, u32[]{:S(2)}, u32[]{:S(2)}) collective-permute-start(bf16[1024,256]{1,0:T(8,128)(2,1)S(1)} %fusion.8), channel_id=1, source_target_pairs={{0,16},{4,12},{8,24},{12,4},{16,0},{20,28},{24,8},{28,20},{1,17},{... | collective-permute-start | bytes 1572872 | tf_op jit(solution)/shard_map/ppermute | solution.py:798
  166.5 13.8 %collective-permute-start.17 = (bf16[1024,256]{1,0:T(8,128)(2,1)S(1)}, bf16[1024,256]{1,0:T(8,128)(2,1)S(1)}, u32[]{:S(2)}, u32[]{:S(2)}) collective-permute-start(bf16[1024,256]{1,0:T(8,128)(2,1)S(1)} %fusion.7), channel_id=1, source_target_pairs={{0,1},{3,2},{4,5},{7,6},{8,9},{11,10},{12,13},{15,14},{16,17},{19,... | collective-permute-start | bytes 1572872 | tf_op jit(solution)/shard_map/ppermute | solution.py:823
  180.4 5.7 %collective-permute-start.20 = (bf16[1024,256]{1,0:T(8,128)(2,1)S(1)}, bf16[1024,256]{1,0:T(8,128)(2,1)S(1)}, u32[]{:S(2)}, u32[]{:S(2)}) collective-permute-start(bf16[1024,256]{1,0:T(8,128)(2,1)S(1)} %add_convert_fusion.7), channel_id=1, source_target_pairs={{1,2},{2,1},{5,6},{6,5},{9,10},{10,9},{13,14},{14,13},{17,18},{18,... | collective-permute-start | bytes 1572872 | tf_op jit(solution)/shard_map/ppermute | solution.py:831
  183.9 12.1 %collective-permute-start.19 = (bf16[1536,256]{1,0:T(8,128)(2,1)S(1)}, bf16[1536,256]{1,0:T(8,128)(2,1)S(1)}, u32[]{:S(2)}, u32[]{:S(2)}) collective-permute-start(bf16[1536,256]{1,0:T(8,128)(2,1)S(1)} %fusion.2), channel_id=1, source_target_pairs={{0,16},{4,12},{8,24},{12,4},{16,0},{20,28},{24,8},{28,20},{1,17},{... | collective-permute-start | bytes 2359304 | tf_op jit(solution)/shard_map/ppermute | solution.py:798
  186.2 17.4 %collective-permute-start.18 = (bf16[1024,256]{1,0:T(8,128)(2,1)S(1)}, bf16[1024,256]{1,0:T(8,128)(2,1)S(1)}, u32[]{:S(2)}, u32[]{:S(2)}) collective-permute-start(bf16[1024,256]{1,0:T(8,128)(2,1)S(1)} %fusion.5), channel_id=1, source_target_pairs={{0,16},{4,12},{8,24},{12,4},{16,0},{20,28},{24,8},{28,20},{1,17},{... | collective-permute-start | bytes 1572872 | tf_op jit(solution)/shard_map/ppermute | solution.py:798
  196.4 22.9 %collective-permute-start.25 = (bf16[1536,256]{1,0:T(8,128)(2,1)S(1)}, bf16[1536,256]{1,0:T(8,128)(2,1)S(1)}, u32[]{:S(2)}, u32[]{:S(2)}) collective-permute-start(bf16[1536,256]{1,0:T(8,128)(2,1)S(1)} %fusion.1), channel_id=1, source_target_pairs={{0,1},{3,2},{4,5},{7,6},{8,9},{11,10},{12,13},{15,14},{16,17},{19,... | collective-permute-start | bytes 2359304 | tf_op jit(solution)/shard_map/ppermute | solution.py:823
  201.3 3.7 %collective-permute-start.22 = (f32[2,768]{1,0:T(2,128)S(1)}, f32[2,768]{1,0:T(2,128)S(1)}, u32[]{:S(2)}, u32[]{:S(2)}) collective-permute-start(f32[2,768]{1,0:T(2,128)S(1)} %add.278), channel_id=1, source_target_pairs={{0,8},{4,20},{8,0},{12,28},{16,24},{20,4},{24,16},{28,12},{1,9},{5... | collective-permute-start | bytes 18440 | tf_op jit(solution)/shard_map/ppermute | solution.py:862
  202.2 18.1 %collective-permute-start.24 = (bf16[1024,256]{1,0:T(8,128)(2,1)S(1)}, bf16[1024,256]{1,0:T(8,128)(2,1)}, u32[]{:S(2)}, u32[]{:S(2)}) collective-permute-start(bf16[1024,256]{1,0:T(8,128)(2,1)S(1)} %add_convert_fusion.6), channel_id=1, source_target_pairs={{1,0},{2,3},{5,4},{6,7},{9,8},{10,11},{13,12},{14,15},{17,16},{18,... | collective-permute-start | bytes 1572872 | tf_op jit(solution)/shard_map/ppermute | solution.py:836
  205.0 22.0 %collective-permute-start.21 = (bf16[1024,256]{1,0:T(8,128)(2,1)S(1)}, bf16[1024,256]{1,0:T(8,128)(2,1)S(1)}, u32[]{:S(2)}, u32[]{:S(2)}) collective-permute-start(bf16[1024,256]{1,0:T(8,128)(2,1)S(1)} %fusion.4), channel_id=1, source_target_pairs={{0,1},{3,2},{4,5},{7,6},{8,9},{11,10},{12,13},{15,14},{16,17},{19,... | collective-permute-start | bytes 1572872 | tf_op jit(solution)/shard_map/ppermute | solution.py:823
  219.5 8.4 %collective-permute-start.27 = (bf16[1536,256]{1,0:T(8,128)(2,1)S(1)}, bf16[1536,256]{1,0:T(8,128)(2,1)S(1)}, u32[]{:S(2)}, u32[]{:S(2)}) collective-permute-start(bf16[1536,256]{1,0:T(8,128)(2,1)S(1)} %add_convert_fusion.3), channel_id=1, source_target_pairs={{1,2},{2,1},{5,6},{6,5},{9,10},{10,9},{13,14},{14,13},{17,18},{18,... | collective-permute-start | bytes 2359304 | tf_op jit(solution)/shard_map/ppermute | solution.py:831
  220.2 2.0 collective-permute-start.23
  227.2 23.5 %collective-permute-start.26 = (bf16[1024,256]{1,0:T(8,128)(2,1)S(1)}, bf16[1024,256]{1,0:T(8,128)(2,1)S(1)}, u32[]{:S(2)}, u32[]{:S(2)}) collective-permute-start(bf16[1024,256]{1,0:T(8,128)(2,1)S(1)} %add_convert_fusion.5), channel_id=1, source_target_pairs={{1,2},{2,1},{5,6},{6,5},{9,10},{10,9},{13,14},{14,13},{17,18},{18,... | collective-permute-start | bytes 1572872 | tf_op jit(solution)/shard_map/ppermute | solution.py:831
  228.1 31.2 %collective-permute-start.30 = (bf16[1536,256]{1,0:T(8,128)(2,1)S(1)}, bf16[1536,256]{1,0:T(8,128)(2,1)S(1)}, u32[]{:S(2)}, u32[]{:S(2)}) collective-permute-start(bf16[1536,256]{1,0:T(8,128)(2,1)S(1)} %add_convert_fusion.2), channel_id=1, source_target_pairs={{1,0},{2,3},{5,4},{6,7},{9,8},{10,11},{13,12},{14,15},{17,16},{18,... | collective-permute-start | bytes 2359304 | tf_op jit(solution)/shard_map/ppermute | solution.py:836
  229.4 30.9 %collective-permute-start.29 = (f32[2,768]{1,0:T(2,128)S(1)}, f32[2,768]{1,0:T(2,128)S(1)}, u32[]{:S(2)}, u32[]{:S(2)}) collective-permute-start(f32[2,768]{1,0:T(2,128)S(1)} %add.304), channel_id=1, source_target_pairs={{0,1},{1,0},{2,3},{3,2},{4,5},{5,4},{6,7},{7,6},{8,9},{9,8},{10,11... | collective-permute-start | bytes 18440 | tf_op jit(solution)/shard_map/ppermute | solution.py:862
  250.8 19.6 %collective-permute-start.28 = (bf16[1024,256]{1,0:T(8,128)(2,1)S(1)}, bf16[1024,256]{1,0:T(8,128)(2,1)S(1)}, u32[]{:S(2)}, u32[]{:S(2)}) collective-permute-start(bf16[1024,256]{1,0:T(8,128)(2,1)S(1)} %add_convert_fusion.4), channel_id=1, source_target_pairs={{1,0},{2,3},{5,4},{6,7},{9,8},{10,11},{13,12},{14,15},{17,16},{18,... | collective-permute-start | bytes 1572872 | tf_op jit(solution)/shard_map/ppermute | solution.py:836
  260.3 9.5 %collective-permute-start.31 = (f32[2,768]{1,0:T(2,128)S(1)}, f32[2,768]{1,0:T(2,128)S(1)}, u32[]{:S(2)}, u32[]{:S(2)}) collective-permute-start(f32[2,768]{1,0:T(2,128)S(1)} %add.308), channel_id=1, source_target_pairs={{0,2},{1,3},{2,0},{3,1},{4,6},{5,7},{6,4},{7,5},{8,10},{9,11},{10,... | collective-permute-start | bytes 18440 | tf_op jit(solution)/shard_map/ppermute | solution.py:862
  261.0 8.7 %copy-start.2 = (f32[2,768]{1,0:T(2,128)S(1)}, f32[2,768]{1,0:T(2,128)}, u32[]{:S(2)}) copy-start(f32[2,768]{1,0:T(2,128)} %gains_ref.1) | copy-start | bytes 18436
  261.0 8.7 %copy-start.3 = (f32[2,768]{1,0:T(2,128)S(1)}, f32[2,768]{1,0:T(2,128)}, u32[]{:S(2)}) copy-start(f32[2,768]{1,0:T(2,128)} %param.25) | copy-start | bytes 18436
  261.0 8.7 %copy-start.4 = (f32[2,768]{1,0:T(2,128)S(1)}, f32[2,768]{1,0:T(2,128)}, u32[]{:S(2)}) copy-start(f32[2,768]{1,0:T(2,128)} %param.24) | copy-start | bytes 18436

commit v7 on v6

--- a/solution.py
+++ b/solution.py
@@ -321,7 +321,7 @@
                 a_scr[rows, slab] = a_t.T
         return carry
 
-    lax.fori_loop(0, nd, attend, 0)
+    lax.fori_loop(0, nd, attend, 0, unroll=True)
 
     wait_for(w_o, w_sems.at[1])
     for r in range(micro):
@@ -448,7 +448,7 @@
                 )
         return carry
 
-    lax.fori_loop(0, nd, attend_back, 0)
+    lax.fori_loop(0, nd, attend_back, 0, unroll=True)
 
     def token_back(j, carry):
         cols = pl.ds(pl.multiple_of(j * B, B), B)

time: 278 us -> 276 us (level)
  no operation moved by 1% of the time
where the time goes in v7:
time: 276 us
  waiting for transfers between devices  130 us (47%)
  Pallas kernels  78.6 us (28%)
  starting transfers between devices  50.3 us (18%)
  other arithmetic  14.4 us (5%)
    pallas_call x1, Pallas kernels, run_layer(): pl.pallas_call(functools.partial(layer_kernel, micro, own, [p.shape[0] fo...  57.6 us
    ppermute x3, waiting for transfers between devices, reduce_and_step(): lax.ppermute(t[part], 'rep', [(0, 1), (3, 2)])  24.9 us
    ppermute x3, waiting for transfers between devices, reduce_and_step(): lax.ppermute(t, 'fsdp', far_pairs)  22.6 us
    ppermute x1, waiting for transfers between devices, gather_pieces(): last_near = lax.ppermute(weights[half:].astype(BF16), 'fsdp', near_pairs)  21.3 us
    pallas_call x3, Pallas kernels, adam_blocks(): pl.pallas_call(functools.partial(adam_kernel, steps), grid=(sum(steps),),...  21.1 us
    ppermute x1, waiting for transfers between devices, gather_pieces(): first_near = lax.ppermute(weights[:half].astype(BF16), 'fsdp', near_pairs)  19.8 us
    ppermute x5, starting transfers between devices, reduce_and_step(): lax.ppermute(gain, axis, pairs)  18.6 us
    ppermute x3, starting transfers between devices, reduce_and_step(): lax.ppermute(t[part], 'rep', [(0, 1), (3, 2)])  12.9 us
  transfers between devices with their start and end apart: 32, of which 16 were waited for; matrix products, arithmetic and copies ran while one was open for 4% of the time, Pallas kernels for 5%

profile of v7, /device:TPU:0, one launch (start us, length us, event | category | flops | bytes accessed | tf_op | source)
XLA Modules:
  0.0 276.0 jit_solution(15812247661677314332)
XLA Ops:
  0.6 2.2 convert_element_type.180.rest_0_
  2.9 3.0 %collective-permute-start.5 = (bf16[14,256,256]{2,1,0:T(8,128)(2,1)S(1)}, bf16[14,256,256]{2,1,0:T(8,128)(2,1)}, u32[]{:S(2)}, u32[]{:S(2)}) collective-permute-start(bf16[14,256,256]{2,1,0:T(8,128)(2,1)S(1)} %convert_element_type.180.rest_0_), channel_id=1, source_target_pairs={{0,16},{4,12},{8,24},{12,4},{16,0},{20,28},{24,8},{28,20},{1,17},{... | collective-permute-start | bytes 5505032 | tf_op jit(solution)/shard_map/ppermute | solution.py:673
  6.1 1.6 collective-permute-start.2
  8.2 21.3 %collective-permute-done.2.rest_3_ = bf16[7,256,256]{2,1,0:T(8,128)(2,1)S(1)} collective-permute-done((bf16[7,256,256]{2,1,0:T(8,128)(2,1)S(1)}, bf16[7,256,256]{2,1,0:T(8,128)(2,1)S(1)}, u32[]{:S(2)}, u32[]{:S(2)}) %collective-permute-start.2) | collective-permute-done | bytes 917536 | tf_op jit(solution)/shard_map/ppermute | solution.py:672
  29.4 19.8 %collective-permute-done.1.rest_2_ = bf16[7,256,256]{2,1,0:T(8,128)(2,1)} collective-permute-done((bf16[7,256,256]{2,1,0:T(8,128)(2,1)S(1)}, bf16[7,256,256]{2,1,0:T(8,128)(2,1)}, u32[]{:S(2)}, u32[]{:S(2)}) %collective-permute-start.1) | collective-permute-done | bytes 917536 | tf_op jit(solution)/shard_map/ppermute | solution.py:671
  49.7 7.0 %collective-permute-done.8.rest_9_ = bf16[7,256,256]{2,1,0:T(8,128)(2,1)} collective-permute-done((bf16[7,256,256]{2,1,0:T(8,128)(2,1)S(1)}, bf16[7,256,256]{2,1,0:T(8,128)(2,1)}, u32[]{:S(2)}, u32[]{:S(2)}) %collective-permute-start.8) | collective-permute-done | bytes 917536 | tf_op jit(solution)/shard_map/ppermute | solution.py:675
  57.3 9.3 %collective-permute-done.7.rest_8_ = bf16[7,256,256]{2,1,0:T(8,128)(2,1)} collective-permute-done((bf16[7,256,256]{2,1,0:T(8,128)(2,1)}, bf16[7,256,256]{2,1,0:T(8,128)(2,1)}, u32[]{:S(2)}, u32[]{:S(2)}) %collective-permute-start.7) | collective-permute-done | bytes 917536 | tf_op jit(solution)/shard_map/ppermute | solution.py:674
  66.6 0.8 copy.35
  67.5 0.6 concatenate.7.slot_ref
  68.2 0.6 select_reduce_fusion.base_ref
  69.4 57.6 %layer.1 = (bf16[512,768]{1,0:T(8,128)(2,1)}, bf16[512,768]{1,0:T(8,128)(2,1)}, f32[2,768]{1,0:T(2,128)}, bf16[16,256,256]{2,1,0:T(8,128)(2,1)}, bf16[16,256,256...) custom-call(s32[108]{0:T(128)} %index_ref.1, s32[8]{0:T(128)} %select_reduce_fusion.base_ref, ...), custom_call_target="tpu_custom_call" | custom-call | flops 23000000512 | bytes 32000000 | tf_op jit(solution)/shard_map/layer/pallas_call | solution.py:479
  127.2 4.2 %collective-permute-done.11 = bf16[16,256,256]{2,1,0:T(8,128)(2,1)S(1)} collective-permute-done((bf16[16,256,256]{2,1,0:T(8,128)(2,1)}, bf16[16,256,256]{2,1,0:T(8,128)(2,1)S(1)}, u32[]{:S(2)}, u32[]{:S(2)}) %collective-permute-start.11) | collective-permute-done | bytes 2097184 | tf_op jit(solution)/shard_map/ppermute | solution.py:647
  131.4 1.5 add_convert_fusion.1
  133.2 1.1 collective-permute-start.14
  134.3 7.6 %collective-permute-done.12 = bf16[40,256,256]{2,1,0:T(8,128)(2,1)S(1)} collective-permute-done((bf16[40,256,256]{2,1,0:T(8,128)(2,1)}, bf16[40,256,256]{2,1,0:T(8,128)(2,1)S(1)}, u32[]{:S(2)}, u32[]{:S(2)}) %collective-permute-start.12) | collective-permute-done | bytes 5242912 | tf_op jit(solution)/shard_map/ppermute | solution.py:647
  141.9 2.7 add_convert_fusion
  144.6 1.2 collective-permute-start.13
  145.8 1.8 collective-permute-start.15
  147.5 2.0 collective-permute-done.15
  149.8 1.8 collective-permute-start.16
  151.6 13.1 %collective-permute-done.16 = bf16[1024,256]{1,0:T(8,128)(2,1)S(1)} collective-permute-done((bf16[1024,256]{1,0:T(8,128)(2,1)S(1)}, bf16[1024,256]{1,0:T(8,128)(2,1)S(1)}, u32[]{:S(2)}, u32[]{:S(2)}) %collective-permute-start.16) | collective-permute-done | bytes 524320 | tf_op jit(solution)/shard_map/ppermute | solution.py:798
  165.1 3.7 %collective-permute-start.17 = (bf16[1024,256]{1,0:T(8,128)(2,1)S(1)}, bf16[1024,256]{1,0:T(8,128)(2,1)S(1)}, u32[]{:S(2)}, u32[]{:S(2)}) collective-permute-start(bf16[1024,256]{1,0:T(8,128)(2,1)S(1)} %fusion.7), channel_id=1, source_target_pairs={{0,1},{3,2},{4,5},{7,6},{8,9},{11,10},{12,13},{15,14},{16,17},{19,... | collective-permute-start | bytes 1572872 | tf_op jit(solution)/shard_map/ppermute | solution.py:823
  168.8 10.1 %collective-permute-done.17 = bf16[1024,256]{1,0:T(8,128)(2,1)S(1)} collective-permute-done((bf16[1024,256]{1,0:T(8,128)(2,1)S(1)}, bf16[1024,256]{1,0:T(8,128)(2,1)S(1)}, u32[]{:S(2)}, u32[]{:S(2)}) %collective-permute-start.17) | collective-permute-done | bytes 524320 | tf_op jit(solution)/shard_map/ppermute | solution.py:823
  179.0 0.7 collective-permute-start.20
  179.7 2.3 collective-permute-done.13
  182.4 2.0 collective-permute-start.19
  185.0 9.5 %collective-permute-done.19 = bf16[1536,256]{1,0:T(8,128)(2,1)S(1)} collective-permute-done((bf16[1536,256]{1,0:T(8,128)(2,1)S(1)}, bf16[1536,256]{1,0:T(8,128)(2,1)S(1)}, u32[]{:S(2)}, u32[]{:S(2)}) %collective-permute-start.19) | collective-permute-done | bytes 786464 | tf_op jit(solution)/shard_map/ppermute | solution.py:798
  194.9 5.0 %collective-permute-start.25 = (bf16[1536,256]{1,0:T(8,128)(2,1)S(1)}, bf16[1536,256]{1,0:T(8,128)(2,1)S(1)}, u32[]{:S(2)}, u32[]{:S(2)}) collective-permute-start(bf16[1536,256]{1,0:T(8,128)(2,1)S(1)} %fusion.1), channel_id=1, source_target_pairs={{0,1},{3,2},{4,5},{7,6},{8,9},{11,10},{12,13},{15,14},{16,17},{19,... | collective-permute-start | bytes 2359304 | tf_op jit(solution)/shard_map/ppermute | solution.py:823
  199.9 0.9 collective-permute-start.22
  200.8 1.3 collective-permute-start.24
  202.4 1.2 collective-permute-done.22
  203.6 4.2 %collective-permute-start.21 = (bf16[1024,256]{1,0:T(8,128)(2,1)S(1)}, bf16[1024,256]{1,0:T(8,128)(2,1)S(1)}, u32[]{:S(2)}, u32[]{:S(2)}) collective-permute-start(bf16[1024,256]{1,0:T(8,128)(2,1)S(1)} %fusion.4), channel_id=1, source_target_pairs={{0,1},{3,2},{4,5},{7,6},{8,9},{11,10},{12,13},{15,14},{16,17},{19,... | collective-permute-start | bytes 1572872 | tf_op jit(solution)/shard_map/ppermute | solution.py:823
  207.8 10.0 %collective-permute-done.25 = bf16[1536,256]{1,0:T(8,128)(2,1)S(1)} collective-permute-done((bf16[1536,256]{1,0:T(8,128)(2,1)S(1)}, bf16[1536,256]{1,0:T(8,128)(2,1)S(1)}, u32[]{:S(2)}, u32[]{:S(2)}) %collective-permute-start.25) | collective-permute-done | bytes 786464 | tf_op jit(solution)/shard_map/ppermute | solution.py:823
  218.0 0.7 collective-permute-start.27
  218.9 1.9 broadcast_select_fusion.2.rest_0_
  220.8 4.8 %collective-permute-done.21 = bf16[1024,256]{1,0:T(8,128)(2,1)S(1)} collective-permute-done((bf16[1024,256]{1,0:T(8,128)(2,1)S(1)}, bf16[1024,256]{1,0:T(8,128)(2,1)S(1)}, u32[]{:S(2)}, u32[]{:S(2)}) %collective-permute-start.21) | collective-permute-done | bytes 524320 | tf_op jit(solution)/shard_map/ppermute | solution.py:823
  225.7 0.7 collective-permute-start.26
  226.6 1.3 collective-permute-start.30
  227.9 15.0 %collective-permute-start.29 = (f32[2,768]{1,0:T(2,128)S(1)}, f32[2,768]{1,0:T(2,128)S(1)}, u32[]{:S(2)}, u32[]{:S(2)}) collective-permute-start(f32[2,768]{1,0:T(2,128)S(1)} %add.304), channel_id=1, source_target_pairs={{0,1},{1,0},{2,3},{3,2},{4,5},{5,4},{6,7},{7,6},{8,9},{9,8},{10,11... | collective-permute-start | bytes 18440 | tf_op jit(solution)/shard_map/ppermute | solution.py:862
  243.0 6.3 %adam.3 = (f32[14,256,256]{2,1,0:T(8,128)}, f32[14,256,256]{2,1,0:T(8,128)}, f32[14,256,256]{2,1,0:T(8,128)}, f32[14,256,256]{2,1,0:T(8,128)}, bf16[14,256,256]{2,1,0:T(8,128)(2,1)}) custom-call(f32[14,256,256]{2,1,0:T(8,128)} %weight_ref.5, f32[14,256,256]{2,1,0:T(8,128)} %first_ref.5, f32[14,256,256]{2,1,0:T(8,128)} %second_ref.5, ...), custom_call_target="tpu_custom_call" | custom-call | flops 805306368 | bytes 11010048 | tf_op jit(solution)/shard_map/adam/pallas_call | solution.py:598
  249.4 1.3 collective-permute-start.28
  250.7 7.1 %collective-permute-done.30 = bf16[1536,256]{1,0:T(8,128)(2,1)S(1)} collective-permute-done((bf16[1536,256]{1,0:T(8,128)(2,1)S(1)}, bf16[1536,256]{1,0:T(8,128)(2,1)S(1)}, u32[]{:S(2)}, u32[]{:S(2)}) %collective-permute-start.30) | collective-permute-done | bytes 786464 | tf_op jit(solution)/shard_map/ppermute | solution.py:836
  257.9 1.0 broadcast_select_fusion.rest_0_
  258.8 0.8 collective-permute-start.31
  259.6 8.5 %adam.4 = (f32[14,256,256]{2,1,0:T(8,128)}, f32[14,256,256]{2,1,0:T(8,128)}, f32[14,256,256]{2,1,0:T(8,128)}, f32[14,256,256]{2,1,0:T(8,128)}, bf16[14,256,256]{2,1,0:T(8,128)(2,1)}) custom-call(f32[14,256,256]{2,1,0:T(8,128)} %weight_ref.5, ...), custom_call_target="tpu_custom_call", output_to_operand_aliasing={{0}: (6, {}), {1}: (7, {}), {2}: (8, {}), {3}: (9, {}), {4}... | custom-call | flops 1207959552 | bytes 16515072 | tf_op jit(solution)/shard_map/adam/pallas_call | solution.py:598
  268.2 0.6 multiply_subtract_fusion
  268.8 0.9 broadcast_select_fusion.1.rest_0_
  269.7 6.3 %adam.5 = (f32[14,256,256]{2,1,0:T(8,128)}, f32[14,256,256]{2,1,0:T(8,128)}, f32[14,256,256]{2,1,0:T(8,128)}, f32[14,256,256]{2,1,0:T(8,128)}, bf16[14,256,256]{2,1,0:T(8,128)(2,1)}) custom-call(f32[14,256,256]{2,1,0:T(8,128)} %weight_ref.5, ...), custom_call_target="tpu_custom_call", output_to_operand_aliasing={{0}: (6, {}), {1}: (7, {}), {2}: (8, {}), {3}: (9, {}), {4}... | custom-call | flops 805306368 | bytes 11010048 | tf_op jit(solution)/shard_map/adam/pallas_call | solution.py:598
  (84 shorter events, 6.1 us)
Async XLA Ops:
  2.9 66.5 %copy-start = (bf16[14,256,256]{2,1,0:T(8,128)(2,1)}, bf16[14,256,256]{2,1,0:T(8,128)(2,1)S(1)}, u32[]{:S(2)}) copy-start(bf16[14,256,256]{2,1,0:T(8,128)(2,1)S(1)} %convert_element_type.180.rest_0_) | copy-start | bytes 5505028
  2.9 63.7 %copy-start.6 = (s32[2,256]{1,0:T(2,128)S(1)}, s32[2,256]{1,0:T(2,128)}, u32[]{:S(2)}) copy-start(s32[2,256]{1,0:T(2,128)} %segments_ref.1) | copy-start | bytes 6148
  2.9 46.3 %collective-permute-start.5 = (bf16[14,256,256]{2,1,0:T(8,128)(2,1)S(1)}, bf16[14,256,256]{2,1,0:T(8,128)(2,1)}, u32[]{:S(2)}, u32[]{:S(2)}) collective-permute-start(bf16[14,256,256]{2,1,0:T(8,128)(2,1)S(1)} %convert_element_type.180.rest_0_), channel_id=1, source_target_pairs={{0,16},{4,12},{8,24},{12,4},{16,0},{20,28},{24,8},{28,20},{1,17},{... | collective-permute-start | bytes 5505032 | tf_op jit(solution)/shard_map/ppermute | solution.py:673
  6.1 23.4 %collective-permute-start.2 = (bf16[7,256,256]{2,1,0:T(8,128)(2,1)S(1)}, bf16[7,256,256]{2,1,0:T(8,128)(2,1)S(1)}, u32[]{:S(2)}, u32[]{:S(2)}) collective-permute-start(bf16[7,256,256]{2,1,0:T(8,128)(2,1)S(1)} %get-tuple-element.206), channel_id=1, source_target_pairs={{0,8},{4,20},{8,0},{12,28},{16,24},{20,4},{24,16},{28,12},{1,9},{5... | collective-permute-start | bytes 2752520 | tf_op jit(solution)/shard_map/ppermute | solution.py:672
  7.6 41.5 %collective-permute-start.1 = (bf16[7,256,256]{2,1,0:T(8,128)(2,1)S(1)}, bf16[7,256,256]{2,1,0:T(8,128)(2,1)}, u32[]{:S(2)}, u32[]{:S(2)}) collective-permute-start(bf16[7,256,256]{2,1,0:T(8,128)(2,1)S(1)} %get-tuple-element.207), channel_id=1, source_target_pairs={{0,8},{4,20},{8,0},{12,28},{16,24},{20,4},{24,16},{28,12},{1,9},{5... | collective-permute-start | bytes 2752520 | tf_op jit(solution)/shard_map/ppermute | solution.py:671
  29.4 40.0 %copy-start.7 = (bf16[7,256,256]{2,1,0:T(8,128)(2,1)}, bf16[7,256,256]{2,1,0:T(8,128)(2,1)S(1)}, u32[]{:S(2)}) copy-start(bf16[7,256,256]{2,1,0:T(8,128)(2,1)S(1)} %collective-permute-done.2.rest_3_) | copy-start | bytes 2752516
  29.4 27.3 %collective-permute-start.8 = (bf16[7,256,256]{2,1,0:T(8,128)(2,1)S(1)}, bf16[7,256,256]{2,1,0:T(8,128)(2,1)}, u32[]{:S(2)}, u32[]{:S(2)}) collective-permute-start(bf16[7,256,256]{2,1,0:T(8,128)(2,1)S(1)} %collective-permute-done.2.rest_3_), channel_id=1, source_target_pairs={{0,16},{4,12},{8,24},{12,4},{16,0},{20,28},{24,8},{28,20},{1,17},{... | collective-permute-start | bytes 2752520 | tf_op jit(solution)/shard_map/ppermute | solution.py:675
  29.4 27.3 %collective-permute-start.4 = (bf16[7,256,256]{2,1,0:T(8,128)(2,1)S(1)}, bf16[7,256,256]{2,1,0:T(8,128)(2,1)}, u32[]{:S(2)}, u32[]{:S(2)}) collective-permute-start(bf16[7,256,256]{2,1,0:T(8,128)(2,1)S(1)} %collective-permute-done.2.rest_3_), channel_id=1, source_target_pairs={{0,4},{4,0},{8,12},{12,8},{16,20},{20,16},{24,28},{28,24},{1,5},{5... | collective-permute-start | bytes 2752520 | tf_op jit(solution)/shard_map/ppermute | solution.py:647
  49.2 17.4 %collective-permute-start.7 = (bf16[7,256,256]{2,1,0:T(8,128)(2,1)}, bf16[7,256,256]{2,1,0:T(8,128)(2,1)}, u32[]{:S(2)}, u32[]{:S(2)}) collective-permute-start(bf16[7,256,256]{2,1,0:T(8,128)(2,1)} %collective-permute-done.1.rest_2_), channel_id=1, source_target_pairs={{0,16},{4,12},{8,24},{12,4},{16,0},{20,28},{24,8},{28,20},{1,17},{... | collective-permute-start | bytes 2752520 | tf_op jit(solution)/shard_map/ppermute | solution.py:674
  49.2 19.6 %collective-permute-start = (bf16[14,256,256]{2,1,0:T(8,128)(2,1)S(1)}, bf16[14,256,256]{2,1,0:T(8,128)(2,1)}, u32[]{:S(2)}, u32[]{:S(2)}) collective-permute-start(bf16[14,256,256]{2,1,0:T(8,128)(2,1)S(1)} %convert_element_type.180.rest_0_), channel_id=1, source_target_pairs={{0,4},{4,0},{8,12},{12,8},{16,20},{20,16},{24,28},{28,24},{1,5},{5... | collective-permute-start | bytes 5505032 | tf_op jit(solution)/shard_map/ppermute | solution.py:647
  49.2 20.2 %collective-permute-start.6 = (bf16[14,256,256]{2,1,0:T(8,128)(2,1)}, bf16[14,256,256]{2,1,0:T(8,128)(2,1)}, u32[]{:S(2)}, u32[]{:S(2)}) collective-permute-start(bf16[14,256,256]{2,1,0:T(8,128)(2,1)} %collective-permute-done.5.rest_6_), channel_id=1, source_target_pairs={{0,4},{4,0},{8,12},{12,8},{16,20},{20,16},{24,28},{28,24},{1,5},{5... | collective-permute-start | bytes 5505032 | tf_op jit(solution)/shard_map/ppermute | solution.py:647
  56.8 12.0 %collective-permute-start.3 = (bf16[7,256,256]{2,1,0:T(8,128)(2,1)}, bf16[7,256,256]{2,1,0:T(8,128)(2,1)}, u32[]{:S(2)}, u32[]{:S(2)}) collective-permute-start(bf16[7,256,256]{2,1,0:T(8,128)(2,1)} %collective-permute-done.1.rest_2_), channel_id=1, source_target_pairs={{0,4},{4,0},{8,12},{12,8},{16,20},{20,16},{24,28},{28,24},{1,5},{5... | collective-permute-start | bytes 2752520 | tf_op jit(solution)/shard_map/ppermute | solution.py:647
  56.8 12.0 %collective-permute-start.10 = (bf16[7,256,256]{2,1,0:T(8,128)(2,1)}, bf16[7,256,256]{2,1,0:T(8,128)(2,1)}, u32[]{:S(2)}, u32[]{:S(2)}) collective-permute-start(bf16[7,256,256]{2,1,0:T(8,128)(2,1)} %collective-permute-done.8.rest_9_), channel_id=1, source_target_pairs={{0,4},{4,0},{8,12},{12,8},{16,20},{20,16},{24,28},{28,24},{1,5},{5... | collective-permute-start | bytes 2752520 | tf_op jit(solution)/shard_map/ppermute | solution.py:647
  66.6 2.8 %collective-permute-start.9 = (bf16[7,256,256]{2,1,0:T(8,128)(2,1)}, bf16[7,256,256]{2,1,0:T(8,128)(2,1)}, u32[]{:S(2)}, u32[]{:S(2)}) collective-permute-start(bf16[7,256,256]{2,1,0:T(8,128)(2,1)} %collective-permute-done.7.rest_8_), channel_id=1, source_target_pairs={{0,4},{4,0},{8,12},{12,8},{16,20},{20,16},{24,28},{28,24},{1,5},{5... | collective-permute-start | bytes 2752520 | tf_op jit(solution)/shard_map/ppermute | solution.py:647
  127.0 4.4 %collective-permute-start.11 = (bf16[16,256,256]{2,1,0:T(8,128)(2,1)}, bf16[16,256,256]{2,1,0:T(8,128)(2,1)S(1)}, u32[]{:S(2)}, u32[]{:S(2)}) collective-permute-start(bf16[16,256,256]{2,1,0:T(8,128)(2,1)} %get-tuple-element.112), channel_id=1, source_target_pairs={{0,4},{4,0},{8,12},{12,8},{16,20},{20,16},{24,28},{28,24},{1,5},{5... | collective-permute-start | bytes 6291464 | tf_op jit(solution)/shard_map/ppermute | solution.py:647
  132.9 12.8 %copy-start.5 = (f32[2,768]{1,0:T(2,128)S(1)}, f32[2,768]{1,0:T(2,128)}, u32[]{:S(2)}) copy-start(f32[2,768]{1,0:T(2,128)} %get-tuple-element.120) | copy-start | bytes 18436
  132.9 16.6 %copy-start.1 = (bf16[16,256,256]{2,1,0:T(8,128)(2,1)S(1)}, bf16[16,256,256]{2,1,0:T(8,128)(2,1)}, u32[]{:S(2)}) copy-start(bf16[16,256,256]{2,1,0:T(8,128)(2,1)} %get-tuple-element.126) | copy-start | bytes 6291460
  133.0 8.9 %collective-permute-start.12 = (bf16[40,256,256]{2,1,0:T(8,128)(2,1)}, bf16[40,256,256]{2,1,0:T(8,128)(2,1)S(1)}, u32[]{:S(2)}, u32[]{:S(2)}) collective-permute-start(bf16[40,256,256]{2,1,0:T(8,128)(2,1)} %get-tuple-element.115), channel_id=1, source_target_pairs={{0,4},{4,0},{8,12},{12,8},{16,20},{20,16},{24,28},{28,24},{1,5},{5... | collective-permute-start | bytes 15728648 | tf_op jit(solution)/shard_map/ppermute | solution.py:647
  133.2 16.3 %collective-permute-start.14 = (bf16[2048,256]{1,0:T(8,128)(2,1)S(1)}, bf16[2048,256]{1,0:T(8,128)(2,1)S(1)}, u32[]{:S(2)}, u32[]{:S(2)}) collective-permute-start(bf16[2048,256]{1,0:T(8,128)(2,1)S(1)} %bitcast.40), channel_id=1, source_target_pairs={{0,8},{4,20},{8,0},{12,28},{16,24},{20,4},{24,16},{28,12},{1,9},{5... | collective-permute-start | bytes 3145736 | tf_op jit(solution)/shard_map/ppermute | solution.py:780
  141.9 40.1 %slice-start = ((s8[5242880]{0:T(1024)(128)(4,1)}), s8[1048576]{0:T(1024)(128)(4,1)S(1)}, s32[]{:S(2)}) async-start(s8[5242880]{0:T(1024)(128)(4,1)} %bitcast.37), calls=%async_computation | async-start | bytes 2097152
  144.6 37.4 %collective-permute-start.13 = (bf16[5120,256]{1,0:T(8,128)(2,1)S(1)}, bf16[5120,256]{1,0:T(8,128)(2,1)S(1)}, u32[]{:S(2)}, u32[]{:S(2)}) collective-permute-start(bf16[5120,256]{1,0:T(8,128)(2,1)S(1)} %bitcast.39), channel_id=1, source_target_pairs={{0,8},{4,20},{8,0},{12,28},{16,24},{20,4},{24,16},{28,12},{1,9},{5... | collective-permute-start | bytes 7864328 | tf_op jit(solution)/shard_map/ppermute | solution.py:780
  145.8 3.8 %collective-permute-start.15 = (f32[2,768]{1,0:T(2,128)S(1)}, f32[2,768]{1,0:T(2,128)S(1)}, u32[]{:S(2)}, u32[]{:S(2)}) collective-permute-start(f32[2,768]{1,0:T(2,128)S(1)} %copy-done.5), channel_id=1, source_target_pairs={{0,16},{4,12},{8,24},{12,4},{16,0},{20,28},{24,8},{28,20},{1,17},{... | collective-permute-start | bytes 18440 | tf_op jit(solution)/shard_map/ppermute | solution.py:862
  149.5 32.5 %slice-start.1 = ((s8[5242880]{0:T(1024)(128)(4,1)}), s8[4194304]{0:T(1024)(128)(4,1)S(1)}, s32[]{:S(2)}) async-start(s8[5242880]{0:T(1024)(128)(4,1)} %bitcast.37), calls=%async_computation.1 | async-start | bytes 8388608
  149.8 14.9 %collective-permute-start.16 = (bf16[1024,256]{1,0:T(8,128)(2,1)S(1)}, bf16[1024,256]{1,0:T(8,128)(2,1)S(1)}, u32[]{:S(2)}, u32[]{:S(2)}) collective-permute-start(bf16[1024,256]{1,0:T(8,128)(2,1)S(1)} %fusion.8), channel_id=1, source_target_pairs={{0,16},{4,12},{8,24},{12,4},{16,0},{20,28},{24,8},{28,20},{1,17},{... | collective-permute-start | bytes 1572872 | tf_op jit(solution)/shard_map/ppermute | solution.py:798
  165.1 13.8 %collective-permute-start.17 = (bf16[1024,256]{1,0:T(8,128)(2,1)S(1)}, bf16[1024,256]{1,0:T(8,128)(2,1)S(1)}, u32[]{:S(2)}, u32[]{:S(2)}) collective-permute-start(bf16[1024,256]{1,0:T(8,128)(2,1)S(1)} %fusion.7), channel_id=1, source_target_pairs={{0,1},{3,2},{4,5},{7,6},{8,9},{11,10},{12,13},{15,14},{16,17},{19,... | collective-permute-start | bytes 1572872 | tf_op jit(solution)/shard_map/ppermute | solution.py:823
  179.0 5.7 %collective-permute-start.20 = (bf16[1024,256]{1,0:T(8,128)(2,1)S(1)}, bf16[1024,256]{1,0:T(8,128)(2,1)S(1)}, u32[]{:S(2)}, u32[]{:S(2)}) collective-permute-start(bf16[1024,256]{1,0:T(8,128)(2,1)S(1)} %add_convert_fusion.7), channel_id=1, source_target_pairs={{1,2},{2,1},{5,6},{6,5},{9,10},{10,9},{13,14},{14,13},{17,18},{18,... | collective-permute-start | bytes 1572872 | tf_op jit(solution)/shard_map/ppermute | solution.py:831
  182.4 12.1 %collective-permute-start.19 = (bf16[1536,256]{1,0:T(8,128)(2,1)S(1)}, bf16[1536,256]{1,0:T(8,128)(2,1)S(1)}, u32[]{:S(2)}, u32[]{:S(2)}) collective-permute-start(bf16[1536,256]{1,0:T(8,128)(2,1)S(1)} %fusion.2), channel_id=1, source_target_pairs={{0,16},{4,12},{8,24},{12,4},{16,0},{20,28},{24,8},{28,20},{1,17},{... | collective-permute-start | bytes 2359304 | tf_op jit(solution)/shard_map/ppermute | solution.py:798
  184.7 17.4 %collective-permute-start.18 = (bf16[1024,256]{1,0:T(8,128)(2,1)S(1)}, bf16[1024,256]{1,0:T(8,128)(2,1)S(1)}, u32[]{:S(2)}, u32[]{:S(2)}) collective-permute-start(bf16[1024,256]{1,0:T(8,128)(2,1)S(1)} %fusion.5), channel_id=1, source_target_pairs={{0,16},{4,12},{8,24},{12,4},{16,0},{20,28},{24,8},{28,20},{1,17},{... | collective-permute-start | bytes 1572872 | tf_op jit(solution)/shard_map/ppermute | solution.py:798
  194.9 22.9 %collective-permute-start.25 = (bf16[1536,256]{1,0:T(8,128)(2,1)S(1)}, bf16[1536,256]{1,0:T(8,128)(2,1)S(1)}, u32[]{:S(2)}, u32[]{:S(2)}) collective-permute-start(bf16[1536,256]{1,0:T(8,128)(2,1)S(1)} %fusion.1), channel_id=1, source_target_pairs={{0,1},{3,2},{4,5},{7,6},{8,9},{11,10},{12,13},{15,14},{16,17},{19,... | collective-permute-start | bytes 2359304 | tf_op jit(solution)/shard_map/ppermute | solution.py:823
  199.9 3.7 %collective-permute-start.22 = (f32[2,768]{1,0:T(2,128)S(1)}, f32[2,768]{1,0:T(2,128)S(1)}, u32[]{:S(2)}, u32[]{:S(2)}) collective-permute-start(f32[2,768]{1,0:T(2,128)S(1)} %add.278), channel_id=1, source_target_pairs={{0,8},{4,20},{8,0},{12,28},{16,24},{20,4},{24,16},{28,12},{1,9},{5... | collective-permute-start | bytes 18440 | tf_op jit(solution)/shard_map/ppermute | solution.py:862
  200.8 18.1 %collective-permute-start.24 = (bf16[1024,256]{1,0:T(8,128)(2,1)S(1)}, bf16[1024,256]{1,0:T(8,128)(2,1)}, u32[]{:S(2)}, u32[]{:S(2)}) collective-permute-start(bf16[1024,256]{1,0:T(8,128)(2,1)S(1)} %add_convert_fusion.6), channel_id=1, source_target_pairs={{1,0},{2,3},{5,4},{6,7},{9,8},{10,11},{13,12},{14,15},{17,16},{18,... | collective-permute-start | bytes 1572872 | tf_op jit(solution)/shard_map/ppermute | solution.py:836
  203.6 22.0 %collective-permute-start.21 = (bf16[1024,256]{1,0:T(8,128)(2,1)S(1)}, bf16[1024,256]{1,0:T(8,128)(2,1)S(1)}, u32[]{:S(2)}, u32[]{:S(2)}) collective-permute-start(bf16[1024,256]{1,0:T(8,128)(2,1)S(1)} %fusion.4), channel_id=1, source_target_pairs={{0,1},{3,2},{4,5},{7,6},{8,9},{11,10},{12,13},{15,14},{16,17},{19,... | collective-permute-start | bytes 1572872 | tf_op jit(solution)/shard_map/ppermute | solution.py:823
  218.0 8.4 %collective-permute-start.27 = (bf16[1536,256]{1,0:T(8,128)(2,1)S(1)}, bf16[1536,256]{1,0:T(8,128)(2,1)S(1)}, u32[]{:S(2)}, u32[]{:S(2)}) collective-permute-start(bf16[1536,256]{1,0:T(8,128)(2,1)S(1)} %add_convert_fusion.3), channel_id=1, source_target_pairs={{1,2},{2,1},{5,6},{6,5},{9,10},{10,9},{13,14},{14,13},{17,18},{18,... | collective-permute-start | bytes 2359304 | tf_op jit(solution)/shard_map/ppermute | solution.py:831
  218.8 2.0 collective-permute-start.23
  225.7 23.6 %collective-permute-start.26 = (bf16[1024,256]{1,0:T(8,128)(2,1)S(1)}, bf16[1024,256]{1,0:T(8,128)(2,1)S(1)}, u32[]{:S(2)}, u32[]{:S(2)}) collective-permute-start(bf16[1024,256]{1,0:T(8,128)(2,1)S(1)} %add_convert_fusion.5), channel_id=1, source_target_pairs={{1,2},{2,1},{5,6},{6,5},{9,10},{10,9},{13,14},{14,13},{17,18},{18,... | collective-permute-start | bytes 1572872 | tf_op jit(solution)/shard_map/ppermute | solution.py:831
  226.6 31.2 %collective-permute-start.30 = (bf16[1536,256]{1,0:T(8,128)(2,1)S(1)}, bf16[1536,256]{1,0:T(8,128)(2,1)S(1)}, u32[]{:S(2)}, u32[]{:S(2)}) collective-permute-start(bf16[1536,256]{1,0:T(8,128)(2,1)S(1)} %add_convert_fusion.2), channel_id=1, source_target_pairs={{1,0},{2,3},{5,4},{6,7},{9,8},{10,11},{13,12},{14,15},{17,16},{18,... | collective-permute-start | bytes 2359304 | tf_op jit(solution)/shard_map/ppermute | solution.py:836
  227.9 30.9 %collective-permute-start.29 = (f32[2,768]{1,0:T(2,128)S(1)}, f32[2,768]{1,0:T(2,128)S(1)}, u32[]{:S(2)}, u32[]{:S(2)}) collective-permute-start(f32[2,768]{1,0:T(2,128)S(1)} %add.304), channel_id=1, source_target_pairs={{0,1},{1,0},{2,3},{3,2},{4,5},{5,4},{6,7},{7,6},{8,9},{9,8},{10,11... | collective-permute-start | bytes 18440 | tf_op jit(solution)/shard_map/ppermute | solution.py:862
  249.4 19.4 %collective-permute-start.28 = (bf16[1024,256]{1,0:T(8,128)(2,1)S(1)}, bf16[1024,256]{1,0:T(8,128)(2,1)S(1)}, u32[]{:S(2)}, u32[]{:S(2)}) collective-permute-start(bf16[1024,256]{1,0:T(8,128)(2,1)S(1)} %add_convert_fusion.4), channel_id=1, source_target_pairs={{1,0},{2,3},{5,4},{6,7},{9,8},{10,11},{13,12},{14,15},{17,16},{18,... | collective-permute-start | bytes 1572872 | tf_op jit(solution)/shard_map/ppermute | solution.py:836
  258.8 9.3 %collective-permute-start.31 = (f32[2,768]{1,0:T(2,128)S(1)}, f32[2,768]{1,0:T(2,128)S(1)}, u32[]{:S(2)}, u32[]{:S(2)}) collective-permute-start(f32[2,768]{1,0:T(2,128)S(1)} %add.308), channel_id=1, source_target_pairs={{0,2},{1,3},{2,0},{3,1},{4,6},{5,7},{6,4},{7,5},{8,10},{9,11},{10,... | collective-permute-start | bytes 18440 | tf_op jit(solution)/shard_map/ppermute | solution.py:862
  259.6 8.5 %copy-start.2 = (f32[2,768]{1,0:T(2,128)S(1)}, f32[2,768]{1,0:T(2,128)}, u32[]{:S(2)}) copy-start(f32[2,768]{1,0:T(2,128)} %gains_ref.1) | copy-start | bytes 18436
  259.6 8.5 %copy-start.3 = (f32[2,768]{1,0:T(2,128)S(1)}, f32[2,768]{1,0:T(2,128)}, u32[]{:S(2)}) copy-start(f32[2,768]{1,0:T(2,128)} %param.25) | copy-start | bytes 18436
  259.6 8.5 %copy-start.4 = (f32[2,768]{1,0:T(2,128)S(1)}, f32[2,768]{1,0:T(2,128)}, u32[]{:S(2)}) copy-start(f32[2,768]{1,0:T(2,128)} %param.24) | copy-start | bytes 18436

commit v8 on v7

--- a/solution.py
+++ b/solution.py
@@ -720,12 +720,14 @@
 
 GROUPS = (((4,),), ((6,), (4,)))
 ORDER = (
-    "grads0 grads1 core0 gain_far near_sum0 near0 core1 near_sum1 near1 gain1 far_sum0_0 far0_0 plane_sum0_0 "
-    "inward0_0a halfway0_0a middle0_0a far_sum1_0 far1_0 far_sum1_1 far1_1 gain_near whole0_0a outward0_0a "
-    "plane_sum1_0 inward1_0a plane_sum1_1 inward1_1a gain2 gain_core halfway1_0a middle1_0a final0_0a gain3 "
-    "gain_pair halfway1_1a middle1_1a whole1_0a outward1_0a step0_0 whole1_1a outward1_1a final1_0a gain4 "
-    "gain_line step1_0 gain5 final1_1a step1_1"
-).split()
+    "grads0", "grads1", "core0", "gain_far", "near_sum0", "near0", "core1", "near_sum1", "near1",
+    "gain1", "far_sum0_0", "far0_0", "plane_sum0_0", "inward0_0a", "halfway0_0a", "middle0_0a",
+    "far_sum1_0", "far1_0", "far_sum1_1", "far1_1", "gain_near", "whole0_0a", "outward0_0a",
+    "plane_sum1_0", "inward1_0a", "plane_sum1_1", "inward1_1a", "gain2", "gain_core", "halfway1_0a",
+    "middle1_0a", "final0_0a", "gain3", "gain_pair", "halfway1_1a", "middle1_1a", "whole1_0a",
+    "outward1_0a", "step0_0", "whole1_1a", "outward1_1a", "final1_0a", "gain4", "gain_line",
+    "step1_0", "gain5", "final1_1a", "step1_1",
+)
 
 
 def group_sizes():

time: 276 us -> 276 us (level)
  no operation moved by 1% of the time
where the time goes in v8:
time: 276 us
  waiting for transfers between devices  130 us (47%)
  Pallas kernels  78.6 us (28%)
  starting transfers between devices  50.3 us (18%)
  other arithmetic  14.4 us (5%)
    pallas_call x1, Pallas kernels, run_layer(): pl.pallas_call(functools.partial(layer_kernel, micro, own, [p.shape[0] fo...  57.5 us
    ppermute x3, waiting for transfers between devices, reduce_and_step(): lax.ppermute(t[part], 'rep', [(0, 1), (3, 2)])  24.8 us
    ppermute x3, waiting for transfers between devices, reduce_and_step(): lax.ppermute(t, 'fsdp', far_pairs)  22.6 us
    ppermute x1, waiting for transfers between devices, gather_pieces(): last_near = lax.ppermute(weights[half:].astype(BF16), 'fsdp', near_pairs)  21.3 us
    pallas_call x3, Pallas kernels, adam_blocks(): pl.pallas_call(functools.partial(adam_kernel, steps), grid=(sum(steps),),...  21.1 us
    ppermute x1, waiting for transfers between devices, gather_pieces(): first_near = lax.ppermute(weights[:half].astype(BF16), 'fsdp', near_pairs)  19.8 us
    ppermute x5, starting transfers between devices, reduce_and_step(): lax.ppermute(gain, axis, pairs)  18.5 us
    ppermute x3, starting transfers between devices, reduce_and_step(): lax.ppermute(t[part], 'rep', [(0, 1), (3, 2)])  12.9 us
  transfers between devices with their start and end apart: 32, of which 16 were waited for; matrix products, arithmetic and copies ran while one was open for 4% of the time, Pallas kernels for 5%

profile of v8, /device:TPU:0, one launch (start us, length us, event | category | flops | bytes accessed | tf_op | source)
XLA Modules:
  0.0 275.9 jit_solution(15812247661677314332)
XLA Ops:
  0.6 2.2 convert_element_type.180.rest_0_
  2.9 3.0 %collective-permute-start.5 = (bf16[14,256,256]{2,1,0:T(8,128)(2,1)S(1)}, bf16[14,256,256]{2,1,0:T(8,128)(2,1)}, u32[]{:S(2)}, u32[]{:S(2)}) collective-permute-start(bf16[14,256,256]{2,1,0:T(8,128)(2,1)S(1)} %convert_element_type.180.rest_0_), channel_id=1, source_target_pairs={{0,16},{4,12},{8,24},{12,4},{16,0},{20,28},{24,8},{28,20},{1,17},{... | collective-permute-start | bytes 5505032 | tf_op jit(solution)/shard_map/ppermute | solution.py:673
  6.1 1.6 collective-permute-start.2
  8.2 21.3 %collective-permute-done.2.rest_3_ = bf16[7,256,256]{2,1,0:T(8,128)(2,1)S(1)} collective-permute-done((bf16[7,256,256]{2,1,0:T(8,128)(2,1)S(1)}, bf16[7,256,256]{2,1,0:T(8,128)(2,1)S(1)}, u32[]{:S(2)}, u32[]{:S(2)}) %collective-permute-start.2) | collective-permute-done | bytes 917536 | tf_op jit(solution)/shard_map/ppermute | solution.py:672
  29.4 19.8 %collective-permute-done.1.rest_2_ = bf16[7,256,256]{2,1,0:T(8,128)(2,1)} collective-permute-done((bf16[7,256,256]{2,1,0:T(8,128)(2,1)S(1)}, bf16[7,256,256]{2,1,0:T(8,128)(2,1)}, u32[]{:S(2)}, u32[]{:S(2)}) %collective-permute-start.1) | collective-permute-done | bytes 917536 | tf_op jit(solution)/shard_map/ppermute | solution.py:671
  49.7 7.0 %collective-permute-done.8.rest_9_ = bf16[7,256,256]{2,1,0:T(8,128)(2,1)} collective-permute-done((bf16[7,256,256]{2,1,0:T(8,128)(2,1)S(1)}, bf16[7,256,256]{2,1,0:T(8,128)(2,1)}, u32[]{:S(2)}, u32[]{:S(2)}) %collective-permute-start.8) | collective-permute-done | bytes 917536 | tf_op jit(solution)/shard_map/ppermute | solution.py:675
  57.3 9.3 %collective-permute-done.7.rest_8_ = bf16[7,256,256]{2,1,0:T(8,128)(2,1)} collective-permute-done((bf16[7,256,256]{2,1,0:T(8,128)(2,1)}, bf16[7,256,256]{2,1,0:T(8,128)(2,1)}, u32[]{:S(2)}, u32[]{:S(2)}) %collective-permute-start.7) | collective-permute-done | bytes 917536 | tf_op jit(solution)/shard_map/ppermute | solution.py:674
  66.6 0.8 copy.35
  67.5 0.6 concatenate.7.slot_ref
  68.2 0.6 select_reduce_fusion.base_ref
  69.4 57.5 %layer.1 = (bf16[512,768]{1,0:T(8,128)(2,1)}, bf16[512,768]{1,0:T(8,128)(2,1)}, f32[2,768]{1,0:T(2,128)}, bf16[16,256,256]{2,1,0:T(8,128)(2,1)}, bf16[16,256,256...) custom-call(s32[108]{0:T(128)} %index_ref.1, s32[8]{0:T(128)} %select_reduce_fusion.base_ref, ...), custom_call_target="tpu_custom_call" | custom-call | flops 23000000512 | bytes 32000000 | tf_op jit(solution)/shard_map/layer/pallas_call | solution.py:479
  127.2 4.2 %collective-permute-done.11 = bf16[16,256,256]{2,1,0:T(8,128)(2,1)S(1)} collective-permute-done((bf16[16,256,256]{2,1,0:T(8,128)(2,1)}, bf16[16,256,256]{2,1,0:T(8,128)(2,1)S(1)}, u32[]{:S(2)}, u32[]{:S(2)}) %collective-permute-start.11) | collective-permute-done | bytes 2097184 | tf_op jit(solution)/shard_map/ppermute | solution.py:647
  131.4 1.5 add_convert_fusion.1
  133.2 1.1 collective-permute-start.14
  134.3 7.6 %collective-permute-done.12 = bf16[40,256,256]{2,1,0:T(8,128)(2,1)S(1)} collective-permute-done((bf16[40,256,256]{2,1,0:T(8,128)(2,1)}, bf16[40,256,256]{2,1,0:T(8,128)(2,1)S(1)}, u32[]{:S(2)}, u32[]{:S(2)}) %collective-permute-start.12) | collective-permute-done | bytes 5242912 | tf_op jit(solution)/shard_map/ppermute | solution.py:647
  141.9 2.7 add_convert_fusion
  144.6 1.2 collective-permute-start.13
  145.8 1.8 collective-permute-start.15
  147.5 2.0 collective-permute-done.15
  149.8 1.8 collective-permute-start.16
  151.6 13.1 %collective-permute-done.16 = bf16[1024,256]{1,0:T(8,128)(2,1)S(1)} collective-permute-done((bf16[1024,256]{1,0:T(8,128)(2,1)S(1)}, bf16[1024,256]{1,0:T(8,128)(2,1)S(1)}, u32[]{:S(2)}, u32[]{:S(2)}) %collective-permute-start.16) | collective-permute-done | bytes 524320 | tf_op jit(solution)/shard_map/ppermute | solution.py:800
  165.1 3.7 %collective-permute-start.17 = (bf16[1024,256]{1,0:T(8,128)(2,1)S(1)}, bf16[1024,256]{1,0:T(8,128)(2,1)S(1)}, u32[]{:S(2)}, u32[]{:S(2)}) collective-permute-start(bf16[1024,256]{1,0:T(8,128)(2,1)S(1)} %fusion.7), channel_id=1, source_target_pairs={{0,1},{3,2},{4,5},{7,6},{8,9},{11,10},{12,13},{15,14},{16,17},{19,... | collective-permute-start | bytes 1572872 | tf_op jit(solution)/shard_map/ppermute | solution.py:825
  168.8 10.0 %collective-permute-done.17 = bf16[1024,256]{1,0:T(8,128)(2,1)S(1)} collective-permute-done((bf16[1024,256]{1,0:T(8,128)(2,1)S(1)}, bf16[1024,256]{1,0:T(8,128)(2,1)S(1)}, u32[]{:S(2)}, u32[]{:S(2)}) %collective-permute-start.17) | collective-permute-done | bytes 524320 | tf_op jit(solution)/shard_map/ppermute | solution.py:825
  179.0 0.7 collective-permute-start.20
  179.7 2.3 collective-permute-done.13
  182.4 2.0 collective-permute-start.19
  184.9 9.5 %collective-permute-done.19 = bf16[1536,256]{1,0:T(8,128)(2,1)S(1)} collective-permute-done((bf16[1536,256]{1,0:T(8,128)(2,1)S(1)}, bf16[1536,256]{1,0:T(8,128)(2,1)S(1)}, u32[]{:S(2)}, u32[]{:S(2)}) %collective-permute-start.19) | collective-permute-done | bytes 786464 | tf_op jit(solution)/shard_map/ppermute | solution.py:800
  194.9 4.9 %collective-permute-start.25 = (bf16[1536,256]{1,0:T(8,128)(2,1)S(1)}, bf16[1536,256]{1,0:T(8,128)(2,1)S(1)}, u32[]{:S(2)}, u32[]{:S(2)}) collective-permute-start(bf16[1536,256]{1,0:T(8,128)(2,1)S(1)} %fusion.1), channel_id=1, source_target_pairs={{0,1},{3,2},{4,5},{7,6},{8,9},{11,10},{12,13},{15,14},{16,17},{19,... | collective-permute-start | bytes 2359304 | tf_op jit(solution)/shard_map/ppermute | solution.py:825
  199.9 0.9 collective-permute-start.22
  200.8 1.3 collective-permute-start.24
  202.4 1.2 collective-permute-done.22
  203.6 4.2 %collective-permute-start.21 = (bf16[1024,256]{1,0:T(8,128)(2,1)S(1)}, bf16[1024,256]{1,0:T(8,128)(2,1)S(1)}, u32[]{:S(2)}, u32[]{:S(2)}) collective-permute-start(bf16[1024,256]{1,0:T(8,128)(2,1)S(1)} %fusion.4), channel_id=1, source_target_pairs={{0,1},{3,2},{4,5},{7,6},{8,9},{11,10},{12,13},{15,14},{16,17},{19,... | collective-permute-start | bytes 1572872 | tf_op jit(solution)/shard_map/ppermute | solution.py:825
  207.8 10.0 %collective-permute-done.25 = bf16[1536,256]{1,0:T(8,128)(2,1)S(1)} collective-permute-done((bf16[1536,256]{1,0:T(8,128)(2,1)S(1)}, bf16[1536,256]{1,0:T(8,128)(2,1)S(1)}, u32[]{:S(2)}, u32[]{:S(2)}) %collective-permute-start.25) | collective-permute-done | bytes 786464 | tf_op jit(solution)/shard_map/ppermute | solution.py:825
  218.0 0.7 collective-permute-start.27
  218.8 1.9 broadcast_select_fusion.2.rest_0_
  220.7 4.8 %collective-permute-done.21 = bf16[1024,256]{1,0:T(8,128)(2,1)S(1)} collective-permute-done((bf16[1024,256]{1,0:T(8,128)(2,1)S(1)}, bf16[1024,256]{1,0:T(8,128)(2,1)S(1)}, u32[]{:S(2)}, u32[]{:S(2)}) %collective-permute-start.21) | collective-permute-done | bytes 524320 | tf_op jit(solution)/shard_map/ppermute | solution.py:825
  225.7 0.7 collective-permute-start.26
  226.6 1.3 collective-permute-start.30
  227.9 15.0 %collective-permute-start.29 = (f32[2,768]{1,0:T(2,128)S(1)}, f32[2,768]{1,0:T(2,128)S(1)}, u32[]{:S(2)}, u32[]{:S(2)}) collective-permute-start(f32[2,768]{1,0:T(2,128)S(1)} %add.304), channel_id=1, source_target_pairs={{0,1},{1,0},{2,3},{3,2},{4,5},{5,4},{6,7},{7,6},{8,9},{9,8},{10,11... | collective-permute-start | bytes 18440 | tf_op jit(solution)/shard_map/ppermute | solution.py:864
  242.9 6.3 %adam.3 = (f32[14,256,256]{2,1,0:T(8,128)}, f32[14,256,256]{2,1,0:T(8,128)}, f32[14,256,256]{2,1,0:T(8,128)}, f32[14,256,256]{2,1,0:T(8,128)}, bf16[14,256,256]{2,1,0:T(8,128)(2,1)}) custom-call(f32[14,256,256]{2,1,0:T(8,128)} %weight_ref.5, f32[14,256,256]{2,1,0:T(8,128)} %first_ref.5, f32[14,256,256]{2,1,0:T(8,128)} %second_ref.5, ...), custom_call_target="tpu_custom_call" | custom-call | flops 805306368 | bytes 11010048 | tf_op jit(solution)/shard_map/adam/pallas_call | solution.py:598
  249.3 1.3 collective-permute-start.28
  250.6 7.1 %collective-permute-done.30 = bf16[1536,256]{1,0:T(8,128)(2,1)S(1)} collective-permute-done((bf16[1536,256]{1,0:T(8,128)(2,1)S(1)}, bf16[1536,256]{1,0:T(8,128)(2,1)S(1)}, u32[]{:S(2)}, u32[]{:S(2)}) %collective-permute-start.30) | collective-permute-done | bytes 786464 | tf_op jit(solution)/shard_map/ppermute | solution.py:838
  257.8 1.0 broadcast_select_fusion.rest_0_
  258.8 0.8 collective-permute-start.31
  259.6 8.5 %adam.4 = (f32[14,256,256]{2,1,0:T(8,128)}, f32[14,256,256]{2,1,0:T(8,128)}, f32[14,256,256]{2,1,0:T(8,128)}, f32[14,256,256]{2,1,0:T(8,128)}, bf16[14,256,256]{2,1,0:T(8,128)(2,1)}) custom-call(f32[14,256,256]{2,1,0:T(8,128)} %weight_ref.5, ...), custom_call_target="tpu_custom_call", output_to_operand_aliasing={{0}: (6, {}), {1}: (7, {}), {2}: (8, {}), {3}: (9, {}), {4}... | custom-call | flops 1207959552 | bytes 16515072 | tf_op jit(solution)/shard_map/adam/pallas_call | solution.py:598
  268.1 0.6 multiply_subtract_fusion
  268.7 0.9 broadcast_select_fusion.1.rest_0_
  269.6 6.3 %adam.5 = (f32[14,256,256]{2,1,0:T(8,128)}, f32[14,256,256]{2,1,0:T(8,128)}, f32[14,256,256]{2,1,0:T(8,128)}, f32[14,256,256]{2,1,0:T(8,128)}, bf16[14,256,256]{2,1,0:T(8,128)(2,1)}) custom-call(f32[14,256,256]{2,1,0:T(8,128)} %weight_ref.5, ...), custom_call_target="tpu_custom_call", output_to_operand_aliasing={{0}: (6, {}), {1}: (7, {}), {2}: (8, {}), {3}: (9, {}), {4}... | custom-call | flops 805306368 | bytes 11010048 | tf_op jit(solution)/shard_map/adam/pallas_call | solution.py:598
  (84 shorter events, 6.0 us)
Async XLA Ops:
  2.9 66.5 %copy-start = (bf16[14,256,256]{2,1,0:T(8,128)(2,1)}, bf16[14,256,256]{2,1,0:T(8,128)(2,1)S(1)}, u32[]{:S(2)}) copy-start(bf16[14,256,256]{2,1,0:T(8,128)(2,1)S(1)} %convert_element_type.180.rest_0_) | copy-start | bytes 5505028
  2.9 63.7 %copy-start.6 = (s32[2,256]{1,0:T(2,128)S(1)}, s32[2,256]{1,0:T(2,128)}, u32[]{:S(2)}) copy-start(s32[2,256]{1,0:T(2,128)} %segments_ref.1) | copy-start | bytes 6148
  2.9 46.3 %collective-permute-start.5 = (bf16[14,256,256]{2,1,0:T(8,128)(2,1)S(1)}, bf16[14,256,256]{2,1,0:T(8,128)(2,1)}, u32[]{:S(2)}, u32[]{:S(2)}) collective-permute-start(bf16[14,256,256]{2,1,0:T(8,128)(2,1)S(1)} %convert_element_type.180.rest_0_), channel_id=1, source_target_pairs={{0,16},{4,12},{8,24},{12,4},{16,0},{20,28},{24,8},{28,20},{1,17},{... | collective-permute-start | bytes 5505032 | tf_op jit(solution)/shard_map/ppermute | solution.py:673
  6.1 23.4 %collective-permute-start.2 = (bf16[7,256,256]{2,1,0:T(8,128)(2,1)S(1)}, bf16[7,256,256]{2,1,0:T(8,128)(2,1)S(1)}, u32[]{:S(2)}, u32[]{:S(2)}) collective-permute-start(bf16[7,256,256]{2,1,0:T(8,128)(2,1)S(1)} %get-tuple-element.206), channel_id=1, source_target_pairs={{0,8},{4,20},{8,0},{12,28},{16,24},{20,4},{24,16},{28,12},{1,9},{5... | collective-permute-start | bytes 2752520 | tf_op jit(solution)/shard_map/ppermute | solution.py:672
  7.6 41.5 %collective-permute-start.1 = (bf16[7,256,256]{2,1,0:T(8,128)(2,1)S(1)}, bf16[7,256,256]{2,1,0:T(8,128)(2,1)}, u32[]{:S(2)}, u32[]{:S(2)}) collective-permute-start(bf16[7,256,256]{2,1,0:T(8,128)(2,1)S(1)} %get-tuple-element.207), channel_id=1, source_target_pairs={{0,8},{4,20},{8,0},{12,28},{16,24},{20,4},{24,16},{28,12},{1,9},{5... | collective-permute-start | bytes 2752520 | tf_op jit(solution)/shard_map/ppermute | solution.py:671
  29.4 40.0 %copy-start.7 = (bf16[7,256,256]{2,1,0:T(8,128)(2,1)}, bf16[7,256,256]{2,1,0:T(8,128)(2,1)S(1)}, u32[]{:S(2)}) copy-start(bf16[7,256,256]{2,1,0:T(8,128)(2,1)S(1)} %collective-permute-done.2.rest_3_) | copy-start | bytes 2752516
  29.4 27.3 %collective-permute-start.8 = (bf16[7,256,256]{2,1,0:T(8,128)(2,1)S(1)}, bf16[7,256,256]{2,1,0:T(8,128)(2,1)}, u32[]{:S(2)}, u32[]{:S(2)}) collective-permute-start(bf16[7,256,256]{2,1,0:T(8,128)(2,1)S(1)} %collective-permute-done.2.rest_3_), channel_id=1, source_target_pairs={{0,16},{4,12},{8,24},{12,4},{16,0},{20,28},{24,8},{28,20},{1,17},{... | collective-permute-start | bytes 2752520 | tf_op jit(solution)/shard_map/ppermute | solution.py:675
  29.4 27.3 %collective-permute-start.4 = (bf16[7,256,256]{2,1,0:T(8,128)(2,1)S(1)}, bf16[7,256,256]{2,1,0:T(8,128)(2,1)}, u32[]{:S(2)}, u32[]{:S(2)}) collective-permute-start(bf16[7,256,256]{2,1,0:T(8,128)(2,1)S(1)} %collective-permute-done.2.rest_3_), channel_id=1, source_target_pairs={{0,4},{4,0},{8,12},{12,8},{16,20},{20,16},{24,28},{28,24},{1,5},{5... | collective-permute-start | bytes 2752520 | tf_op jit(solution)/shard_map/ppermute | solution.py:647
  49.2 17.4 %collective-permute-start.7 = (bf16[7,256,256]{2,1,0:T(8,128)(2,1)}, bf16[7,256,256]{2,1,0:T(8,128)(2,1)}, u32[]{:S(2)}, u32[]{:S(2)}) collective-permute-start(bf16[7,256,256]{2,1,0:T(8,128)(2,1)} %collective-permute-done.1.rest_2_), channel_id=1, source_target_pairs={{0,16},{4,12},{8,24},{12,4},{16,0},{20,28},{24,8},{28,20},{1,17},{... | collective-permute-start | bytes 2752520 | tf_op jit(solution)/shard_map/ppermute | solution.py:674
  49.2 19.6 %collective-permute-start = (bf16[14,256,256]{2,1,0:T(8,128)(2,1)S(1)}, bf16[14,256,256]{2,1,0:T(8,128)(2,1)}, u32[]{:S(2)}, u32[]{:S(2)}) collective-permute-start(bf16[14,256,256]{2,1,0:T(8,128)(2,1)S(1)} %convert_element_type.180.rest_0_), channel_id=1, source_target_pairs={{0,4},{4,0},{8,12},{12,8},{16,20},{20,16},{24,28},{28,24},{1,5},{5... | collective-permute-start | bytes 5505032 | tf_op jit(solution)/shard_map/ppermute | solution.py:647
  49.2 20.2 %collective-permute-start.6 = (bf16[14,256,256]{2,1,0:T(8,128)(2,1)}, bf16[14,256,256]{2,1,0:T(8,128)(2,1)}, u32[]{:S(2)}, u32[]{:S(2)}) collective-permute-start(bf16[14,256,256]{2,1,0:T(8,128)(2,1)} %collective-permute-done.5.rest_6_), channel_id=1, source_target_pairs={{0,4},{4,0},{8,12},{12,8},{16,20},{20,16},{24,28},{28,24},{1,5},{5... | collective-permute-start | bytes 5505032 | tf_op jit(solution)/shard_map/ppermute | solution.py:647
  56.8 12.0 %collective-permute-start.3 = (bf16[7,256,256]{2,1,0:T(8,128)(2,1)}, bf16[7,256,256]{2,1,0:T(8,128)(2,1)}, u32[]{:S(2)}, u32[]{:S(2)}) collective-permute-start(bf16[7,256,256]{2,1,0:T(8,128)(2,1)} %collective-permute-done.1.rest_2_), channel_id=1, source_target_pairs={{0,4},{4,0},{8,12},{12,8},{16,20},{20,16},{24,28},{28,24},{1,5},{5... | collective-permute-start | bytes 2752520 | tf_op jit(solution)/shard_map/ppermute | solution.py:647
  56.8 12.0 %collective-permute-start.10 = (bf16[7,256,256]{2,1,0:T(8,128)(2,1)}, bf16[7,256,256]{2,1,0:T(8,128)(2,1)}, u32[]{:S(2)}, u32[]{:S(2)}) collective-permute-start(bf16[7,256,256]{2,1,0:T(8,128)(2,1)} %collective-permute-done.8.rest_9_), channel_id=1, source_target_pairs={{0,4},{4,0},{8,12},{12,8},{16,20},{20,16},{24,28},{28,24},{1,5},{5... | collective-permute-start | bytes 2752520 | tf_op jit(solution)/shard_map/ppermute | solution.py:647
  66.6 2.8 %collective-permute-start.9 = (bf16[7,256,256]{2,1,0:T(8,128)(2,1)}, bf16[7,256,256]{2,1,0:T(8,128)(2,1)}, u32[]{:S(2)}, u32[]{:S(2)}) collective-permute-start(bf16[7,256,256]{2,1,0:T(8,128)(2,1)} %collective-permute-done.7.rest_8_), channel_id=1, source_target_pairs={{0,4},{4,0},{8,12},{12,8},{16,20},{20,16},{24,28},{28,24},{1,5},{5... | collective-permute-start | bytes 2752520 | tf_op jit(solution)/shard_map/ppermute | solution.py:647
  127.0 4.4 %collective-permute-start.11 = (bf16[16,256,256]{2,1,0:T(8,128)(2,1)}, bf16[16,256,256]{2,1,0:T(8,128)(2,1)S(1)}, u32[]{:S(2)}, u32[]{:S(2)}) collective-permute-start(bf16[16,256,256]{2,1,0:T(8,128)(2,1)} %get-tuple-element.112), channel_id=1, source_target_pairs={{0,4},{4,0},{8,12},{12,8},{16,20},{20,16},{24,28},{28,24},{1,5},{5... | collective-permute-start | bytes 6291464 | tf_op jit(solution)/shard_map/ppermute | solution.py:647
  132.9 12.8 %copy-start.5 = (f32[2,768]{1,0:T(2,128)S(1)}, f32[2,768]{1,0:T(2,128)}, u32[]{:S(2)}) copy-start(f32[2,768]{1,0:T(2,128)} %get-tuple-element.120) | copy-start | bytes 18436
  132.9 16.6 %copy-start.1 = (bf16[16,256,256]{2,1,0:T(8,128)(2,1)S(1)}, bf16[16,256,256]{2,1,0:T(8,128)(2,1)}, u32[]{:S(2)}) copy-start(bf16[16,256,256]{2,1,0:T(8,128)(2,1)} %get-tuple-element.126) | copy-start | bytes 6291460
  132.9 8.9 %collective-permute-start.12 = (bf16[40,256,256]{2,1,0:T(8,128)(2,1)}, bf16[40,256,256]{2,1,0:T(8,128)(2,1)S(1)}, u32[]{:S(2)}, u32[]{:S(2)}) collective-permute-start(bf16[40,256,256]{2,1,0:T(8,128)(2,1)} %get-tuple-element.115), channel_id=1, source_target_pairs={{0,4},{4,0},{8,12},{12,8},{16,20},{20,16},{24,28},{28,24},{1,5},{5... | collective-permute-start | bytes 15728648 | tf_op jit(solution)/shard_map/ppermute | solution.py:647
  133.2 16.4 %collective-permute-start.14 = (bf16[2048,256]{1,0:T(8,128)(2,1)S(1)}, bf16[2048,256]{1,0:T(8,128)(2,1)S(1)}, u32[]{:S(2)}, u32[]{:S(2)}) collective-permute-start(bf16[2048,256]{1,0:T(8,128)(2,1)S(1)} %bitcast.40), channel_id=1, source_target_pairs={{0,8},{4,20},{8,0},{12,28},{16,24},{20,4},{24,16},{28,12},{1,9},{5... | collective-permute-start | bytes 3145736 | tf_op jit(solution)/shard_map/ppermute | solution.py:782
  141.9 40.1 %slice-start = ((s8[5242880]{0:T(1024)(128)(4,1)}), s8[1048576]{0:T(1024)(128)(4,1)S(1)}, s32[]{:S(2)}) async-start(s8[5242880]{0:T(1024)(128)(4,1)} %bitcast.37), calls=%async_computation | async-start | bytes 2097152
  144.6 37.4 %collective-permute-start.13 = (bf16[5120,256]{1,0:T(8,128)(2,1)S(1)}, bf16[5120,256]{1,0:T(8,128)(2,1)S(1)}, u32[]{:S(2)}, u32[]{:S(2)}) collective-permute-start(bf16[5120,256]{1,0:T(8,128)(2,1)S(1)} %bitcast.39), channel_id=1, source_target_pairs={{0,8},{4,20},{8,0},{12,28},{16,24},{20,4},{24,16},{28,12},{1,9},{5... | collective-permute-start | bytes 7864328 | tf_op jit(solution)/shard_map/ppermute | solution.py:782
  145.8 3.8 %collective-permute-start.15 = (f32[2,768]{1,0:T(2,128)S(1)}, f32[2,768]{1,0:T(2,128)S(1)}, u32[]{:S(2)}, u32[]{:S(2)}) collective-permute-start(f32[2,768]{1,0:T(2,128)S(1)} %copy-done.5), channel_id=1, source_target_pairs={{0,16},{4,12},{8,24},{12,4},{16,0},{20,28},{24,8},{28,20},{1,17},{... | collective-permute-start | bytes 18440 | tf_op jit(solution)/shard_map/ppermute | solution.py:864
  149.5 32.5 %slice-start.1 = ((s8[5242880]{0:T(1024)(128)(4,1)}), s8[4194304]{0:T(1024)(128)(4,1)S(1)}, s32[]{:S(2)}) async-start(s8[5242880]{0:T(1024)(128)(4,1)} %bitcast.37), calls=%async_computation.1 | async-start | bytes 8388608
  149.8 14.9 %collective-permute-start.16 = (bf16[1024,256]{1,0:T(8,128)(2,1)S(1)}, bf16[1024,256]{1,0:T(8,128)(2,1)S(1)}, u32[]{:S(2)}, u32[]{:S(2)}) collective-permute-start(bf16[1024,256]{1,0:T(8,128)(2,1)S(1)} %fusion.8), channel_id=1, source_target_pairs={{0,16},{4,12},{8,24},{12,4},{16,0},{20,28},{24,8},{28,20},{1,17},{... | collective-permute-start | bytes 1572872 | tf_op jit(solution)/shard_map/ppermute | solution.py:800
  165.1 13.8 %collective-permute-start.17 = (bf16[1024,256]{1,0:T(8,128)(2,1)S(1)}, bf16[1024,256]{1,0:T(8,128)(2,1)S(1)}, u32[]{:S(2)}, u32[]{:S(2)}) collective-permute-start(bf16[1024,256]{1,0:T(8,128)(2,1)S(1)} %fusion.7), channel_id=1, source_target_pairs={{0,1},{3,2},{4,5},{7,6},{8,9},{11,10},{12,13},{15,14},{16,17},{19,... | collective-permute-start | bytes 1572872 | tf_op jit(solution)/shard_map/ppermute | solution.py:825
  179.0 5.7 %collective-permute-start.20 = (bf16[1024,256]{1,0:T(8,128)(2,1)S(1)}, bf16[1024,256]{1,0:T(8,128)(2,1)S(1)}, u32[]{:S(2)}, u32[]{:S(2)}) collective-permute-start(bf16[1024,256]{1,0:T(8,128)(2,1)S(1)} %add_convert_fusion.7), channel_id=1, source_target_pairs={{1,2},{2,1},{5,6},{6,5},{9,10},{10,9},{13,14},{14,13},{17,18},{18,... | collective-permute-start | bytes 1572872 | tf_op jit(solution)/shard_map/ppermute | solution.py:833
  182.4 12.1 %collective-permute-start.19 = (bf16[1536,256]{1,0:T(8,128)(2,1)S(1)}, bf16[1536,256]{1,0:T(8,128)(2,1)S(1)}, u32[]{:S(2)}, u32[]{:S(2)}) collective-permute-start(bf16[1536,256]{1,0:T(8,128)(2,1)S(1)} %fusion.2), channel_id=1, source_target_pairs={{0,16},{4,12},{8,24},{12,4},{16,0},{20,28},{24,8},{28,20},{1,17},{... | collective-permute-start | bytes 2359304 | tf_op jit(solution)/shard_map/ppermute | solution.py:800
  184.7 17.4 %collective-permute-start.18 = (bf16[1024,256]{1,0:T(8,128)(2,1)S(1)}, bf16[1024,256]{1,0:T(8,128)(2,1)S(1)}, u32[]{:S(2)}, u32[]{:S(2)}) collective-permute-start(bf16[1024,256]{1,0:T(8,128)(2,1)S(1)} %fusion.5), channel_id=1, source_target_pairs={{0,16},{4,12},{8,24},{12,4},{16,0},{20,28},{24,8},{28,20},{1,17},{... | collective-permute-start | bytes 1572872 | tf_op jit(solution)/shard_map/ppermute | solution.py:800
  194.9 22.9 %collective-permute-start.25 = (bf16[1536,256]{1,0:T(8,128)(2,1)S(1)}, bf16[1536,256]{1,0:T(8,128)(2,1)S(1)}, u32[]{:S(2)}, u32[]{:S(2)}) collective-permute-start(bf16[1536,256]{1,0:T(8,128)(2,1)S(1)} %fusion.1), channel_id=1, source_target_pairs={{0,1},{3,2},{4,5},{7,6},{8,9},{11,10},{12,13},{15,14},{16,17},{19,... | collective-permute-start | bytes 2359304 | tf_op jit(solution)/shard_map/ppermute | solution.py:825
  199.9 3.7 %collective-permute-start.22 = (f32[2,768]{1,0:T(2,128)S(1)}, f32[2,768]{1,0:T(2,128)S(1)}, u32[]{:S(2)}, u32[]{:S(2)}) collective-permute-start(f32[2,768]{1,0:T(2,128)S(1)} %add.278), channel_id=1, source_target_pairs={{0,8},{4,20},{8,0},{12,28},{16,24},{20,4},{24,16},{28,12},{1,9},{5... | collective-permute-start | bytes 18440 | tf_op jit(solution)/shard_map/ppermute | solution.py:864
  200.8 18.0 %collective-permute-start.24 = (bf16[1024,256]{1,0:T(8,128)(2,1)S(1)}, bf16[1024,256]{1,0:T(8,128)(2,1)}, u32[]{:S(2)}, u32[]{:S(2)}) collective-permute-start(bf16[1024,256]{1,0:T(8,128)(2,1)S(1)} %add_convert_fusion.6), channel_id=1, source_target_pairs={{1,0},{2,3},{5,4},{6,7},{9,8},{10,11},{13,12},{14,15},{17,16},{18,... | collective-permute-start | bytes 1572872 | tf_op jit(solution)/shard_map/ppermute | solution.py:838
  203.6 22.0 %collective-permute-start.21 = (bf16[1024,256]{1,0:T(8,128)(2,1)S(1)}, bf16[1024,256]{1,0:T(8,128)(2,1)S(1)}, u32[]{:S(2)}, u32[]{:S(2)}) collective-permute-start(bf16[1024,256]{1,0:T(8,128)(2,1)S(1)} %fusion.4), channel_id=1, source_target_pairs={{0,1},{3,2},{4,5},{7,6},{8,9},{11,10},{12,13},{15,14},{16,17},{19,... | collective-permute-start | bytes 1572872 | tf_op jit(solution)/shard_map/ppermute | solution.py:825
  218.0 8.4 %collective-permute-start.27 = (bf16[1536,256]{1,0:T(8,128)(2,1)S(1)}, bf16[1536,256]{1,0:T(8,128)(2,1)S(1)}, u32[]{:S(2)}, u32[]{:S(2)}) collective-permute-start(bf16[1536,256]{1,0:T(8,128)(2,1)S(1)} %add_convert_fusion.3), channel_id=1, source_target_pairs={{1,2},{2,1},{5,6},{6,5},{9,10},{10,9},{13,14},{14,13},{17,18},{18,... | collective-permute-start | bytes 2359304 | tf_op jit(solution)/shard_map/ppermute | solution.py:833
  218.7 2.0 collective-permute-start.23
  225.7 23.5 %collective-permute-start.26 = (bf16[1024,256]{1,0:T(8,128)(2,1)S(1)}, bf16[1024,256]{1,0:T(8,128)(2,1)S(1)}, u32[]{:S(2)}, u32[]{:S(2)}) collective-permute-start(bf16[1024,256]{1,0:T(8,128)(2,1)S(1)} %add_convert_fusion.5), channel_id=1, source_target_pairs={{1,2},{2,1},{5,6},{6,5},{9,10},{10,9},{13,14},{14,13},{17,18},{18,... | collective-permute-start | bytes 1572872 | tf_op jit(solution)/shard_map/ppermute | solution.py:833
  226.6 31.2 %collective-permute-start.30 = (bf16[1536,256]{1,0:T(8,128)(2,1)S(1)}, bf16[1536,256]{1,0:T(8,128)(2,1)S(1)}, u32[]{:S(2)}, u32[]{:S(2)}) collective-permute-start(bf16[1536,256]{1,0:T(8,128)(2,1)S(1)} %add_convert_fusion.2), channel_id=1, source_target_pairs={{1,0},{2,3},{5,4},{6,7},{9,8},{10,11},{13,12},{14,15},{17,16},{18,... | collective-permute-start | bytes 2359304 | tf_op jit(solution)/shard_map/ppermute | solution.py:838
  227.9 30.9 %collective-permute-start.29 = (f32[2,768]{1,0:T(2,128)S(1)}, f32[2,768]{1,0:T(2,128)S(1)}, u32[]{:S(2)}, u32[]{:S(2)}) collective-permute-start(f32[2,768]{1,0:T(2,128)S(1)} %add.304), channel_id=1, source_target_pairs={{0,1},{1,0},{2,3},{3,2},{4,5},{5,4},{6,7},{7,6},{8,9},{9,8},{10,11... | collective-permute-start | bytes 18440 | tf_op jit(solution)/shard_map/ppermute | solution.py:864
  249.3 19.4 %collective-permute-start.28 = (bf16[1024,256]{1,0:T(8,128)(2,1)S(1)}, bf16[1024,256]{1,0:T(8,128)(2,1)S(1)}, u32[]{:S(2)}, u32[]{:S(2)}) collective-permute-start(bf16[1024,256]{1,0:T(8,128)(2,1)S(1)} %add_convert_fusion.4), channel_id=1, source_target_pairs={{1,0},{2,3},{5,4},{6,7},{9,8},{10,11},{13,12},{14,15},{17,16},{18,... | collective-permute-start | bytes 1572872 | tf_op jit(solution)/shard_map/ppermute | solution.py:838
  258.8 9.3 %collective-permute-start.31 = (f32[2,768]{1,0:T(2,128)S(1)}, f32[2,768]{1,0:T(2,128)S(1)}, u32[]{:S(2)}, u32[]{:S(2)}) collective-permute-start(f32[2,768]{1,0:T(2,128)S(1)} %add.308), channel_id=1, source_target_pairs={{0,2},{1,3},{2,0},{3,1},{4,6},{5,7},{6,4},{7,5},{8,10},{9,11},{10,... | collective-permute-start | bytes 18440 | tf_op jit(solution)/shard_map/ppermute | solution.py:864
  259.6 8.5 %copy-start.2 = (f32[2,768]{1,0:T(2,128)S(1)}, f32[2,768]{1,0:T(2,128)}, u32[]{:S(2)}) copy-start(f32[2,768]{1,0:T(2,128)} %gains_ref.1) | copy-start | bytes 18436
  259.6 8.5 %copy-start.3 = (f32[2,768]{1,0:T(2,128)S(1)}, f32[2,768]{1,0:T(2,128)}, u32[]{:S(2)}) copy-start(f32[2,768]{1,0:T(2,128)} %param.25) | copy-start | bytes 18436
  259.6 8.5 %copy-start.4 = (f32[2,768]{1,0:T(2,128)S(1)}, f32[2,768]{1,0:T(2,128)}, u32[]{:S(2)}) copy-start(f32[2,768]{1,0:T(2,128)} %param.24) | copy-start | bytes 18436
